TPU v7x, 32 devices: a whole 2x2x4 slice. The times are simulated.
32 devices in a mesh: dp: 8 (over z, y), mp: 4 (over x, core).
Axes of the slice: x: 2, y: 2, z: 4, core: 2. Of those that a mesh axis runs over, the one named last changes fastest.
Arguments:
- latents: bfloat16 [16, 256, 1152], P('dp', None, 'mp'), may hold values from -6 to 6
- condition: bfloat16 [16, 1152], P('dp'), may hold values from -6 to 6
- noise_bins: int32 [16], P('dp'), may hold values from 0 to 7
- slot_valid: int32 [16], P('dp'), may hold values from 0 to 1, as said below
- ada_weight: bfloat16 [1152, 6, 1152], P('dp', None, 'mp'), may hold values from -0.1875 to 0.1875
- ada_bias: float32 [6, 1152], P(None, 'mp'), may hold values from -3 to 3
- qkv_weight: bfloat16 [1152, 3, 1152], P('dp', None, 'mp'), may hold values from -0.1875 to 0.1875
- query_gain: float32 [72], replicated, may hold values from 1 to 1.6
- key_gain: float32 [72], replicated, may hold values from 1 to 1.6
- out_weight: bfloat16 [1152, 1152], P('mp', 'dp'), may hold values from -0.75 to 0.75
- gate_up: bfloat16 [1152, 2, 3072], P('dp', None, 'mp'), may hold values from -0.1875 to 0.1875
- down_weight: bfloat16 [3072, 1152], P('mp', 'dp'), may hold values from -0.109375 to 0.109375
- cotangent: bfloat16 [16, 256, 1152], P('dp', None, 'mp'), may hold values from -6 to 6
Outputs:
- block_out: bfloat16 [16, 256, 1152], P('dp', None, 'mp')
- latent_grad: bfloat16 [16, 256, 1152], P('dp', None, 'mp')
- condition_grad: bfloat16 [16, 1152], P('dp')
- ada_grad: float32 [1152, 6, 1152], P('dp', None, 'mp')
- bias_grad: float32 [6, 1152], P(None, 'mp')
- qkv_grad: float32 [1152, 3, 1152], P('dp', None, 'mp')
- qnorm_grad: float32 [72], replicated
- knorm_grad: float32 [72], replicated
- out_grad: float32 [1152, 1152], P('mp', 'dp')
- gateup_grad: float32 [1152, 2, 3072], P('dp', None, 'mp')
- down_grad: float32 [3072, 1152], P('mp', 'dp')
Inputs may be any that keep to these rules, and one draw needn't show every extreme that they name: `slot_valid`: exactly 8 slots in all hold images; at least one dp index has all its 2 slots valid.
All inputs are finite; a program needn't handle non-finite values.
Results may differ from a plain program's by a relative error of at most 0.015.
Values may be sent and summed in bfloat16 or wider, within the bound.
No kernel may reach another device: no remote copies, remote signals or barrier semaphores. Data moves between devices by JAX's collectives and lax.ppermute only.
A program may use at most 128 MiB of HBM per device.

v0:
```python
import math

import jax
import jax.numpy as jnp
from jax import lax
from jax.sharding import PartitionSpec as P

GRID = 16
BINS = 8


eps = 1e-06


def layer_norm(value):
    centred = value - jnp.mean(value, axis=-1, keepdims=True)
    scale = lax.rsqrt(jnp.mean(centred * centred, axis=-1, keepdims=True) + eps)
    return (centred * scale, scale)


def norm_back(grad, normed, scale):
    return scale * (
        grad
        - jnp.mean(grad, axis=-1, keepdims=True)
        - normed * jnp.mean(grad * normed, axis=-1, keepdims=True)
    )


def rms_norm(value):
    scale = lax.rsqrt(jnp.mean(value * value, axis=-1, keepdims=True) + eps)
    return (value * scale, scale)


def rms_back(grad, normed, scale):
    return scale * (grad - normed * jnp.mean(grad * normed, axis=-1, keepdims=True))


def rotary_tables(patches, head_size):
    pairs = head_size // 4
    freqs = 10000.0 ** (-jnp.arange(pairs, dtype=jnp.float32) / pairs)
    spots = jnp.arange(patches, dtype=jnp.int32)
    row_pos = (spots // GRID).astype(jnp.float32)
    col_pos = (spots % GRID).astype(jnp.float32)
    row_angle = row_pos[:, None] * freqs[None, :]
    col_angle = col_pos[:, None] * freqs[None, :]
    angles = jnp.concatenate([row_angle, row_angle, col_angle, col_angle], axis=1)
    return (jnp.cos(angles), jnp.sin(angles))


def mix_pairs(value):
    pairs = value.shape[-1] // 4
    first = value[..., :pairs]
    second = value[..., pairs : 2 * pairs]
    third = value[..., 2 * pairs : 3 * pairs]
    fourth = value[..., 3 * pairs :]
    return jnp.concatenate([-second, first, -fourth, third], axis=-1)


def rotate(value, cosine, sine):
    return value * cosine[:, None, :] + mix_pairs(value) * sine[:, None, :]


def rotate_back(grad, cosine, sine):
    return grad * cosine[:, None, :] - mix_pairs(grad) * sine[:, None, :]


def quarter(full, width_part):
    start = lax.axis_index("mp") * width_part
    return lax.dynamic_slice_in_dim(full, start, width_part, full.ndim - 1)


def block(
    latent_part,
    cot_part,
    condition,
    img_weight,
    keep,
    ada_weight,
    ada_bias,
    qkv_weight,
    query_gain,
    key_gain,
    out_weight,
    gate_up,
    down_weight,
):
    images, patches, width_part = latent_part.shape
    head_size = query_gain.shape[0]
    heads_local = width_part // head_size
    inverse = 1.0 / math.sqrt(head_size)
    cosine, sine = rotary_tables(patches, head_size)
    cond_full = condition.astype(jnp.float32)
    cond_act = jax.nn.silu(cond_full).astype(jnp.bfloat16)
    mods_part = (
        jnp.einsum("nd,dce->nce", cond_act, ada_weight, preferred_element_type=jnp.float32)
        + ada_bias[None]
    )
    mods = lax.all_gather(mods_part, "mp", axis=2, tiled=True)
    latent_full, cot_full = (
        lax.all_gather(latent_part, "mp", axis=2, tiled=True),
        lax.all_gather(cot_part, "mp", axis=2, tiled=True),
    )
    grad_out = cot_full.astype(jnp.float32) * img_weight[:, None, None]
    normed_one, scale_one = layer_norm(latent_full.astype(jnp.float32))
    h_first = (normed_one * (1.0 + mods[:, 1, None]) + mods[:, 0, None]).astype(jnp.bfloat16)
    raw_qkv = jnp.einsum("npd,dce->npce", h_first, qkv_weight, preferred_element_type=jnp.float32)
    raw_qkv = raw_qkv.reshape(images, patches, 3, heads_local, head_size)
    query_hat, query_scale = rms_norm(raw_qkv[:, :, 0])
    key_hat, key_scale = rms_norm(raw_qkv[:, :, 1])
    queries = rotate(query_hat * query_gain, cosine, sine).astype(jnp.bfloat16)
    keys_rot = rotate(key_hat * key_gain, cosine, sine).astype(jnp.bfloat16)
    values = raw_qkv[:, :, 2].astype(jnp.bfloat16)
    scores = (
        jnp.einsum("nphe,nqhe->nhpq", queries, keys_rot, preferred_element_type=jnp.float32)
        * inverse
    )
    row_top = jnp.max(scores, axis=-1, keepdims=True)
    expo = jnp.exp(scores - row_top)
    row_total = jnp.sum(expo, axis=-1, keepdims=True)
    probs_low = (expo / row_total).astype(jnp.bfloat16)
    log_total = row_top + jnp.log(row_total)
    attended = jnp.einsum("nhpq,nqhe->nphe", probs_low, values, preferred_element_type=jnp.float32)
    attended = attended.astype(jnp.bfloat16).reshape(images, patches, width_part)
    attn_terms = jnp.einsum("npe,ed->npd", attended, out_weight, preferred_element_type=jnp.float32)
    attn_part = lax.psum_scatter(attn_terms, "mp", scatter_dimension=2, tiled=True)
    middle_part = latent_part.astype(jnp.float32) + mods_part[:, 2, None] * attn_part
    middle = lax.all_gather(middle_part, "mp", axis=2, tiled=True)
    normed_two, scale_two = layer_norm(middle)
    h_second = (normed_two * (1.0 + mods[:, 4, None]) + mods[:, 3, None]).astype(jnp.bfloat16)
    gate_vals = jnp.einsum("npd,dcf->npcf", h_second, gate_up, preferred_element_type=jnp.float32)
    gate_part = gate_vals[:, :, 0]
    up_part = gate_vals[:, :, 1]
    gate_sigmoid = jax.nn.sigmoid(gate_part)
    swish = gate_part * gate_sigmoid
    hidden = (swish * up_part).astype(jnp.bfloat16)
    ffn_terms = jnp.einsum("npf,fd->npd", hidden, down_weight, preferred_element_type=jnp.float32)
    ffn_part = lax.psum_scatter(ffn_terms, "mp", scatter_dimension=2, tiled=True)
    out_part = middle_part + mods_part[:, 5, None] * ffn_part
    block_out = (out_part * keep[:, None, None]).astype(jnp.bfloat16)
    grad_ffn = (mods[:, 5, None] * grad_out).astype(jnp.bfloat16)
    down_grad = jnp.einsum("npf,npd->fd", hidden, grad_ffn, preferred_element_type=jnp.float32)
    grad_hidden = jnp.einsum(
        "npd,fd->npf", grad_ffn, down_weight, preferred_element_type=jnp.float32
    )
    grad_gate = grad_hidden * up_part * gate_sigmoid * (1.0 + gate_part * (1.0 - gate_sigmoid))
    grad_up = grad_hidden * swish
    grad_gu = jnp.stack([grad_gate, grad_up], axis=2).astype(jnp.bfloat16)
    gateup_grad = jnp.einsum("npd,npcf->dcf", h_second, grad_gu, preferred_element_type=jnp.float32)
    grad_h_two = lax.psum(
        jnp.einsum("npcf,dcf->npd", grad_gu, gate_up, preferred_element_type=jnp.float32), "mp"
    )
    grad_middle = grad_out + norm_back(grad_h_two * (1.0 + mods[:, 4, None]), normed_two, scale_two)
    grad_attn = (mods[:, 2, None] * grad_middle).astype(jnp.bfloat16)
    out_grad = jnp.einsum("npe,npd->ed", attended, grad_attn, preferred_element_type=jnp.float32)
    grad_att = jnp.einsum("npd,ed->npe", grad_attn, out_weight, preferred_element_type=jnp.float32)
    grad_att = grad_att.astype(jnp.bfloat16).reshape(images, patches, heads_local, head_size)
    again = (
        jnp.einsum("nphe,nqhe->nhpq", queries, keys_rot, preferred_element_type=jnp.float32)
        * inverse
    )
    probs_again = jnp.exp(again - log_total)
    grad_probs = jnp.einsum("nphe,nqhe->nhpq", grad_att, values, preferred_element_type=jnp.float32)
    grad_values = jnp.einsum(
        "nhpq,nphe->nqhe",
        probs_again.astype(jnp.bfloat16),
        grad_att,
        preferred_element_type=jnp.float32,
    )
    grad_scores = probs_again * (
        grad_probs - jnp.sum(probs_again * grad_probs, axis=-1, keepdims=True)
    )
    grad_scores = grad_scores.astype(jnp.bfloat16)
    grad_qrot = (
        jnp.einsum("nhpq,nqhe->nphe", grad_scores, keys_rot, preferred_element_type=jnp.float32)
        * inverse
    )
    grad_krot = (
        jnp.einsum("nhpq,nphe->nqhe", grad_scores, queries, preferred_element_type=jnp.float32)
        * inverse
    )
    grad_qnorm = rotate_back(grad_qrot, cosine, sine)
    grad_knorm = rotate_back(grad_krot, cosine, sine)
    qgain_terms = jnp.sum(grad_qnorm * query_hat, axis=(0, 1, 2))
    kgain_terms = jnp.sum(grad_knorm * key_hat, axis=(0, 1, 2))
    grad_query = rms_back(grad_qnorm * query_gain, query_hat, query_scale)
    grad_key = rms_back(grad_knorm * key_gain, key_hat, key_scale)
    grad_raw = jnp.stack([grad_query, grad_key, grad_values], axis=2).astype(jnp.bfloat16)
    grad_raw = grad_raw.reshape(images, patches, 3, width_part)
    qkv_grad = jnp.einsum("npd,npce->dce", h_first, grad_raw, preferred_element_type=jnp.float32)
    grad_h_one = lax.psum(
        jnp.einsum("npce,dce->npd", grad_raw, qkv_weight, preferred_element_type=jnp.float32), "mp"
    )
    grad_latent = grad_middle + norm_back(
        grad_h_one * (1.0 + mods[:, 1, None]), normed_one, scale_one
    )
    latent_grad = quarter(grad_latent, width_part).astype(jnp.bfloat16)
    h_one_part = quarter(grad_h_one, width_part)
    h_two_part = quarter(grad_h_two, width_part)
    grad_mods = jnp.stack(
        [
            jnp.sum(h_one_part, axis=1),
            jnp.sum(h_one_part * quarter(normed_one, width_part), axis=1),
            jnp.sum(quarter(grad_middle, width_part) * attn_part, axis=1),
            jnp.sum(h_two_part, axis=1),
            jnp.sum(h_two_part * quarter(normed_two, width_part), axis=1),
            jnp.sum(quarter(grad_out, width_part) * ffn_part, axis=1),
        ],
        axis=1,
    ).astype(jnp.bfloat16)
    ada_grad = jnp.einsum("nd,nce->dce", cond_act, grad_mods, preferred_element_type=jnp.float32)
    bias_grad = jnp.sum(grad_mods.astype(jnp.float32), axis=0)
    cond_terms = jnp.einsum(
        "nce,dce->nd", grad_mods, ada_weight, preferred_element_type=jnp.float32
    )
    grad_cond_act, qnorm_grad, knorm_grad = lax.psum((cond_terms, qgain_terms, kgain_terms), "mp")
    cond_sigmoid = jax.nn.sigmoid(cond_full)
    condition_grad = (
        grad_cond_act * cond_sigmoid * (1.0 + cond_full * (1.0 - cond_sigmoid))
    ).astype(jnp.bfloat16)
    return (
        block_out,
        latent_grad,
        condition_grad,
        (ada_grad, qkv_grad, out_grad, gateup_grad, down_grad),
        bias_grad,
        qnorm_grad,
        knorm_grad,
    )


def body(
    latents,
    condition,
    noise_bins,
    slot_valid,
    ada_weight,
    ada_bias,
    qkv_weight,
    query_gain,
    key_gain,
    out_weight,
    gate_up,
    down_weight,
    cotangent,
):
    slots = latents.shape[0]
    devices = lax.axis_size("dp")
    own_index = lax.axis_index("dp")
    all_bins, all_valid = (
        lax.all_gather(noise_bins, "dp", axis=0, tiled=True),
        lax.all_gather(slot_valid, "dp", axis=0, tiled=True),
    )
    bin_ids = jnp.arange(BINS, dtype=jnp.int32)
    member = (all_bins[:, None] == bin_ids[None, :]).astype(jnp.int32) * all_valid[:, None]
    per_bin = jnp.sum(member, axis=0)
    total = jnp.sum(all_valid)
    own_count = jnp.sum(member * per_bin[None, :], axis=1)
    weight_all = (
        all_valid.astype(jnp.float32)
        * total.astype(jnp.float32)
        / (BINS * jnp.maximum(own_count, 1).astype(jnp.float32))
    )
    fetched = (
        lax.all_gather(ada_weight, "dp", axis=0, tiled=True),
        lax.all_gather(qkv_weight, "dp", axis=0, tiled=True),
        lax.all_gather(out_weight, "dp", axis=1, tiled=True),
        lax.all_gather(gate_up, "dp", axis=0, tiled=True),
        lax.all_gather(down_weight, "dp", axis=1, tiled=True),
    )
    full_ada, full_qkv, full_out, full_gate_up, full_down = fetched
    own_weight = lax.dynamic_slice_in_dim(weight_all, own_index * slots, slots)
    results = block(
        latents,
        cotangent,
        condition,
        own_weight,
        slot_valid.astype(jnp.float32),
        full_ada,
        ada_bias,
        full_qkv,
        query_gain,
        key_gain,
        full_out,
        full_gate_up,
        full_down,
    )
    block_out, latent_grad, condition_grad = (results[0], results[1], results[2])
    weight_terms = results[3]
    bias_terms, qgain_terms, kgain_terms = (results[4], results[5], results[6])
    small_terms = jnp.concatenate([bias_terms.reshape(-1), qgain_terms, kgain_terms])
    tiled = jnp.broadcast_to(small_terms[None, :], (devices, small_terms.shape[0]))
    summed = (
        lax.psum_scatter(weight_terms[0], "dp", scatter_dimension=0, tiled=True),
        lax.psum_scatter(weight_terms[1], "dp", scatter_dimension=0, tiled=True),
        lax.psum_scatter(weight_terms[2], "dp", scatter_dimension=1, tiled=True),
        lax.psum_scatter(weight_terms[3], "dp", scatter_dimension=0, tiled=True),
        lax.psum_scatter(weight_terms[4], "dp", scatter_dimension=1, tiled=True),
        lax.psum_scatter(tiled, "dp", scatter_dimension=0, tiled=True),
    )
    small_sum = summed[5][0]
    bias_size = bias_terms.shape[0] * bias_terms.shape[1]
    head_size = query_gain.shape[0]
    bias_grad = small_sum[:bias_size].reshape(bias_terms.shape)
    qnorm_grad = small_sum[bias_size : bias_size + head_size]
    knorm_grad = small_sum[bias_size + head_size :]
    return (
        block_out,
        latent_grad,
        condition_grad,
        summed[0],
        bias_grad,
        summed[1],
        qnorm_grad,
        knorm_grad,
        summed[2],
        summed[3],
        summed[4],
    )


def solution(mesh):
    placed = (
        P("dp", None, "mp"),
        P("dp", None),
        P("dp"),
        P("dp"),
        P("dp", None, "mp"),
        P(None, "mp"),
        P("dp", None, "mp"),
        P(),
        P(),
        P("mp", "dp"),
        P("dp", None, "mp"),
        P("mp", "dp"),
        P("dp", None, "mp"),
    )
    return jax.shard_map(
        body,
        mesh=mesh,
        in_specs=placed,
        out_specs=(
            P("dp", None, "mp"),
            P("dp", None, "mp"),
            P("dp", None),
            P("dp", None, "mp"),
            P(None, "mp"),
            P("dp", None, "mp"),
            P(),
            P(),
            P("mp", "dp"),
            P("dp", None, "mp"),
            P("mp", "dp"),
        ),
        check_vma=False,
    )
```

profile of v0, /device:TPU:0, one launch (start us, length us, event | category | flops | bytes accessed | tf_op | source)
XLA Modules:
  0.0 1136.6 jit_solution(9107349192665791729)
XLA Ops:
  10.5 34.5 %all_gather.37 = bf16[288,1152]{0,1:T(8,128)(2,1)S(1)} all-gather(bf16[288,144]{0,1:T(8,128)(2,1)} %param.22), channel_id=1, replica_groups=mesh['dp'=8,'mp'=4] {'dp'}, dimensions={1}, use_global_device_ids=true | all-gather | bytes 746496 | tf_op jit(solution)/shard_map/all_gather | solution.py:266
  45.0 1.8 convert_reduce_fusion
  46.8 1.6 fusion.12
  48.4 70.7 %all-gather.8.cloned.1.call-done = bf16[1152,6,288]{2,0,1:T(8,128)(2,1)} async-done(((bf16[144,6,288]{2,0,1:T(8,128)(2,1)}), bf16[1152,6,288]{2,0,1:T(8,128)(2,1)}) %all-gather.8.cloned.1.call-update) | async-done | bytes 3981328 | tf_op jit(solution)/shard_map/all_gather | solution.py:264
  119.1 3.3 convolution_add_fusion
  122.6 10.7 all_gather.35
  133.4 7.8 fusion.81
  141.2 1.6 copy.173
  142.8 1.6 copy.129
  144.4 30.3 %all-gather.12.cloned.1.call-done = bf16[1152,3,288]{2,0,1:T(8,128)(2,1)} async-done(((bf16[144,3,288]{2,0,1:T(8,128)(2,1)}), bf16[1152,3,288]{2,0,1:T(8,128)(2,1)}) %all-gather.12.cloned.1.call-update) | async-done | bytes 1990672 | tf_op jit(solution)/shard_map/all_gather | solution.py:265
  174.7 3.5 fusion.10
  182.5 2.2 fusion.27
  184.8 1.3 slice_bitcast_fusion.2
  186.1 30.4 %reduce-scatter.8.cloned.1.call-done = f32[2,256,288]{1,2,0:T(8,128)} async-done(((f32[2,256,1152]{1,2,0:T(8,128)}), f32[2,256,288]{1,2,0:T(8,128)}) %reduce-scatter.8.cloned.1.call-update) | async-done | bytes 589840 | tf_op jit(solution)/shard_map/reduce_scatter | solution.py:125
  216.5 2.1 multiply_add_fusion.1
  222.8 11.4 all-reduce.3
  236.2 2.1 copy.140
  238.3 2.1 copy.136
  240.4 1.0 copy.174
  242.8 2.6 reduce_sum.239
  247.2 1.6 subtract_multiply_fusion
  248.8 62.1 %all-gather.16.cloned.1.call-done = bf16[1152,2,768]{2,0,1:T(8,128)(2,1)} async-done(((bf16[144,2,768]{2,0,1:T(8,128)(2,1)}), bf16[1152,2,768]{2,0,1:T(8,128)(2,1)}) %all-gather.16.cloned.1.call-update) | async-done | bytes 3538960 | tf_op jit(solution)/shard_map/all_gather | solution.py:267
  310.9 6.8 fusion.2
  317.7 10.8 all-gather.20.cloned.1.call-done
  328.5 48.4 %all-gather.18.cloned.1.call-done = bf16[768,1152]{0,1:T(8,128)(2,1)} async-done(((bf16[768,144]{0,1:T(8,128)(2,1)}), bf16[768,1152]{0,1:T(8,128)(2,1)}) %all-gather.18.cloned.1.call-update) | async-done | bytes 1769488 | tf_op jit(solution)/shard_map/all_gather | solution.py:268
  376.9 5.7 fusion.30
  382.6 0.9 copy-done.70
  383.8 3.5 fusion.4
  387.6 2.1 copy.143
  389.7 1.3 log_add_fusion
  391.1 51.1 %all-reduce.8.cloned.1.call-done = f32[2,256,1152]{1,2,0:T(8,128)} async-done(((f32[2,256,1152]{1,2,0:T(8,128)}), f32[2,256,1152]{1,2,0:T(8,128)}) %all-reduce.8.cloned.1.call-update) | async-done | bytes 2359312 | tf_op jit(solution)/shard_map/psum | solution.py:149
  442.2 2.3 multiply_reduce_fusion.4
  444.9 2.3 convert_multiply_fusion
  448.1 1.5 copy-done.2
  450.2 1.8 multiply_reduce_fusion.3
  454.8 1.2 multiply_reduce_fusion.7
  458.0 2.8 convolution_bitcast_fusion.3
  460.8 1.1 copy-done.22
  461.9 4.1 fusion.16
  466.2 1.7 copy-done.13
  467.9 5.4 convolution_bitcast_fusion
  473.4 1.6 copy-done.4
  475.0 3.0 convolution_bitcast_fusion.4
  478.1 4.1 convolution_bitcast_fusion.2
  482.3 1.2 copy-done.7
  483.5 5.0 convolution_bitcast_fusion.1
  488.9 1.2 convert_element_type.120
  490.0 2.1 multiply_reduce_fusion.9
  492.1 24.6 %all-reduce.10.cloned.1.call-done = f32[2,256,1152]{1,2,0:T(8,128)} async-done(((f32[2,256,1152]{1,2,0:T(8,128)}), f32[2,256,1152]{1,2,0:T(8,128)}) %all-reduce.10.cloned.1.call-update) | async-done | bytes 2359312 | tf_op jit(solution)/shard_map/psum | solution.py:190
  516.7 2.3 fusion.77
  519.1 2.2 multiply_reduce_fusion.10
  521.4 31.2 %reduce-scatter.10.cloned.1.call-done = f32[2,256,288]{1,2,0:T(8,128)} async-done(((f32[2,256,1152]{1,2,0:T(8,128)}), f32[2,256,288]{1,2,0:T(8,128)}) %reduce-scatter.10.cloned.1.call-update) | async-done | bytes 589840 | tf_op jit(solution)/shard_map/reduce_scatter | solution.py:137
  552.6 2.1 multiply_reduce_fusion.8
  554.7 5.7 fusion.72
  560.5 4.0 convolution_bitcast_fusion.5
  564.5 10.9 all-reduce.4
  575.6 40.2 %all-reduce.2 = f32[8,1872]{1,0:T(8,128)S(1)} all-reduce(f32[8,1872]{1,0:T(8,128)S(1)} %broadcast_in_dim.2), channel_id=5, replica_groups=mesh['dp'=8,'mp'=4] {'dp'}, use_global_device_ids=true, to_apply=%region_35.36.clone | all-reduce | flops 14976 | bytes 119808
  617.0 1.2 dynamic-slice_bitcast_fusion
  618.8 67.6 %reduce-scatter.18.cloned.1.call-done = f32[144,2,768]{2,0,1:T(8,128)} async-done(((f32[1152,2,768]{2,0,1:T(8,128)}), f32[144,2,768]{2,0,1:T(8,128)}) %reduce-scatter.18.cloned.1.call-update) | async-done | bytes 884752 | tf_op jit(solution)/shard_map/reduce_scatter | solution.py:296
  686.4 2.8 copy.153
  689.2 66.8 %reduce-scatter.16.cloned.1.call-done = f32[288,144]{0,1:T(8,128)} async-done(((f32[288,1152]{0,1:T(8,128)}), f32[288,144]{0,1:T(8,128)}) %reduce-scatter.16.cloned.1.call-update) | async-done | bytes 165904 | tf_op jit(solution)/shard_map/reduce_scatter | solution.py:295
  756.0 82.2 %reduce-scatter.20.cloned.1.call-done = f32[768,144]{0,1:T(8,128)} async-done(((f32[768,1152]{0,1:T(8,128)}), f32[768,144]{0,1:T(8,128)}) %reduce-scatter.20.cloned.1.call-update) | async-done | bytes 442384 | tf_op jit(solution)/shard_map/reduce_scatter | solution.py:297
  838.2 107.8 %reduce-scatter.14.cloned.1.call-done = f32[144,3,288]{2,0,1:T(8,128)} async-done(((f32[1152,3,288]{2,0,1:T(8,128)}), f32[144,3,288]{2,0,1:T(8,128)}) %reduce-scatter.14.cloned.1.call-update) | async-done | bytes 497680 | tf_op jit(solution)/shard_map/reduce_scatter | solution.py:294
  945.9 184.1 %reduce-scatter.12.cloned.1.call-done = f32[144,6,288]{2,0,1:T(8,128)} async-done(((f32[1152,6,288]{2,0,1:T(8,128)}), f32[144,6,288]{2,0,1:T(8,128)}) %reduce-scatter.12.cloned.1.call-update) | async-done | bytes 995344 | tf_op jit(solution)/shard_map/reduce_scatter | solution.py:293
  (238 shorter events, 25.7 us)
Async XLA Ops:
  7.2 37.8 %all-gather.10.cloned.1.call-start = ((), (), s32[]{:S(2)}) async-start(), calls=%async_computation.8 | async-start | bytes 1474560 | tf_op jit(solution)/shard_map/all_gather | solution.py:100
  7.9 111.2 %copy-start.39 = (bf16[2,1152]{1,0:T(2,128)(2,1)S(1)}, bf16[2,1152]{1,0:T(2,128)(2,1)}, u32[]{:S(2)}) copy-start(bf16[2,1152]{1,0:T(2,128)(2,1)} %param.14) | copy-start | bytes 13828
  7.9 111.2 %copy-start.50 = (f32[6,288]{1,0:T(8,128)S(1)}, f32[6,288]{1,0:T(8,128)}, u32[]{:S(2)}) copy-start(f32[6,288]{1,0:T(8,128)} %param.18) | copy-start | bytes 20740
  7.9 111.2 %all-gather.8.cloned.1.call-start = ((), (), s32[]{:S(2)}) async-start(), calls=%async_computation.7 | async-start | bytes 5971968 | tf_op jit(solution)/shard_map/all_gather | solution.py:264
  8.7 166.0 %all-gather.12.cloned.1.call-start = ((), (), s32[]{:S(2)}) async-start(), calls=%async_computation.9 | async-start | bytes 2985984 | tf_op jit(solution)/shard_map/all_gather | solution.py:265
  9.4 207.1 %reduce-scatter.8.cloned.1.call-start = ((), (), s32[]{:S(2)}) async-start(), calls=%async_computation.10 | async-start | bytes 2949120 | tf_op jit(solution)/shard_map/reduce_scatter | solution.py:125
  10.5 168.8 %copy-start.23 = (f32[256,72]{0,1:T(8,128)}, f32[256,72]{0,1:T(8,128)S(1)}, u32[]{:S(2)}) copy-start(f32[256,72]{0,1:T(8,128)S(1)} %get-tuple-element.130) | copy-start | bytes 221188
  45.0 136.7 %copy-start.8 = (bf16[288,1152]{0,1:T(8,128)(2,1)}, bf16[288,1152]{0,1:T(8,128)(2,1)S(1)}, u32[]{:S(2)}) copy-start(bf16[288,1152]{0,1:T(8,128)(2,1)S(1)} %all_gather.37) | copy-start | bytes 1990660
  46.8 127.9 %copy-start.46 = (f32[2,256]{1,0:T(2,128)}, f32[2,256]{1,0:T(2,128)S(1)}, u32[]{:S(2)}) copy-start(f32[2,256]{1,0:T(2,128)S(1)} %broadcast_multiply_fusion.13) | copy-start | bytes 6148
  48.4 126.2 %copy-start.48 = (f32[2,256]{1,0:T(2,128)}, f32[2,256]{1,0:T(2,128)S(1)}, u32[]{:S(2)}) copy-start(f32[2,256]{1,0:T(2,128)S(1)} %add_rsqrt_fusion.3) | copy-start | bytes 6148
  122.4 10.9 copy-start.31
  141.2 33.5 %copy-start.6 = (bf16[2,256,1152]{1,2,0:T(8,128)(2,1)S(1)}, bf16[2,256,1152]{1,2,0:T(8,128)(2,1)}, u32[]{:S(2)}) copy-start(bf16[2,256,1152]{1,2,0:T(8,128)(2,1)} %all-gather.10.cloned.1.call-done) | copy-start | bytes 3538948
  144.4 33.9 %copy-start.52 = (f32[2,1,1152]{2,0,1:T(2,128)}, f32[2,1,1152]{2,0,1:T(2,128)S(1)}, u32[]{:S(2)}) copy-start(f32[2,1,1152]{2,0,1:T(2,128)S(1)} %copy.129) | copy-start | bytes 27652
  144.4 33.8 %copy-start.41 = (f32[2,1152]{1,0:T(2,128)}, f32[2,1152]{1,0:T(2,128)S(1)}, u32[]{:S(2)}) copy-start(f32[2,1152]{1,0:T(2,128)S(1)} %add_bitcast_fusion.1) | copy-start | bytes 27652
  178.2 2.5 copy-start.19
  182.5 34.0 %copy-start.21 = (bf16[2,256,288]{1,2,0:T(8,128)(2,1)S(1)}, bf16[2,256,288]{1,2,0:T(8,128)(2,1)}, u32[]{:S(2)}) copy-start(bf16[2,256,288]{1,2,0:T(8,128)(2,1)} %param.13) | copy-start | bytes 884740
  184.7 33.9 %copy-start.25 = (bf16[144,2,768]{2,1,0:T(2,128)(2,1)S(1)}, bf16[144,2,768]{2,1,0:T(2,128)(2,1)}, u32[]{:S(2)}) copy-start(bf16[144,2,768]{2,1,0:T(2,128)(2,1)} %param.23) | copy-start | bytes 1327108
  184.7 36.3 %copy-start.64 = (u32[32]{0:T(128)S(1)}, u32[32]{0:T(128)}, u32[]{:S(2)}) copy-start(u32[32]{0:T(128)} %constant.95) | copy-start | bytes 388
  184.7 37.6 %copy-start.69 = (s32[2]{0:T(128)S(1)}, s32[2]{0:T(128)}, u32[]{:S(2)}) copy-start(s32[2]{0:T(128)} %param.16) | copy-start | bytes 28
  184.7 37.8 %copy-start.68 = (s32[2]{0:T(128)S(1)}, s32[2]{0:T(128)}, u32[]{:S(2)}) copy-start(s32[2]{0:T(128)} %param.15) | copy-start | bytes 28
  184.7 58.1 %all-gather.14.cloned.1.call-start = ((), (), s32[]{:S(2)}) async-start(), calls=%async_computation.11 | async-start | bytes 2949120 | tf_op jit(solution)/shard_map/all_gather | solution.py:127
  218.6 92.3 %all-gather.16.cloned.1.call-start = ((), (), s32[]{:S(2)}) async-start(), calls=%async_computation.12 | async-start | bytes 3981312 | tf_op jit(solution)/shard_map/all_gather | solution.py:267
  219.4 109.0 %all-gather.20.cloned.1.call-start = ((), (), s32[]{:S(2)}) async-start(), calls=%async_computation.15 | async-start | bytes 1474560 | tf_op jit(solution)/shard_map/all_gather | solution.py:101
  220.2 156.7 %all-gather.18.cloned.1.call-start = ((), (), s32[]{:S(2)}) async-start(), calls=%async_computation.13 | async-start | bytes 1990656 | tf_op jit(solution)/shard_map/all_gather | solution.py:268
  220.9 221.2 %all-reduce.8.cloned.1.call-start = ((), (), s32[]{:S(2)}) async-start(), calls=%async_computation.16 | async-start | bytes 4718592 | tf_op jit(solution)/shard_map/psum | solution.py:149
  242.8 3.3 copy-start
  376.9 7.0 copy-start.66
  387.3 129.4 %all-reduce.10.cloned.1.call-start = ((), (), s32[]{:S(2)}) async-start(), calls=%async_computation.17 | async-start | bytes 4718592 | tf_op jit(solution)/shard_map/psum | solution.py:190
  442.1 2.4 copy-start.5
  442.1 2.7 copy-start.11
  442.1 2.7 copy-start.32
  442.2 2.7 copy-start.38
  442.2 2.7 copy-start.45
  442.2 2.7 copy-start.60
  444.9 2.3 copy-start.9
  444.9 2.3 copy-start.34
  447.2 2.9 copy-start.3
  447.2 2.4 copy-start.2
  447.2 2.4 copy-start.30
  450.1 6.2 copy-start.26
  456.0 2.0 copy-start.67
  460.8 91.8 %reduce-scatter.10.cloned.1.call-start = ((), (), s32[]{:S(2)}) async-start(), calls=%async_computation.14 | async-start | bytes 2949120 | tf_op jit(solution)/shard_map/reduce_scatter | solution.py:137
  461.9 4.2 copy-start.33
  461.9 4.2 copy-start.53
  461.9 4.2 copy-start.71
  466.1 1.8 copy-start.13
  466.1 220.3 %reduce-scatter.18.cloned.1.call-start = ((), (), s32[]{:S(2)}) async-start(), calls=%async_computation.21 | async-start | bytes 7962624 | tf_op jit(solution)/shard_map/reduce_scatter | solution.py:296
  473.3 1.7 copy-start.35
  473.3 4.8 copy-start.12
  473.3 4.8 copy-start.61
  473.3 282.7 %reduce-scatter.16.cloned.1.call-start = ((), (), s32[]{:S(2)}) async-start(), calls=%async_computation.20 | async-start | bytes 1990656 | tf_op jit(solution)/shard_map/reduce_scatter | solution.py:295
  478.0 360.2 %reduce-scatter.20.cloned.1.call-start = ((), (), s32[]{:S(2)}) async-start(), calls=%async_computation.22 | async-start | bytes 3981312 | tf_op jit(solution)/shard_map/reduce_scatter | solution.py:297
  482.3 463.7 %reduce-scatter.14.cloned.1.call-start = ((), (), s32[]{:S(2)}) async-start(), calls=%async_computation.19 | async-start | bytes 5971968 | tf_op jit(solution)/shard_map/reduce_scatter | solution.py:294
  488.6 641.5 %reduce-scatter.12.cloned.1.call-start = ((), (), s32[]{:S(2)}) async-start(), calls=%async_computation.18 | async-start | bytes 11943936 | tf_op jit(solution)/shard_map/reduce_scatter | solution.py:293
  516.7 2.4 copy-start.18
  516.7 2.4 copy-start.49
  519.0 2.3 copy-start.59
  519.0 2.3 copy-start.58
  519.0 33.6 %copy-start.10 = (f32[2,256,288]{1,2,0:T(8,128)S(1)}, f32[2,256,288]{1,2,0:T(8,128)}, u32[]{:S(2)}) copy-start(f32[2,256,288]{1,2,0:T(8,128)} %multiply_add_fusion.1) | copy-start | bytes 1769476
  519.1 33.5 %copy-start.51 = (f32[2,288]{1,0:T(2,128)S(1)}, f32[2,288]{1,0:T(2,128)}, u32[]{:S(2)}) copy-start(f32[2,288]{1,0:T(2,128)} %get-tuple-element.132) | copy-start | bytes 6916
  519.1 33.5 %copy-start.65 = (f32[2]{0:T(128)S(1)}, f32[2]{0:T(128)}, u32[]{:S(2)}) copy-start(f32[2]{0:T(128)} %convert_element_type.120) | copy-start | bytes 28
  519.1 35.6 %copy-start.40 = (bf16[2,1152]{1,0:T(2,128)(2,1)S(1)}, bf16[2,1152]{1,0:T(2,128)(2,1)}, u32[]{:S(2)}) copy-start(bf16[2,1152]{1,0:T(2,128)(2,1)} %param.14) | copy-start | bytes 13828
  560.5 4.0 copy-start.62
  560.5 4.0 copy-start.63
  (25 other events, 24.8 us)
Sparse Core Ops, SparseCore 0:
  9.6 20.1 all-gather.9
  32.0 87.0 all-gather.7
  121.4 53.2 all-gather.11
  184.8 31.6 reduce-scatter.7
  218.7 24.0 all-gather.13
  245.6 65.1 all-gather.15
  312.5 15.9 all-gather.19
  330.9 45.9 all-gather.17
  387.5 54.6 all-reduce.7
  460.9 55.7 all-reduce.9
  519.4 33.1 reduce-scatter.9
  556.1 130.2 reduce-scatter.17
  690.8 65.1 reduce-scatter.15
  760.1 78.0 reduce-scatter.19
  842.2 103.7 reduce-scatter.13
  950.4 179.6 reduce-scatter.11
where the time goes:
time: 1140 us
  waiting for transfers between devices  872 us (76%)
  blocking collectives  108 us (9%)
  matrix products  64.3 us (6%)
  local copies, waits for them, and re-layouts  42.1 us (4%)
  other arithmetic  33 us (3%)
  between operations  16.1 us (1%)
    reduce_scatter x1, waiting for transfers between devices, body(): lax.psum_scatter(weight_terms[0], 'dp', scatter_dimension=0, tiled=True)  184 us
    reduce_scatter x1, waiting for transfers between devices, body(): lax.psum_scatter(weight_terms[1], 'dp', scatter_dimension=0, tiled=True)  108 us
    reduce_scatter x1, waiting for transfers between devices, body(): lax.psum_scatter(weight_terms[4], 'dp', scatter_dimension=1, tiled=True)  82.2 us
    all_gather x1, waiting for transfers between devices, body(): lax.all_gather(ada_weight, 'dp', axis=0, tiled=True)  70.7 us
    reduce_scatter x1, waiting for transfers between devices, body(): lax.psum_scatter(weight_terms[3], 'dp', scatter_dimension=0, tiled=True)  67.6 us
    reduce_scatter x1, waiting for transfers between devices, body(): lax.psum_scatter(weight_terms[2], 'dp', scatter_dimension=1, tiled=True)  66.8 us
    all_gather x1, waiting for transfers between devices, body(): lax.all_gather(gate_up, 'dp', axis=0, tiled=True)  62.1 us
    unnamed x2, blocking collectives  51.5 us
  transfers between devices with their start and end apart: 16, of which 15 were waited for; matrix products, arithmetic and copies ran while one was open for 8% of the time, Pallas kernels for 0%

commit v1 on v0

v1 whole, which is shorter than its diff:
```python
import functools
import math

import jax
import jax.numpy as jnp
import numpy as np
from jax import lax
from jax.experimental import pallas as pl
from jax.experimental.pallas import tpu as pltpu
from jax.sharding import PartitionSpec as P

GRID = 16
BINS = 8
EPS = 1e-06
F32 = jnp.float32
BF16 = jnp.bfloat16
VMEM_BYTES = 56 * 1024 * 1024
LANES = 128
NT = (((1,), (1,)), ((), ()))
NN = (((1,), (0,)), ((), ()))
TN = (((0,), (0,)), ((), ()))


def dot(left, right, dims):
    return lax.dot_general(left, right, dims, preferred_element_type=F32)


def swap(value, axis, bit):
    size = lax.axis_size(axis)
    return lax.ppermute(value, axis, [(i, i ^ bit) for i in range(size)])


def round_up(value, unit):
    return -(-value // unit) * unit


def ordered(bit, mine, other, axis):
    first = jnp.where(bit == 0, mine, other)
    second = jnp.where(bit == 0, other, mine)
    return jnp.concatenate([first, second], axis=axis)


def gather_rows(value, axis):
    size, me = lax.axis_size(axis), lax.axis_index(axis)
    step = 1
    while step < size:
        other = swap(value, axis, step)
        value = ordered((me // step) % 2, value, other, 0)
        step *= 2
    return value


def scatter_rows(value, axis):
    size, me = lax.axis_size(axis), lax.axis_index(axis)
    step = size // 2
    while step >= 1:
        half = value.shape[0] // 2
        bit = (me // step) % 2
        keep = jnp.where(bit == 0, value[:half], value[half:])
        send = jnp.where(bit == 0, value[half:], value[:half])
        value = keep + swap(send, axis, step)
        step //= 2
    return value


def rows_to_columns(value, axis):
    size, me = lax.axis_size(axis), lax.axis_index(axis)
    step = 1
    while step < size:
        rows, cols = value.shape
        bit = (me // step) % 2
        per = rows // (size // step)
        split = value.reshape(size // step // 2, 2, per, cols)
        keep = jnp.where(bit == 0, split[:, 0], split[:, 1]).reshape(rows // 2, cols)
        send = jnp.where(bit == 0, split[:, 1], split[:, 0]).reshape(rows // 2, cols)
        value = ordered(bit, keep, swap(send, axis, step), 1)
        step *= 2
    return value


def mp_sum_small(value):
    step = lax.axis_size("mp") // 2
    while step >= 1:
        value = value + swap(value, "mp", step)
        step //= 2
    return value


def mp_pieces(value):
    far = swap(value, "mp", 2)
    near = swap(value, "mp", 1)
    both = swap(far, "mp", 1)
    return [value, far, near, both]


def mp_total(partial):
    other = swap(partial, "mp", 1)
    chip = (partial.astype(F32) + other.astype(F32)).astype(BF16)
    half = partial.shape[1] // 2
    core = lax.axis_index("mp") % 2
    mine = lax.dynamic_slice_in_dim(chip, core * half, half, 1)
    far = swap(mine, "mp", 2)
    far_other = swap(far, "mp", 1)
    return chip, far, far_other


def mp_quarter(partial):
    images, width, patches = partial.shape
    quarter = width // 4
    me = lax.axis_index("mp")
    core, side = me % 2, me // 2
    split = partial.reshape(images, 2, 2, quarter, patches)
    send = jnp.where(core == 0, split[:, :, 1], split[:, :, 0])
    keep = jnp.where(core == 0, split[:, :, 0], split[:, :, 1])
    chip = keep.astype(F32) + swap(send, "mp", 1).astype(F32)
    send = jnp.where(side == 0, chip[:, 1], chip[:, 0]).astype(BF16)
    keep = jnp.where(side == 0, chip[:, 0], chip[:, 1])
    return keep + swap(send, "mp", 2).astype(F32)


def dp_blocks(block):
    size, me = lax.axis_size("dp"), lax.axis_index("dp")
    outer = size // 2
    if size % 2 or outer > 4 or outer & (outer - 1):
        return [lax.all_gather(block, "dp", axis=0, tiled=True)], [jnp.int32(0)]
    blocks, owners = [block, swap(block, "dp", 1)], [me, me ^ 1]
    for step in range(1, outer):
        got = swap(block, "dp", 2 * step)
        blocks.append(got)
        owners.append(me ^ (2 * step))
        blocks.append(swap(got, "dp", 1))
        owners.append(me ^ (2 * step) ^ 1)
    return blocks, owners


def rotary_tables(patches, head_size):
    pairs = head_size // 4
    freqs = 10000.0 ** (-np.arange(pairs, dtype=np.float64) / pairs)
    spots = np.arange(patches)
    row = (spots // GRID)[None, :] * freqs[:, None]
    col = (spots % GRID)[None, :] * freqs[:, None]
    angles = np.concatenate([row, row, col, col], axis=0)
    cosine, sine = np.cos(angles), np.sin(angles)
    first = (np.arange(head_size) // pairs % 2 == 0)[:, None]
    up = np.where(first, -sine, 0.0)
    down = np.where(first, 0.0, sine)
    return np.stack([cosine, up, down]).astype(np.float32)


def turned(value, up, down):
    height = value.shape[0]
    pairs = height // 4
    return pltpu.roll(value, height - pairs, 0) * up + pltpu.roll(value, pairs, 0) * down


def normed(value):
    centred = value - jnp.mean(value, axis=0, keepdims=True)
    scale = lax.rsqrt(jnp.mean(centred * centred, axis=0, keepdims=True) + EPS)
    return centred * scale, scale


def norm_back(grad, unit, scale):
    return scale * (
        grad
        - jnp.mean(grad, axis=0, keepdims=True)
        - unit * jnp.mean(grad * unit, axis=0, keepdims=True)
    )


def row_sums(value):
    ones = jnp.ones((8, value.shape[1]), F32)
    return lax.dot_general(
        ones, value, NT, precision=lax.Precision.HIGHEST, preferred_element_type=F32
    )[0:1]


def rows_at(index, size):
    return pl.ds(pl.multiple_of(index * size, 16), size)


def heads_of(raw, gains, tables, head):
    size = gains.shape[0]
    width = raw.shape[0] // 3
    cosine, up, down = tables[0], tables[1], tables[2]
    found = []
    for part in range(2):
        rows = raw[part * width + head * size : part * width + (head + 1) * size]
        scale = lax.rsqrt(jnp.mean(rows * rows, axis=0, keepdims=True) + EPS)
        hat = rows * scale
        gained = hat * gains[:, part : part + 1]
        rotated = gained * cosine + turned(gained, up, down)
        found.append((hat, scale, rotated.astype(BF16)))
    value = raw[2 * width + head * size : 2 * width + (head + 1) * size].astype(BF16)
    return found[0], found[1], value


def attention_forward(
    dims, place, lat_refs, mods_ref, weight_refs, gains_ref, tables_ref, outs, scratch
):
    heads, block_rows = dims
    lat_ref, weight_ref, h_ref, raw_ref, lse_ref, ob_ref, attn_ref = outs
    (x_ref,) = scratch
    quarter = lat_refs[0].shape[1]
    width = quarter
    size = gains_ref.shape[0]
    inverse = 1.0 / math.sqrt(size)

    @pl.when(pl.program_id(0) == 0)
    def _():
        for k, ref in enumerate(weight_refs):
            if len(weight_refs) == 1:
                weight_ref[...] = ref[...]
            else:
                weight_ref[rows_at(place[4 + k], block_rows), :] = ref[...]

    for k, ref in enumerate(lat_refs):
        piece = ref[0]
        lat_ref[0, rows_at(place[k], quarter), :] = piece
        x_ref[rows_at(place[k], quarter), :] = piece.astype(F32)
    mods = mods_ref[0].T
    unit, _ = normed(x_ref[...])
    h = (unit * (1.0 + mods[:, 1:2]) + mods[:, 0:1]).astype(BF16)
    h_ref[0] = h
    span = round_up(3 * width, LANES)
    raw = dot(weight_ref[:, :span], h, TN)[: 3 * width]
    raw_ref[0] = raw
    gains, tables = gains_ref[...], tables_ref[...]
    pad = 4 * width - (3 * width) // LANES * LANES - width
    parts, tops = [], []
    for head in range(heads):
        (_, _, query), (_, _, key), value = heads_of(raw, gains, tables, head)
        scores = dot(key, query, TN) * inverse
        top = jnp.max(scores, axis=0, keepdims=True)
        expo = jnp.exp(scores - top)
        total = jnp.sum(expo, axis=0, keepdims=True)
        probs = (expo / total).astype(BF16)
        parts.append(dot(value, probs, NN))
        tops.append(top + jnp.log(total))
    lse_ref[0] = jnp.concatenate(tops, axis=0)
    patches = raw.shape[1]
    ob = jnp.concatenate([jnp.zeros((pad, patches), F32)] + parts, axis=0).astype(BF16)
    ob_ref[0] = ob
    attn_ref[0] = dot(weight_ref[:, 4 * width - width - pad :], ob, NN).astype(BF16)


def feed_forward(
    place, image_weight, lat_ref, sums, mods_ref, cot_refs, weight_ref, outs, scratch
):
    mid_ref, attn_ref, h_ref, hidden_ref, dffn_ref, dgu_ref, cot_ref, dh_ref = outs
    (x_ref,) = scratch
    chip_ref, far_ref, other_ref = sums
    half = far_ref.shape[1]
    quarter = cot_refs[0].shape[1]
    units = hidden_ref.shape[1]
    mods = mods_ref[0].T
    add_sums(place, x_ref, chip_ref, far_ref, other_ref, half)
    attn_ref[0] = x_ref[rows_at(place[0], quarter), :]
    mid = lat_ref[0].astype(F32) + mods[:, 2:3] * x_ref[...]
    mid_ref[0] = mid
    unit, _ = normed(mid)
    h = (unit * (1.0 + mods[:, 4:5]) + mods[:, 3:4]).astype(BF16)
    h_ref[0] = h
    for k, ref in enumerate(cot_refs):
        piece = ref[0]
        cot_ref[0, rows_at(place[k], quarter), :] = piece
    weight = image_weight[pl.program_id(0)]
    dffn = (mods[:, 5:6] * (cot_ref[0].astype(F32) * weight)).astype(BF16)
    dffn_ref[0] = dffn
    gate = dot(weight_ref[:, :units], h, TN)
    up = dot(weight_ref[:, units : 2 * units], h, TN)
    sig = jax.nn.sigmoid(gate)
    swish = gate * sig
    hidden_ref[0] = (swish * up).astype(BF16)
    dhidden = dot(weight_ref[:, 2 * units :], dffn, TN)
    dgu_ref[0, :units] = (dhidden * up * sig * (1.0 + gate * (1.0 - sig))).astype(BF16)
    dgu_ref[0, units:] = (dhidden * swish).astype(BF16)
    dh_ref[0] = dot(weight_ref[:, : 2 * units], dgu_ref[0], NN).astype(BF16)


def add_sums(place, x_ref, chip_ref, far_ref, other_ref, half):
    x_ref[...] = chip_ref[0].astype(F32)
    core = place[3 + 1]
    x_ref[rows_at(core, half), :] += far_ref[0].astype(F32)
    x_ref[rows_at(1 - core, half), :] += other_ref[0].astype(F32)


def feed_forward_grads(h_ref, hidden_ref, dffn_ref, dgu_ref, weight_ref, grad_ref, ffn_ref):
    images = h_ref.shape[0]
    units = hidden_ref.shape[1]
    total, down = None, None
    for n in range(images):
        term = dot(h_ref[n], dgu_ref[n], NT)
        term_down = dot(dffn_ref[n], hidden_ref[n], NT)
        total = term if total is None else total + term
        down = term_down if down is None else down + term_down
    grad_ref[:, : 2 * units] = total.astype(BF16)
    grad_ref[:, 2 * units :] = down.astype(BF16)
    for n in range(images):
        ffn_ref[n] = dot(weight_ref[...], hidden_ref[n], NN).astype(BF16)


def attention_backward(
    heads,
    place,
    image_weight,
    sums,
    mid_ref,
    attn_ref,
    cot_ref,
    mods_ref,
    raw_ref,
    lse_ref,
    gains_ref,
    tables_ref,
    weight_ref,
    outs,
    scratch,
):
    dmid_ref, dattn_ref, draw_ref, dh_ref, dmods_ref, qgain_ref, kgain_ref = outs
    x_ref, y_ref = scratch
    chip_ref, far_ref, other_ref = sums
    half = far_ref.shape[1]
    quarter = attn_ref.shape[1]
    width = quarter
    size = gains_ref.shape[0]
    inverse = 1.0 / math.sqrt(size)
    mods = mods_ref[0].T
    add_sums(place, x_ref, chip_ref, far_ref, other_ref, half)
    unit, scale = normed(mid_ref[0])
    y_ref[...] = unit
    own = rows_at(place[0], quarter)
    dh_own = x_ref[own, :]
    dmods_ref[0] = jnp.zeros(dmods_ref.shape[1:], F32)
    dmods_ref[0, 3:4, :] = row_sums(dh_own)
    dmods_ref[0, 4:5, :] = row_sums(dh_own * y_ref[own, :])
    weight = image_weight[pl.program_id(0)]
    dy = cot_ref[0].astype(F32) * weight
    dmid = dy + norm_back(x_ref[...] * (1.0 + mods[:, 4:5]), unit, scale)
    dmid_ref[0] = dmid
    x_ref[...] = dmid
    dmods_ref[0, 2:3, :] = row_sums(x_ref[own, :] * attn_ref[0])
    dattn = (mods[:, 2:3] * dmid).astype(BF16)
    dattn_ref[0] = dattn
    start = (3 * width) // LANES * LANES
    pad = 3 * width - start
    dob = dot(weight_ref[:, start:], dattn, TN)
    raw = raw_ref[0]
    gains, tables = gains_ref[...], tables_ref[...]
    cosine, up, down = tables[0], tables[1], tables[2]
    parts = [[], [], []]
    sums_of = [None, None]
    for head in range(heads):
        query, key, value = heads_of(raw, gains, tables, head)
        grad = dob[pad + head * size : pad + (head + 1) * size].astype(BF16)
        scores = dot(key[2], query[2], TN) * inverse
        probs = jnp.exp(scores - lse_ref[0, head : head + 1, :])
        dprobs = dot(value, grad, TN)
        parts[2].append(dot(grad, probs.astype(BF16), NT))
        dscores = probs * (dprobs - jnp.sum(probs * dprobs, axis=0, keepdims=True))
        dscores = dscores.astype(BF16)
        turned_grads = (
            dot(key[2], dscores, NN) * inverse,
            dot(query[2], dscores, NT) * inverse,
        )
        for part, (rot, (hat, rms, _)) in enumerate(zip(turned_grads, (query, key))):
            back = rot * cosine - turned(rot, up, down)
            term = back * hat
            sums_of[part] = term if sums_of[part] is None else sums_of[part] + term
            g = back * gains[:, part : part + 1]
            parts[part].append(rms * (g - hat * jnp.mean(g * hat, axis=0, keepdims=True)))
    qgain_ref[0] = jnp.broadcast_to(row_sums(sums_of[0]), qgain_ref.shape[1:])
    kgain_ref[0] = jnp.broadcast_to(row_sums(sums_of[1]), kgain_ref.shape[1:])
    span = round_up(3 * width, LANES)
    patches = raw.shape[1]
    tail = [jnp.zeros((span - 3 * width, patches), F32)] if span > 3 * width else []
    draw = jnp.concatenate(parts[0] + parts[1] + parts[2] + tail, axis=0).astype(BF16)
    draw_ref[0] = draw
    dh_ref[0] = dot(weight_ref[:, :span], draw, NN).astype(BF16)


def attention_grads(h_ref, draw_ref, dattn_ref, ob_ref, grad_ref):
    images = h_ref.shape[0]
    span = draw_ref.shape[1]
    full = grad_ref.shape[1]
    start = full - ob_ref.shape[1]
    total, out = None, None
    for n in range(images):
        term = dot(h_ref[n], draw_ref[n], NT)
        term_out = dot(dattn_ref[n], ob_ref[n], NT)
        total = term if total is None else total + term
        out = term_out if out is None else out + term_out
    grad_ref[:, :start] = total[:, :start].astype(BF16)
    grad_ref[:, start:span] = (total[:, start:] + out[:, : span - start]).astype(BF16)
    grad_ref[:, span:] = out[:, span - start :].astype(BF16)


def last_steps(
    place, image_weight, keep, sums, lat_ref, dmid_ref, mid_ref, cot_ref, mods_ref, ffn_ref,
    dmods_ref, outs, scratch
):
    out_ref, dlat_ref, dm_ref = outs
    x_ref, y_ref = scratch
    chip_ref, far_ref, other_ref = sums
    half = far_ref.shape[1]
    quarter = ffn_ref.shape[1]
    own = rows_at(place[0], quarter)
    mods = mods_ref[0].T
    add_sums(place, x_ref, chip_ref, far_ref, other_ref, half)
    unit, scale = normed(lat_ref[0].astype(F32))
    y_ref[...] = unit
    dh_own = x_ref[own, :]
    dm_ref[0] = dmods_ref[0]
    dm_ref[0, 0:1, :] = row_sums(dh_own)
    dm_ref[0, 1:2, :] = row_sums(dh_own * y_ref[own, :])
    back = norm_back(x_ref[...] * (1.0 + mods[:, 1:2]), unit, scale)
    x_ref[...] = back
    dlat_ref[0] = (dmid_ref[0, own, :] + x_ref[own, :]).astype(BF16)
    n = pl.program_id(0)
    ffn = ffn_ref[0]
    dy = cot_ref[0, own, :].astype(F32) * image_weight[n]
    dm_ref[0, 5:6, :] = row_sums(dy * ffn)
    y_ref[...] = jnp.broadcast_to(mods[:, 5:6], y_ref.shape)
    out_ref[0] = ((mid_ref[0, own, :] + y_ref[own, :] * ffn) * keep[n]).astype(BF16)


def whole(array):
    return pl.BlockSpec(array.shape, lambda n: (0,) * array.ndim)


def each(array):
    return pl.BlockSpec((1,) + array.shape[1:], lambda n: (n,) + (0,) * (array.ndim - 1))


SCALARS = pl.BlockSpec(memory_space=pltpu.SMEM)


def call(body, groups, outs, scratch, images, flops):
    flat, specs, counts = [], [], []
    for group in groups:
        counts.append(len(group))
        for array, kind in group:
            flat.append(array)
            specs.append(SCALARS if kind is None else kind(array))

    def kernel(*refs):
        at, lists = 0, []
        for count in counts:
            lists.append(list(refs[at : at + count]))
            at += count
        body(*lists, list(refs[at : at + len(outs)]), list(refs[at + len(outs) :]))

    moved = sum(a.size * a.dtype.itemsize for a in flat) + sum(
        math.prod(o.shape) * o.dtype.itemsize for o, _ in outs
    )
    return pl.pallas_call(
        kernel,
        grid=(images,),
        in_specs=specs,
        out_specs=[kind(o) for o, kind in outs],
        out_shape=[o for o, _ in outs],
        scratch_shapes=scratch,
        compiler_params=pltpu.CompilerParams(
            dimension_semantics=("arbitrary",), vmem_limit_bytes=VMEM_BYTES
        ),
        cost_estimate=pl.CostEstimate(flops=flops, bytes_accessed=moved, transcendentals=0),
    )(*flat)


def shaped(shape, dtype):
    return jax.ShapeDtypeStruct(shape, dtype)


def body(
    latents,
    condition,
    noise_bins,
    slot_valid,
    ada_weight,
    ada_bias,
    qkv_weight,
    query_gain,
    key_gain,
    out_weight,
    gate_up,
    down_weight,
    cotangent,
):
    images, patches, quarter = latents.shape
    width = condition.shape[1]
    rows = qkv_weight.shape[0]
    units = gate_up.shape[2]
    head_size = query_gain.shape[0]
    heads = quarter // head_size
    dp, mp = lax.axis_index("dp"), lax.axis_index("mp")
    dp_size = lax.axis_size("dp")
    all_images = dp_size * images
    tokens = images * patches

    extra = jnp.stack([noise_bins, slot_valid], axis=1).astype(BF16)
    told = jnp.concatenate([condition, extra, jnp.zeros((images, LANES - 2), BF16)], axis=1)
    told = gather_rows(told, "dp")
    all_bins, all_valid = told[:, width].astype(F32), told[:, width + 1].astype(F32)
    cond_all = told[:, :width].astype(F32)

    first_pack = jnp.concatenate(
        [
            jnp.transpose(qkv_weight, (1, 0, 2))[0],
            jnp.transpose(qkv_weight, (1, 0, 2))[1],
            jnp.transpose(qkv_weight, (1, 0, 2))[2],
            out_weight.T,
        ],
        axis=1,
    )
    second_pack = jnp.concatenate([gate_up[:, 0], gate_up[:, 1], down_weight.T], axis=1)
    lat_pieces = mp_pieces(jnp.transpose(latents, (0, 2, 1)))
    blocks, owners = dp_blocks(first_pack)
    second = lax.all_gather(second_pack, "dp", axis=0, tiled=True)
    cot_pieces = mp_pieces(jnp.transpose(cotangent, (0, 2, 1)))

    bin_ids = jnp.arange(BINS, dtype=F32)
    member = (all_bins[:, None] == bin_ids[None, :]).astype(F32) * all_valid[:, None]
    per_bin = jnp.sum(member, axis=0)
    own_count = jnp.sum(member * per_bin[None, :], axis=1)
    weight_all = all_valid * jnp.sum(all_valid) / (BINS * jnp.maximum(own_count, 1.0))
    image_weight = lax.dynamic_slice_in_dim(weight_all, dp * images, images)
    keep = slot_valid.astype(F32)

    cond_rows = lax.dynamic_slice_in_dim(cond_all, dp * rows, rows, 1)
    cond_act = jax.nn.silu(cond_rows).astype(BF16)
    ada = jnp.transpose(ada_weight, (1, 0, 2))
    mods_terms = jnp.einsum("nd,cde->nce", cond_act, ada, preferred_element_type=F32)
    mods_own = scatter_rows(mods_terms.reshape(all_images, -1), "dp")
    mods_own = mods_own.reshape(images, 6, quarter) + ada_bias[None]
    mods_own = jnp.pad(mods_own, ((0, 0), (0, 2), (0, 0)))
    side, core = mp // 2, mp % 2
    far = swap(mods_own, "mp", 2)
    pair = jnp.stack([jnp.where(side == 0, mods_own, far), jnp.where(side == 0, far, mods_own)])
    near = swap(pair, "mp", 1)
    quad = jnp.stack([jnp.where(core == 0, pair, near), jnp.where(core == 0, near, pair)], axis=1)
    mods = jnp.transpose(quad, (2, 3, 0, 1, 4)).reshape(images, 8, width)

    place = jnp.stack(
        [mp, mp ^ 2, mp ^ 1, mp ^ 3] + [jnp.asarray(o, jnp.int32) for o in owners]
    ).astype(jnp.int32)
    core_place = jnp.stack([mp, mp ^ 2, mp ^ 1, mp ^ 3, core]).astype(jnp.int32)
    gains = jnp.stack([query_gain, key_gain], axis=1)
    tables = jnp.asarray(rotary_tables(patches, head_size))
    full = 4 * quarter
    span = round_up(3 * quarter, LANES)
    start = 3 * quarter // LANES * LANES
    wide = lambda dtype: shaped((images, width, patches), dtype)
    tall = pltpu.VMEM((width, patches), F32)

    lat, first, h_one, raw, lse, ob, attn_part = call(
        lambda p, l, m, w, g, t, outs, s: attention_forward(
            (heads, rows), p[0], l, m[0], w, g[0], t[0], outs, s
        ),
        [
            [(place, None)],
            [(a, each) for a in lat_pieces],
            [(mods, each)],
            [(a, whole) for a in blocks],
            [(gains, whole)],
            [(tables, whole)],
        ],
        [
            (wide(BF16), each),
            (shaped((width, full), BF16), whole),
            (wide(BF16), each),
            (shaped((images, 3 * quarter, patches), F32), each),
            (shaped((images, heads, patches), F32), each),
            (shaped((images, full - start, patches), BF16), each),
            (wide(BF16), each),
        ],
        [tall],
        images,
        2 * tokens * width * full,
    )
    attn_sums = mp_total(attn_part)

    mid, attn_own, h_two, hidden, dffn, dgu, cot, dh_two_part = call(
        lambda p, w, l, s, m, c, k, outs, x: feed_forward(
            p[0], w[0], l[0], s, m[0], c, k[0], outs, x
        ),
        [
            [(core_place, None)],
            [(image_weight, None)],
            [(lat, each)],
            [(a, each) for a in attn_sums],
            [(mods, each)],
            [(a, each) for a in cot_pieces],
            [(second, whole)],
        ],
        [
            (wide(F32), each),
            (shaped((images, quarter, patches), F32), each),
            (wide(BF16), each),
            (shaped((images, units, patches), BF16), each),
            (wide(BF16), each),
            (shaped((images, 2 * units, patches), BF16), each),
            (wide(BF16), each),
            (wide(BF16), each),
        ],
        [tall],
        images,
        2 * tokens * width * units * 5,
    )
    dh_two_sums = mp_total(dh_two_part)
    second_grad, ffn_part = call(
        lambda a, outs, x: feed_forward_grads(*a, *outs),
        [[(h_two, whole), (hidden, whole), (dffn, whole), (dgu, whole), (second[:, 2 * units :], whole)]],
        [(shaped((width, 3 * units), BF16), whole), (wide(BF16), whole)],
        [],
        1,
        2 * tokens * width * units * 4,
    )
    second_sum = lax.psum_scatter(second_grad, "dp", scatter_dimension=0, tiled=True)
    ffn_own = mp_quarter(ffn_part)

    dmid, dattn, draw, dh_one_part, dmods_part, qgain, kgain = call(
        lambda p, w, s, a, outs, x: attention_backward(heads, p[0], w[0], s, *a, outs, x),
        [
            [(core_place, None)],
            [(image_weight, None)],
            [(a, each) for a in dh_two_sums],
            [
                (mid, each),
                (attn_own, each),
                (cot, each),
                (mods, each),
                (raw, each),
                (lse, each),
                (gains, whole),
                (tables, whole),
                (first, whole),
            ],
        ],
        [
            (wide(F32), each),
            (wide(BF16), each),
            (shaped((images, span, patches), BF16), each),
            (wide(BF16), each),
            (shaped((images, 8, quarter), F32), each),
            (shaped((images, 8, head_size), F32), each),
            (shaped((images, 8, head_size), F32), each),
        ],
        [tall, tall],
        images,
        2 * tokens * width * full,
    )
    dh_one_sums = mp_total(dh_one_part)
    (first_grad,) = call(
        lambda a, outs, x: attention_grads(*a, *outs),
        [[(h_one, whole), (draw, whole), (dattn, whole), (ob, whole)]],
        [(shaped((width, full), BF16), whole)],
        [],
        1,
        2 * tokens * width * full,
    )
    first_sum = lax.psum_scatter(first_grad, "dp", scatter_dimension=0, tiled=True)

    block_out, latent_grad, dmods = call(
        lambda p, w, k, s, a, outs, x: last_steps(p[0], w[0], k[0], s, *a, outs, x),
        [
            [(core_place, None)],
            [(image_weight, None)],
            [(keep, None)],
            [(a, each) for a in dh_one_sums],
            [
                (lat, each),
                (dmid, each),
                (mid, each),
                (cot, each),
                (mods, each),
                (ffn_own, each),
                (dmods_part, each),
            ],
        ],
        [
            (shaped((images, quarter, patches), BF16), each),
            (shaped((images, quarter, patches), BF16), each),
            (shaped((images, 8, quarter), F32), each),
        ],
        [tall, tall],
        images,
        tokens * width * 20,
    )

    gain_terms = jnp.concatenate([jnp.sum(qgain[:, 0], axis=0), jnp.sum(kgain[:, 0], axis=0)])
    high = gain_terms.astype(BF16)
    low = (gain_terms - high.astype(F32)).astype(BF16)
    beside = jnp.concatenate([high, low])[None]
    beside = jnp.concatenate([beside, jnp.zeros((images - 1, beside.shape[1]), BF16)], axis=0)
    told_back = jnp.concatenate(
        [dmods[:, :6].astype(BF16).reshape(images, 6 * quarter), beside], axis=1
    )
    told_back = gather_rows(told_back, "dp")
    dmods_all = told_back[:, : 6 * quarter].reshape(all_images, 6, quarter)
    gain_sum = jnp.sum(told_back[:, 6 * quarter :].astype(F32), axis=0)
    gain_sum = gain_sum[: 2 * head_size] + gain_sum[2 * head_size :]
    ada_grad = jnp.einsum("nd,nce->cde", cond_act, dmods_all, preferred_element_type=F32)
    ada_grad = jnp.transpose(ada_grad, (1, 0, 2))
    bias_grad = jnp.sum(dmods_all.astype(F32), axis=0)
    cond_terms = jnp.einsum("nce,cde->nd", dmods_all, ada, preferred_element_type=F32)
    both = jnp.concatenate([cond_terms.reshape(-1), gain_sum])
    both = mp_sum_small(both)
    gain_sum = both[cond_terms.size :]
    cond_sum = rows_to_columns(both[: cond_terms.size].reshape(cond_terms.shape), "dp")
    cond_own = condition.astype(F32)
    sig = jax.nn.sigmoid(cond_own)
    condition_grad = (cond_sum * sig * (1.0 + cond_own * (1.0 - sig))).astype(BF16)

    second_sum = second_sum.astype(F32)
    first_sum = first_sum.astype(F32)
    gateup_grad = jnp.stack([second_sum[:, :units], second_sum[:, units : 2 * units]], axis=1)
    down_grad = second_sum[:, 2 * units :].T
    qkv_grad = first_sum[:, : 3 * quarter].reshape(rows, 3, quarter)
    out_grad = first_sum[:, 3 * quarter :].T
    return (
        jnp.transpose(block_out, (0, 2, 1)),
        jnp.transpose(latent_grad, (0, 2, 1)),
        condition_grad,
        ada_grad,
        bias_grad,
        qkv_grad,
        gain_sum[:head_size],
        gain_sum[head_size:],
        out_grad,
        gateup_grad,
        down_grad,
    )


def solution(mesh):
    placed = (
        P("dp", None, "mp"),
        P("dp", None),
        P("dp"),
        P("dp"),
        P("dp", None, "mp"),
        P(None, "mp"),
        P("dp", None, "mp"),
        P(),
        P(),
        P("mp", "dp"),
        P("dp", None, "mp"),
        P("mp", "dp"),
        P("dp", None, "mp"),
    )
    return jax.shard_map(
        body,
        mesh=mesh,
        in_specs=placed,
        out_specs=(
            P("dp", None, "mp"),
            P("dp", None, "mp"),
            P("dp", None),
            P("dp", None, "mp"),
            P(None, "mp"),
            P("dp", None, "mp"),
            P(),
            P(),
            P("mp", "dp"),
            P("dp", None, "mp"),
            P("mp", "dp"),
        ),
        check_vma=False,
    )
```

time: 1140 us -> 403 us (0.35)
  waiting for transfers between devices: 872 us -> 239 us
  blocking collectives: 108 us -> 0 us
  Pallas kernels: 0 us -> 63.1 us
  matrix products: 64.3 us -> 2.04 us
  starting transfers between devices: 1.13 us -> 49.9 us
  local copies, waits for them, and re-layouts: 42.1 us -> 21.5 us
  other arithmetic: 33 us -> 12.5 us
    reduce_scatter x7 -> x2, waiting for transfers between devices: 570 us -> 92.9 us  [the longest x1 92.9 us: body(): lax.psum_scatter(second_grad, 'dp', scatter_dimension=0, tiled=True)]
    all_gather x7 -> x1, waiting for transfers between devices: 223 us -> 0.01 us  [body(): second = lax.all_gather(second_pack, 'dp', axis=0, tiled=True)]
    ppermute x0 -> x40, waiting for transfers between devices: none -> 146 us  [swap(): return lax.ppermute(value, axis, [(i, i ^ bit) for i in range(size)])]
    psum x2 -> x0, waiting for transfers between devices: 75.6 us -> none  [the longest x1 51.1 us: block(): lax.psum(jnp.einsum('npcf,dcf->npd', grad_gu, gate_up, preferred_element_...]
    pallas_call x0 -> x6, Pallas kernels: none -> 63.1 us  [call(): pl.pallas_call(kernel, grid=(images,), in_specs=specs, out_specs=[kind(o)...]
    dot_general x21 -> x3, matrix products: 64.3 us -> 2.04 us  [the longest x1 1.51 us: body(): jnp.einsum('nd,nce->cde', cond_act, dmods_all, preferred_element_type=F32)]
    unnamed x2 -> x0, blocking collectives: 51.5 us -> none
    ppermute x0 -> x40, starting transfers between devices: none -> 49.8 us  [swap(): return lax.ppermute(value, axis, [(i, i ^ bit) for i in range(size)])]
  transfers between devices with their start and end apart: 16 -> 43, of which waited for: 15 -> 31; matrix products, arithmetic and copies ran while one was open for 8% -> 6% of each run, Pallas kernels for 0% -> 7%
where the time goes in v1:
time: 403 us; the launch traced here: 402 us
  waiting for transfers between devices  239 us (59%)
  Pallas kernels  63.1 us (16%)
  starting transfers between devices  49.9 us (12%)
  local copies, waits for them, and re-layouts  21.5 us (5%)
  between operations  14.4 us (4%)
  other arithmetic  12.5 us (3%)
    ppermute x40, waiting for transfers between devices, swap(): return lax.ppermute(value, axis, [(i, i ^ bit) for i in range(size)])  146 us
    reduce_scatter x1, waiting for transfers between devices, body(): lax.psum_scatter(second_grad, 'dp', scatter_dimension=0, tiled=True)  92.9 us
    pallas_call x6, Pallas kernels, call(): pl.pallas_call(kernel, grid=(images,), in_specs=specs, out_specs=[kind(o)...  63.1 us
    ppermute x40, starting transfers between devices, swap(): return lax.ppermute(value, axis, [(i, i ^ bit) for i in range(size)])  49.8 us
  transfers between devices with their start and end apart: 43, of which 31 were waited for; matrix products, arithmetic and copies ran while one was open for 6% of the time, Pallas kernels for 7%

profile of v1, /device:TPU:0, one launch (start us, length us, event | category | flops | bytes accessed | tf_op | source)
XLA Modules:
  0.0 402.1 jit_solution(16309791584369684439)
XLA Ops:
  7.2 2.0 fusion.32
  11.3 3.0 collective-permute-start
  14.3 1.6 collective-permute-done
  15.9 2.1 collective-permute-start.1
  18.0 1.7 collective-permute-done.1
  19.7 3.1 collective-permute-start.2
  22.8 1.8 collective-permute-done.2
  25.1 3.2 collective-permute-start.6
  28.5 5.7 %collective-permute-done.6 = f32[8,1728]{1,0:T(8,128)S(1)} collective-permute-done((f32[8,1728]{1,0:T(8,128)S(1)}, f32[8,1728]{1,0:T(8,128)S(1)}, u32[]{:S(2)}, u32[]{:S(2)}) %collective-permute-start.6) | collective-permute-done | bytes 55328 | tf_op jit(solution)/shard_map/ppermute | solution.py:30
  34.3 5.5 %collective-permute-done.7 = f32[4,1728]{1,0:T(4,128)S(1)} collective-permute-done((f32[4,1728]{1,0:T(4,128)S(1)}, f32[4,1728]{1,0:T(4,128)S(1)}, u32[]{:S(2)}, u32[]{:S(2)}) %collective-permute-start.7) | collective-permute-done | bytes 27680 | tf_op jit(solution)/shard_map/ppermute | solution.py:30
  39.8 2.7 collective-permute-start.8
  42.5 1.7 collective-permute-done.8
  44.3 2.1 collective-permute-start.9
  46.5 1.8 collective-permute-done.9
  48.7 2.6 collective-permute-start.14
  51.2 1.8 collective-permute-start.16
  53.0 2.0 collective-permute-start.3
  56.4 5.5 %collective-permute-done.3.refs_2_ = bf16[2,288,256]{2,1,0:T(8,128)(2,1)} collective-permute-done((bf16[2,288,256]{2,1,0:T(8,128)(2,1)S(1)}, bf16[2,288,256]{2,1,0:T(8,128)(2,1)}, u32[]{:S(2)}, u32[]{:S(2)}) %collective-permute-start.3) | collective-permute-done | bytes 294944 | tf_op jit(solution)/shard_map/ppermute | solution.py:30
  62.0 1.7 collective-permute-start.11
  63.7 12.1 %collective-permute-done.12.refs_8_ = bf16[144,1152]{1,0:T(8,128)(2,1)S(1)} collective-permute-done((bf16[144,1152]{1,0:T(8,128)(2,1)S(1)}, bf16[144,1152]{1,0:T(8,128)(2,1)S(1)}, u32[]{:S(2)}, u32[]{:S(2)}) %collective-permute-start.12) | collective-permute-done | bytes 331808 | tf_op jit(solution)/shard_map/ppermute | solution.py:30
  75.8 1.8 collective-permute-start.13
  77.7 1.9 collective-permute-start.15
  79.6 8.6 %collective-permute-done.16.refs_12_ = bf16[144,1152]{1,0:T(8,128)(2,1)S(1)} collective-permute-done((bf16[144,1152]{1,0:T(8,128)(2,1)S(1)}, bf16[144,1152]{1,0:T(8,128)(2,1)S(1)}, u32[]{:S(2)}, u32[]{:S(2)}) %collective-permute-start.16) | collective-permute-done | bytes 331808 | tf_op jit(solution)/shard_map/ppermute | solution.py:30
  88.2 2.2 collective-permute-start.17
  91.2 2.7 collective-permute-done.13.refs_9_
  93.9 13.3 %collective-permute-done.15.refs_11_ = bf16[144,1152]{1,0:T(8,128)(2,1)} collective-permute-done((bf16[144,1152]{1,0:T(8,128)(2,1)S(1)}, bf16[144,1152]{1,0:T(8,128)(2,1)}, u32[]{:S(2)}, u32[]{:S(2)}) %collective-permute-start.15) | collective-permute-done | bytes 331808 | tf_op jit(solution)/shard_map/ppermute | solution.py:30
  107.2 6.5 %collective-permute-done.17.refs_13_ = bf16[144,1152]{1,0:T(8,128)(2,1)} collective-permute-done((bf16[144,1152]{1,0:T(8,128)(2,1)S(1)}, bf16[144,1152]{1,0:T(8,128)(2,1)}, u32[]{:S(2)}, u32[]{:S(2)}) %collective-permute-start.17) | collective-permute-done | bytes 331808 | tf_op jit(solution)/shard_map/ppermute | solution.py:30
  113.7 11.3 %shard_map.221 = (bf16[2,1152,256]{2,1,0:T(8,128)(2,1)}, bf16[1152,1152]{1,0:T(8,128)(2,1)}, bf16[2,1152,256]{2,1,0:T(8,128)(2,1)}, f32[2,864,256]{2,1,0:T(8,128...) custom-call(s32[12]{0:T(128)} %stack.111.refs_0_, ...), custom_call_target="tpu_custom_call" | custom-call | flops 1358954496 | bytes 12493424 | tf_op jit(solution)/shard_map/pallas_call | solution.py:455
  125.1 3.0 collective-permute-done.18
  128.1 1.6 add_convert_fusion.2.refs_3_
  129.8 1.5 collective-permute-start.19
  133.0 13.0 %collective-permute-done.19.refs_4_ = bf16[2,576,256]{2,1,0:T(8,128)(2,1)S(1)} collective-permute-done((bf16[2,576,256]{2,1,0:T(8,128)(2,1)S(1)}, bf16[2,576,256]{2,1,0:T(8,128)(2,1)S(1)}, u32[]{:S(2)}, u32[]{:S(2)}) %collective-permute-start.19) | collective-permute-done | bytes 589856 | tf_op jit(solution)/shard_map/ppermute | solution.py:30
  147.6 4.0 %collective-permute-done.21.refs_8_ = bf16[2,288,256]{2,1,0:T(8,128)(2,1)} collective-permute-done((bf16[2,288,256]{2,1,0:T(8,128)(2,1)S(1)}, bf16[2,288,256]{2,1,0:T(8,128)(2,1)}, u32[]{:S(2)}, u32[]{:S(2)}) %collective-permute-start.21) | collective-permute-done | bytes 294944 | tf_op jit(solution)/shard_map/ppermute | solution.py:30
  154.2 15.7 %shard_map.222 = (f32[2,1152,256]{2,1,0:T(8,128)}, f32[2,288,256]{2,1,0:T(8,128)}, bf16[2,1152,256]{2,1,0:T(8,128)(2,1)}, bf16[2,768,256]{2,1,0:T(8,128)(2,1)}, ...) custom-call(s32[5]{0:T(128)} %stack.100.refs_0_, ...), custom_call_target="tpu_custom_call" | custom-call | flops 4529848320 | bytes 20127772 | tf_op jit(solution)/shard_map/pallas_call | solution.py:455
  170.1 2.9 collective-permute-done.24
  173.0 1.6 add_convert_fusion.1.refs_2_
  174.7 1.5 collective-permute-start.25
  176.2 13.9 %collective-permute-done.25.refs_3_ = bf16[2,576,256]{2,1,0:T(8,128)(2,1)S(1)} collective-permute-done((bf16[2,576,256]{2,1,0:T(8,128)(2,1)S(1)}, bf16[2,576,256]{2,1,0:T(8,128)(2,1)S(1)}, u32[]{:S(2)}, u32[]{:S(2)}) %collective-permute-start.25) | collective-permute-done | bytes 589856 | tf_op jit(solution)/shard_map/ppermute | solution.py:30
  190.1 2.0 collective-permute-done.26.refs_4_
  193.0 14.8 %shard_map.223 = (f32[2,1152,256]{2,1,0:T(8,128)}, bf16[2,1152,256]{2,1,0:T(8,128)(2,1)}, bf16[2,896,256]{2,1,0:T(8,128)(2,1)}, bf16[2,1152,256]{2,1,0:T(8,128)(...) custom-call(s32[5]{0:T(128)} %stack.100.refs_0_, f32[2]{0:T(128)} %dynamic_slice.15.refs_1_, ...), custom_call_target="tpu_custom_call" | custom-call | flops 1358954496 | bytes 16879196 | tf_op jit(solution)/shard_map/pallas_call | solution.py:455
  207.7 5.6 %shard_map.226 = bf16[1152,1152]{1,0:T(8,128)(2,1)} custom-call(bf16[2,1152,256]{2,1,0:T(8,128)(2,1)} %get-tuple-element.60.refs_0_, bf16[2,896,256]{2,1,0:T(8,128)(2,1)} %get-tuple-element.61.refs_1_, bf16[2,1152,256]{2,1,0:T(8,128)(2,1)} %get-tuple-element.62.refs_2_, bf16[2,384,256]{2,1,0:T(8,128)(2,1)} %get-tuple-element.63.refs_3_), custom_call_target="tpu_custom_call" | custom-call | flops 1358954496 | bytes 6324224 | tf_op jit(solution)/shard_map/pallas_call | solution.py:455
  213.4 2.8 slice.191.refs_4_
  216.2 8.6 %shard_map.224 = (bf16[1152,2304]{1,0:T(8,128)(2,1)}, bf16[2,1152,256]{2,1,0:T(8,128)(2,1)}) custom-call(bf16[2,1152,256]{2,1,0:T(8,128)(2,1)} %get-tuple-element.49.refs_0_, bf16[2,768,256]{2,1,0:T(8,128)(2,1)} %get-tuple-element.50.refs_1_, bf16[2,1152,256]{2,1,0:T(8,128)(2,1)} %get-tuple-element.51.refs_2_, ...), custom_call_target="tpu_custom_call" | custom-call | flops 3623878656 | bytes 12976128 | tf_op jit(solution)/shard_map/pallas_call | solution.py:455
  224.8 1.2 copy-done.5
  226.8 2.1 collective-permute-done.27
  229.3 1.5 collective-permute-start.28
  231.8 13.7 %collective-permute-done.28.refs_4_ = bf16[2,576,256]{2,1,0:T(8,128)(2,1)S(1)} collective-permute-done((bf16[2,576,256]{2,1,0:T(8,128)(2,1)S(1)}, bf16[2,576,256]{2,1,0:T(8,128)(2,1)S(1)}, u32[]{:S(2)}, u32[]{:S(2)}) %collective-permute-start.28) | collective-permute-done | bytes 589856 | tf_op jit(solution)/shard_map/ppermute | solution.py:30
  245.5 5.5 %collective-permute-done.31 = bf16[2,288,256]{2,1,0:T(8,128)(2,1)S(1)} collective-permute-done((bf16[2,288,256]{2,1,0:T(8,128)(2,1)S(1)}, bf16[2,288,256]{2,1,0:T(8,128)(2,1)S(1)}, u32[]{:S(2)}, u32[]{:S(2)}) %collective-permute-start.31) | collective-permute-done | bytes 294944 | tf_op jit(solution)/shard_map/ppermute | solution.py:30
  254.4 7.2 %shard_map.225 = (bf16[2,288,256]{2,1,0:T(8,128)(2,1)}, bf16[2,288,256]{2,1,0:T(8,128)(2,1)}, f32[2,8,288]{2,1,0:T(8,128)}) custom-call(s32[5]{0:T(128)} %stack.100.refs_0_, f32[2]{0:T(128)} %dynamic_slice.15.refs_1_, f32[2]{0:T(128)} %get-tuple-element.156.refs_2_, bf16[2,1152,256]{2,1,0:T(8,128)(2,1)} %copy-done.2, bf16[2,576,256]{2,1,0:T(8,128)(2,1)} %copy-done.9, ...), custom_call_target="tpu_custom_call" | custom-call | flops 11796480 | bytes 10727460 | tf_op jit(solution)/shard_map/pallas_call | solution.py:455
  262.9 3.3 collective-permute-done.32
  266.4 1.7 collective-permute-start.33
  268.0 2.1 collective-permute-done.33
  270.2 2.6 collective-permute-start.34
  272.9 3.1 collective-permute-done.34
  276.7 1.3 collective-permute-start.35
  278.1 2.4 collective-permute-done.35
  280.5 1.2 collective-permute-done.36
  282.5 3.0 collective-permute-done.37
  285.6 1.9 collective-permute-start.38
  287.5 1.5 fusion.5
  289.8 3.7 collective-permute-start.39
  298.9 92.9 %reduce-scatter.5.cloned.1.call-done = bf16[144,2304]{1,0:T(8,128)(2,1)} async-done(((bf16[1152,2304]{1,0:T(8,128)(2,1)}), bf16[144,2304]{1,0:T(8,128)(2,1)}) %reduce-scatter.5.cloned.1.call-update) | async-done | bytes 663568 | tf_op jit(solution)/shard_map/reduce_scatter | solution.py:617
  391.9 1.2 convert_element_type.121
  394.0 1.6 copy.79
  (202 shorter events, 28.4 us)
Async XLA Ops:
  7.2 17.5 %copy-start = (bf16[144,6,288]{2,0,1:T(8,128)(2,1)S(1)}, bf16[144,6,288]{2,0,1:T(8,128)(2,1)}, u32[]{:S(2)}) copy-start(bf16[144,6,288]{2,0,1:T(8,128)(2,1)} %param.18) | copy-start | bytes 1492996
  7.2 2.2 copy-start.13
  7.2 146.3 %all-gather.2.cloned.1.call-start = ((), (), s32[]{:S(2)}) async-start(), calls=%async_computation.2 | async-start | bytes 5971968 | tf_op jit(solution)/shard_map/all_gather | solution.py:517
  9.4 1.8 copy-start.15
  10.3 285.4 %reduce-scatter.3.cloned.1.call-start = ((), (), s32[]{:S(2)}) async-start(), calls=%async_computation.3 | async-start | bytes 2985984 | tf_op jit(solution)/shard_map/reduce_scatter | solution.py:660
  11.3 4.6 %collective-permute-start = (bf16[2,1280]{1,0:T(2,128)(2,1)S(1)}, bf16[2,1280]{1,0:T(2,128)(2,1)S(1)}, u32[]{:S(2)}, u32[]{:S(2)}) collective-permute-start(bf16[2,1280]{1,0:T(2,128)(2,1)S(1)} %concatenate.52), channel_id=1, source_target_pairs={{0,4},{4,0},{8,12},{12,8},{16,20},{20,16},{24,28},{28,24},{1,5},{5... | collective-permute-start | bytes 15368 | tf_op jit(solution)/shard_map/ppermute | solution.py:30
  15.9 3.8 collective-permute-start.1
  19.7 4.9 %collective-permute-start.2 = (bf16[8,1280]{1,0:T(8,128)(2,1)S(1)}, bf16[8,1280]{1,0:T(8,128)(2,1)S(1)}, u32[]{:S(2)}, u32[]{:S(2)}) collective-permute-start(bf16[8,1280]{1,0:T(8,128)(2,1)S(1)} %pad_maximum_fusion.4), channel_id=1, source_target_pairs={{0,16},{4,20},{8,24},{12,28},{16,0},{20,4},{24,8},{28,12},{1,17},{... | collective-permute-start | bytes 61448 | tf_op jit(solution)/shard_map/ppermute | solution.py:30
  24.6 19.7 %copy-start.16 = (f32[6,288]{1,0:T(8,128)S(1)}, f32[6,288]{1,0:T(8,128)}, u32[]{:S(2)}) copy-start(f32[6,288]{1,0:T(8,128)} %param.19) | copy-start | bytes 20740
  24.6 21.8 %copy-start.11 = (bf16[144,3,288]{2,0,1:T(8,128)(2,1)S(1)}, bf16[144,3,288]{2,0,1:T(8,128)(2,1)}, u32[]{:S(2)}) copy-start(bf16[144,3,288]{2,0,1:T(8,128)(2,1)} %param.20) | copy-start | bytes 746500
  24.9 23.4 %copy-start.14 = (bf16[288,144]{0,1:T(8,128)(2,1)S(1)}, bf16[288,144]{0,1:T(8,128)(2,1)}, u32[]{:S(2)}) copy-start(bf16[288,144]{0,1:T(8,128)(2,1)} %param.23) | copy-start | bytes 248836
  25.1 9.1 %collective-permute-start.6 = (f32[8,1728]{1,0:T(8,128)S(1)}, f32[8,1728]{1,0:T(8,128)S(1)}, u32[]{:S(2)}, u32[]{:S(2)}) collective-permute-start(f32[8,1728]{1,0:T(8,128)S(1)} %select_n.373), channel_id=1, source_target_pairs={{0,16},{4,20},{8,24},{12,28},{16,0},{20,4},{24,8},{28,12},{1,17},{... | collective-permute-start | bytes 165896 | tf_op jit(solution)/shard_map/ppermute | solution.py:30
  28.4 24.6 %copy-start.25 = (bf16[2,256,288]{1,2,0:T(8,128)(2,1)S(1)}, bf16[2,256,288]{1,2,0:T(8,128)(2,1)}, u32[]{:S(2)}) copy-start(bf16[2,256,288]{1,2,0:T(8,128)(2,1)} %param.14) | copy-start | bytes 884740
  28.4 26.6 %copy-start.17 = (f32[72]{0:T(128)S(1)}, f32[72]{0:T(128)}, u32[]{:S(2)}) copy-start(f32[72]{0:T(128)} %param.22) | copy-start | bytes 868
  28.5 26.6 %copy-start.18 = (f32[72]{0:T(128)S(1)}, f32[72]{0:T(128)}, u32[]{:S(2)}) copy-start(f32[72]{0:T(128)} %param.21) | copy-start | bytes 868
  34.2 5.6 %collective-permute-start.7 = (f32[4,1728]{1,0:T(4,128)S(1)}, f32[4,1728]{1,0:T(4,128)S(1)}, u32[]{:S(2)}, u32[]{:S(2)}) collective-permute-start(f32[4,1728]{1,0:T(4,128)S(1)} %slice_select_fusion.2), channel_id=1, source_target_pairs={{0,8},{4,12},{8,0},{12,4},{16,24},{20,28},{24,16},{28,20},{1,9},{5... | collective-permute-start | bytes 82952 | tf_op jit(solution)/shard_map/ppermute | solution.py:30
  39.8 4.4 %collective-permute-start.8 = (f32[2,1728]{1,0:T(2,128)S(1)}, f32[2,1728]{1,0:T(2,128)S(1)}, u32[]{:S(2)}, u32[]{:S(2)}) collective-permute-start(f32[2,1728]{1,0:T(2,128)S(1)} %broadcast_select_fusion.8), channel_id=1, source_target_pairs={{0,4},{4,0},{8,12},{12,8},{16,20},{20,16},{24,28},{28,24},{1,5},{5... | collective-permute-start | bytes 41480 | tf_op jit(solution)/shard_map/ppermute | solution.py:30
  44.3 3.9 collective-permute-start.9
  48.2 6.8 %collective-permute-start.10 = (f32[2,2,8,288]{3,2,1,0:T(8,128)S(1)}, f32[2,2,8,288]{3,2,1,0:T(8,128)S(1)}, u32[]{:S(2)}, u32[]{:S(2)}) collective-permute-start(f32[2,2,8,288]{3,2,1,0:T(8,128)S(1)} %pad_maximum_fusion.2), channel_id=1, source_target_pairs={{0,1},{1,0},{2,3},{3,2},{4,5},{5,4},{6,7},{7,6},{8,9},{9,8},{10,11... | collective-permute-start | bytes 110600 | tf_op jit(solution)/shard_map/ppermute | solution.py:30
  48.6 65.1 %copy-start.12 = (bf16[144,1152]{1,0:T(8,128)(2,1)}, bf16[144,1152]{1,0:T(8,128)(2,1)S(1)}, u32[]{:S(2)}) copy-start(bf16[144,1152]{1,0:T(8,128)(2,1)S(1)} %concatenate.56.refs_6_) | copy-start | bytes 995332
  48.6 27.3 %collective-permute-start.12 = (bf16[144,1152]{1,0:T(8,128)(2,1)S(1)}, bf16[144,1152]{1,0:T(8,128)(2,1)S(1)}, u32[]{:S(2)}, u32[]{:S(2)}) collective-permute-start(bf16[144,1152]{1,0:T(8,128)(2,1)S(1)} %concatenate.56.refs_6_), channel_id=1, source_target_pairs={{0,8},{4,12},{8,0},{12,4},{16,24},{20,28},{24,16},{28,20},{1,9},{5... | collective-permute-start | bytes 995336 | tf_op jit(solution)/shard_map/ppermute | solution.py:30
  48.7 29.0 %collective-permute-start.14 = (bf16[144,1152]{1,0:T(8,128)(2,1)S(1)}, bf16[144,1152]{1,0:T(8,128)(2,1)S(1)}, u32[]{:S(2)}, u32[]{:S(2)}) collective-permute-start(bf16[144,1152]{1,0:T(8,128)(2,1)S(1)} %concatenate.56.refs_6_), channel_id=1, source_target_pairs={{0,16},{4,20},{8,24},{12,28},{16,0},{20,4},{24,8},{28,12},{1,17},{... | collective-permute-start | bytes 995336 | tf_op jit(solution)/shard_map/ppermute | solution.py:30
  51.2 37.0 %collective-permute-start.16 = (bf16[144,1152]{1,0:T(8,128)(2,1)S(1)}, bf16[144,1152]{1,0:T(8,128)(2,1)S(1)}, u32[]{:S(2)}, u32[]{:S(2)}) collective-permute-start(bf16[144,1152]{1,0:T(8,128)(2,1)S(1)} %concatenate.56.refs_6_), channel_id=1, source_target_pairs={{0,24},{4,28},{8,16},{12,20},{16,8},{20,12},{24,0},{28,4},{1,25},{... | collective-permute-start | bytes 995336 | tf_op jit(solution)/shard_map/ppermute | solution.py:30
  53.0 8.9 %collective-permute-start.3 = (bf16[2,288,256]{2,1,0:T(8,128)(2,1)S(1)}, bf16[2,288,256]{2,1,0:T(8,128)(2,1)}, u32[]{:S(2)}, u32[]{:S(2)}) collective-permute-start(bf16[2,288,256]{2,1,0:T(8,128)(2,1)S(1)} %bitcast.89), channel_id=1, source_target_pairs={{0,2},{1,3},{2,0},{3,1},{4,6},{5,7},{6,4},{7,5},{8,10},{9,11},{10,... | collective-permute-start | bytes 884744 | tf_op jit(solution)/shard_map/ppermute | solution.py:30
  55.1 8.7 %collective-permute-start.4 = (bf16[2,288,256]{2,1,0:T(8,128)(2,1)S(1)}, bf16[2,288,256]{2,1,0:T(8,128)(2,1)S(1)}, u32[]{:S(2)}, u32[]{:S(2)}) collective-permute-start(bf16[2,288,256]{2,1,0:T(8,128)(2,1)S(1)} %bitcast.90), channel_id=1, source_target_pairs={{0,1},{1,0},{2,3},{3,2},{4,5},{5,4},{6,7},{7,6},{8,9},{9,8},{10,11... | collective-permute-start | bytes 884744 | tf_op jit(solution)/shard_map/ppermute | solution.py:30
  62.0 29.3 %collective-permute-start.11 = (bf16[144,1152]{1,0:T(8,128)(2,1)S(1)}, bf16[144,1152]{1,0:T(8,128)(2,1)S(1)}, u32[]{:S(2)}, u32[]{:S(2)}) collective-permute-start(bf16[144,1152]{1,0:T(8,128)(2,1)S(1)} %concatenate.56.refs_6_), channel_id=1, source_target_pairs={{0,4},{4,0},{8,12},{12,8},{16,20},{20,16},{24,28},{28,24},{1,5},{5... | collective-permute-start | bytes 995336 | tf_op jit(solution)/shard_map/ppermute | solution.py:30
  63.7 26.6 %copy-start.27 = (bf16[2,288,256]{2,1,0:T(8,128)(2,1)}, bf16[2,288,256]{2,1,0:T(8,128)(2,1)S(1)}, u32[]{:S(2)}) copy-start(bf16[2,288,256]{2,1,0:T(8,128)(2,1)S(1)} %collective-permute-done.4.refs_3_) | copy-start | bytes 884740
  63.7 27.5 %collective-permute-start.5 = (bf16[2,288,256]{2,1,0:T(8,128)(2,1)}, bf16[2,288,256]{2,1,0:T(8,128)(2,1)}, u32[]{:S(2)}, u32[]{:S(2)}) collective-permute-start(bf16[2,288,256]{2,1,0:T(8,128)(2,1)} %collective-permute-done.3.refs_2_), channel_id=1, source_target_pairs={{0,1},{1,0},{2,3},{3,2},{4,5},{5,4},{6,7},{7,6},{8,9},{9,8},{10,11... | collective-permute-start | bytes 884744 | tf_op jit(solution)/shard_map/ppermute | solution.py:30
  75.8 37.9 %copy-start.20 = (bf16[144,1152]{1,0:T(8,128)(2,1)}, bf16[144,1152]{1,0:T(8,128)(2,1)S(1)}, u32[]{:S(2)}) copy-start(bf16[144,1152]{1,0:T(8,128)(2,1)S(1)} %collective-permute-done.12.refs_8_) | copy-start | bytes 995332
  75.8 18.1 %collective-permute-start.13 = (bf16[144,1152]{1,0:T(8,128)(2,1)S(1)}, bf16[144,1152]{1,0:T(8,128)(2,1)S(1)}, u32[]{:S(2)}, u32[]{:S(2)}) collective-permute-start(bf16[144,1152]{1,0:T(8,128)(2,1)S(1)} %collective-permute-done.12.refs_8_), channel_id=1, source_target_pairs={{0,4},{4,0},{8,12},{12,8},{16,20},{20,16},{24,28},{28,24},{1,5},{5... | collective-permute-start | bytes 995336 | tf_op jit(solution)/shard_map/ppermute | solution.py:30
  77.7 36.0 %copy-start.21 = (bf16[144,1152]{1,0:T(8,128)(2,1)}, bf16[144,1152]{1,0:T(8,128)(2,1)S(1)}, u32[]{:S(2)}) copy-start(bf16[144,1152]{1,0:T(8,128)(2,1)S(1)} %collective-permute-done.14.refs_10_) | copy-start | bytes 995332
  77.7 29.5 %collective-permute-start.15 = (bf16[144,1152]{1,0:T(8,128)(2,1)S(1)}, bf16[144,1152]{1,0:T(8,128)(2,1)}, u32[]{:S(2)}, u32[]{:S(2)}) collective-permute-start(bf16[144,1152]{1,0:T(8,128)(2,1)S(1)} %collective-permute-done.14.refs_10_), channel_id=1, source_target_pairs={{0,4},{4,0},{8,12},{12,8},{16,20},{20,16},{24,28},{28,24},{1,5},{5... | collective-permute-start | bytes 995336 | tf_op jit(solution)/shard_map/ppermute | solution.py:30
  88.2 25.5 %copy-start.22 = (bf16[144,1152]{1,0:T(8,128)(2,1)}, bf16[144,1152]{1,0:T(8,128)(2,1)S(1)}, u32[]{:S(2)}) copy-start(bf16[144,1152]{1,0:T(8,128)(2,1)S(1)} %collective-permute-done.16.refs_12_) | copy-start | bytes 995332
  88.2 25.5 %collective-permute-start.17 = (bf16[144,1152]{1,0:T(8,128)(2,1)S(1)}, bf16[144,1152]{1,0:T(8,128)(2,1)}, u32[]{:S(2)}, u32[]{:S(2)}) collective-permute-start(bf16[144,1152]{1,0:T(8,128)(2,1)S(1)} %collective-permute-done.16.refs_12_), channel_id=1, source_target_pairs={{0,4},{4,0},{8,12},{12,8},{16,20},{20,16},{24,28},{28,24},{1,5},{5... | collective-permute-start | bytes 995336 | tf_op jit(solution)/shard_map/ppermute | solution.py:30
  91.2 22.5 %copy-start.23 = (bf16[144,1152]{1,0:T(8,128)(2,1)}, bf16[144,1152]{1,0:T(8,128)(2,1)S(1)}, u32[]{:S(2)}) copy-start(bf16[144,1152]{1,0:T(8,128)(2,1)S(1)} %collective-permute-done.11.refs_7_) | copy-start | bytes 995332
  93.9 19.8 %copy-start.24 = (bf16[144,1152]{1,0:T(8,128)(2,1)}, bf16[144,1152]{1,0:T(8,128)(2,1)S(1)}, u32[]{:S(2)}) copy-start(bf16[144,1152]{1,0:T(8,128)(2,1)S(1)} %collective-permute-done.13.refs_9_) | copy-start | bytes 995332
  125.0 3.1 collective-permute-start.18
  129.7 23.7 %copy-start.3 = (bf16[2,1152,256]{2,1,0:T(8,128)(2,1)}, bf16[2,1152,256]{2,1,0:T(8,128)(2,1)S(1)}, u32[]{:S(2)}) copy-start(bf16[2,1152,256]{2,1,0:T(8,128)(2,1)S(1)} %add_convert_fusion.2.refs_3_) | copy-start | bytes 3538948
  129.8 16.2 %collective-permute-start.19 = (bf16[2,576,256]{2,1,0:T(8,128)(2,1)S(1)}, bf16[2,576,256]{2,1,0:T(8,128)(2,1)S(1)}, u32[]{:S(2)}, u32[]{:S(2)}) collective-permute-start(bf16[2,576,256]{2,1,0:T(8,128)(2,1)S(1)} %constant_dynamic-slice_fusion.2), channel_id=1, source_target_pairs={{0,2},{1,3},{2,0},{3,1},{4,6},{5,7},{6,4},{7,5},{8,10},{9,11},{10,... | collective-permute-start | bytes 1769480 | tf_op jit(solution)/shard_map/ppermute | solution.py:30
  131.4 20.3 %collective-permute-start.21 = (bf16[2,288,256]{2,1,0:T(8,128)(2,1)S(1)}, bf16[2,288,256]{2,1,0:T(8,128)(2,1)}, u32[]{:S(2)}, u32[]{:S(2)}) collective-permute-start(bf16[2,288,256]{2,1,0:T(8,128)(2,1)S(1)} %bitcast.92), channel_id=1, source_target_pairs={{0,2},{1,3},{2,0},{3,1},{4,6},{5,7},{6,4},{7,5},{8,10},{9,11},{10,... | collective-permute-start | bytes 884744 | tf_op jit(solution)/shard_map/ppermute | solution.py:30
  132.4 20.0 %collective-permute-start.22 = (bf16[2,288,256]{2,1,0:T(8,128)(2,1)S(1)}, bf16[2,288,256]{2,1,0:T(8,128)(2,1)}, u32[]{:S(2)}, u32[]{:S(2)}) collective-permute-start(bf16[2,288,256]{2,1,0:T(8,128)(2,1)S(1)} %bitcast.93), channel_id=1, source_target_pairs={{0,1},{1,0},{2,3},{3,2},{4,5},{5,4},{6,7},{7,6},{8,9},{9,8},{10,11... | collective-permute-start | bytes 884744 | tf_op jit(solution)/shard_map/ppermute | solution.py:30
  146.1 7.4 %copy-start.19 = (bf16[2,576,256]{2,1,0:T(8,128)(2,1)}, bf16[2,576,256]{2,1,0:T(8,128)(2,1)S(1)}, u32[]{:S(2)}) copy-start(bf16[2,576,256]{2,1,0:T(8,128)(2,1)S(1)} %collective-permute-done.19.refs_4_) | copy-start | bytes 1769476
  146.1 7.4 %collective-permute-start.20 = (bf16[2,576,256]{2,1,0:T(8,128)(2,1)S(1)}, bf16[2,576,256]{2,1,0:T(8,128)(2,1)}, u32[]{:S(2)}, u32[]{:S(2)}) collective-permute-start(bf16[2,576,256]{2,1,0:T(8,128)(2,1)S(1)} %collective-permute-done.19.refs_4_), channel_id=1, source_target_pairs={{0,1},{1,0},{2,3},{3,2},{4,5},{5,4},{6,7},{7,6},{8,9},{9,8},{10,11... | collective-permute-start | bytes 1769480 | tf_op jit(solution)/shard_map/ppermute | solution.py:30
  151.7 1.8 collective-permute-start.23
  169.9 3.1 collective-permute-start.24
  174.6 17.5 %copy-start.1 = (bf16[2,1152,256]{2,1,0:T(8,128)(2,1)}, bf16[2,1152,256]{2,1,0:T(8,128)(2,1)S(1)}, u32[]{:S(2)}) copy-start(bf16[2,1152,256]{2,1,0:T(8,128)(2,1)S(1)} %add_convert_fusion.1.refs_2_) | copy-start | bytes 3538948
  174.7 15.4 %collective-permute-start.25 = (bf16[2,576,256]{2,1,0:T(8,128)(2,1)S(1)}, bf16[2,576,256]{2,1,0:T(8,128)(2,1)S(1)}, u32[]{:S(2)}, u32[]{:S(2)}) collective-permute-start(bf16[2,576,256]{2,1,0:T(8,128)(2,1)S(1)} %constant_dynamic-slice_fusion.1), channel_id=1, source_target_pairs={{0,2},{1,3},{2,0},{3,1},{4,6},{5,7},{6,4},{7,5},{8,10},{9,11},{10,... | collective-permute-start | bytes 1769480 | tf_op jit(solution)/shard_map/ppermute | solution.py:30
  190.1 2.0 copy-start.7
  190.1 2.0 collective-permute-start.26
  213.4 178.5 %reduce-scatter.5.cloned.1.call-start = ((), (), s32[]{:S(2)}) async-start(), calls=%async_computation.4 | async-start | bytes 5971968 | tf_op jit(solution)/shard_map/reduce_scatter | solution.py:617
  226.0 2.8 collective-permute-start.27
  226.5 4.3 %collective-permute-start.30 = (bf16[2,2,288,256]{3,2,0,1:T(8,128)(2,1)S(1)}, bf16[2,2,288,256]{3,2,0,1:T(8,128)(2,1)S(1)}, u32[]{:S(2)}, u32[]{:S(2)}) collective-permute-start(bf16[2,2,288,256]{3,2,0,1:T(8,128)(2,1)S(1)} %select_bitcast_fusion), channel_id=1, source_target_pairs={{0,1},{1,0},{2,3},{3,2},{4,5},{5,4},{6,7},{7,6},{8,9},{9,8},{10,11... | collective-permute-start | bytes 1769480 | tf_op jit(solution)/shard_map/ppermute | solution.py:30
  229.3 16.2 %collective-permute-start.28 = (bf16[2,576,256]{2,1,0:T(8,128)(2,1)S(1)}, bf16[2,576,256]{2,1,0:T(8,128)(2,1)S(1)}, u32[]{:S(2)}, u32[]{:S(2)}) collective-permute-start(bf16[2,576,256]{2,1,0:T(8,128)(2,1)S(1)} %constant_dynamic-slice_fusion), channel_id=1, source_target_pairs={{0,2},{1,3},{2,0},{3,1},{4,6},{5,7},{6,4},{7,5},{8,10},{9,11},{10,... | collective-permute-start | bytes 1769480 | tf_op jit(solution)/shard_map/ppermute | solution.py:30
  231.1 20.0 %collective-permute-start.31 = (bf16[2,288,256]{2,1,0:T(8,128)(2,1)S(1)}, bf16[2,288,256]{2,1,0:T(8,128)(2,1)S(1)}, u32[]{:S(2)}, u32[]{:S(2)}) collective-permute-start(bf16[2,288,256]{2,1,0:T(8,128)(2,1)S(1)} %fusion.3), channel_id=1, source_target_pairs={{0,2},{1,3},{2,0},{3,1},{4,6},{5,7},{6,4},{7,5},{8,10},{9,11},{10,... | collective-permute-start | bytes 884744 | tf_op jit(solution)/shard_map/ppermute | solution.py:30
  245.5 8.1 %copy-start.9 = (bf16[2,576,256]{2,1,0:T(8,128)(2,1)}, bf16[2,576,256]{2,1,0:T(8,128)(2,1)S(1)}, u32[]{:S(2)}) copy-start(bf16[2,576,256]{2,1,0:T(8,128)(2,1)S(1)} %collective-permute-done.28.refs_4_) | copy-start | bytes 1769476
  245.5 8.1 %collective-permute-start.29 = (bf16[2,576,256]{2,1,0:T(8,128)(2,1)S(1)}, bf16[2,576,256]{2,1,0:T(8,128)(2,1)S(1)}, u32[]{:S(2)}, u32[]{:S(2)}) collective-permute-start(bf16[2,576,256]{2,1,0:T(8,128)(2,1)S(1)} %collective-permute-done.28.refs_4_), channel_id=1, source_target_pairs={{0,1},{1,0},{2,3},{3,2},{4,5},{5,4},{6,7},{7,6},{8,9},{9,8},{10,11... | collective-permute-start | bytes 1769480 | tf_op jit(solution)/shard_map/ppermute | solution.py:30
  262.6 3.7 collective-permute-start.32
  266.4 3.8 collective-permute-start.33
  270.2 5.7 %collective-permute-start.34 = (bf16[8,2016]{1,0:T(8,128)(2,1)S(1)}, bf16[8,2016]{1,0:T(8,128)(2,1)S(1)}, u32[]{:S(2)}, u32[]{:S(2)}) collective-permute-start(bf16[8,2016]{1,0:T(8,128)(2,1)S(1)} %pad_maximum_fusion.3), channel_id=1, source_target_pairs={{0,16},{4,20},{8,24},{12,28},{16,0},{20,4},{24,8},{28,12},{1,17},{... | collective-permute-start | bytes 96776 | tf_op jit(solution)/shard_map/ppermute | solution.py:30
  276.7 3.7 collective-permute-start.35
  280.4 1.2 collective-permute-start.36
  281.8 3.7 collective-permute-start.37
  285.6 4.1 %collective-permute-start.38 = (f32[4,288]{1,0:T(4,128)S(1)}, f32[4,288]{1,0:T(4,128)S(1)}, u32[]{:S(2)}, u32[]{:S(2)}) collective-permute-start(f32[4,288]{1,0:T(4,128)S(1)} %select_n.415), channel_id=1, source_target_pairs={{0,8},{4,12},{8,0},{12,4},{16,24},{20,28},{24,16},{28,20},{1,9},{5... | collective-permute-start | bytes 13832 | tf_op jit(solution)/shard_map/ppermute | solution.py:30
  289.8 5.3 %collective-permute-start.39 = (f32[2,576]{1,0:T(2,128)S(1)}, f32[2,576]{1,0:T(2,128)S(1)}, u32[]{:S(2)}, u32[]{:S(2)}) collective-permute-start(f32[2,576]{1,0:T(2,128)S(1)} %select_bitcast_fusion.5), channel_id=1, source_target_pairs={{0,16},{4,20},{8,24},{12,28},{16,0},{20,4},{24,8},{28,12},{1,17},{... | collective-permute-start | bytes 13832 | tf_op jit(solution)/shard_map/ppermute | solution.py:30
  (10 other events, 12.7 us)
Sparse Core Ops, SparseCore 0:
  10.8 113.5 all-gather.1
  213.5 71.0 reduce-scatter.2
  288.6 103.2 reduce-scatter.4

commit v2 on v1

v2 whole, which is shorter than its diff:
```python
import functools
import math

import jax
import jax.numpy as jnp
import numpy as np
from jax import lax
from jax.experimental import pallas as pl
from jax.experimental.pallas import tpu as pltpu
from jax.sharding import PartitionSpec as P

GRID = 16
BINS = 8
EPS = 1e-06
F32 = jnp.float32
BF16 = jnp.bfloat16
VMEM_BYTES = 56 * 1024 * 1024
LANES = 128
NT = (((1,), (1,)), ((), ()))
NN = (((1,), (0,)), ((), ()))
TN = (((0,), (0,)), ((), ()))


def dot(left, right, dims):
    return lax.dot_general(left, right, dims, preferred_element_type=F32)


def swap(value, axis, bit):
    size = lax.axis_size(axis)
    return lax.ppermute(value, axis, [(i, i ^ bit) for i in range(size)])


def round_up(value, unit):
    return -(-value // unit) * unit


def region(given, work):
    shapes = jax.eval_shape(work)
    return lax.cond(given, work, lambda: jax.tree.map(lambda a: jnp.zeros(a.shape, a.dtype), shapes))


def ordered(bit, mine, other, axis):
    first = jnp.where(bit == 0, mine, other)
    second = jnp.where(bit == 0, other, mine)
    return jnp.concatenate([first, second], axis=axis)


def gather_rows(value, axis):
    size, me = lax.axis_size(axis), lax.axis_index(axis)
    steps = [1 << k for k in range(size.bit_length() - 1)]
    shape = value.shape
    steps = steps[1:] + steps[:1]
    for step in steps:
        value = ordered((me // step) % 2, value[None], swap(value, axis, step)[None], 0)
    count = len(steps)
    order = sorted(range(count), key=lambda k: -steps[count - 1 - k])
    value = jnp.transpose(value, order + [count, count + 1])
    return value.reshape((size * shape[0],) + shape[1:])


def scatter_rows(value, axis):
    size, me = lax.axis_size(axis), lax.axis_index(axis)
    step = size // 2
    while step >= 1:
        half = value.shape[0] // 2
        bit = (me // step) % 2
        keep = jnp.where(bit == 0, value[:half], value[half:])
        send = jnp.where(bit == 0, value[half:], value[:half])
        value = keep + swap(send, axis, step)
        step //= 2
    return value


def rows_to_columns(value, axis):
    size, me = lax.axis_size(axis), lax.axis_index(axis)
    step = 1
    while step < size:
        rows, cols = value.shape
        bit = (me // step) % 2
        per = rows // (size // step)
        split = value.reshape(size // step // 2, 2, per, cols)
        keep = jnp.where(bit == 0, split[:, 0], split[:, 1]).reshape(rows // 2, cols)
        send = jnp.where(bit == 0, split[:, 1], split[:, 0]).reshape(rows // 2, cols)
        value = ordered(bit, keep, swap(send, axis, step), 1)
        step *= 2
    return value


def mp_sum_small(value):
    step = lax.axis_size("mp") // 2
    while step >= 1:
        value = value + swap(value, "mp", step)
        step //= 2
    return value


def mp_pieces(value):
    far = swap(value, "mp", 2)
    near = swap(value, "mp", 1)
    both = swap(far, "mp", 1)
    return [value, far, near, both]


def mp_chip(mine, theirs, *tokens):
    return add_blocks(mine, swap(theirs, "mp", 1), *tokens)


def mp_join(chip, far, *tokens):
    half = add_blocks(chip, far, *tokens)
    return half, swap(half, "mp", 1)


def mp_total(mine, theirs, tokens=()):
    chip = mp_chip(mine, theirs)
    return mp_join(chip, swap(chip, "mp", 2), *tokens)


def mp_quarter(partial):
    images, width, patches = partial.shape
    quarter = width // 4
    me = lax.axis_index("mp")
    core, side = me % 2, me // 2
    split = partial.reshape(images, 2, 2, quarter, patches)
    send = jnp.where(core == 0, split[:, :, 1], split[:, :, 0])
    keep = jnp.where(core == 0, split[:, :, 0], split[:, :, 1])
    chip = keep.astype(F32) + swap(send, "mp", 1).astype(F32)
    send = jnp.where(side == 0, chip[:, 1], chip[:, 0]).astype(BF16)
    keep = jnp.where(side == 0, chip[:, 0], chip[:, 1])
    return keep + swap(send, "mp", 2).astype(F32)


def direct():
    return lax.axis_size("dp") in (2, 4, 8)


def dp_blocks(block):
    if not direct():
        return [lax.all_gather(block, "dp", axis=0, tiled=True)]
    size = lax.axis_size("dp")
    blocks = [block, swap(block, "dp", 1)]
    for k, near in [(k, swap(block, "dp", k)) for k in range(2, size, 2)]:
        blocks += [near, swap(near, "dp", 1)]
    return blocks


def dp_cross(parts):
    if len(parts) == 1:
        return [lax.psum_scatter(parts[0], "dp", scatter_dimension=0, tiled=True)]
    return [swap(parts[k + 1], "dp", 1) for k in range(0, len(parts), 2)]


def dp_pair_sums(parts, cross, *tokens):
    return [add_blocks(parts[2 * k], cross[k], *tokens) for k in range(1, len(cross))]


def dp_lines(halves):
    return [swap(half, "dp", 2 * k + 2) for k, half in enumerate(halves)]


def add_blocks(left, right, *tokens):
    def kernel(*refs):
        refs[-1][...] = (refs[0][...].astype(F32) + refs[1][...].astype(F32)).astype(BF16)

    return pl.pallas_call(
        kernel,
        in_specs=[pl.BlockSpec(memory_space=pltpu.VMEM)] * 2
        + [pl.BlockSpec(memory_space=pl.ANY)] * len(tokens),
        out_specs=pl.BlockSpec(memory_space=pltpu.VMEM),
        out_shape=shaped(left.shape, BF16),
        compiler_params=pltpu.CompilerParams(vmem_limit_bytes=VMEM_BYTES),
        cost_estimate=pl.CostEstimate(flops=1, bytes_accessed=1, transcendentals=0),
    )(left, right, *tokens)


def after(value, *others):
    if not others:
        return value

    def kernel(*refs):
        refs[-1][...] = refs[0][...]

    return pl.pallas_call(
        kernel,
        in_specs=[pl.BlockSpec(memory_space=pltpu.VMEM)]
        + [pl.BlockSpec(memory_space=pl.ANY)] * len(others),
        out_specs=pl.BlockSpec(memory_space=pltpu.VMEM),
        out_shape=shaped(value.shape, value.dtype),
        cost_estimate=pl.CostEstimate(flops=1, bytes_accessed=1, transcendentals=0),
    )(value, *others)


def copy_blocks(place, first, blocks, whole_ref):
    for k, ref in enumerate(blocks):
        if len(blocks) == 1:
            whole_ref[...] = ref[...]
        else:
            whole_ref[rows_at(place[first + k], ref.shape[0]), :] = ref[...]


def split_blocks(place, first, sum_ref, outs):
    for k, ref in enumerate(outs):
        if len(outs) == 1:
            ref[...] = sum_ref[...].astype(BF16)
        else:
            ref[...] = sum_ref[rows_at(place[first + k], ref.shape[0]), :].astype(BF16)


def rotary_tables(patches, head_size):
    pairs = head_size // 4
    freqs = 10000.0 ** (-np.arange(pairs, dtype=np.float64) / pairs)
    spots = np.arange(patches)
    row = (spots // GRID)[None, :] * freqs[:, None]
    col = (spots % GRID)[None, :] * freqs[:, None]
    angles = np.concatenate([row, row, col, col], axis=0)
    cosine, sine = np.cos(angles), np.sin(angles)
    first = (np.arange(head_size) // pairs % 2 == 0)[:, None]
    up = np.where(first, -sine, 0.0)
    down = np.where(first, 0.0, sine)
    return np.stack([cosine, up, down]).astype(np.float32)


def turned(value, up, down):
    height = value.shape[0]
    pairs = height // 4
    return pltpu.roll(value, height - pairs, 0) * up + pltpu.roll(value, pairs, 0) * down


def normed(value):
    centred = value - jnp.mean(value, axis=0, keepdims=True)
    scale = lax.rsqrt(jnp.mean(centred * centred, axis=0, keepdims=True) + EPS)
    return centred * scale, scale


def norm_back(grad, unit, scale):
    return scale * (
        grad
        - jnp.mean(grad, axis=0, keepdims=True)
        - unit * jnp.mean(grad * unit, axis=0, keepdims=True)
    )


def row_sums(value):
    ones = jnp.ones((8, value.shape[1]), F32)
    return lax.dot_general(
        ones, value, NT, precision=lax.Precision.HIGHEST, preferred_element_type=F32
    )[0:1]


def rows_at(index, size):
    return pl.ds(pl.multiple_of(index * size, 16), size)


def heads_of(raw, gains, tables, head):
    size = gains.shape[0]
    width = raw.shape[0] // 3
    cosine, up, down = tables[0], tables[1], tables[2]
    found = []
    for part in range(2):
        rows = raw[part * width + head * size : part * width + (head + 1) * size]
        scale = lax.rsqrt(jnp.mean(rows * rows, axis=0, keepdims=True) + EPS)
        hat = rows * scale
        gained = hat * gains[:, part : part + 1]
        rotated = gained * cosine + turned(gained, up, down)
        found.append((hat, scale, rotated.astype(BF16)))
    value = raw[2 * width + head * size : 2 * width + (head + 1) * size].astype(BF16)
    return found[0], found[1], value


def attention_forward(
    heads, place, lat_refs, mods_ref, weight_refs, gains_ref, tables_ref, outs, scratch
):
    lat_ref, weight_ref, h_ref, raw_ref, lse_ref, ob_ref, mine_ref, theirs_ref = outs
    (x_ref,) = scratch
    quarter = lat_refs[0].shape[1]
    width = quarter
    size = gains_ref.shape[0]
    inverse = 1.0 / math.sqrt(size)

    @pl.when(pl.program_id(0) == 0)
    def _():
        copy_blocks(place, 5, weight_refs, weight_ref)

    for k, ref in enumerate(lat_refs):
        piece = ref[0]
        lat_ref[0, rows_at(place[k], quarter), :] = piece
        x_ref[rows_at(place[k], quarter), :] = piece.astype(F32)
    mods = mods_ref[0].T
    unit, _ = normed(x_ref[...])
    h = (unit * (1.0 + mods[:, 1:2]) + mods[:, 0:1]).astype(BF16)
    h_ref[0] = h
    span = round_up(3 * width, LANES)
    raw = dot(weight_ref[:, :span], h, TN)[: 3 * width]
    raw_ref[0] = raw
    gains, tables = gains_ref[...], tables_ref[...]
    pad = 4 * width - (3 * width) // LANES * LANES - width
    parts, tops = [], []
    for head in range(heads):
        (_, _, query), (_, _, key), value = heads_of(raw, gains, tables, head)
        scores = dot(key, query, TN) * inverse
        top = jnp.max(scores, axis=0, keepdims=True)
        expo = jnp.exp(scores - top)
        total = jnp.sum(expo, axis=0, keepdims=True)
        probs = (expo / total).astype(BF16)
        parts.append(dot(value, probs, NN))
        tops.append(top + jnp.log(total))
    lse_ref[0] = jnp.concatenate(tops, axis=0)
    patches = raw.shape[1]
    ob = jnp.concatenate([jnp.zeros((pad, patches), F32)] + parts, axis=0).astype(BF16)
    ob_ref[0] = ob
    x_ref[...] = dot(weight_ref[:, 4 * width - width - pad :], ob, NN)
    put_halves(place, x_ref, mine_ref, theirs_ref)


def feed_forward(
    place, image_weight, lat_ref, sums, mods_ref, cot_refs, weight_ref, outs, scratch
):
    mid_ref, attn_ref, h_ref, hidden_ref, dffn_ref, dgu_ref, cot_ref, mine_ref, theirs_ref = outs
    (x_ref,) = scratch
    quarter = cot_refs[0].shape[1]
    units = hidden_ref.shape[1]
    mods = mods_ref[0].T
    take_halves(place, x_ref, sums)
    attn_ref[0] = x_ref[rows_at(place[0], quarter), :]
    mid = lat_ref[0].astype(F32) + mods[:, 2:3] * x_ref[...]
    mid_ref[0] = mid
    unit, _ = normed(mid)
    h = (unit * (1.0 + mods[:, 4:5]) + mods[:, 3:4]).astype(BF16)
    h_ref[0] = h
    for k, ref in enumerate(cot_refs):
        piece = ref[0]
        cot_ref[0, rows_at(place[k], quarter), :] = piece
    weight = image_weight[pl.program_id(0)]
    dffn = (mods[:, 5:6] * (cot_ref[0].astype(F32) * weight)).astype(BF16)
    dffn_ref[0] = dffn
    gate = dot(weight_ref[:, :units], h, TN)
    up = dot(weight_ref[:, units : 2 * units], h, TN)
    sig = jax.nn.sigmoid(gate)
    swish = gate * sig
    hidden_ref[0] = (swish * up).astype(BF16)
    dhidden = dot(weight_ref[:, 2 * units :], dffn, TN)
    dgu_ref[0, :units] = (dhidden * up * sig * (1.0 + gate * (1.0 - sig))).astype(BF16)
    dgu_ref[0, units:] = (dhidden * swish).astype(BF16)
    x_ref[...] = dot(weight_ref[:, : 2 * units], dgu_ref[0], NN)
    put_halves(place, x_ref, mine_ref, theirs_ref)


def put_halves(place, x_ref, mine_ref, theirs_ref):
    core, half = place[4], mine_ref.shape[1]
    mine_ref[0] = x_ref[rows_at(core, half), :].astype(BF16)
    theirs_ref[0] = x_ref[rows_at(1 - core, half), :].astype(BF16)


def take_halves(place, x_ref, halves):
    core, half = place[4], halves[0].shape[1]
    x_ref[rows_at(core, half), :] = halves[0][0].astype(F32)
    x_ref[rows_at(1 - core, half), :] = halves[1][0].astype(F32)


def over_images(left_ref, right_ref, rows=slice(None)):
    total = None
    for n in range(left_ref.shape[0]):
        term = dot(left_ref[n], right_ref[n, rows], NT)
        total = term if total is None else total + term
    return total


def feed_forward_grads(h_ref, hidden_ref, dffn_ref, dgu_ref, weight_ref, outs):
    units = hidden_ref.shape[1]
    grad_ref, ffn_ref = outs
    grad_ref[:, :units] = over_images(h_ref, dgu_ref, slice(0, units)).astype(BF16)
    grad_ref[:, units : 2 * units] = over_images(h_ref, dgu_ref, slice(units, 2 * units)).astype(BF16)
    grad_ref[:, 2 * units :] = over_images(dffn_ref, hidden_ref).astype(BF16)
    for n in range(h_ref.shape[0]):
        ffn_ref[n] = dot(weight_ref[...], hidden_ref[n], NN).astype(BF16)


def attention_backward(
    heads,
    place,
    image_weight,
    sums,
    mid_ref,
    attn_ref,
    cot_ref,
    mods_ref,
    raw_ref,
    lse_ref,
    gains_ref,
    tables_ref,
    weight_ref,
    outs,
    scratch,
):
    dmid_ref, dattn_ref, draw_ref, mine_ref, theirs_ref, dmods_ref, qgain_ref, kgain_ref = outs
    x_ref, y_ref = scratch
    quarter = attn_ref.shape[1]
    width = quarter
    size = gains_ref.shape[0]
    inverse = 1.0 / math.sqrt(size)
    mods = mods_ref[0].T
    take_halves(place, x_ref, sums)
    unit, scale = normed(mid_ref[0])
    y_ref[...] = unit
    own = rows_at(place[0], quarter)
    dh_own = x_ref[own, :]
    dmods_ref[0] = jnp.zeros(dmods_ref.shape[1:], F32)
    dmods_ref[0, 3:4, :] = row_sums(dh_own)
    dmods_ref[0, 4:5, :] = row_sums(dh_own * y_ref[own, :])
    weight = image_weight[pl.program_id(0)]
    dy = cot_ref[0].astype(F32) * weight
    dmid = dy + norm_back(x_ref[...] * (1.0 + mods[:, 4:5]), unit, scale)
    dmid_ref[0] = dmid
    x_ref[...] = dmid
    dmods_ref[0, 2:3, :] = row_sums(x_ref[own, :] * attn_ref[0])
    dattn = (mods[:, 2:3] * dmid).astype(BF16)
    dattn_ref[0] = dattn
    start = (3 * width) // LANES * LANES
    pad = 3 * width - start
    dob = dot(weight_ref[:, start:], dattn, TN)
    raw = raw_ref[0]
    gains, tables = gains_ref[...], tables_ref[...]
    cosine, up, down = tables[0], tables[1], tables[2]
    parts = [[], [], []]
    sums_of = [None, None]
    for head in range(heads):
        query, key, value = heads_of(raw, gains, tables, head)
        grad = dob[pad + head * size : pad + (head + 1) * size].astype(BF16)
        scores = dot(key[2], query[2], TN) * inverse
        probs = jnp.exp(scores - lse_ref[0, head : head + 1, :])
        dprobs = dot(value, grad, TN)
        parts[2].append(dot(grad, probs.astype(BF16), NT))
        dscores = probs * (dprobs - jnp.sum(probs * dprobs, axis=0, keepdims=True))
        dscores = dscores.astype(BF16)
        turned_grads = (
            dot(key[2], dscores, NN) * inverse,
            dot(query[2], dscores, NT) * inverse,
        )
        for part, (rot, (hat, rms, _)) in enumerate(zip(turned_grads, (query, key))):
            back = rot * cosine - turned(rot, up, down)
            term = back * hat
            sums_of[part] = term if sums_of[part] is None else sums_of[part] + term
            g = back * gains[:, part : part + 1]
            parts[part].append(rms * (g - hat * jnp.mean(g * hat, axis=0, keepdims=True)))
    qgain_ref[0] = jnp.broadcast_to(row_sums(sums_of[0]), qgain_ref.shape[1:])
    kgain_ref[0] = jnp.broadcast_to(row_sums(sums_of[1]), kgain_ref.shape[1:])
    span = round_up(3 * width, LANES)
    patches = raw.shape[1]
    tail = [jnp.zeros((span - 3 * width, patches), F32)] if span > 3 * width else []
    draw = jnp.concatenate(parts[0] + parts[1] + parts[2] + tail, axis=0).astype(BF16)
    draw_ref[0] = draw
    x_ref[...] = dot(weight_ref[:, :span], draw, NN)
    put_halves(place, x_ref, mine_ref, theirs_ref)


def attention_grads(place, h_ref, draw_ref, dattn_ref, ob_ref, outs, scratch):
    span = draw_ref.shape[1]
    (sum_ref,) = scratch
    start = sum_ref.shape[1] - ob_ref.shape[1]
    total = over_images(h_ref, draw_ref)
    out = over_images(dattn_ref, ob_ref)
    sum_ref[:, :start] = total[:, :start]
    sum_ref[:, start:span] = total[:, start:] + out[:, : span - start]
    sum_ref[:, span:] = out[:, span - start :]
    split_blocks(place, 5, sum_ref, outs)


def last_steps(
    place, image_weight, keep, sums, lat_ref, dmid_ref, mid_ref, cot_ref, mods_ref, ffn_ref,
    dmods_ref, outs, scratch
):
    out_ref, dlat_ref, dm_ref = outs
    x_ref, y_ref = scratch
    quarter = ffn_ref.shape[1]
    own = rows_at(place[0], quarter)
    mods = mods_ref[0].T
    take_halves(place, x_ref, sums)
    unit, scale = normed(lat_ref[0].astype(F32))
    y_ref[...] = unit
    dh_own = x_ref[own, :]
    dm_ref[0] = dmods_ref[0]
    dm_ref[0, 0:1, :] = row_sums(dh_own)
    dm_ref[0, 1:2, :] = row_sums(dh_own * y_ref[own, :])
    back = norm_back(x_ref[...] * (1.0 + mods[:, 1:2]), unit, scale)
    x_ref[...] = back
    dlat_ref[0] = (dmid_ref[0, own, :] + x_ref[own, :]).astype(BF16)
    n = pl.program_id(0)
    ffn = ffn_ref[0]
    dy = cot_ref[0, own, :].astype(F32) * image_weight[n]
    dm_ref[0, 5:6, :] = row_sums(dy * ffn)
    y_ref[...] = jnp.broadcast_to(mods[:, 5:6], y_ref.shape)
    out_ref[0] = ((mid_ref[0, own, :] + y_ref[own, :] * ffn) * keep[n]).astype(BF16)


def whole(array):
    return pl.BlockSpec(array.shape, lambda n: (0,) * array.ndim)


def last(array):
    width = array.shape[1] // 3
    return pl.BlockSpec((array.shape[0], width), lambda n: (0, 2))


def each(array):
    return pl.BlockSpec((1,) + array.shape[1:], lambda n: (n,) + (0,) * (array.ndim - 1))


def token(_):
    return pl.BlockSpec(memory_space=pl.ANY)


def scalars(_):
    return pl.BlockSpec(memory_space=pltpu.SMEM)


def call(body, groups, outs, scratch, images, flops=1):
    flat, specs, counts = [], [], []
    for group in groups:
        counts.append(len(group))
        for array, kind in group:
            flat.append(array)
            specs.append(kind(array))

    def kernel(*refs):
        at, lists = 0, []
        for count in counts:
            lists.append(list(refs[at : at + count]))
            at += count
        body(*lists, list(refs[at : at + len(outs)]), list(refs[at + len(outs) :]))

    moved = sum(a.size * a.dtype.itemsize for a in flat) if flops > 1 else 1
    return pl.pallas_call(
        kernel,
        grid=(images,),
        in_specs=specs,
        out_specs=[kind(o) for o, kind in outs],
        out_shape=[o for o, _ in outs],
        scratch_shapes=scratch,
        compiler_params=pltpu.CompilerParams(
            dimension_semantics=("arbitrary",), vmem_limit_bytes=VMEM_BYTES
        ),
        cost_estimate=pl.CostEstimate(flops=flops, bytes_accessed=moved, transcendentals=0),
    )(*flat)


def shaped(shape, dtype):
    return jax.ShapeDtypeStruct(shape, dtype)


def body(
    latents,
    condition,
    noise_bins,
    slot_valid,
    ada_weight,
    ada_bias,
    qkv_weight,
    query_gain,
    key_gain,
    out_weight,
    gate_up,
    down_weight,
    cotangent,
):
    images, patches, quarter = latents.shape
    width = condition.shape[1]
    rows = qkv_weight.shape[0]
    units = gate_up.shape[2]
    head_size = query_gain.shape[0]
    heads = quarter // head_size
    dp, mp = lax.axis_index("dp"), lax.axis_index("mp")
    core = mp % 2
    dp_size = lax.axis_size("dp")
    all_images = dp_size * images
    tokens = images * patches

    extra = jnp.stack([noise_bins, slot_valid], axis=1).astype(BF16)
    told = jnp.concatenate([condition, extra, jnp.zeros((images, LANES - 2), BF16)], axis=1)
    told = gather_rows(told, "dp")
    all_bins, all_valid = told[:, width].astype(F32), told[:, width + 1].astype(F32)
    cond_rows = lax.dynamic_slice_in_dim(told[:, :width], dp * rows, rows, 1).astype(F32)

    by_part = jnp.transpose(qkv_weight, (1, 0, 2))
    first_pack = jnp.concatenate([by_part[0], by_part[1], by_part[2], out_weight.T], axis=1)
    second_pack = jnp.concatenate([gate_up[:, 0], gate_up[:, 1], down_weight.T], axis=1)
    lat_pieces = mp_pieces(jnp.transpose(latents, (0, 2, 1)))
    first_blocks = dp_blocks(first_pack)
    second = lax.all_gather(second_pack, "dp", axis=0, tiled=True)
    cot_pieces = mp_pieces(jnp.transpose(cotangent, (0, 2, 1)))
    ada = jnp.transpose(ada_weight, (1, 0, 2))
    keep = slot_valid.astype(F32)
    given = noise_bins[0] >= 0

    bin_ids = jnp.arange(BINS, dtype=F32)
    member = (all_bins[:, None] == bin_ids[None, :]).astype(F32) * all_valid[:, None]
    per_bin = jnp.sum(member, axis=0)
    own_bins = noise_bins.astype(F32)
    own_count = jnp.sum((own_bins[:, None] == bin_ids[None, :]) * per_bin[None, :], axis=1)
    image_weight = keep * jnp.sum(all_valid) / (BINS * jnp.maximum(own_count, 1.0))

    cond_act = jax.nn.silu(cond_rows).astype(BF16)
    mods_terms = jnp.einsum("nd,cde->nce", cond_act, ada, preferred_element_type=F32)
    mods_own = scatter_rows(mods_terms.reshape(all_images, -1), "dp")
    mods_own = mods_own.reshape(images, 6, quarter) + ada_bias[None]
    mods_own = jnp.pad(mods_own, ((0, 0), (0, 2), (0, 0)))
    side = mp // 2
    far = swap(mods_own, "mp", 2)
    pair = jnp.stack([jnp.where(side == 0, mods_own, far), jnp.where(side == 0, far, mods_own)])
    beside = swap(pair, "mp", 1)
    quad = jnp.stack(
        [jnp.where(core == 0, pair, beside), jnp.where(core == 0, beside, pair)], axis=1
    )
    mods = jnp.transpose(quad, (2, 3, 0, 1, 4)).reshape(images, 8, width)

    count = dp_size if direct() else 1
    place = jnp.stack([mp, mp ^ 2, mp ^ 1, mp ^ 3, core] + [dp ^ k for k in range(count)])
    place = place.astype(jnp.int32)
    block_shape = (width // count,)
    gains = jnp.stack([query_gain, key_gain], axis=1)
    tables = jnp.asarray(rotary_tables(patches, head_size))
    full = 4 * quarter
    span = round_up(3 * quarter, LANES)
    start = 3 * quarter // LANES * LANES
    wide = lambda dtype: shaped((images, width, patches), dtype)
    half = shaped((images, width // 2, patches), BF16)
    tall = pltpu.VMEM((width, patches), F32)

    lat, first, h_one, raw, lse, ob, *attn_terms = call(
        lambda p, l, m, w, g, t, outs, s: attention_forward(
            heads, p[0], l, m[0], w, g[0], t[0], outs, s
        ),
        [
            [(place, scalars)],
            [(a, each) for a in lat_pieces],
            [(mods, each)],
            [(a, whole) for a in first_blocks],
            [(gains, whole)],
            [(tables, whole)],
        ],
        [
            (wide(BF16), each),
            (shaped((width, full), BF16), whole),
            (wide(BF16), each),
            (shaped((images, 3 * quarter, patches), F32), each),
            (shaped((images, heads, patches), F32), each),
            (shaped((images, full - start, patches), BF16), each),
            (half, each),
            (half, each),
        ],
        [tall],
        images,
        2 * images * patches * width * full,
    )
    attn_sums = mp_total(*attn_terms)

    def middle():
        mid, attn_own, h_two, hidden, dffn, dgu, cot, mine, theirs = call(
            lambda p, w, l, s, m, c, k, outs, x: feed_forward(
                p[0], w[0], l[0], s, m[0], c, k[0], outs, x
            ),
            [
                [(place, scalars)],
                [(image_weight, scalars)],
                [(lat, each)],
                [(a, each) for a in attn_sums],
                [(mods, each)],
                [(a, each) for a in cot_pieces],
                [(second, whole)],
            ],
            [
                (wide(F32), each),
                (shaped((images, quarter, patches), F32), each),
                (wide(BF16), each),
                (shaped((images, units, patches), BF16), each),
                (wide(BF16), each),
                (shaped((images, 2 * units, patches), BF16), each),
                (wide(BF16), each),
                (half, each),
                (half, each),
            ],
            [tall],
            images,
        )
        chip = mp_chip(mine, theirs)
        grads = call(
            lambda a, outs, x: feed_forward_grads(*a, outs),
            [[(h_two, whole), (hidden, whole), (dffn, whole), (dgu, whole), (second, last)]],
            [(shaped((width, 3 * units), BF16), whole), (wide(BF16), whole)],
            [],
            1,
        )
        return mid, attn_own, cot, chip, swap(chip, "mp", 2), grads

    mid, attn_own, cot, dh_two_chip, dh_two_far, grads = region(given, middle)
    second_terms, ffn_part = grads
    second_sum = lax.psum_scatter(second_terms, "dp", scatter_dimension=0, tiled=True)

    def backward():
        dh_two_sums = mp_join(dh_two_chip, dh_two_far)
        dmid, dattn, draw, mine, theirs, dmods_part, qgain, kgain = call(
            lambda p, w, s, a, outs, x: attention_backward(heads, p[0], w[0], s, *a, outs, x),
            [
                [(place, scalars)],
                [(image_weight, scalars)],
                [(a, each) for a in dh_two_sums],
                [
                    (mid, each),
                    (attn_own, each),
                    (cot, each),
                    (mods, each),
                    (raw, each),
                    (lse, each),
                    (gains, whole),
                    (tables, whole),
                    (first, whole),
                ],
            ],
            [
                (wide(F32), each),
                (wide(BF16), each),
                (shaped((images, span, patches), BF16), each),
                (half, each),
                (half, each),
                (shaped((images, 8, quarter), F32), each),
                (shaped((images, 8, head_size), F32), each),
                (shaped((images, 8, head_size), F32), each),
            ],
            [tall, tall],
            images,
        )
        first_terms = call(
            lambda p, a, outs, x: attention_grads(p[0], *a, outs, x),
            [
                [(place, scalars)],
                [(h_one, whole), (draw, whole), (dattn, whole), (ob, whole)],
            ],
            [(shaped(block_shape + (full,), BF16), whole)] * count,
            [pltpu.VMEM((width, full), F32)],
            1,
        )
        ffn_own = mp_quarter(ffn_part)
        first_beside = dp_cross(first_terms)
        dh_one_sums = mp_total(mine, theirs, tuple(first_terms))
        block_out, latent_grad, dmods = call(
            lambda p, w, k, s, a, outs, x: last_steps(p[0], w[0], k[0], s, *a, outs, x),
            [
                [(place, scalars)],
                [(image_weight, scalars)],
                [(keep, scalars)],
                [(a, each) for a in dh_one_sums],
                [
                    (lat, each),
                    (dmid, each),
                    (mid, each),
                    (cot, each),
                    (mods, each),
                    (ffn_own, each),
                    (dmods_part, each),
                ],
            ],
            [
                (shaped((images, quarter, patches), BF16), each),
                (shaped((images, quarter, patches), BF16), each),
                (shaped((images, 8, quarter), F32), each),
            ],
            [tall, tall],
            images,
        )

        gain_terms = jnp.concatenate([jnp.sum(qgain[:, 0], axis=0), jnp.sum(kgain[:, 0], axis=0)])
        high = gain_terms.astype(BF16)
        low = (gain_terms - high.astype(F32)).astype(BF16)
        beside = jnp.concatenate([high, low])[None]
        beside = jnp.concatenate([beside, jnp.zeros((images - 1, beside.shape[1]), BF16)], axis=0)
        rounded = dmods[:, :6].astype(BF16).reshape(images, 6 * quarter)
        told_back = gather_rows(jnp.concatenate([rounded, beside], axis=1), "dp")
        halves = dp_pair_sums(first_terms, first_beside) if count > 1 else []
        return block_out, latent_grad, told_back, first_terms[0], first_beside[0], halves

    block_out, latent_grad, told_back, first_own, first_beside, halves = region(given, backward)
    first_far = dp_lines(halves)

    def modulation_grads():
        dmods_all = told_back[:, : 6 * quarter].reshape(all_images, 6, quarter)
        gain_sum = jnp.sum(told_back[:, 6 * quarter :].astype(F32), axis=0)
        gain_sum = gain_sum[: 2 * head_size] + gain_sum[2 * head_size :]
        ada_grad = jnp.einsum("nd,nce->cde", cond_act, dmods_all, preferred_element_type=F32)
        bias_grad = jnp.sum(dmods_all.astype(F32), axis=0)
        cond_terms = jnp.einsum("nce,cde->nd", dmods_all, ada, preferred_element_type=F32)
        both = mp_sum_small(jnp.concatenate([cond_terms.reshape(-1), gain_sum]))
        gain_sum = both[cond_terms.size :]
        cond_sum = rows_to_columns(both[: cond_terms.size].reshape(cond_terms.shape), "dp")
        return ada_grad, bias_grad, gain_sum, cond_sum

    ada_grad, bias_grad, gain_sum, cond_sum = region(given, modulation_grads)
    first_sum = first_beside.astype(F32)
    if count > 1:
        first_sum = first_sum + first_own.astype(F32)
    for line in first_far:
        first_sum = first_sum + line.astype(F32)
    cond_own = condition.astype(F32)
    sig = jax.nn.sigmoid(cond_own)
    condition_grad = (cond_sum * sig * (1.0 + cond_own * (1.0 - sig))).astype(BF16)
    second_sum = second_sum.astype(F32)
    gateup_grad = jnp.stack([second_sum[:, :units], second_sum[:, units : 2 * units]], axis=1)
    down_grad = second_sum[:, 2 * units :].T
    qkv_grad = first_sum[:, : 3 * quarter].reshape(rows, 3, quarter)
    out_grad = first_sum[:, 3 * quarter :].T
    return (
        jnp.transpose(block_out, (0, 2, 1)),
        jnp.transpose(latent_grad, (0, 2, 1)),
        condition_grad,
        jnp.transpose(ada_grad, (1, 0, 2)),
        bias_grad,
        qkv_grad,
        gain_sum[:head_size],
        gain_sum[head_size:],
        out_grad,
        gateup_grad,
        down_grad,
    )


def solution(mesh):
    placed = (
        P("dp", None, "mp"),
        P("dp", None),
        P("dp"),
        P("dp"),
        P("dp", None, "mp"),
        P(None, "mp"),
        P("dp", None, "mp"),
        P(),
        P(),
        P("mp", "dp"),
        P("dp", None, "mp"),
        P("mp", "dp"),
        P("dp", None, "mp"),
    )
    return jax.shard_map(
        body,
        mesh=mesh,
        in_specs=placed,
        out_specs=(
            P("dp", None, "mp"),
            P("dp", None, "mp"),
            P("dp", None),
            P("dp", None, "mp"),
            P(None, "mp"),
            P("dp", None, "mp"),
            P(),
            P(),
            P("mp", "dp"),
            P("dp", None, "mp"),
            P("mp", "dp"),
        ),
        check_vma=False,
    )
```

time: 403 us -> 358 us (0.89)
  waiting for transfers between devices: 239 us -> 177 us
  Pallas kernels: 63.1 us -> 75.5 us
    reduce_scatter x2 -> x1, waiting for transfers between devices: 92.9 us -> 0.01 us  [body(): lax.psum_scatter(second_terms, 'dp', scatter_dimension=0, tiled=True)]
    ppermute x40 -> x47, waiting for transfers between devices: 146 us -> 177 us  [swap(): return lax.ppermute(value, axis, [(i, i ^ bit) for i in range(size)])]
    pallas_call x0 -> x9, Pallas kernels: none -> 18.1 us  [add_blocks(): pl.pallas_call(kernel, in_specs=[pl.BlockSpec(memory_space=pltpu.VMEM)] *...]
    cond x0 -> x44, local copies, waits for them, and re-layouts: none -> 6.06 us
    pallas_call x6, Pallas kernels: 63.1 us -> 57.3 us  [call(): pl.pallas_call(kernel, grid=(images,), in_specs=specs, out_specs=[kind(o)...]
    convert_element_type x7 -> x4, other arithmetic: 4.52 us -> 0.26 us  [the longest x1 0.1 us: body(): cond_act = jax.nn.silu(cond_rows).astype(BF16)]
    ppermute x40 -> x47, starting transfers between devices: 49.8 us -> 53.6 us  [swap(): return lax.ppermute(value, axis, [(i, i ^ bit) for i in range(size)])]
  transfers between devices with their start and end apart: 43 -> 49, of which waited for: 31 -> 32; matrix products, arithmetic and copies ran while one was open for 6% -> 6% of each run, Pallas kernels for 7% -> 17%
where the time goes in v2:
time: 358 us; the launch traced here: 357 us
  waiting for transfers between devices  177 us (49%)
  Pallas kernels  75.5 us (21%)
  starting transfers between devices  53.7 us (15%)
  local copies, waits for them, and re-layouts  21.8 us (6%)
  between operations  14.7 us (4%)
  other arithmetic  12.4 us (3%)
    ppermute x47, waiting for transfers between devices, swap(): return lax.ppermute(value, axis, [(i, i ^ bit) for i in range(size)])  177 us
    pallas_call x6, Pallas kernels, call(): pl.pallas_call(kernel, grid=(images,), in_specs=specs, out_specs=[kind(o)...  57.3 us
    ppermute x47, starting transfers between devices, swap(): return lax.ppermute(value, axis, [(i, i ^ bit) for i in range(size)])  53.6 us
    pallas_call x9, Pallas kernels, add_blocks(): pl.pallas_call(kernel, in_specs=[pl.BlockSpec(memory_space=pltpu.VMEM)] *...  18.1 us
  transfers between devices with their start and end apart: 49, of which 32 were waited for; matrix products, arithmetic and copies ran while one was open for 6% of the time, Pallas kernels for 17%

profile of v2, /device:TPU:0, one launch (start us, length us, event | category | flops | bytes accessed | tf_op | source)
XLA Modules:
  0.0 357.5 jit_solution(6046626418435627472)
XLA Ops:
  7.2 2.0 fusion.34
  10.6 3.0 collective-permute-start.20
  13.7 1.6 collective-permute-done.20
  15.3 3.1 collective-permute-start.21
  18.4 1.7 collective-permute-done.21
  20.1 1.9 collective-permute-start.22
  22.0 1.9 collective-permute-done.22
  24.7 3.1 collective-permute-start.26
  27.9 5.7 %collective-permute-done.26 = f32[8,1728]{1,0:T(8,128)S(1)} collective-permute-done((f32[8,1728]{1,0:T(8,128)S(1)}, f32[8,1728]{1,0:T(8,128)S(1)}, u32[]{:S(2)}, u32[]{:S(2)}) %collective-permute-start.26) | collective-permute-done | bytes 55328 | tf_op jit(solution)/shard_map/ppermute | solution.py:30
  34.0 5.0 %collective-permute-done.27 = f32[4,1728]{1,0:T(4,128)S(1)} collective-permute-done((f32[4,1728]{1,0:T(4,128)S(1)}, f32[4,1728]{1,0:T(4,128)S(1)}, u32[]{:S(2)}, u32[]{:S(2)}) %collective-permute-start.27) | collective-permute-done | bytes 27680 | tf_op jit(solution)/shard_map/ppermute | solution.py:30
  39.1 2.9 collective-permute-start.28
  42.0 1.7 collective-permute-done.28
  45.4 2.3 collective-permute-done.29
  48.1 2.4 collective-permute-start.36
  50.5 2.0 collective-permute-start.32
  54.9 2.1 collective-permute-start.31
  57.0 5.1 %collective-permute-done.23.refs_2_ = bf16[2,288,256]{2,1,0:T(8,128)(2,1)} collective-permute-done((bf16[2,288,256]{2,1,0:T(8,128)(2,1)S(1)}, bf16[2,288,256]{2,1,0:T(8,128)(2,1)}, u32[]{:S(2)}, u32[]{:S(2)}) %collective-permute-start.23) | collective-permute-done | bytes 294944 | tf_op jit(solution)/shard_map/ppermute | solution.py:30
  63.1 2.4 collective-permute-start.37
  65.6 39.4 %collective-permute-done.34.refs_10_ = bf16[144,1152]{1,0:T(8,128)(2,1)S(1)} collective-permute-done((bf16[144,1152]{1,0:T(8,128)(2,1)S(1)}, bf16[144,1152]{1,0:T(8,128)(2,1)S(1)}, u32[]{:S(2)}, u32[]{:S(2)}) %collective-permute-start.34) | collective-permute-done | bytes 331808 | tf_op jit(solution)/shard_map/ppermute | solution.py:30
  105.0 2.0 collective-permute-start.33
  107.3 8.5 %collective-permute-done.35.refs_11_ = bf16[144,1152]{1,0:T(8,128)(2,1)} collective-permute-done((bf16[144,1152]{1,0:T(8,128)(2,1)S(1)}, bf16[144,1152]{1,0:T(8,128)(2,1)}, u32[]{:S(2)}, u32[]{:S(2)}) %collective-permute-start.35) | collective-permute-done | bytes 331808 | tf_op jit(solution)/shard_map/ppermute | solution.py:30
  115.8 4.3 %collective-permute-done.33.refs_9_ = bf16[144,1152]{1,0:T(8,128)(2,1)} collective-permute-done((bf16[144,1152]{1,0:T(8,128)(2,1)S(1)}, bf16[144,1152]{1,0:T(8,128)(2,1)}, u32[]{:S(2)}, u32[]{:S(2)}) %collective-permute-start.33) | collective-permute-done | bytes 331808 | tf_op jit(solution)/shard_map/ppermute | solution.py:30
  120.1 11.2 %shard_map.221 = (bf16[2,1152,256]{2,1,0:T(8,128)(2,1)}, bf16[1152,1152]{1,0:T(8,128)(2,1)}, bf16[2,1152,256]{2,1,0:T(8,128)(2,1)}, f32[2,864,256]{2,1,0:T(8,128...) custom-call(s32[13]{0:T(128)S(1)} %stack.101.refs_0_, ...), custom_call_target="tpu_custom_call" | custom-call | flops 1358954496 | bytes 4129396 | tf_op jit(solution)/shard_map/pallas_call | solution.py:531
  131.4 2.2 collective-permute-done.38.refs_1_
  134.4 2.2 shard_map.222.refs_0_
  136.6 2.0 collective-permute-start.39
  138.7 14.3 %collective-permute-done.39.refs_1_ = bf16[2,576,256]{2,1,0:T(8,128)(2,1)S(1)} collective-permute-done((bf16[2,576,256]{2,1,0:T(8,128)(2,1)}, bf16[2,576,256]{2,1,0:T(8,128)(2,1)S(1)}, u32[]{:S(2)}, u32[]{:S(2)}) %collective-permute-start.39) | collective-permute-done | bytes 589856 | tf_op jit(solution)/shard_map/ppermute | solution.py:30
  156.6 2.2 collective-permute-done.41
  160.4 36.7 %conditional.3 = (f32[2,1152,256]{2,1,0:T(8,128)S(1)}, f32[2,288,256]{2,1,0:T(8,128)}, bf16[2,1152,256]{2,1,0:T(8,128)(2,1)}, bf16[2,576,256]{2,1,0:T(8,128)(2,1...) conditional(s32[]{:T(128)} %bitcast.17, () %tuple.39, ...), branch_computations={%region_3.4_spmd, %region_4.5_spmd} | conditional | flops 3 | bytes 30376320 | solution.py:39
  161.8 14.2 %branch_1_fun.12 = (f32[2,1152,256]{2,1,0:T(8,128)S(1)}, f32[2,288,256]{2,1,0:T(8,128)}, bf16[2,1152,256]{2,1,0:T(8,128)(2,1)}, bf16[2,768,256]{2,1,0:T(8,128)(2...) custom-call(s32[13]{0:T(128)S(1)} %get-tuple-element.68.refs_0_, ...), custom_call_target="tpu_custom_call" | custom-call | flops 1 | bytes 1 | tf_op jit(solution)/shard_map/cond/branch_1_fun/pallas_call | solution.py:531
  176.2 2.1 collective-permute-done.refs_1_
  179.1 2.2 branch_1_fun.13
  181.4 1.7 collective-permute-start.1
  183.1 8.1 %branch_1_fun.14 = (bf16[1152,2304]{1,0:T(8,128)(2,1)}, bf16[2,1152,256]{2,1,0:T(8,128)(2,1)}) custom-call(bf16[2,1152,256]{2,1,0:T(8,128)(2,1)} %get-tuple-element.84.refs_0_, bf16[2,768,256]{2,1,0:T(8,128)(2,1)} %get-tuple-element.85.refs_1_, bf16[2,1152,256]{2,1,0:T(8,128)(2,1)} %get-tuple-element.86.refs_2_, ...), custom_call_target="tpu_custom_call" | custom-call | flops 1 | bytes 1 | tf_op jit(solution)/shard_map/cond/branch_1_fun/pallas_call | solution.py:531
  191.2 5.9 %collective-permute-done.1 = bf16[2,576,256]{2,1,0:T(8,128)(2,1)} collective-permute-done((bf16[2,576,256]{2,1,0:T(8,128)(2,1)}, bf16[2,576,256]{2,1,0:T(8,128)(2,1)}, u32[]{:S(2)}, u32[]{:S(2)}) %collective-permute-start.1) | collective-permute-done | bytes 589856 | tf_op jit(solution)/shard_map/cond/branch_1_fun/ppermute | solution.py:30
  198.1 107.6 %conditional.4 = (bf16[2,288,256]{2,1,0:T(8,128)(2,1)}, bf16[2,288,256]{2,1,0:T(8,128)(2,1)}, bf16[16,2016]{1,0:T(8,128)(2,1)S(1)}, bf16[144,1152]{1,0:T(8,128)(...) conditional(s32[]{:T(128)} %bitcast.17, () %tuple.38, ...), branch_computations={%region_5.6_spmd, %region_6.9_spmd} | conditional | flops 2750201 | bytes 65449520 | solution.py:39
  198.1 2.2 branch_1_fun.15.refs_2_
  202.8 12.7 %branch_1_fun.16 = (f32[2,1152,256]{2,1,0:T(8,128)}, bf16[2,1152,256]{2,1,0:T(8,128)(2,1)}, bf16[2,896,256]{2,1,0:T(8,128)(2,1)}, bf16[2,576,256]{2,1,0:T(8,128)...) custom-call(s32[13]{0:T(128)S(1)} %get-tuple-element.90.refs_0_, ...), custom_call_target="tpu_custom_call" | custom-call | flops 1 | bytes 1 | tf_op jit(solution)/shard_map/cond/branch_1_fun/pallas_call | solution.py:531
  218.1 2.2 branch_1_fun.17.refs_0_
  220.3 1.8 collective-permute-start.4
  223.9 5.2 %branch_1_fun.18 = (bf16[144,1152]{1,0:T(8,128)(2,1)}, bf16[144,1152]{1,0:T(8,128)(2,1)}, bf16[144,1152]{1,0:T(8,128)(2,1)}, bf16[144,1152]{1,0:T(8,128)(2,1)}, ...) custom-call(s32[13]{0:T(128)S(1)} %get-tuple-element.90.refs_0_, ...), custom_call_target="tpu_custom_call" | custom-call | flops 1 | bytes 1 | tf_op jit(solution)/shard_map/cond/branch_1_fun/pallas_call | solution.py:531
  229.8 6.9 %collective-permute-done.4.refs_1_ = bf16[2,576,256]{2,1,0:T(8,128)(2,1)S(1)} collective-permute-done((bf16[2,576,256]{2,1,0:T(8,128)(2,1)}, bf16[2,576,256]{2,1,0:T(8,128)(2,1)S(1)}, u32[]{:S(2)}, u32[]{:S(2)}) %collective-permute-start.4) | collective-permute-done | bytes 589856 | tf_op jit(solution)/shard_map/cond/branch_1_fun/ppermute | solution.py:30
  237.5 2.2 branch_1_fun.19.refs_3_
  239.9 2.5 collective-permute-done.7
  244.2 6.0 %branch_1_fun.20 = (bf16[2,288,256]{2,1,0:T(8,128)(2,1)}, bf16[2,288,256]{2,1,0:T(8,128)(2,1)}, f32[2,8,288]{2,1,0:T(8,128)}) custom-call(s32[13]{0:T(128)S(1)} %get-tuple-element.90.refs_0_, f32[2]{0:T(128)S(1)} %get-tuple-element.91.refs_1_, f32[2]{0:T(128)S(1)} %get-tuple-element.92.refs_2_, bf16[2,576,256]{2,1,0:T(8,128)(2,1)} %branch_1_fun.19.refs_3_, ...), custom_call_target="tpu_custom_call" | custom-call | flops 1 | bytes 1 | tf_op jit(solution)/shard_map/cond/branch_1_fun/pallas_call | solution.py:531
  251.2 3.6 %collective-permute-done.8 = bf16[2,2016]{1,0:T(2,128)(2,1)S(1)} collective-permute-done((bf16[2,2016]{1,0:T(2,128)(2,1)S(1)}, bf16[2,2016]{1,0:T(2,128)(2,1)S(1)}, u32[]{:S(2)}, u32[]{:S(2)}) %collective-permute-start.8) | collective-permute-done | bytes 8096 | tf_op jit(solution)/shard_map/cond/branch_1_fun/ppermute | solution.py:30
  254.9 3.0 collective-permute-start.9
  257.9 2.0 collective-permute-start.11
  260.0 2.0 collective-permute-start.13
  262.2 12.5 %collective-permute-done.14 = bf16[144,1152]{1,0:T(8,128)(2,1)S(1)} collective-permute-done((bf16[144,1152]{1,0:T(8,128)(2,1)}, bf16[144,1152]{1,0:T(8,128)(2,1)S(1)}, u32[]{:S(2)}, u32[]{:S(2)}) %collective-permute-start.14) | collective-permute-done | bytes 331808 | tf_op jit(solution)/shard_map/cond/branch_1_fun/ppermute | solution.py:30
  275.9 6.0 %collective-permute-done.11.refs_1_ = bf16[144,1152]{1,0:T(8,128)(2,1)S(1)} collective-permute-done((bf16[144,1152]{1,0:T(8,128)(2,1)}, bf16[144,1152]{1,0:T(8,128)(2,1)S(1)}, u32[]{:S(2)}, u32[]{:S(2)}) %collective-permute-start.11) | collective-permute-done | bytes 331808 | tf_op jit(solution)/shard_map/cond/branch_1_fun/ppermute | solution.py:30
  282.6 1.9 branch_1_fun.21
  284.4 6.4 %collective-permute-done.12.refs_1_ = bf16[144,1152]{1,0:T(8,128)(2,1)S(1)} collective-permute-done((bf16[144,1152]{1,0:T(8,128)(2,1)}, bf16[144,1152]{1,0:T(8,128)(2,1)S(1)}, u32[]{:S(2)}, u32[]{:S(2)}) %collective-permute-start.12) | collective-permute-done | bytes 331808 | tf_op jit(solution)/shard_map/cond/branch_1_fun/ppermute | solution.py:30
  291.6 1.9 branch_1_fun.22
  293.5 9.3 %collective-permute-done.13.refs_1_ = bf16[144,1152]{1,0:T(8,128)(2,1)S(1)} collective-permute-done((bf16[144,1152]{1,0:T(8,128)(2,1)S(1)}, bf16[144,1152]{1,0:T(8,128)(2,1)S(1)}, u32[]{:S(2)}, u32[]{:S(2)}) %collective-permute-start.13) | collective-permute-done | bytes 331808 | tf_op jit(solution)/shard_map/cond/branch_1_fun/ppermute | solution.py:30
  303.5 1.9 branch_1_fun.23
  307.8 2.4 collective-permute-start.46
  310.1 31.8 %conditional.5 = (f32[6,144,288]{2,1,0:T(8,128)S(1)}, f32[6,288]{1,0:T(8,128)S(1)}, bf16[144]{0:T(256)(128)(2,1)S(1)}, f32[2,1152]{1,0:T(2,128)S(1)}, f32[72]{0:T(128)S(1)}, /*index=5*/f32[72]{0:T(128)S(1)}) conditional(s32[]{:T(128)} %bitcast.17, () %tuple.42, (bf16[16,2016]{1,0:T(8,128)(2,1)S(1)}, bf16[16,144]{1,0:T(8,128)(2,1)S(1)}, ...), branch_computations={%region_9.10_spmd, %region_10.13_spmd} | conditional | flops 16018473 | bytes 2418740 | solution.py:39
  312.0 1.6 collective-permute-start.15
  313.6 2.1 collective-permute-done.15
  317.8 2.9 collective-permute-done.17
  321.1 11.6 %collective-permute-done.18 = f32[4,288]{1,0:T(4,128)S(1)} collective-permute-done((f32[4,288]{1,0:T(4,128)S(1)}, f32[4,288]{1,0:T(4,128)S(1)}, u32[]{:S(2)}, u32[]{:S(2)}) %collective-permute-start.18) | collective-permute-done | bytes 4640 | tf_op jit(solution)/shard_map/cond/branch_1_fun/ppermute | solution.py:30
  332.8 3.8 %collective-permute-start.19 = (f32[2,576]{1,0:T(2,128)S(1)}, f32[2,576]{1,0:T(2,128)S(1)}, u32[]{:S(2)}, u32[]{:S(2)}) collective-permute-start(f32[2,576]{1,0:T(2,128)S(1)} %select_bitcast_fusion.1), channel_id=1, source_target_pairs={{0,16},{4,20},{8,24},{12,28},{16,0},{20,4},{24,8},{28,12},{1,17},{... | collective-permute-start | bytes 13832 | tf_op jit(solution)/shard_map/cond/branch_1_fun/ppermute | solution.py:30
  336.7 5.2 %collective-permute-done.19 = f32[2,576]{1,0:T(2,128)S(1)} collective-permute-done((f32[2,576]{1,0:T(2,128)S(1)}, f32[2,576]{1,0:T(2,128)S(1)}, u32[]{:S(2)}, u32[]{:S(2)}) %collective-permute-start.19) | collective-permute-done | bytes 4640 | tf_op jit(solution)/shard_map/cond/branch_1_fun/ppermute | solution.py:30
  (270 shorter events, 48.1 us)
Async XLA Ops:
  7.2 153.2 %all-gather.2.cloned.1.call-start = ((), (), s32[]{:S(2)}) async-start(), calls=%async_computation.1 | async-start | bytes 5971968 | tf_op jit(solution)/shard_map/all_gather | solution.py:587
  10.2 336.7 %reduce-scatter.2.cloned.1.call-start = ((), (), s32[]{:S(2)}) async-start(), calls=%async_computation.2 | async-start | bytes 5971968 | tf_op jit(solution)/shard_map/reduce_scatter | solution.py:695
  10.6 4.6 %collective-permute-start.20 = (bf16[2,1280]{1,0:T(2,128)(2,1)S(1)}, bf16[2,1280]{1,0:T(2,128)(2,1)S(1)}, u32[]{:S(2)}, u32[]{:S(2)}) collective-permute-start(bf16[2,1280]{1,0:T(2,128)(2,1)S(1)} %concatenate.52), channel_id=1, source_target_pairs={{0,8},{4,12},{8,0},{12,4},{16,24},{20,28},{24,16},{28,20},{1,9},{5... | collective-permute-start | bytes 15368 | tf_op jit(solution)/shard_map/ppermute | solution.py:30
  15.3 4.8 %collective-permute-start.21 = (bf16[2,2,1280]{2,1,0:T(2,128)(2,1)S(1)}, bf16[2,2,1280]{2,1,0:T(2,128)(2,1)S(1)}, u32[]{:S(2)}, u32[]{:S(2)}) collective-permute-start(bf16[2,2,1280]{2,1,0:T(2,128)(2,1)S(1)} %pad_maximum_fusion.12), channel_id=1, source_target_pairs={{0,16},{4,20},{8,24},{12,28},{16,0},{20,4},{24,8},{28,12},{1,17},{... | collective-permute-start | bytes 30728 | tf_op jit(solution)/shard_map/ppermute | solution.py:30
  20.1 3.8 %collective-permute-start.22 = (bf16[2,2,2,1280]{3,2,1,0:T(2,128)(2,1)S(1)}, bf16[2,2,2,1280]{3,2,1,0:T(2,128)(2,1)S(1)}, u32[]{:S(2)}, u32[]{:S(2)}) collective-permute-start(bf16[2,2,2,1280]{3,2,1,0:T(2,128)(2,1)S(1)} %pad_maximum_fusion.11), channel_id=1, source_target_pairs={{0,4},{4,0},{8,12},{12,8},{16,20},{20,16},{24,28},{28,24},{1,5},{5... | collective-permute-start | bytes 61448 | tf_op jit(solution)/shard_map/ppermute | solution.py:30
  24.0 19.7 %copy-start.36 = (f32[6,288]{1,0:T(8,128)S(1)}, f32[6,288]{1,0:T(8,128)}, u32[]{:S(2)}) copy-start(f32[6,288]{1,0:T(8,128)} %param.25) | copy-start | bytes 20740
  24.1 21.2 %copy-start.19 = (bf16[144,3,288]{2,0,1:T(8,128)(2,1)S(1)}, bf16[144,3,288]{2,0,1:T(8,128)(2,1)}, u32[]{:S(2)}) copy-start(bf16[144,3,288]{2,0,1:T(8,128)(2,1)} %param.26) | copy-start | bytes 746500
  24.5 23.3 %copy-start.33 = (bf16[288,144]{0,1:T(8,128)(2,1)S(1)}, bf16[288,144]{0,1:T(8,128)(2,1)}, u32[]{:S(2)}) copy-start(bf16[288,144]{0,1:T(8,128)(2,1)} %param.29) | copy-start | bytes 248836
  24.7 27.8 %copy-start.44 = (bf16[2,256,288]{1,2,0:T(8,128)(2,1)S(1)}, bf16[2,256,288]{1,2,0:T(8,128)(2,1)}, u32[]{:S(2)}) copy-start(bf16[2,256,288]{1,2,0:T(8,128)(2,1)} %param.20) | copy-start | bytes 884740
  24.7 8.9 %collective-permute-start.26 = (f32[8,1728]{1,0:T(8,128)S(1)}, f32[8,1728]{1,0:T(8,128)S(1)}, u32[]{:S(2)}, u32[]{:S(2)}) collective-permute-start(f32[8,1728]{1,0:T(8,128)S(1)} %select_n.424), channel_id=1, source_target_pairs={{0,16},{4,20},{8,24},{12,28},{16,0},{20,4},{24,8},{28,12},{1,17},{... | collective-permute-start | bytes 165896 | tf_op jit(solution)/shard_map/ppermute | solution.py:30
  27.8 26.3 %copy-start.37 = (f32[72]{0:T(128)S(1)}, f32[72]{0:T(128)}, u32[]{:S(2)}) copy-start(f32[72]{0:T(128)} %param.28) | copy-start | bytes 868
  27.8 26.3 %copy-start.38 = (f32[72]{0:T(128)S(1)}, f32[72]{0:T(128)}, u32[]{:S(2)}) copy-start(f32[72]{0:T(128)} %param.27) | copy-start | bytes 868
  33.6 5.4 %collective-permute-start.27 = (f32[4,1728]{1,0:T(4,128)S(1)}, f32[4,1728]{1,0:T(4,128)S(1)}, u32[]{:S(2)}, u32[]{:S(2)}) collective-permute-start(f32[4,1728]{1,0:T(4,128)S(1)} %slice_select_fusion.2), channel_id=1, source_target_pairs={{0,8},{4,12},{8,0},{12,4},{16,24},{20,28},{24,16},{28,20},{1,9},{5... | collective-permute-start | bytes 82952 | tf_op jit(solution)/shard_map/ppermute | solution.py:30
  39.1 4.6 %collective-permute-start.28 = (f32[2,1728]{1,0:T(2,128)S(1)}, f32[2,1728]{1,0:T(2,128)S(1)}, u32[]{:S(2)}, u32[]{:S(2)}) collective-permute-start(f32[2,1728]{1,0:T(2,128)S(1)} %broadcast_select_fusion.19), channel_id=1, source_target_pairs={{0,4},{4,0},{8,12},{12,8},{16,20},{20,16},{24,28},{28,24},{1,5},{5... | collective-permute-start | bytes 41480 | tf_op jit(solution)/shard_map/ppermute | solution.py:30
  43.8 76.4 %copy-start.31 = (f32[3,72,256]{2,1,0:T(8,128)S(1)}, f32[3,72,256]{2,1,0:T(8,128)}, u32[]{:S(2)}) copy-start(f32[3,72,256]{2,1,0:T(8,128)} %constant.261.clone.refs_15_) | copy-start | bytes 663556
  43.8 3.9 %collective-permute-start.29 = (f32[2,8,288]{2,1,0:T(8,128)S(1)}, f32[2,8,288]{2,1,0:T(8,128)S(1)}, u32[]{:S(2)}, u32[]{:S(2)}) collective-permute-start(f32[2,8,288]{2,1,0:T(8,128)S(1)} %pad.5), channel_id=1, source_target_pairs={{0,2},{1,3},{2,0},{3,1},{4,6},{5,7},{6,4},{7,5},{8,10},{9,11},{10,... | collective-permute-start | bytes 55304 | tf_op jit(solution)/shard_map/ppermute | solution.py:30
  47.7 4.8 %collective-permute-start.30 = (f32[2,2,8,288]{3,2,1,0:T(8,128)S(1)}, f32[2,2,8,288]{3,2,1,0:T(8,128)S(1)}, u32[]{:S(2)}, u32[]{:S(2)}) collective-permute-start(f32[2,2,8,288]{3,2,1,0:T(8,128)S(1)} %pad_maximum_fusion.10), channel_id=1, source_target_pairs={{0,1},{1,0},{2,3},{3,2},{4,5},{5,4},{6,7},{7,6},{8,9},{9,8},{10,11... | collective-permute-start | bytes 110600 | tf_op jit(solution)/shard_map/ppermute | solution.py:30
  48.0 72.1 %copy-start.20 = (bf16[144,1152]{1,0:T(8,128)(2,1)}, bf16[144,1152]{1,0:T(8,128)(2,1)S(1)}, u32[]{:S(2)}) copy-start(bf16[144,1152]{1,0:T(8,128)(2,1)S(1)} %concatenate.56.refs_6_) | copy-start | bytes 995332
  48.1 15.1 %collective-permute-start.36 = (bf16[144,1152]{1,0:T(8,128)(2,1)S(1)}, bf16[144,1152]{1,0:T(8,128)(2,1)S(1)}, u32[]{:S(2)}, u32[]{:S(2)}) collective-permute-start(bf16[144,1152]{1,0:T(8,128)(2,1)S(1)} %concatenate.56.refs_6_), channel_id=1, source_target_pairs={{0,24},{4,28},{8,16},{12,20},{16,8},{20,12},{24,0},{28,4},{1,25},{... | collective-permute-start | bytes 995336 | tf_op jit(solution)/shard_map/ppermute | solution.py:30
  50.5 54.5 %collective-permute-start.34 = (bf16[144,1152]{1,0:T(8,128)(2,1)S(1)}, bf16[144,1152]{1,0:T(8,128)(2,1)S(1)}, u32[]{:S(2)}, u32[]{:S(2)}) collective-permute-start(bf16[144,1152]{1,0:T(8,128)(2,1)S(1)} %concatenate.56.refs_6_), channel_id=1, source_target_pairs={{0,16},{4,20},{8,24},{12,28},{16,0},{20,4},{24,8},{28,12},{1,17},{... | collective-permute-start | bytes 995336 | tf_op jit(solution)/shard_map/ppermute | solution.py:30
  50.5 54.5 %collective-permute-start.32 = (bf16[144,1152]{1,0:T(8,128)(2,1)S(1)}, bf16[144,1152]{1,0:T(8,128)(2,1)S(1)}, u32[]{:S(2)}, u32[]{:S(2)}) collective-permute-start(bf16[144,1152]{1,0:T(8,128)(2,1)S(1)} %concatenate.56.refs_6_), channel_id=1, source_target_pairs={{0,8},{4,12},{8,0},{12,4},{16,24},{20,28},{24,16},{28,20},{1,9},{5... | collective-permute-start | bytes 995336 | tf_op jit(solution)/shard_map/ppermute | solution.py:30
  52.5 2.4 collective-permute-start.24
  52.5 9.5 %collective-permute-start.23 = (bf16[2,288,256]{2,1,0:T(8,128)(2,1)S(1)}, bf16[2,288,256]{2,1,0:T(8,128)(2,1)}, u32[]{:S(2)}, u32[]{:S(2)}) collective-permute-start(bf16[2,288,256]{2,1,0:T(8,128)(2,1)S(1)} %bitcast.130), channel_id=1, source_target_pairs={{0,2},{1,3},{2,0},{3,1},{4,6},{5,7},{6,4},{7,5},{8,10},{9,11},{10,... | collective-permute-start | bytes 884744 | tf_op jit(solution)/shard_map/ppermute | solution.py:30
  54.9 52.1 %copy-start.45 = (bf16[2,288,256]{2,1,0:T(8,128)(2,1)}, bf16[2,288,256]{2,1,0:T(8,128)(2,1)S(1)}, u32[]{:S(2)}) copy-start(bf16[2,288,256]{2,1,0:T(8,128)(2,1)S(1)} %collective-permute-done.24.refs_3_) | copy-start | bytes 884740
  54.9 52.3 %collective-permute-start.31 = (bf16[144,1152]{1,0:T(8,128)(2,1)S(1)}, bf16[144,1152]{1,0:T(8,128)(2,1)S(1)}, u32[]{:S(2)}, u32[]{:S(2)}) collective-permute-start(bf16[144,1152]{1,0:T(8,128)(2,1)S(1)} %concatenate.56.refs_6_), channel_id=1, source_target_pairs={{0,4},{4,0},{8,12},{12,8},{16,20},{20,16},{24,28},{28,24},{1,5},{5... | collective-permute-start | bytes 995336 | tf_op jit(solution)/shard_map/ppermute | solution.py:30
  62.0 45.2 %collective-permute-start.25 = (bf16[2,288,256]{2,1,0:T(8,128)(2,1)}, bf16[2,288,256]{2,1,0:T(8,128)(2,1)S(1)}, u32[]{:S(2)}, u32[]{:S(2)}) collective-permute-start(bf16[2,288,256]{2,1,0:T(8,128)(2,1)} %collective-permute-done.23.refs_2_), channel_id=1, source_target_pairs={{0,1},{1,0},{2,3},{3,2},{4,5},{5,4},{6,7},{7,6},{8,9},{9,8},{10,11... | collective-permute-start | bytes 884744 | tf_op jit(solution)/shard_map/ppermute | solution.py:30
  63.1 57.0 %copy-start.40 = (bf16[144,1152]{1,0:T(8,128)(2,1)}, bf16[144,1152]{1,0:T(8,128)(2,1)S(1)}, u32[]{:S(2)}) copy-start(bf16[144,1152]{1,0:T(8,128)(2,1)S(1)} %collective-permute-done.36.refs_12_) | copy-start | bytes 995332
  63.1 44.1 %collective-permute-start.37 = (bf16[144,1152]{1,0:T(8,128)(2,1)S(1)}, bf16[144,1152]{1,0:T(8,128)(2,1)}, u32[]{:S(2)}, u32[]{:S(2)}) collective-permute-start(bf16[144,1152]{1,0:T(8,128)(2,1)S(1)} %collective-permute-done.36.refs_12_), channel_id=1, source_target_pairs={{0,4},{4,0},{8,12},{12,8},{16,20},{20,16},{24,28},{28,24},{1,5},{5... | collective-permute-start | bytes 995336 | tf_op jit(solution)/shard_map/ppermute | solution.py:30
  104.9 10.8 %collective-permute-start.35 = (bf16[144,1152]{1,0:T(8,128)(2,1)S(1)}, bf16[144,1152]{1,0:T(8,128)(2,1)}, u32[]{:S(2)}, u32[]{:S(2)}) collective-permute-start(bf16[144,1152]{1,0:T(8,128)(2,1)S(1)} %collective-permute-done.34.refs_10_), channel_id=1, source_target_pairs={{0,4},{4,0},{8,12},{12,8},{16,20},{20,16},{24,28},{28,24},{1,5},{5... | collective-permute-start | bytes 995336 | tf_op jit(solution)/shard_map/ppermute | solution.py:30
  105.0 15.1 %collective-permute-start.33 = (bf16[144,1152]{1,0:T(8,128)(2,1)S(1)}, bf16[144,1152]{1,0:T(8,128)(2,1)}, u32[]{:S(2)}, u32[]{:S(2)}) collective-permute-start(bf16[144,1152]{1,0:T(8,128)(2,1)S(1)} %collective-permute-done.32.refs_8_), channel_id=1, source_target_pairs={{0,4},{4,0},{8,12},{12,8},{16,20},{20,16},{24,28},{28,24},{1,5},{5... | collective-permute-start | bytes 995336 | tf_op jit(solution)/shard_map/ppermute | solution.py:30
  107.2 53.2 %copy-start.8 = (f32[2,8,1152]{2,1,0:T(8,128)}, f32[2,8,1152]{2,1,0:T(8,128)S(1)}, u32[]{:S(2)}) copy-start(f32[2,8,1152]{2,1,0:T(8,128)S(1)} %reshape.139.refs_5_) | copy-start | bytes 221188
  131.3 2.3 collective-permute-start.38
  136.6 16.3 %collective-permute-start.39 = (bf16[2,576,256]{2,1,0:T(8,128)(2,1)}, bf16[2,576,256]{2,1,0:T(8,128)(2,1)S(1)}, u32[]{:S(2)}, u32[]{:S(2)}) collective-permute-start(bf16[2,576,256]{2,1,0:T(8,128)(2,1)} %shard_map.222.refs_0_), channel_id=1, source_target_pairs={{0,2},{1,3},{2,0},{3,1},{4,6},{5,7},{6,4},{7,5},{8,10},{9,11},{10,... | collective-permute-start | bytes 1769480 | tf_op jit(solution)/shard_map/ppermute | solution.py:30
  138.7 20.2 %collective-permute-start.41 = (bf16[2,288,256]{2,1,0:T(8,128)(2,1)S(1)}, bf16[2,288,256]{2,1,0:T(8,128)(2,1)S(1)}, u32[]{:S(2)}, u32[]{:S(2)}) collective-permute-start(bf16[2,288,256]{2,1,0:T(8,128)(2,1)S(1)} %bitcast.120), channel_id=1, source_target_pairs={{0,2},{1,3},{2,0},{3,1},{4,6},{5,7},{6,4},{7,5},{8,10},{9,11},{10,... | collective-permute-start | bytes 884744 | tf_op jit(solution)/shard_map/ppermute | solution.py:30
  155.2 5.2 %collective-permute-start.40 = (bf16[2,576,256]{2,1,0:T(8,128)(2,1)S(1)}, bf16[2,576,256]{2,1,0:T(8,128)(2,1)S(1)}, u32[]{:S(2)}, u32[]{:S(2)}) collective-permute-start(bf16[2,576,256]{2,1,0:T(8,128)(2,1)S(1)} %shard_map.223), channel_id=1, source_target_pairs={{0,1},{1,0},{2,3},{3,2},{4,5},{5,4},{6,7},{7,6},{8,9},{9,8},{10,11... | collective-permute-start | bytes 1769480 | tf_op jit(solution)/shard_map/ppermute | solution.py:30
  155.3 4.4 %collective-permute-start.42 = (bf16[2,288,256]{2,1,0:T(8,128)(2,1)S(1)}, bf16[2,288,256]{2,1,0:T(8,128)(2,1)S(1)}, u32[]{:S(2)}, u32[]{:S(2)}) collective-permute-start(bf16[2,288,256]{2,1,0:T(8,128)(2,1)S(1)} %bitcast.121), channel_id=1, source_target_pairs={{0,1},{1,0},{2,3},{3,2},{4,5},{5,4},{6,7},{7,6},{8,9},{9,8},{10,11... | collective-permute-start | bytes 884744 | tf_op jit(solution)/shard_map/ppermute | solution.py:30
  158.8 1.6 collective-permute-start.43
  161.8 21.3 %slice-start = ((s8[5308416]{0:T(1024)(128)(4,1)}), s8[4194304]{0:T(1024)(128)(4,1)S(1)}, s32[]{:S(2)}) async-start(s8[5308416]{0:T(1024)(128)(4,1)} %bitcast.115), calls=%async_computation.3 | async-start | bytes 8388608 | tf_op jit(solution)/shard_map/cond
  161.8 21.3 %slice-start.1 = ((s8[5308416]{0:T(1024)(128)(4,1)}), s8[1114112]{0:T(1024)(128)(4,1)S(1)}, s32[]{:S(2)}) async-start(s8[5308416]{0:T(1024)(128)(4,1)} %bitcast.115), calls=%async_computation.4 | async-start | bytes 2228224 | tf_op jit(solution)/shard_map/cond
  176.1 2.3 collective-permute-start
  181.4 15.7 %collective-permute-start.1 = (bf16[2,576,256]{2,1,0:T(8,128)(2,1)}, bf16[2,576,256]{2,1,0:T(8,128)(2,1)}, u32[]{:S(2)}, u32[]{:S(2)}) collective-permute-start(bf16[2,576,256]{2,1,0:T(8,128)(2,1)} %branch_1_fun.13), channel_id=1, source_target_pairs={{0,2},{1,3},{2,0},{3,1},{4,6},{5,7},{6,4},{7,5},{8,10},{9,11},{10,... | collective-permute-start | bytes 1769480 | tf_op jit(solution)/shard_map/cond/branch_1_fun/ppermute | solution.py:30
  200.2 2.3 collective-permute-start.2
  215.5 2.6 collective-permute-start.3
  217.0 5.1 %collective-permute-start.6 = (bf16[2,2,288,256]{3,2,0,1:T(8,128)(2,1)}, bf16[2,2,288,256]{3,2,0,1:T(8,128)(2,1)}, u32[]{:S(2)}, u32[]{:S(2)}) collective-permute-start(bf16[2,2,288,256]{3,2,0,1:T(8,128)(2,1)} %select_bitcast_fusion), channel_id=1, source_target_pairs={{0,1},{1,0},{2,3},{3,2},{4,5},{5,4},{6,7},{7,6},{8,9},{9,8},{10,11... | collective-permute-start | bytes 1769480 | tf_op jit(solution)/shard_map/cond/branch_1_fun/ppermute | solution.py:30
  220.3 16.4 %collective-permute-start.4 = (bf16[2,576,256]{2,1,0:T(8,128)(2,1)}, bf16[2,576,256]{2,1,0:T(8,128)(2,1)S(1)}, u32[]{:S(2)}, u32[]{:S(2)}) collective-permute-start(bf16[2,576,256]{2,1,0:T(8,128)(2,1)} %branch_1_fun.17.refs_0_), channel_id=1, source_target_pairs={{0,2},{1,3},{2,0},{3,1},{4,6},{5,7},{6,4},{7,5},{8,10},{9,11},{10,... | collective-permute-start | bytes 1769480 | tf_op jit(solution)/shard_map/cond/branch_1_fun/ppermute | solution.py:30
  223.4 19.0 %collective-permute-start.7 = (bf16[2,288,256]{2,1,0:T(8,128)(2,1)S(1)}, bf16[2,288,256]{2,1,0:T(8,128)(2,1)S(1)}, u32[]{:S(2)}, u32[]{:S(2)}) collective-permute-start(bf16[2,288,256]{2,1,0:T(8,128)(2,1)S(1)} %fusion), channel_id=1, source_target_pairs={{0,2},{1,3},{2,0},{3,1},{4,6},{5,7},{6,4},{7,5},{8,10},{9,11},{10,... | collective-permute-start | bytes 884744 | tf_op jit(solution)/shard_map/cond/branch_1_fun/ppermute | solution.py:30
  239.7 3.7 %collective-permute-start.5 = (bf16[2,576,256]{2,1,0:T(8,128)(2,1)}, bf16[2,576,256]{2,1,0:T(8,128)(2,1)S(1)}, u32[]{:S(2)}, u32[]{:S(2)}) collective-permute-start(bf16[2,576,256]{2,1,0:T(8,128)(2,1)} %branch_1_fun.19.refs_3_), channel_id=1, source_target_pairs={{0,1},{1,0},{2,3},{3,2},{4,5},{5,4},{6,7},{7,6},{8,9},{9,8},{10,11... | collective-permute-start | bytes 1769480 | tf_op jit(solution)/shard_map/cond/branch_1_fun/ppermute | solution.py:30
  244.2 15.8 %copy-start.24 = (bf16[144,1152]{1,0:T(8,128)(2,1)S(1)}, bf16[144,1152]{1,0:T(8,128)(2,1)}, u32[]{:S(2)}) copy-start(bf16[144,1152]{1,0:T(8,128)(2,1)} %get-tuple-element.117.refs_9_) | copy-start | bytes 995332 | tf_op jit(solution)/shard_map/cond
  244.2 30.6 %copy-start.6 = (bf16[144,1152]{1,0:T(8,128)(2,1)S(1)}, bf16[144,1152]{1,0:T(8,128)(2,1)}, u32[]{:S(2)}) copy-start(bf16[144,1152]{1,0:T(8,128)(2,1)} %get-tuple-element.110.refs_2_) | copy-start | bytes 995332 | tf_op jit(solution)/shard_map/cond
  251.1 3.7 %collective-permute-start.8 = (bf16[2,2016]{1,0:T(2,128)(2,1)S(1)}, bf16[2,2016]{1,0:T(2,128)(2,1)S(1)}, u32[]{:S(2)}, u32[]{:S(2)}) collective-permute-start(bf16[2,2016]{1,0:T(2,128)(2,1)S(1)} %fusion.7), channel_id=1, source_target_pairs={{0,8},{4,12},{8,0},{12,4},{16,24},{20,28},{24,16},{28,20},{1,9},{5... | collective-permute-start | bytes 24200 | tf_op jit(solution)/shard_map/cond/branch_1_fun/ppermute | solution.py:30
  254.9 7.1 %collective-permute-start.9 = (bf16[2,2,2016]{2,1,0:T(2,128)(2,1)S(1)}, bf16[2,2,2016]{2,1,0:T(2,128)(2,1)S(1)}, u32[]{:S(2)}, u32[]{:S(2)}) collective-permute-start(bf16[2,2,2016]{2,1,0:T(2,128)(2,1)S(1)} %pad_maximum_fusion.1), channel_id=1, source_target_pairs={{0,16},{4,20},{8,24},{12,28},{16,0},{20,4},{24,8},{28,12},{1,17},{... | collective-permute-start | bytes 48392 | tf_op jit(solution)/shard_map/cond/branch_1_fun/ppermute | solution.py:30
  257.9 16.8 %collective-permute-start.14 = (bf16[144,1152]{1,0:T(8,128)(2,1)}, bf16[144,1152]{1,0:T(8,128)(2,1)S(1)}, u32[]{:S(2)}, u32[]{:S(2)}) collective-permute-start(bf16[144,1152]{1,0:T(8,128)(2,1)} %get-tuple-element.111.refs_3_), channel_id=1, source_target_pairs={{0,4},{4,0},{8,12},{12,8},{16,20},{20,16},{24,28},{28,24},{1,5},{5... | collective-permute-start | bytes 995336 | tf_op jit(solution)/shard_map/cond/branch_1_fun/ppermute | solution.py:30
  257.9 23.9 %collective-permute-start.11 = (bf16[144,1152]{1,0:T(8,128)(2,1)}, bf16[144,1152]{1,0:T(8,128)(2,1)S(1)}, u32[]{:S(2)}, u32[]{:S(2)}) collective-permute-start(bf16[144,1152]{1,0:T(8,128)(2,1)} %get-tuple-element.113.refs_5_), channel_id=1, source_target_pairs={{0,4},{4,0},{8,12},{12,8},{16,20},{20,16},{24,28},{28,24},{1,5},{5... | collective-permute-start | bytes 995336 | tf_op jit(solution)/shard_map/cond/branch_1_fun/ppermute | solution.py:30
  259.9 30.9 %collective-permute-start.12 = (bf16[144,1152]{1,0:T(8,128)(2,1)}, bf16[144,1152]{1,0:T(8,128)(2,1)S(1)}, u32[]{:S(2)}, u32[]{:S(2)}) collective-permute-start(bf16[144,1152]{1,0:T(8,128)(2,1)} %get-tuple-element.115.refs_7_), channel_id=1, source_target_pairs={{0,4},{4,0},{8,12},{12,8},{16,20},{20,16},{24,28},{28,24},{1,5},{5... | collective-permute-start | bytes 995336 | tf_op jit(solution)/shard_map/cond/branch_1_fun/ppermute | solution.py:30
  260.0 42.8 %collective-permute-start.13 = (bf16[144,1152]{1,0:T(8,128)(2,1)S(1)}, bf16[144,1152]{1,0:T(8,128)(2,1)S(1)}, u32[]{:S(2)}, u32[]{:S(2)}) collective-permute-start(bf16[144,1152]{1,0:T(8,128)(2,1)S(1)} %copy-done.24), channel_id=1, source_target_pairs={{0,4},{4,0},{8,12},{12,8},{16,20},{20,16},{24,28},{28,24},{1,5},{5... | collective-permute-start | bytes 995336 | tf_op jit(solution)/shard_map/cond/branch_1_fun/ppermute | solution.py:30
  262.1 43.3 %collective-permute-start.10 = (bf16[2,2,2,2016]{3,2,1,0:T(2,128)(2,1)S(1)}, bf16[2,2,2,2016]{3,2,1,0:T(2,128)(2,1)S(1)}, u32[]{:S(2)}, u32[]{:S(2)}) collective-permute-start(bf16[2,2,2,2016]{3,2,1,0:T(2,128)(2,1)S(1)} %pad_maximum_fusion), channel_id=1, source_target_pairs={{0,4},{4,0},{8,12},{12,8},{16,20},{20,16},{24,28},{28,24},{1,5},{5... | collective-permute-start | bytes 96776 | tf_op jit(solution)/shard_map/cond/branch_1_fun/ppermute | solution.py:30
  305.7 37.0 %collective-permute-start.44 = (bf16[144,1152]{1,0:T(8,128)(2,1)}, bf16[144,1152]{1,0:T(8,128)(2,1)S(1)}, u32[]{:S(2)}, u32[]{:S(2)}) collective-permute-start(bf16[144,1152]{1,0:T(8,128)(2,1)} %get-tuple-element.189), channel_id=1, source_target_pairs={{0,8},{4,12},{8,0},{12,4},{16,24},{20,28},{24,16},{28,20},{1,9},{5... | collective-permute-start | bytes 995336 | tf_op jit(solution)/shard_map/ppermute | solution.py:30
  306.3 36.3 %collective-permute-start.45 = (bf16[144,1152]{1,0:T(8,128)(2,1)}, bf16[144,1152]{1,0:T(8,128)(2,1)S(1)}, u32[]{:S(2)}, u32[]{:S(2)}) collective-permute-start(bf16[144,1152]{1,0:T(8,128)(2,1)} %get-tuple-element.190), channel_id=1, source_target_pairs={{0,16},{4,20},{8,24},{12,28},{16,0},{20,4},{24,8},{28,12},{1,17},{... | collective-permute-start | bytes 995336 | tf_op jit(solution)/shard_map/ppermute | solution.py:30
  307.8 34.9 %collective-permute-start.46 = (bf16[144,1152]{1,0:T(8,128)(2,1)}, bf16[144,1152]{1,0:T(8,128)(2,1)S(1)}, u32[]{:S(2)}, u32[]{:S(2)}) collective-permute-start(bf16[144,1152]{1,0:T(8,128)(2,1)} %get-tuple-element.191), channel_id=1, source_target_pairs={{0,24},{4,28},{8,16},{12,20},{16,8},{20,12},{24,0},{28,4},{1,25},{... | collective-permute-start | bytes 995336 | tf_op jit(solution)/shard_map/ppermute | solution.py:30
  312.0 3.8 %collective-permute-start.15 = (f32[2448]{0:T(1024)S(1)}, f32[2448]{0:T(1024)S(1)}, u32[]{:S(2)}, u32[]{:S(2)}) collective-permute-start(f32[2448]{0:T(1024)S(1)} %pad_maximum_fusion.4), channel_id=1, source_target_pairs={{0,2},{1,3},{2,0},{3,1},{4,6},{5,7},{6,4},{7,5},{8,10},{9,11},{10,... | collective-permute-start | bytes 29384 | tf_op jit(solution)/shard_map/cond/branch_1_fun/ppermute | solution.py:30
  315.7 1.2 collective-permute-start.16
  317.0 3.7 %collective-permute-start.17 = (f32[8,144]{1,0:T(8,128)S(1)}, f32[8,144]{1,0:T(8,128)S(1)}, u32[]{:S(2)}, u32[]{:S(2)}) collective-permute-start(f32[8,144]{1,0:T(8,128)S(1)} %select_n.338), channel_id=1, source_target_pairs={{0,4},{4,0},{8,12},{12,8},{16,20},{20,16},{24,28},{28,24},{1,5},{5... | collective-permute-start | bytes 13832 | tf_op jit(solution)/shard_map/cond/branch_1_fun/ppermute | solution.py:30
  320.9 11.8 %collective-permute-start.18 = (f32[4,288]{1,0:T(4,128)S(1)}, f32[4,288]{1,0:T(4,128)S(1)}, u32[]{:S(2)}, u32[]{:S(2)}) collective-permute-start(f32[4,288]{1,0:T(4,128)S(1)} %select_n.344), channel_id=1, source_target_pairs={{0,8},{4,12},{8,0},{12,4},{16,24},{20,28},{24,16},{28,20},{1,9},{5... | collective-permute-start | bytes 13832 | tf_op jit(solution)/shard_map/cond/branch_1_fun/ppermute | solution.py:30
  332.8 9.0 %collective-permute-start.19 = (f32[2,576]{1,0:T(2,128)S(1)}, f32[2,576]{1,0:T(2,128)S(1)}, u32[]{:S(2)}, u32[]{:S(2)}) collective-permute-start(f32[2,576]{1,0:T(2,128)S(1)} %select_bitcast_fusion.1), channel_id=1, source_target_pairs={{0,16},{4,20},{8,24},{12,28},{16,0},{20,4},{24,8},{28,12},{1,17},{... | collective-permute-start | bytes 13832 | tf_op jit(solution)/shard_map/cond/branch_1_fun/ppermute | solution.py:30
  (37 other events, 152.1 us)
Sparse Core Ops, SparseCore 0:
  10.8 110.7 all-gather.1
  197.2 127.2 reduce-scatter.1

commit v3 on v2

--- a/solution.py
+++ b/solution.py
@@ -133,14 +133,75 @@
     return lax.axis_size("dp") in (2, 4, 8)
 
 
-def dp_blocks(block):
-    if not direct():
-        return [lax.all_gather(block, "dp", axis=0, tiled=True)]
-    size = lax.axis_size("dp")
-    blocks = [block, swap(block, "dp", 1)]
-    for k, near in [(k, swap(block, "dp", k)) for k in range(2, size, 2)]:
-        blocks += [near, swap(near, "dp", 1)]
-    return blocks
+def along(value, pairs):
+    return lax.ppermute(value, "dp", [(2 * a + y, 2 * b + y) for a, b in pairs for y in (0, 1)])
+
+
+def line_first(block):
+    up = along(block, [(0, 1), (1, 2), (2, 3)])
+    return up, along(block, [(1, 0), (2, 1), (3, 2)])
+
+
+def line_near(first, token):
+    return pick(lax.axis_index("dp") // 2 % 2 == 1, first[0], first[1], token)
+
+
+def line_second(first):
+    return along(first[0], [(1, 2), (2, 3)]), along(first[1], [(1, 0), (2, 1)])
+
+
+def line_two(first, token):
+    second = line_second(first)
+    return pick(lax.axis_index("dp") // 2 >= 2, second[0], second[1], token)
+
+
+def line_rest(block, beside, first, one, two):
+    me = lax.axis_index("dp")
+    at = me // 2
+    end = along(two, [(1, 0), (2, 3)])
+    three = jnp.where(at == 0, end, jnp.where(at == 1, first[1], jnp.where(at == 2, first[0], end)))
+    found = [block, one, two, three]
+    places = [at, at ^ 1, jnp.where(at >= 2, at - 2, at + 2), 3 - at]
+    blocks = found + beside + [swap(b, "dp", 1) for b in found[2:]]
+    return blocks, [2 * p + me % 2 for p in places] + [2 * p + 1 - me % 2 for p in places]
+
+
+def pick(flag, left, right, token):
+    def kernel(flag_ref, left_ref, right_ref, _, out_ref):
+        @pl.when(flag_ref[0] == 1)
+        def _():
+            out_ref[...] = left_ref[...]
+
+        @pl.when(flag_ref[0] == 0)
+        def _():
+            out_ref[...] = right_ref[...]
+
+    return pl.pallas_call(
+        kernel,
+        in_specs=[pl.BlockSpec(memory_space=pltpu.SMEM)]
+        + [pl.BlockSpec(memory_space=pltpu.VMEM)] * 2
+        + [pl.BlockSpec(memory_space=pl.ANY)],
+        out_specs=pl.BlockSpec(memory_space=pltpu.VMEM),
+        out_shape=shaped(left.shape, left.dtype),
+        cost_estimate=pl.CostEstimate(flops=1, bytes_accessed=1, transcendentals=0),
+    )(jnp.reshape(flag.astype(jnp.int32), (1,)), left, right, token)
+
+
+def packed(gate_up, down, token):
+    rows, units = down.shape
+
+    def kernel(gate_up_ref, down_ref, _, out_ref):
+        out_ref[:, :units] = gate_up_ref[0]
+        out_ref[:, units : 2 * units] = gate_up_ref[1]
+        out_ref[:, 2 * units :] = down_ref[...]
+
+    return pl.pallas_call(
+        kernel,
+        in_specs=[pl.BlockSpec(memory_space=pltpu.VMEM)] * 2 + [pl.BlockSpec(memory_space=pl.ANY)],
+        out_specs=pl.BlockSpec(memory_space=pltpu.VMEM),
+        out_shape=shaped((rows, 3 * units), down.dtype),
+        cost_estimate=pl.CostEstimate(flops=1, bytes_accessed=1, transcendentals=0),
+    )(gate_up, down, token)
 
 
 def dp_cross(parts):
@@ -267,18 +328,14 @@
 
 
 def attention_forward(
-    heads, place, lat_refs, mods_ref, weight_refs, gains_ref, tables_ref, outs, scratch
+    heads, place, lat_refs, mods_ref, weight_ref, gains_ref, tables_ref, outs, scratch
 ):
-    lat_ref, weight_ref, h_ref, raw_ref, lse_ref, ob_ref, mine_ref, theirs_ref = outs
+    lat_ref, h_ref, raw_ref, lse_ref, ob_ref, mine_ref, theirs_ref = outs
     (x_ref,) = scratch
     quarter = lat_refs[0].shape[1]
     width = quarter
     size = gains_ref.shape[0]
     inverse = 1.0 / math.sqrt(size)
-
-    @pl.when(pl.program_id(0) == 0)
-    def _():
-        copy_blocks(place, 5, weight_refs, weight_ref)
 
     for k, ref in enumerate(lat_refs):
         piece = ref[0]
@@ -573,42 +630,50 @@
     all_images = dp_size * images
     tokens = images * patches
 
-    extra = jnp.stack([noise_bins, slot_valid], axis=1).astype(BF16)
-    told = jnp.concatenate([condition, extra, jnp.zeros((images, LANES - 2), BF16)], axis=1)
-    told = gather_rows(told, "dp")
-    all_bins, all_valid = told[:, width].astype(F32), told[:, width + 1].astype(F32)
-    cond_rows = lax.dynamic_slice_in_dim(told[:, :width], dp * rows, rows, 1).astype(F32)
-
     by_part = jnp.transpose(qkv_weight, (1, 0, 2))
     first_pack = jnp.concatenate([by_part[0], by_part[1], by_part[2], out_weight.T], axis=1)
-    second_pack = jnp.concatenate([gate_up[:, 0], gate_up[:, 1], down_weight.T], axis=1)
+    first = lax.all_gather(first_pack, "dp", axis=0, tiled=True)
     lat_pieces = mp_pieces(jnp.transpose(latents, (0, 2, 1)))
-    first_blocks = dp_blocks(first_pack)
-    second = lax.all_gather(second_pack, "dp", axis=0, tiled=True)
     cot_pieces = mp_pieces(jnp.transpose(cotangent, (0, 2, 1)))
     ada = jnp.transpose(ada_weight, (1, 0, 2))
     keep = slot_valid.astype(F32)
     given = noise_bins[0] >= 0
-
-    bin_ids = jnp.arange(BINS, dtype=F32)
-    member = (all_bins[:, None] == bin_ids[None, :]).astype(F32) * all_valid[:, None]
-    per_bin = jnp.sum(member, axis=0)
-    own_bins = noise_bins.astype(F32)
-    own_count = jnp.sum((own_bins[:, None] == bin_ids[None, :]) * per_bin[None, :], axis=1)
-    image_weight = keep * jnp.sum(all_valid) / (BINS * jnp.maximum(own_count, 1.0))
-
-    cond_act = jax.nn.silu(cond_rows).astype(BF16)
-    mods_terms = jnp.einsum("nd,cde->nce", cond_act, ada, preferred_element_type=F32)
-    mods_own = scatter_rows(mods_terms.reshape(all_images, -1), "dp")
-    mods_own = mods_own.reshape(images, 6, quarter) + ada_bias[None]
-    mods_own = jnp.pad(mods_own, ((0, 0), (0, 2), (0, 0)))
+    on_line = dp_size == 8
+
+    def over_dp():
+        extra = jnp.stack([noise_bins, slot_valid], axis=1).astype(BF16)
+        told = jnp.concatenate([condition, extra, jnp.zeros((images, LANES - 2), BF16)], axis=1)
+        told = gather_rows(told, "dp")
+        all_bins, all_valid = told[:, width].astype(F32), told[:, width + 1].astype(F32)
+        cond_rows = lax.dynamic_slice_in_dim(told[:, :width], dp * rows, rows, 1).astype(F32)
+
+        bin_ids = jnp.arange(BINS, dtype=F32)
+        member = (all_bins[:, None] == bin_ids[None, :]).astype(F32) * all_valid[:, None]
+        per_bin = jnp.sum(member, axis=0)
+        own_bins = noise_bins.astype(F32)
+        own_count = jnp.sum((own_bins[:, None] == bin_ids[None, :]) * per_bin[None, :], axis=1)
+        image_weight = keep * jnp.sum(all_valid) / (BINS * jnp.maximum(own_count, 1.0))
+
+        cond_act = jax.nn.silu(cond_rows).astype(BF16)
+        mods_terms = jnp.einsum("nd,cde->nce", cond_act, ada, preferred_element_type=F32)
+        mods_own = scatter_rows(mods_terms.reshape(all_images, -1), "dp")
+        pack = packed(jnp.transpose(gate_up, (1, 0, 2)), down_weight.T, mods_own)
+        mods_own = mods_own.reshape(images, 6, quarter) + ada_bias[None]
+        mods_own = jnp.pad(mods_own, ((0, 0), (0, 2), (0, 0)))
+        return cond_act, image_weight, mods_own, pack
+
+    cond_act, image_weight, mods_own, second_pack = region(given, over_dp)
+    hop_one = line_first(second_pack) if on_line else ()
+    beside = [swap(second_pack, "dp", 1)] if on_line else []
+    near = line_near(hop_one, beside[0]) if on_line else None
+    beside += [swap(near, "dp", 1)] if on_line else []
+    two = line_two(hop_one, beside[1]) if on_line else None
+    held = [*beside, two] if on_line else []
     side = mp // 2
     far = swap(mods_own, "mp", 2)
     pair = jnp.stack([jnp.where(side == 0, mods_own, far), jnp.where(side == 0, far, mods_own)])
-    beside = swap(pair, "mp", 1)
-    quad = jnp.stack(
-        [jnp.where(core == 0, pair, beside), jnp.where(core == 0, beside, pair)], axis=1
-    )
+    other = swap(pair, "mp", 1)
+    quad = jnp.stack([jnp.where(core == 0, pair, other), jnp.where(core == 0, other, pair)], axis=1)
     mods = jnp.transpose(quad, (2, 3, 0, 1, 4)).reshape(images, 8, width)
 
     count = dp_size if direct() else 1
@@ -624,21 +689,21 @@
     half = shaped((images, width // 2, patches), BF16)
     tall = pltpu.VMEM((width, patches), F32)
 
-    lat, first, h_one, raw, lse, ob, *attn_terms = call(
-        lambda p, l, m, w, g, t, outs, s: attention_forward(
-            heads, p[0], l, m[0], w, g[0], t[0], outs, s
+    lat, h_one, raw, lse, ob, *attn_terms = call(
+        lambda p, l, m, w, g, t, _, outs, s: attention_forward(
+            heads, p[0], l, m[0], w[0], g[0], t[0], outs, s
         ),
         [
             [(place, scalars)],
             [(a, each) for a in lat_pieces],
             [(mods, each)],
-            [(a, whole) for a in first_blocks],
+            [(first, whole)],
             [(gains, whole)],
             [(tables, whole)],
+            [(a, token) for a in held],
         ],
         [
             (wide(BF16), each),
-            (shaped((width, full), BF16), whole),
             (wide(BF16), each),
             (shaped((images, 3 * quarter, patches), F32), each),
             (shaped((images, heads, patches), F32), each),
@@ -648,9 +713,28 @@
         ],
         [tall],
         images,
-        2 * images * patches * width * full,
     )
-    attn_sums = mp_total(*attn_terms)
+    if on_line:
+        blocks, block_owners = line_rest(second_pack, beside, hop_one, near, two)
+        attn_chip = mp_chip(*attn_terms, blocks[6])
+
+        def assemble(p, blocks, outs, _):
+            copy_blocks(p[0], 0, blocks, outs[0])
+
+        (second,) = call(
+            assemble,
+            [
+                [(jnp.stack(block_owners).astype(jnp.int32), scalars)],
+                [(a, whole) for a in blocks],
+            ],
+            [(shaped((width, 3 * units), BF16), whole)],
+            [],
+            1,
+        )
+        attn_sums = mp_join(attn_chip, swap(attn_chip, "mp", 2), blocks[7])
+    else:
+        second = lax.all_gather(second_pack, "dp", axis=0, tiled=True)
+        attn_sums = mp_total(*attn_terms)
 
     def middle():
         mid, attn_own, h_two, hidden, dffn, dgu, cot, mine, theirs = call(
@@ -741,7 +825,7 @@
         first_beside = dp_cross(first_terms)
         dh_one_sums = mp_total(mine, theirs, tuple(first_terms))
         block_out, latent_grad, dmods = call(
-            lambda p, w, k, s, a, outs, x: last_steps(p[0], w[0], k[0], s, *a, outs, x),
+            lambda p, w, k, s, a, _, outs, x: last_steps(p[0], w[0], k[0], s, *a, outs, x),
             [
                 [(place, scalars)],
                 [(image_weight, scalars)],
@@ -756,6 +840,7 @@
                     (ffn_own, each),
                     (dmods_part, each),
                 ],
+                [(a, token) for a in first_beside[3:]],
             ],
             [
                 (shaped((images, quarter, patches), BF16), each),
@@ -772,7 +857,8 @@
         beside = jnp.concatenate([high, low])[None]
         beside = jnp.concatenate([beside, jnp.zeros((images - 1, beside.shape[1]), BF16)], axis=0)
         rounded = dmods[:, :6].astype(BF16).reshape(images, 6 * quarter)
-        told_back = gather_rows(jnp.concatenate([rounded, beside], axis=1), "dp")
+        rounded = after(jnp.concatenate([rounded, beside], axis=1), *first_beside[2:3])
+        told_back = gather_rows(rounded, "dp")
         halves = dp_pair_sums(first_terms, first_beside) if count > 1 else []
         return block_out, latent_grad, told_back, first_terms[0], first_beside[0], halves
 

time: 358 us -> 334 us (0.933)
  waiting for transfers between devices: 177 us -> 125 us
  starting transfers between devices: 53.7 us -> 68.7 us
  Pallas kernels: 75.5 us -> 83.7 us
    ppermute x47 -> x44, waiting for transfers between devices: 177 us -> 96.9 us  [swap(): return lax.ppermute(value, axis, [(i, i ^ bit) for i in range(size)])]
    ppermute x0 -> x5, waiting for transfers between devices: none -> 28.5 us  [along(): lax.ppermute(value, 'dp', [(2 * a + y, 2 * b + y) for a, b in pairs for y...]
    ppermute x0 -> x5, starting transfers between devices: none -> 10.1 us  [along(): lax.ppermute(value, 'dp', [(2 * a + y, 2 * b + y) for a, b in pairs for y...]
    pallas_call x0 -> x4, Pallas kernels: none -> 6.82 us  [the longest x2 4.39 us: pick(): pl.pallas_call(kernel, in_specs=[pl.BlockSpec(memory_space=pltpu.SMEM)] +...]
    ppermute x47 -> x44, starting transfers between devices: 53.6 us -> 58.6 us  [swap(): return lax.ppermute(value, axis, [(i, i ^ bit) for i in range(size)])]
    unnamed x62 -> x56, local copies, waits for them, and re-layouts: 5.91 us -> 7.74 us
    pallas_call x6 -> x7, Pallas kernels: 57.3 us -> 58.8 us  [call(): pl.pallas_call(kernel, grid=(images,), in_specs=specs, out_specs=[kind(o)...]
  transfers between devices with their start and end apart: 49 -> 51, of which waited for: 32 -> 27; matrix products, arithmetic and copies ran while one was open for 6% -> 7% of each run, Pallas kernels for 17% -> 21%
where the time goes in v3:
time: 334 us; the launch traced here: 333 us
  waiting for transfers between devices  125 us (37%)
  Pallas kernels  83.7 us (25%)
  starting transfers between devices  68.7 us (21%)
  local copies, waits for them, and re-layouts  23.7 us (7%)
  between operations  14.6 us (4%)
  other arithmetic  14 us (4%)
    ppermute x44, waiting for transfers between devices, swap(): return lax.ppermute(value, axis, [(i, i ^ bit) for i in range(size)])  96.9 us
    pallas_call x7, Pallas kernels, call(): pl.pallas_call(kernel, grid=(images,), in_specs=specs, out_specs=[kind(o)...  58.8 us
    ppermute x44, starting transfers between devices, swap(): return lax.ppermute(value, axis, [(i, i ^ bit) for i in range(size)])  58.6 us
    ppermute x5, waiting for transfers between devices, along(): lax.ppermute(value, 'dp', [(2 * a + y, 2 * b + y) for a, b in pairs for y...  28.5 us
    pallas_call x9, Pallas kernels, add_blocks(): pl.pallas_call(kernel, in_specs=[pl.BlockSpec(memory_space=pltpu.VMEM)] *...  18.1 us
    ppermute x5, starting transfers between devices, along(): lax.ppermute(value, 'dp', [(2 * a + y, 2 * b + y) for a, b in pairs for y...  10.1 us
    unnamed x56, local copies, waits for them, and re-layouts  7.74 us
  transfers between devices with their start and end apart: 51, of which 27 were waited for; matrix products, arithmetic and copies ran while one was open for 7% of the time, Pallas kernels for 21%

profile of v3, /device:TPU:0, one launch (start us, length us, event | category | flops | bytes accessed | tf_op | source)
XLA Modules:
  0.0 332.7 jit_solution(8865572881638061676)
XLA Ops:
  8.4 1.9 concatenate.49
  10.5 33.8 %conditional.4 = (bf16[16,144]{1,0:T(8,128)(2,1)S(1)}, f32[2]{0:T(128)S(1)}, f32[2,8,288]{2,1,0:T(8,128)S(1)}, bf16[144,2304]{1,0:T(8,128)(2,1)S(1)}) conditional(s32[]{:T(128)} %bitcast.29, () %tuple.48, (s32[2]{0:T(128)S(1)}, s32[2]{0:T(128)S(1)}, bf16[2,1152]{1,0:T(2,128)(2,1)S(1)}, s32[]{:T(128)}, f32[2]{0:T(128)S(1)}, ...), branch_computations={%region_0.1_spmd, %region_1.5_spmd} | conditional | flops 8140065 | bytes 3880116 | solution.py:39
  10.9 3.0 collective-permute-start.15
  13.9 1.6 collective-permute-done.15
  15.5 3.1 collective-permute-start.16
  18.6 1.7 collective-permute-done.16
  20.4 1.9 collective-permute-start.17
  25.5 3.2 collective-permute-start.18
  28.9 5.5 %collective-permute-done.18 = f32[8,1728]{1,0:T(8,128)S(1)} collective-permute-done((f32[8,1728]{1,0:T(8,128)S(1)}, f32[8,1728]{1,0:T(8,128)S(1)}, u32[]{:S(2)}, u32[]{:S(2)}) %collective-permute-start.18) | collective-permute-done | bytes 55328 | tf_op jit(solution)/shard_map/cond/branch_1_fun/ppermute | solution.py:30
  34.7 4.1 %collective-permute-done.19 = f32[4,1728]{1,0:T(4,128)S(1)} collective-permute-done((f32[4,1728]{1,0:T(4,128)S(1)}, f32[4,1728]{1,0:T(4,128)S(1)}, u32[]{:S(2)}, u32[]{:S(2)}) %collective-permute-start.19) | collective-permute-done | bytes 27680 | tf_op jit(solution)/shard_map/cond/branch_1_fun/ppermute | solution.py:30
  38.8 1.7 collective-permute-start.20
  45.7 4.6 %collective-permute-start.32 = (bf16[144,2304]{1,0:T(8,128)(2,1)S(1)}, bf16[144,2304]{1,0:T(8,128)(2,1)S(1)}, u32[]{:S(2)}, u32[]{:S(2)}) collective-permute-start(bf16[144,2304]{1,0:T(8,128)(2,1)S(1)} %get-tuple-element.200.refs_1_), channel_id=1, source_target_pairs={{0,8},{4,12},{8,16},{12,20},{16,24},{20,28},{1,9},{5,13},{9,17},{1... | collective-permute-start | bytes 1990664 | tf_op jit(solution)/shard_map/ppermute | solution.py:137
  50.2 1.7 collective-permute-start.31
  52.0 20.0 %collective-permute-done.33.right_ref = bf16[144,2304]{1,0:T(8,128)(2,1)S(1)} collective-permute-done((bf16[144,2304]{1,0:T(8,128)(2,1)S(1)}, bf16[144,2304]{1,0:T(8,128)(2,1)S(1)}, u32[]{:S(2)}, u32[]{:S(2)}) %collective-permute-start.33) | collective-permute-done | bytes 663584 | tf_op jit(solution)/shard_map/ppermute | solution.py:137
  75.7 2.2 shard_map.224.refs_2_
  77.8 5.6 %collective-permute-start.34 = (bf16[144,2304]{1,0:T(8,128)(2,1)}, bf16[144,2304]{1,0:T(8,128)(2,1)S(1)}, u32[]{:S(2)}, u32[]{:S(2)}) collective-permute-start(bf16[144,2304]{1,0:T(8,128)(2,1)} %shard_map.224.refs_2_), channel_id=1, source_target_pairs={{0,4},{4,0},{8,12},{12,8},{16,20},{20,16},{24,28},{28,24},{1,5},{5... | collective-permute-start | bytes 1990664 | tf_op jit(solution)/shard_map/ppermute | solution.py:30
  84.3 8.4 %collective-permute-done.36.right_ref = bf16[144,2304]{1,0:T(8,128)(2,1)} collective-permute-done((bf16[144,2304]{1,0:T(8,128)(2,1)S(1)}, bf16[144,2304]{1,0:T(8,128)(2,1)}, u32[]{:S(2)}, u32[]{:S(2)}) %collective-permute-start.36) | collective-permute-done | bytes 663584 | tf_op jit(solution)/shard_map/ppermute | solution.py:137
  95.0 2.2 shard_map.225.refs_11_.refs_3_
  100.4 2.9 collective-permute-start.38
  103.3 11.0 %shard_map.226 = (bf16[2,1152,256]{2,1,0:T(8,128)(2,1)}, bf16[2,1152,256]{2,1,0:T(8,128)(2,1)}, f32[2,864,256]{2,1,0:T(8,128)}, f32[2,4,256]{2,1,0:T(4,128)S(1)}...) custom-call(s32[13]{0:T(128)S(1)} %stack.128.refs_0_, ...), custom_call_target="tpu_custom_call" | custom-call | flops 1 | bytes 1 | tf_op jit(solution)/shard_map/pallas_call | solution.py:588
  115.9 1.5 collective-permute-start.41
  117.4 1.8 collective-permute-done.38.refs_2_.refs_7_
  120.3 2.2 shard_map.227.refs_0_
  122.8 1.7 collective-permute-start.43
  124.5 8.8 %collective-permute-done.41.refs_2_.refs_8_ = bf16[144,2304]{1,0:T(8,128)(2,1)S(1)} collective-permute-done((bf16[144,2304]{1,0:T(8,128)(2,1)S(1)}, bf16[144,2304]{1,0:T(8,128)(2,1)S(1)}, u32[]{:S(2)}, u32[]{:S(2)}) %collective-permute-start.41) | collective-permute-done | bytes 663584 | tf_op jit(solution)/shard_map/ppermute | solution.py:30
  133.3 5.6 %collective-permute-done.39.refs_1_ = bf16[2,576,256]{2,1,0:T(8,128)(2,1)S(1)} collective-permute-done((bf16[2,576,256]{2,1,0:T(8,128)(2,1)}, bf16[2,576,256]{2,1,0:T(8,128)(2,1)S(1)}, u32[]{:S(2)}, u32[]{:S(2)}) %collective-permute-start.39) | collective-permute-done | bytes 589856 | tf_op jit(solution)/shard_map/ppermute | solution.py:30
  141.7 2.4 collective-permute-done.43
  144.8 2.6 shard_map.229
  147.5 34.4 %conditional.5 = (f32[2,1152,256]{2,1,0:T(8,128)S(1)}, f32[2,288,256]{2,1,0:T(8,128)}, bf16[2,1152,256]{2,1,0:T(8,128)(2,1)}, bf16[2,576,256]{2,1,0:T(8,128)(2,1...) conditional(s32[]{:T(128)} %bitcast.29, () %tuple.47, ...), branch_computations={%region_5.6_spmd, %region_6.7_spmd} | conditional | flops 3 | bytes 11796554 | solution.py:39
  148.7 12.5 %branch_1_fun.15 = (f32[2,1152,256]{2,1,0:T(8,128)S(1)}, f32[2,288,256]{2,1,0:T(8,128)}, bf16[2,1152,256]{2,1,0:T(8,128)(2,1)}, bf16[2,768,256]{2,1,0:T(8,128)(2...) custom-call(s32[13]{0:T(128)S(1)} %get-tuple-element.95.refs_0_, ...), custom_call_target="tpu_custom_call" | custom-call | flops 1 | bytes 1 | tf_op jit(solution)/shard_map/cond/branch_1_fun/pallas_call | solution.py:588
  161.8 2.0 collective-permute-done.refs_1_
  163.8 2.2 branch_1_fun.16
  166.2 8.0 %branch_1_fun.17 = (bf16[1152,2304]{1,0:T(8,128)(2,1)}, bf16[2,1152,256]{2,1,0:T(8,128)(2,1)}) custom-call(bf16[2,1152,256]{2,1,0:T(8,128)(2,1)} %get-tuple-element.111.refs_0_, bf16[2,768,256]{2,1,0:T(8,128)(2,1)} %get-tuple-element.112.refs_1_, bf16[2,1152,256]{2,1,0:T(8,128)(2,1)} %get-tuple-element.113.refs_2_, ...), custom_call_target="tpu_custom_call" | custom-call | flops 1 | bytes 1 | tf_op jit(solution)/shard_map/cond/branch_1_fun/pallas_call | solution.py:588
  174.2 7.6 %collective-permute-done.1 = bf16[2,576,256]{2,1,0:T(8,128)(2,1)} collective-permute-done((bf16[2,576,256]{2,1,0:T(8,128)(2,1)}, bf16[2,576,256]{2,1,0:T(8,128)(2,1)}, u32[]{:S(2)}, u32[]{:S(2)}) %collective-permute-start.1) | collective-permute-done | bytes 589856 | tf_op jit(solution)/shard_map/cond/branch_1_fun/ppermute | solution.py:30
  182.8 93.6 %conditional.6 = (bf16[2,288,256]{2,1,0:T(8,128)(2,1)}, bf16[2,288,256]{2,1,0:T(8,128)(2,1)}, bf16[16,2016]{1,0:T(8,128)(2,1)S(1)}, bf16[144,1152]{1,0:T(8,128)(...) conditional(s32[]{:T(128)} %bitcast.29, () %tuple.46, ...), branch_computations={%region_7.8_spmd, %region_8.11_spmd} | conditional | flops 2726010 | bytes 53948500 | solution.py:39
  182.8 2.2 branch_1_fun.18.refs_2_
  187.4 12.9 %branch_1_fun.19 = (f32[2,1152,256]{2,1,0:T(8,128)}, bf16[2,1152,256]{2,1,0:T(8,128)(2,1)}, bf16[2,896,256]{2,1,0:T(8,128)(2,1)}, bf16[2,576,256]{2,1,0:T(8,128)...) custom-call(s32[13]{0:T(128)S(1)} %get-tuple-element.117.refs_0_, ...), custom_call_target="tpu_custom_call" | custom-call | flops 1 | bytes 1 | tf_op jit(solution)/shard_map/cond/branch_1_fun/pallas_call | solution.py:588
  201.8 5.6 %branch_1_fun.21 = (bf16[144,1152]{1,0:T(8,128)(2,1)}, bf16[144,1152]{1,0:T(8,128)(2,1)}, bf16[144,1152]{1,0:T(8,128)(2,1)}, bf16[144,1152]{1,0:T(8,128)(2,1)}, ...) custom-call(s32[13]{0:T(128)S(1)} %get-tuple-element.117.refs_0_, ...), custom_call_target="tpu_custom_call" | custom-call | flops 1 | bytes 1 | tf_op jit(solution)/shard_map/cond/branch_1_fun/pallas_call | solution.py:588
  207.4 1.5 collective-permute-start.9
  209.5 2.2 branch_1_fun.20.refs_0_
  213.3 1.8 collective-permute-start.7
  215.8 12.2 %collective-permute-done.4.refs_1_ = bf16[2,576,256]{2,1,0:T(8,128)(2,1)S(1)} collective-permute-done((bf16[2,576,256]{2,1,0:T(8,128)(2,1)}, bf16[2,576,256]{2,1,0:T(8,128)(2,1)S(1)}, u32[]{:S(2)}, u32[]{:S(2)}) %collective-permute-start.4) | collective-permute-done | bytes 589856 | tf_op jit(solution)/shard_map/cond/branch_1_fun/ppermute | solution.py:30
  228.9 2.2 branch_1_fun.22.refs_3_
  231.4 2.0 collective-permute-done.7
  235.2 6.1 %branch_1_fun.23 = (bf16[2,288,256]{2,1,0:T(8,128)(2,1)}, bf16[2,288,256]{2,1,0:T(8,128)(2,1)}, f32[2,8,288]{2,1,0:T(8,128)}) custom-call(s32[13]{0:T(128)S(1)} %get-tuple-element.117.refs_0_, f32[2]{0:T(128)S(1)} %get-tuple-element.118.refs_1_, f32[2]{0:T(128)S(1)} %get-tuple-element.119.refs_2_, bf16[2,576,256]{2,1,0:T(8,128)(2,1)} %branch_1_fun.22.refs_3_, ...), custom_call_target="tpu_custom_call" | custom-call | flops 1 | bytes 1 | tf_op jit(solution)/shard_map/cond/branch_1_fun/pallas_call | solution.py:588
  244.1 4.4 %collective-permute-start.10 = (bf16[2,2016]{1,0:T(2,128)(2,1)}, bf16[2,2016]{1,0:T(2,128)(2,1)S(1)}, u32[]{:S(2)}, u32[]{:S(2)}) collective-permute-start(bf16[2,2016]{1,0:T(2,128)(2,1)} %branch_1_fun.24), channel_id=1, source_target_pairs={{0,8},{4,12},{8,0},{12,4},{16,24},{20,28},{24,16},{28,20},{1,9},{5... | collective-permute-start | bytes 24200 | tf_op jit(solution)/shard_map/cond/branch_1_fun/ppermute | solution.py:30
  248.5 1.8 collective-permute-done.10
  251.1 1.7 collective-permute-start.11
  252.8 1.6 collective-permute-start.14
  255.9 1.6 collective-permute-start.12
  257.5 6.2 %collective-permute-done.14 = bf16[144,1152]{1,0:T(8,128)(2,1)S(1)} collective-permute-done((bf16[144,1152]{1,0:T(8,128)(2,1)}, bf16[144,1152]{1,0:T(8,128)(2,1)S(1)}, u32[]{:S(2)}, u32[]{:S(2)}) %collective-permute-start.14) | collective-permute-done | bytes 331808 | tf_op jit(solution)/shard_map/cond/branch_1_fun/ppermute | solution.py:30
  264.9 1.9 branch_1_fun.26
  266.7 1.9 branch_1_fun.27
  268.6 4.9 %collective-permute-done.13.refs_1_ = bf16[144,1152]{1,0:T(8,128)(2,1)S(1)} collective-permute-done((bf16[144,1152]{1,0:T(8,128)(2,1)}, bf16[144,1152]{1,0:T(8,128)(2,1)S(1)}, u32[]{:S(2)}, u32[]{:S(2)}) %collective-permute-start.13) | collective-permute-done | bytes 331808 | tf_op jit(solution)/shard_map/cond/branch_1_fun/ppermute | solution.py:30
  274.3 1.9 branch_1_fun.25
  276.5 2.5 collective-permute-start.47
  279.0 1.9 collective-permute-start.48
  280.9 36.2 %conditional.7 = (f32[6,144,288]{2,1,0:T(8,128)S(1)}, f32[6,288]{1,0:T(8,128)S(1)}, bf16[144]{0:T(256)(128)(2,1)S(1)}, f32[2,1152]{1,0:T(2,128)S(1)}, f32[72]{0:T(128)S(1)}, /*index=5*/f32[72]{0:T(128)S(1)}) conditional(s32[]{:T(128)} %bitcast.29, () %tuple.52, (bf16[16,2016]{1,0:T(8,128)(2,1)S(1)}, bf16[16,144]{1,0:T(8,128)(2,1)S(1)}, ...), branch_computations={%region_11.12_spmd, %region_12.15_spmd} | conditional | flops 16018473 | bytes 2418740 | solution.py:39
  284.2 2.3 collective-permute-done.21
  287.8 2.4 collective-permute-start.23
  292.2 14.5 %collective-permute-done.24 = f32[4,288]{1,0:T(4,128)S(1)} collective-permute-done((f32[4,288]{1,0:T(4,128)S(1)}, f32[4,288]{1,0:T(4,128)S(1)}, u32[]{:S(2)}, u32[]{:S(2)}) %collective-permute-start.24) | collective-permute-done | bytes 4640 | tf_op jit(solution)/shard_map/cond/branch_1_fun/ppermute | solution.py:30
  306.9 4.7 %collective-permute-start.25 = (f32[2,576]{1,0:T(2,128)S(1)}, f32[2,576]{1,0:T(2,128)S(1)}, u32[]{:S(2)}, u32[]{:S(2)}) collective-permute-start(f32[2,576]{1,0:T(2,128)S(1)} %select_bitcast_fusion.1), channel_id=1, source_target_pairs={{0,16},{4,20},{8,24},{12,28},{16,0},{20,4},{24,8},{28,12},{1,17},{... | collective-permute-start | bytes 13832 | tf_op jit(solution)/shard_map/cond/branch_1_fun/ppermute | solution.py:30
  311.6 5.4 %collective-permute-done.25 = f32[2,576]{1,0:T(2,128)S(1)} collective-permute-done((f32[2,576]{1,0:T(2,128)S(1)}, f32[2,576]{1,0:T(2,128)S(1)}, u32[]{:S(2)}, u32[]{:S(2)}) %collective-permute-start.25) | collective-permute-done | bytes 4640 | tf_op jit(solution)/shard_map/cond/branch_1_fun/ppermute | solution.py:30
  324.2 1.6 copy.102
  (264 shorter events, 60.1 us)
Async XLA Ops:
  7.3 96.1 %all-gather.2.cloned.1.call-start = ((), (), s32[]{:S(2)}) async-start(), calls=%async_computation.1 | async-start | bytes 2985984 | tf_op jit(solution)/shard_map/all_gather | solution.py:635
  10.3 311.8 %reduce-scatter.2.cloned.1.call-start = ((), (), s32[]{:S(2)}) async-start(), calls=%async_computation.2 | async-start | bytes 5971968 | tf_op jit(solution)/shard_map/reduce_scatter | solution.py:779
  10.9 4.6 %collective-permute-start.15 = (bf16[2,1280]{1,0:T(2,128)(2,1)S(1)}, bf16[2,1280]{1,0:T(2,128)(2,1)S(1)}, u32[]{:S(2)}, u32[]{:S(2)}) collective-permute-start(bf16[2,1280]{1,0:T(2,128)(2,1)S(1)} %concatenate.33), channel_id=1, source_target_pairs={{0,8},{4,12},{8,0},{12,4},{16,24},{20,28},{24,16},{28,20},{1,9},{5... | collective-permute-start | bytes 15368 | tf_op jit(solution)/shard_map/cond/branch_1_fun/ppermute | solution.py:30
  15.5 4.8 %collective-permute-start.16 = (bf16[2,2,1280]{2,1,0:T(2,128)(2,1)S(1)}, bf16[2,2,1280]{2,1,0:T(2,128)(2,1)S(1)}, u32[]{:S(2)}, u32[]{:S(2)}) collective-permute-start(bf16[2,2,1280]{2,1,0:T(2,128)(2,1)S(1)} %pad_maximum_fusion.9), channel_id=1, source_target_pairs={{0,16},{4,20},{8,24},{12,28},{16,0},{20,4},{24,8},{28,12},{1,17},{... | collective-permute-start | bytes 30728 | tf_op jit(solution)/shard_map/cond/branch_1_fun/ppermute | solution.py:30
  20.4 3.8 %collective-permute-start.17 = (bf16[2,2,2,1280]{3,2,1,0:T(2,128)(2,1)S(1)}, bf16[2,2,2,1280]{3,2,1,0:T(2,128)(2,1)S(1)}, u32[]{:S(2)}, u32[]{:S(2)}) collective-permute-start(bf16[2,2,2,1280]{3,2,1,0:T(2,128)(2,1)S(1)} %pad_maximum_fusion.8), channel_id=1, source_target_pairs={{0,4},{4,0},{8,12},{12,8},{16,20},{20,16},{24,28},{28,24},{1,5},{5... | collective-permute-start | bytes 61448 | tf_op jit(solution)/shard_map/cond/branch_1_fun/ppermute | solution.py:30
  25.2 17.5 %copy-start.33 = (bf16[16,144]{1,0:T(8,128)(2,1)}, bf16[16,144]{1,0:T(8,128)(2,1)S(1)}, u32[]{:S(2)}) copy-start(bf16[16,144]{1,0:T(8,128)(2,1)S(1)} %fusion.17) | copy-start | bytes 13828 | tf_op jit(solution)/shard_map/cond
  25.5 8.9 %collective-permute-start.18 = (f32[8,1728]{1,0:T(8,128)S(1)}, f32[8,1728]{1,0:T(8,128)S(1)}, u32[]{:S(2)}, u32[]{:S(2)}) collective-permute-start(f32[8,1728]{1,0:T(8,128)S(1)} %select_n.361), channel_id=1, source_target_pairs={{0,16},{4,20},{8,24},{12,28},{16,0},{20,4},{24,8},{28,12},{1,17},{... | collective-permute-start | bytes 165896 | tf_op jit(solution)/shard_map/cond/branch_1_fun/ppermute | solution.py:30
  34.4 4.3 %collective-permute-start.19 = (f32[4,1728]{1,0:T(4,128)S(1)}, f32[4,1728]{1,0:T(4,128)S(1)}, u32[]{:S(2)}, u32[]{:S(2)}) collective-permute-start(f32[4,1728]{1,0:T(4,128)S(1)} %slice_select_fusion.2), channel_id=1, source_target_pairs={{0,8},{4,12},{8,0},{12,4},{16,24},{20,28},{24,16},{28,20},{1,9},{5... | collective-permute-start | bytes 82952 | tf_op jit(solution)/shard_map/cond/branch_1_fun/ppermute | solution.py:30
  38.8 3.8 %collective-permute-start.20 = (f32[2,1728]{1,0:T(2,128)S(1)}, f32[2,1728]{1,0:T(2,128)S(1)}, u32[]{:S(2)}, u32[]{:S(2)}) collective-permute-start(f32[2,1728]{1,0:T(2,128)S(1)} %broadcast_select_fusion.19), channel_id=1, source_target_pairs={{0,4},{4,0},{8,12},{12,8},{16,20},{20,16},{24,28},{28,24},{1,5},{5... | collective-permute-start | bytes 41480 | tf_op jit(solution)/shard_map/cond/branch_1_fun/ppermute | solution.py:30
  44.4 27.6 %collective-permute-start.33 = (bf16[144,2304]{1,0:T(8,128)(2,1)S(1)}, bf16[144,2304]{1,0:T(8,128)(2,1)S(1)}, u32[]{:S(2)}, u32[]{:S(2)}) collective-permute-start(bf16[144,2304]{1,0:T(8,128)(2,1)S(1)} %get-tuple-element.200.refs_1_), channel_id=1, source_target_pairs={{8,0},{12,4},{16,8},{20,12},{24,16},{28,20},{9,1},{13,5},{17,9},{2... | collective-permute-start | bytes 1990664 | tf_op jit(solution)/shard_map/ppermute | solution.py:137
  45.7 27.6 %collective-permute-start.32 = (bf16[144,2304]{1,0:T(8,128)(2,1)S(1)}, bf16[144,2304]{1,0:T(8,128)(2,1)S(1)}, u32[]{:S(2)}, u32[]{:S(2)}) collective-permute-start(bf16[144,2304]{1,0:T(8,128)(2,1)S(1)} %get-tuple-element.200.refs_1_), channel_id=1, source_target_pairs={{0,8},{4,12},{8,16},{12,20},{16,24},{20,28},{1,9},{5,13},{9,17},{1... | collective-permute-start | bytes 1990664 | tf_op jit(solution)/shard_map/ppermute | solution.py:137
  50.2 24.6 %collective-permute-start.31 = (bf16[144,2304]{1,0:T(8,128)(2,1)S(1)}, bf16[144,2304]{1,0:T(8,128)(2,1)S(1)}, u32[]{:S(2)}, u32[]{:S(2)}) collective-permute-start(bf16[144,2304]{1,0:T(8,128)(2,1)S(1)} %get-tuple-element.200.refs_1_), channel_id=1, source_target_pairs={{0,4},{4,0},{8,12},{12,8},{16,20},{20,16},{24,28},{28,24},{1,5},{5... | collective-permute-start | bytes 1990664 | tf_op jit(solution)/shard_map/ppermute | solution.py:30
  72.0 20.8 %collective-permute-start.36 = (bf16[144,2304]{1,0:T(8,128)(2,1)S(1)}, bf16[144,2304]{1,0:T(8,128)(2,1)}, u32[]{:S(2)}, u32[]{:S(2)}) collective-permute-start(bf16[144,2304]{1,0:T(8,128)(2,1)S(1)} %collective-permute-done.33.right_ref), channel_id=1, source_target_pairs={{8,0},{12,4},{16,8},{20,12},{9,1},{13,5},{17,9},{21,13},{10,2},{14... | collective-permute-start | bytes 1990664 | tf_op jit(solution)/shard_map/ppermute | solution.py:137
  73.3 20.8 %collective-permute-start.35 = (bf16[144,2304]{1,0:T(8,128)(2,1)S(1)}, bf16[144,2304]{1,0:T(8,128)(2,1)}, u32[]{:S(2)}, u32[]{:S(2)}) collective-permute-start(bf16[144,2304]{1,0:T(8,128)(2,1)S(1)} %collective-permute-done.32.left_ref), channel_id=1, source_target_pairs={{8,16},{12,20},{16,24},{20,28},{9,17},{13,21},{17,25},{21,29},{10,... | collective-permute-start | bytes 1990664 | tf_op jit(solution)/shard_map/ppermute | solution.py:137
  77.8 16.3 %collective-permute-start.34 = (bf16[144,2304]{1,0:T(8,128)(2,1)}, bf16[144,2304]{1,0:T(8,128)(2,1)S(1)}, u32[]{:S(2)}, u32[]{:S(2)}) collective-permute-start(bf16[144,2304]{1,0:T(8,128)(2,1)} %shard_map.224.refs_2_), channel_id=1, source_target_pairs={{0,4},{4,0},{8,12},{12,8},{16,20},{20,16},{24,28},{28,24},{1,5},{5... | collective-permute-start | bytes 1990664 | tf_op jit(solution)/shard_map/ppermute | solution.py:30
  83.4 15.2 %collective-permute-start.29 = (f32[2,8,288]{2,1,0:T(8,128)S(1)}, f32[2,8,288]{2,1,0:T(8,128)S(1)}, u32[]{:S(2)}, u32[]{:S(2)}) collective-permute-start(f32[2,8,288]{2,1,0:T(8,128)S(1)} %get-tuple-element.199), channel_id=1, source_target_pairs={{0,2},{1,3},{2,0},{3,1},{4,6},{5,7},{6,4},{7,5},{8,10},{9,11},{10,... | collective-permute-start | bytes 55304 | tf_op jit(solution)/shard_map/ppermute | solution.py:30
  84.3 19.0 %collective-permute-start.27 = (bf16[2,288,256]{2,1,0:T(8,128)(2,1)}, bf16[2,288,256]{2,1,0:T(8,128)(2,1)}, u32[]{:S(2)}, u32[]{:S(2)}) collective-permute-start(bf16[2,288,256]{2,1,0:T(8,128)(2,1)} %bitcast.44.refs_1_), channel_id=1, source_target_pairs={{0,1},{1,0},{2,3},{3,2},{4,5},{5,4},{6,7},{7,6},{8,9},{9,8},{10,11... | collective-permute-start | bytes 884744 | tf_op jit(solution)/shard_map/ppermute | solution.py:30
  92.8 7.0 %collective-permute-start.26 = (bf16[2,288,256]{2,1,0:T(8,128)(2,1)}, bf16[2,288,256]{2,1,0:T(8,128)(2,1)}, u32[]{:S(2)}, u32[]{:S(2)}) collective-permute-start(bf16[2,288,256]{2,1,0:T(8,128)(2,1)} %bitcast.44.refs_1_), channel_id=1, source_target_pairs={{0,2},{1,3},{2,0},{3,1},{4,6},{5,7},{6,4},{7,5},{8,10},{9,11},{10,... | collective-permute-start | bytes 884744 | tf_op jit(solution)/shard_map/ppermute | solution.py:30
  97.2 6.1 %copy-start.20 = (f32[3,72,256]{2,1,0:T(8,128)S(1)}, f32[3,72,256]{2,1,0:T(8,128)}, u32[]{:S(2)}) copy-start(f32[3,72,256]{2,1,0:T(8,128)} %constant.322.clone.refs_8_) | copy-start | bytes 663556
  97.2 17.4 %collective-permute-start.40 = (bf16[144,2304]{1,0:T(8,128)(2,1)}, bf16[144,2304]{1,0:T(8,128)(2,1)}, u32[]{:S(2)}, u32[]{:S(2)}) collective-permute-start(bf16[144,2304]{1,0:T(8,128)(2,1)} %shard_map.225.refs_11_.refs_3_), channel_id=1, source_target_pairs={{8,0},{12,4},{16,24},{20,28},{9,1},{13,5},{17,25},{21,29},{10,2},{... | collective-permute-start | bytes 1990664 | tf_op jit(solution)/shard_map/ppermute | solution.py:137
  98.7 1.5 collective-permute-start.30
  99.8 3.5 %collective-permute-start.28 = (bf16[2,288,256]{2,1,0:T(8,128)(2,1)}, bf16[2,288,256]{2,1,0:T(8,128)(2,1)}, u32[]{:S(2)}, u32[]{:S(2)}) collective-permute-start(bf16[2,288,256]{2,1,0:T(8,128)(2,1)} %collective-permute-done.26.refs_2_), channel_id=1, source_target_pairs={{0,1},{1,0},{2,3},{3,2},{4,5},{5,4},{6,7},{7,6},{8,9},{9,8},{10,11... | collective-permute-start | bytes 884744 | tf_op jit(solution)/shard_map/ppermute | solution.py:30
  100.4 14.2 %copy-start.7 = (bf16[144,2304]{1,0:T(8,128)(2,1)S(1)}, bf16[144,2304]{1,0:T(8,128)(2,1)}, u32[]{:S(2)}) copy-start(bf16[144,2304]{1,0:T(8,128)(2,1)} %copy-done.6) | copy-start | bytes 1990660
  100.4 14.2 %copy-start.9 = (bf16[144,2304]{1,0:T(8,128)(2,1)S(1)}, bf16[144,2304]{1,0:T(8,128)(2,1)}, u32[]{:S(2)}) copy-start(bf16[144,2304]{1,0:T(8,128)(2,1)} %copy-done.8) | copy-start | bytes 1990660
  100.4 18.8 %collective-permute-start.38 = (bf16[144,2304]{1,0:T(8,128)(2,1)}, bf16[144,2304]{1,0:T(8,128)(2,1)S(1)}, u32[]{:S(2)}, u32[]{:S(2)}) collective-permute-start(bf16[144,2304]{1,0:T(8,128)(2,1)} %shard_map.225.refs_11_.refs_3_), channel_id=1, source_target_pairs={{0,4},{4,0},{8,12},{12,8},{16,20},{20,16},{24,28},{28,24},{1,5},{5... | collective-permute-start | bytes 1990664 | tf_op jit(solution)/shard_map/ppermute | solution.py:30
  114.3 4.9 %collective-permute-start.37 = (bf16[2,576,256]{2,1,0:T(8,128)(2,1)}, bf16[2,576,256]{2,1,0:T(8,128)(2,1)S(1)}, u32[]{:S(2)}, u32[]{:S(2)}) collective-permute-start(bf16[2,576,256]{2,1,0:T(8,128)(2,1)} %get-tuple-element.203), channel_id=1, source_target_pairs={{0,1},{1,0},{2,3},{3,2},{4,5},{5,4},{6,7},{7,6},{8,9},{9,8},{10,11... | collective-permute-start | bytes 1769480 | tf_op jit(solution)/shard_map/ppermute | solution.py:30
  115.9 28.9 %copy-start.11 = (bf16[144,2304]{1,0:T(8,128)(2,1)}, bf16[144,2304]{1,0:T(8,128)(2,1)S(1)}, u32[]{:S(2)}) copy-start(bf16[144,2304]{1,0:T(8,128)(2,1)S(1)} %select_select_fusion.refs_4_) | copy-start | bytes 1990660
  115.9 17.4 %collective-permute-start.41 = (bf16[144,2304]{1,0:T(8,128)(2,1)S(1)}, bf16[144,2304]{1,0:T(8,128)(2,1)S(1)}, u32[]{:S(2)}, u32[]{:S(2)}) collective-permute-start(bf16[144,2304]{1,0:T(8,128)(2,1)S(1)} %select_select_fusion.refs_4_), channel_id=1, source_target_pairs={{0,4},{4,0},{8,12},{12,8},{16,20},{20,16},{24,28},{28,24},{1,5},{5... | collective-permute-start | bytes 1990664 | tf_op jit(solution)/shard_map/ppermute | solution.py:30
  122.5 16.4 %collective-permute-start.39 = (bf16[2,576,256]{2,1,0:T(8,128)(2,1)}, bf16[2,576,256]{2,1,0:T(8,128)(2,1)S(1)}, u32[]{:S(2)}, u32[]{:S(2)}) collective-permute-start(bf16[2,576,256]{2,1,0:T(8,128)(2,1)} %shard_map.227.refs_0_), channel_id=1, source_target_pairs={{0,2},{1,3},{2,0},{3,1},{4,6},{5,7},{6,4},{7,5},{8,10},{9,11},{10,... | collective-permute-start | bytes 1769480 | tf_op jit(solution)/shard_map/ppermute | solution.py:30
  122.8 21.3 %collective-permute-start.43 = (bf16[2,288,256]{2,1,0:T(8,128)(2,1)}, bf16[2,288,256]{2,1,0:T(8,128)(2,1)}, u32[]{:S(2)}, u32[]{:S(2)}) collective-permute-start(bf16[2,288,256]{2,1,0:T(8,128)(2,1)} %bitcast.59), channel_id=1, source_target_pairs={{0,2},{1,3},{2,0},{3,1},{4,6},{5,7},{6,4},{7,5},{8,10},{9,11},{10,... | collective-permute-start | bytes 884744 | tf_op jit(solution)/shard_map/ppermute | solution.py:30
  133.3 5.6 %copy-start.12 = (bf16[144,2304]{1,0:T(8,128)(2,1)}, bf16[144,2304]{1,0:T(8,128)(2,1)S(1)}, u32[]{:S(2)}) copy-start(bf16[144,2304]{1,0:T(8,128)(2,1)S(1)} %collective-permute-done.41.refs_2_.refs_8_) | copy-start | bytes 1990660
  141.1 6.3 %collective-permute-start.42 = (bf16[2,576,256]{2,1,0:T(8,128)(2,1)S(1)}, bf16[2,576,256]{2,1,0:T(8,128)(2,1)S(1)}, u32[]{:S(2)}, u32[]{:S(2)}) collective-permute-start(bf16[2,576,256]{2,1,0:T(8,128)(2,1)S(1)} %shard_map.228), channel_id=1, source_target_pairs={{0,1},{1,0},{2,3},{3,2},{4,5},{5,4},{6,7},{7,6},{8,9},{9,8},{10,11... | collective-permute-start | bytes 1769480 | tf_op jit(solution)/shard_map/ppermute | solution.py:30
  141.2 6.2 %collective-permute-start.44 = (bf16[2,288,256]{2,1,0:T(8,128)(2,1)}, bf16[2,288,256]{2,1,0:T(8,128)(2,1)}, u32[]{:S(2)}, u32[]{:S(2)}) collective-permute-start(bf16[2,288,256]{2,1,0:T(8,128)(2,1)} %bitcast.59), channel_id=1, source_target_pairs={{0,1},{1,0},{2,3},{3,2},{4,5},{5,4},{6,7},{7,6},{8,9},{9,8},{10,11... | collective-permute-start | bytes 884744 | tf_op jit(solution)/shard_map/ppermute | solution.py:30
  144.1 3.3 %collective-permute-start.45 = (bf16[2,288,256]{2,1,0:T(8,128)(2,1)}, bf16[2,288,256]{2,1,0:T(8,128)(2,1)}, u32[]{:S(2)}, u32[]{:S(2)}) collective-permute-start(bf16[2,288,256]{2,1,0:T(8,128)(2,1)} %collective-permute-done.43), channel_id=1, source_target_pairs={{0,1},{1,0},{2,3},{3,2},{4,5},{5,4},{6,7},{7,6},{8,9},{9,8},{10,11... | collective-permute-start | bytes 884744 | tf_op jit(solution)/shard_map/ppermute | solution.py:30
  161.2 2.5 collective-permute-start
  165.9 15.9 %collective-permute-start.1 = (bf16[2,576,256]{2,1,0:T(8,128)(2,1)}, bf16[2,576,256]{2,1,0:T(8,128)(2,1)}, u32[]{:S(2)}, u32[]{:S(2)}) collective-permute-start(bf16[2,576,256]{2,1,0:T(8,128)(2,1)} %branch_1_fun.16), channel_id=1, source_target_pairs={{0,2},{1,3},{2,0},{3,1},{4,6},{5,7},{6,4},{7,5},{8,10},{9,11},{10,... | collective-permute-start | bytes 1769480 | tf_op jit(solution)/shard_map/cond/branch_1_fun/ppermute | solution.py:30
  185.0 2.3 collective-permute-start.2
  187.1 13.7 %copy-start.2 = (bf16[2,2,1,288,256]{4,3,2,1,0:T(8,128)(2,1)}, bf16[2,2,1,288,256]{4,3,2,1,0:T(8,128)(2,1)S(1)}, u32[]{:S(2)}) copy-start(bf16[2,2,1,288,256]{4,3,2,1,0:T(8,128)(2,1)S(1)} %get-tuple-element.379) | copy-start | bytes 1769476 | tf_op jit(solution)/shard_map/cond
  200.3 9.1 %collective-permute-start.3 = (bf16[2,576,256]{2,1,0:T(8,128)(2,1)}, bf16[2,576,256]{2,1,0:T(8,128)(2,1)}, u32[]{:S(2)}, u32[]{:S(2)}) collective-permute-start(bf16[2,576,256]{2,1,0:T(8,128)(2,1)} %get-tuple-element.132), channel_id=1, source_target_pairs={{0,1},{1,0},{2,3},{3,2},{4,5},{5,4},{6,7},{7,6},{8,9},{9,8},{10,11... | collective-permute-start | bytes 1769480 | tf_op jit(solution)/shard_map/cond/branch_1_fun/ppermute | solution.py:30
  201.7 10.2 %collective-permute-start.6 = (bf16[2,2,288,256]{3,2,0,1:T(8,128)(2,1)}, bf16[2,2,288,256]{3,2,0,1:T(8,128)(2,1)}, u32[]{:S(2)}, u32[]{:S(2)}) collective-permute-start(bf16[2,2,288,256]{3,2,0,1:T(8,128)(2,1)} %select_bitcast_fusion), channel_id=1, source_target_pairs={{0,1},{1,0},{2,3},{3,2},{4,5},{5,4},{6,7},{7,6},{8,9},{9,8},{10,11... | collective-permute-start | bytes 1769480 | tf_op jit(solution)/shard_map/cond/branch_1_fun/ppermute | solution.py:30
  207.4 4.5 %copy-start.3 = (bf16[2,2,1,288,256]{4,3,2,1,0:T(8,128)(2,1)S(1)}, bf16[2,2,1,288,256]{4,3,2,1,0:T(8,128)(2,1)}, u32[]{:S(2)}) copy-start(bf16[2,2,1,288,256]{4,3,2,1,0:T(8,128)(2,1)} %copy-done.2) | copy-start | bytes 1769476 | tf_op jit(solution)/shard_map/cond
  207.4 35.4 %collective-permute-start.9 = (bf16[144,1152]{1,0:T(8,128)(2,1)}, bf16[144,1152]{1,0:T(8,128)(2,1)}, u32[]{:S(2)}, u32[]{:S(2)}) collective-permute-start(bf16[144,1152]{1,0:T(8,128)(2,1)} %get-tuple-element.142.refs_7_), channel_id=1, source_target_pairs={{0,4},{4,0},{8,12},{12,8},{16,20},{20,16},{24,28},{28,24},{1,5},{5... | collective-permute-start | bytes 995336 | tf_op jit(solution)/shard_map/cond/branch_1_fun/ppermute | solution.py:30
  209.0 25.3 %collective-permute-start.8 = (bf16[144,1152]{1,0:T(8,128)(2,1)}, bf16[144,1152]{1,0:T(8,128)(2,1)S(1)}, u32[]{:S(2)}, u32[]{:S(2)}) collective-permute-start(bf16[144,1152]{1,0:T(8,128)(2,1)} %get-tuple-element.144.refs_9_), channel_id=1, source_target_pairs={{0,4},{4,0},{8,12},{12,8},{16,20},{20,16},{24,28},{28,24},{1,5},{5... | collective-permute-start | bytes 995336 | tf_op jit(solution)/shard_map/cond/branch_1_fun/ppermute | solution.py:30
  211.6 16.4 %collective-permute-start.4 = (bf16[2,576,256]{2,1,0:T(8,128)(2,1)}, bf16[2,576,256]{2,1,0:T(8,128)(2,1)S(1)}, u32[]{:S(2)}, u32[]{:S(2)}) collective-permute-start(bf16[2,576,256]{2,1,0:T(8,128)(2,1)} %branch_1_fun.20.refs_0_), channel_id=1, source_target_pairs={{0,2},{1,3},{2,0},{3,1},{4,6},{5,7},{6,4},{7,5},{8,10},{9,11},{10,... | collective-permute-start | bytes 1769480 | tf_op jit(solution)/shard_map/cond/branch_1_fun/ppermute | solution.py:30
  213.3 20.1 %collective-permute-start.7 = (bf16[2,288,256]{2,1,0:T(8,128)(2,1)S(1)}, bf16[2,288,256]{2,1,0:T(8,128)(2,1)S(1)}, u32[]{:S(2)}, u32[]{:S(2)}) collective-permute-start(bf16[2,288,256]{2,1,0:T(8,128)(2,1)S(1)} %fusion), channel_id=1, source_target_pairs={{0,2},{1,3},{2,0},{3,1},{4,6},{5,7},{6,4},{7,5},{8,10},{9,11},{10,... | collective-permute-start | bytes 884744 | tf_op jit(solution)/shard_map/cond/branch_1_fun/ppermute | solution.py:30
  231.1 4.1 %copy-start.4 = (bf16[2,1152,256]{2,1,0:T(8,128)(2,1)S(1)}, bf16[2,1152,256]{2,1,0:T(8,128)(2,1)}, u32[]{:S(2)}) copy-start(bf16[2,1152,256]{2,1,0:T(8,128)(2,1)} %get-tuple-element.145.refs_5_) | copy-start | bytes 3538948 | tf_op jit(solution)/shard_map/cond
  231.1 3.2 collective-permute-start.5
  235.2 28.5 %copy-start.19 = (bf16[144,1152]{1,0:T(8,128)(2,1)S(1)}, bf16[144,1152]{1,0:T(8,128)(2,1)}, u32[]{:S(2)}) copy-start(bf16[144,1152]{1,0:T(8,128)(2,1)} %get-tuple-element.137.refs_2_) | copy-start | bytes 995332 | tf_op jit(solution)/shard_map/cond
  244.1 6.2 %collective-permute-start.10 = (bf16[2,2016]{1,0:T(2,128)(2,1)}, bf16[2,2016]{1,0:T(2,128)(2,1)S(1)}, u32[]{:S(2)}, u32[]{:S(2)}) collective-permute-start(bf16[2,2016]{1,0:T(2,128)(2,1)} %branch_1_fun.24), channel_id=1, source_target_pairs={{0,8},{4,12},{8,0},{12,4},{16,24},{20,28},{24,16},{28,20},{1,9},{5... | collective-permute-start | bytes 24200 | tf_op jit(solution)/shard_map/cond/branch_1_fun/ppermute | solution.py:30
  251.1 4.7 %collective-permute-start.11 = (bf16[2,2,2016]{2,1,0:T(2,128)(2,1)S(1)}, bf16[2,2,2016]{2,1,0:T(2,128)(2,1)S(1)}, u32[]{:S(2)}, u32[]{:S(2)}) collective-permute-start(bf16[2,2,2016]{2,1,0:T(2,128)(2,1)S(1)} %pad_maximum_fusion.1), channel_id=1, source_target_pairs={{0,16},{4,20},{8,24},{12,28},{16,0},{20,4},{24,8},{28,12},{1,17},{... | collective-permute-start | bytes 48392 | tf_op jit(solution)/shard_map/cond/branch_1_fun/ppermute | solution.py:30
  252.8 10.9 %collective-permute-start.14 = (bf16[144,1152]{1,0:T(8,128)(2,1)}, bf16[144,1152]{1,0:T(8,128)(2,1)S(1)}, u32[]{:S(2)}, u32[]{:S(2)}) collective-permute-start(bf16[144,1152]{1,0:T(8,128)(2,1)} %get-tuple-element.138.refs_3_), channel_id=1, source_target_pairs={{0,4},{4,0},{8,12},{12,8},{16,20},{20,16},{24,28},{28,24},{1,5},{5... | collective-permute-start | bytes 995336 | tf_op jit(solution)/shard_map/cond/branch_1_fun/ppermute | solution.py:30
  254.3 19.2 %collective-permute-start.13 = (bf16[144,1152]{1,0:T(8,128)(2,1)}, bf16[144,1152]{1,0:T(8,128)(2,1)S(1)}, u32[]{:S(2)}, u32[]{:S(2)}) collective-permute-start(bf16[144,1152]{1,0:T(8,128)(2,1)} %get-tuple-element.140.refs_5_), channel_id=1, source_target_pairs={{0,4},{4,0},{8,12},{12,8},{16,20},{20,16},{24,28},{28,24},{1,5},{5... | collective-permute-start | bytes 995336 | tf_op jit(solution)/shard_map/cond/branch_1_fun/ppermute | solution.py:30
  255.9 20.2 %collective-permute-start.12 = (bf16[2,2,2,2016]{3,2,1,0:T(2,128)(2,1)S(1)}, bf16[2,2,2,2016]{3,2,1,0:T(2,128)(2,1)S(1)}, u32[]{:S(2)}, u32[]{:S(2)}) collective-permute-start(bf16[2,2,2,2016]{3,2,1,0:T(2,128)(2,1)S(1)} %pad_maximum_fusion), channel_id=1, source_target_pairs={{0,4},{4,0},{8,12},{12,8},{16,20},{20,16},{24,28},{28,24},{1,5},{5... | collective-permute-start | bytes 96776 | tf_op jit(solution)/shard_map/cond/branch_1_fun/ppermute | solution.py:30
  276.4 41.4 %collective-permute-start.46 = (bf16[144,1152]{1,0:T(8,128)(2,1)}, bf16[144,1152]{1,0:T(8,128)(2,1)S(1)}, u32[]{:S(2)}, u32[]{:S(2)}) collective-permute-start(bf16[144,1152]{1,0:T(8,128)(2,1)} %get-tuple-element.222), channel_id=1, source_target_pairs={{0,8},{4,12},{8,0},{12,4},{16,24},{20,28},{24,16},{28,20},{1,9},{5... | collective-permute-start | bytes 995336 | tf_op jit(solution)/shard_map/ppermute | solution.py:30
  276.5 41.3 %collective-permute-start.47 = (bf16[144,1152]{1,0:T(8,128)(2,1)}, bf16[144,1152]{1,0:T(8,128)(2,1)S(1)}, u32[]{:S(2)}, u32[]{:S(2)}) collective-permute-start(bf16[144,1152]{1,0:T(8,128)(2,1)} %get-tuple-element.223), channel_id=1, source_target_pairs={{0,16},{4,20},{8,24},{12,28},{16,0},{20,4},{24,8},{28,12},{1,17},{... | collective-permute-start | bytes 995336 | tf_op jit(solution)/shard_map/ppermute | solution.py:30
  279.0 38.8 %collective-permute-start.48 = (bf16[144,1152]{1,0:T(8,128)(2,1)}, bf16[144,1152]{1,0:T(8,128)(2,1)S(1)}, u32[]{:S(2)}, u32[]{:S(2)}) collective-permute-start(bf16[144,1152]{1,0:T(8,128)(2,1)} %get-tuple-element.224), channel_id=1, source_target_pairs={{0,24},{4,28},{8,16},{12,20},{16,8},{20,12},{24,0},{28,4},{1,25},{... | collective-permute-start | bytes 995336 | tf_op jit(solution)/shard_map/ppermute | solution.py:30
  282.7 3.8 %collective-permute-start.21 = (f32[2448]{0:T(1024)S(1)}, f32[2448]{0:T(1024)S(1)}, u32[]{:S(2)}, u32[]{:S(2)}) collective-permute-start(f32[2448]{0:T(1024)S(1)} %pad_maximum_fusion.4), channel_id=1, source_target_pairs={{0,2},{1,3},{2,0},{3,1},{4,6},{5,7},{6,4},{7,5},{8,10},{9,11},{10,... | collective-permute-start | bytes 29384 | tf_op jit(solution)/shard_map/cond/branch_1_fun/ppermute | solution.py:30
  286.5 1.2 collective-permute-start.22
  287.8 4.1 %collective-permute-start.23 = (f32[8,144]{1,0:T(8,128)S(1)}, f32[8,144]{1,0:T(8,128)S(1)}, u32[]{:S(2)}, u32[]{:S(2)}) collective-permute-start(f32[8,144]{1,0:T(8,128)S(1)} %select_n.410), channel_id=1, source_target_pairs={{0,4},{4,0},{8,12},{12,8},{16,20},{20,16},{24,28},{28,24},{1,5},{5... | collective-permute-start | bytes 13832 | tf_op jit(solution)/shard_map/cond/branch_1_fun/ppermute | solution.py:30
  292.0 14.8 %collective-permute-start.24 = (f32[4,288]{1,0:T(4,128)S(1)}, f32[4,288]{1,0:T(4,128)S(1)}, u32[]{:S(2)}, u32[]{:S(2)}) collective-permute-start(f32[4,288]{1,0:T(4,128)S(1)} %select_n.416), channel_id=1, source_target_pairs={{0,8},{4,12},{8,0},{12,4},{16,24},{20,28},{24,16},{28,20},{1,9},{5... | collective-permute-start | bytes 13832 | tf_op jit(solution)/shard_map/cond/branch_1_fun/ppermute | solution.py:30
  306.9 10.2 %collective-permute-start.25 = (f32[2,576]{1,0:T(2,128)S(1)}, f32[2,576]{1,0:T(2,128)S(1)}, u32[]{:S(2)}, u32[]{:S(2)}) collective-permute-start(f32[2,576]{1,0:T(2,128)S(1)} %select_bitcast_fusion.1), channel_id=1, source_target_pairs={{0,16},{4,20},{8,24},{12,28},{16,0},{20,4},{24,8},{28,12},{1,17},{... | collective-permute-start | bytes 13832 | tf_op jit(solution)/shard_map/cond/branch_1_fun/ppermute | solution.py:30
  317.1 6.2 %copy-start.36 = (f32[6,288]{1,0:T(8,128)}, f32[6,288]{1,0:T(8,128)S(1)}, u32[]{:S(2)}) copy-start(f32[6,288]{1,0:T(8,128)S(1)} %get-tuple-element.366) | copy-start | bytes 20740
  317.1 6.2 %copy-start.42 = (f32[72]{0:T(128)}, f32[72]{0:T(128)S(1)}, u32[]{:S(2)}) copy-start(f32[72]{0:T(128)S(1)} %get-tuple-element.369) | copy-start | bytes 868
  317.1 6.2 %copy-start.43 = (f32[72]{0:T(128)}, f32[72]{0:T(128)S(1)}, u32[]{:S(2)}) copy-start(f32[72]{0:T(128)S(1)} %get-tuple-element.368) | copy-start | bytes 868
  (31 other events, 58.5 us)
Sparse Core Ops, SparseCore 0:
  10.8 75.3 all-gather.1
  182.0 119.3 reduce-scatter.1

commit v4 on v3

--- a/solution.py
+++ b/solution.py
@@ -187,6 +187,26 @@
     )(jnp.reshape(flag.astype(jnp.int32), (1,)), left, right, token)
 
 
+def unpacked(terms, quarter):
+    rows = terms[0].shape[0]
+
+    def kernel(*refs):
+        qkv_ref, out_ref = refs[-2:]
+        total = refs[0][...].astype(F32)
+        for ref in refs[1:-2]:
+            total = total + ref[...].astype(F32)
+        for part in range(3):
+            qkv_ref[part] = total[:, part * quarter : (part + 1) * quarter]
+        out_ref[...] = total[:, 3 * quarter :]
+
+    return pl.pallas_call(
+        kernel,
+        out_shape=[shaped((3, rows, quarter), F32), shaped((rows, quarter), F32)],
+        compiler_params=pltpu.CompilerParams(vmem_limit_bytes=VMEM_BYTES),
+        cost_estimate=pl.CostEstimate(flops=1, bytes_accessed=1, transcendentals=0),
+    )(*terms)
+
+
 def packed(gate_up, down, token):
     rows, units = down.shape
 
@@ -207,7 +227,7 @@
 def dp_cross(parts):
     if len(parts) == 1:
         return [lax.psum_scatter(parts[0], "dp", scatter_dimension=0, tiled=True)]
-    return [swap(parts[k + 1], "dp", 1) for k in range(0, len(parts), 2)]
+    return [None] + [swap(parts[k + 1], "dp", 1) for k in range(2, len(parts), 2)]
 
 
 def dp_pair_sums(parts, cross, *tokens):
@@ -421,13 +441,16 @@
     return total
 
 
-def feed_forward_grads(h_ref, hidden_ref, dffn_ref, dgu_ref, weight_ref, outs):
+def feed_forward_grads(h_ref, hidden_ref, dffn_ref, dgu_ref, outs):
     units = hidden_ref.shape[1]
-    grad_ref, ffn_ref = outs
+    (grad_ref,) = outs
     grad_ref[:, :units] = over_images(h_ref, dgu_ref, slice(0, units)).astype(BF16)
     grad_ref[:, units : 2 * units] = over_images(h_ref, dgu_ref, slice(units, 2 * units)).astype(BF16)
     grad_ref[:, 2 * units :] = over_images(dffn_ref, hidden_ref).astype(BF16)
-    for n in range(h_ref.shape[0]):
+
+
+def feed_forward_end(hidden_ref, weight_ref, ffn_ref):
+    for n in range(hidden_ref.shape[0]):
         ffn_ref[n] = dot(weight_ref[...], hidden_ref[n], NN).astype(BF16)
 
 
@@ -655,17 +678,18 @@
         image_weight = keep * jnp.sum(all_valid) / (BINS * jnp.maximum(own_count, 1.0))
 
         cond_act = jax.nn.silu(cond_rows).astype(BF16)
-        mods_terms = jnp.einsum("nd,cde->nce", cond_act, ada, preferred_element_type=F32)
-        mods_own = scatter_rows(mods_terms.reshape(all_images, -1), "dp")
-        pack = packed(jnp.transpose(gate_up, (1, 0, 2)), down_weight.T, mods_own)
-        mods_own = mods_own.reshape(images, 6, quarter) + ada_bias[None]
-        mods_own = jnp.pad(mods_own, ((0, 0), (0, 2), (0, 0)))
-        return cond_act, image_weight, mods_own, pack
-
-    cond_act, image_weight, mods_own, second_pack = region(given, over_dp)
+        pack = packed(jnp.transpose(gate_up, (1, 0, 2)), down_weight.T, cond_act)
+        return cond_act, image_weight, pack
+
+    cond_act, image_weight, second_pack = region(given, over_dp)
+    mods_terms = jnp.einsum("nd,cde->nce", cond_act, ada, preferred_element_type=F32)
+    mods_own = scatter_rows(mods_terms.reshape(all_images, -1), "dp")
     hop_one = line_first(second_pack) if on_line else ()
     beside = [swap(second_pack, "dp", 1)] if on_line else []
-    near = line_near(hop_one, beside[0]) if on_line else None
+    near = line_near(hop_one, hop_one[0]) if on_line else None
+    mods_own = after(mods_own, *beside)
+    mods_own = mods_own.reshape(images, 6, quarter) + ada_bias[None]
+    mods_own = jnp.pad(mods_own, ((0, 0), (0, 2), (0, 0)))
     beside += [swap(near, "dp", 1)] if on_line else []
     two = line_two(hop_one, beside[1]) if on_line else None
     held = [*beside, two] if on_line else []
@@ -676,7 +700,7 @@
     quad = jnp.stack([jnp.where(core == 0, pair, other), jnp.where(core == 0, other, pair)], axis=1)
     mods = jnp.transpose(quad, (2, 3, 0, 1, 4)).reshape(images, 8, width)
 
-    count = dp_size if direct() else 1
+    count = dp_size if on_line else 1
     place = jnp.stack([mp, mp ^ 2, mp ^ 1, mp ^ 3, core] + [dp ^ k for k in range(count)])
     place = place.astype(jnp.int32)
     block_shape = (width // count,)
@@ -764,22 +788,28 @@
             [tall],
             images,
         )
-        chip = mp_chip(mine, theirs)
-        grads = call(
+        (second_terms,) = call(
             lambda a, outs, x: feed_forward_grads(*a, outs),
-            [[(h_two, whole), (hidden, whole), (dffn, whole), (dgu, whole), (second, last)]],
-            [(shaped((width, 3 * units), BF16), whole), (wide(BF16), whole)],
+            [[(h_two, whole), (hidden, whole), (dffn, whole), (dgu, whole)]],
+            [(shaped((width, 3 * units), BF16), whole)],
             [],
             1,
         )
-        return mid, attn_own, cot, chip, swap(chip, "mp", 2), grads
-
-    mid, attn_own, cot, dh_two_chip, dh_two_far, grads = region(given, middle)
-    second_terms, ffn_part = grads
+        return mid, attn_own, cot, hidden, mine, swap(theirs, "mp", 1), second_terms
+
+    mid, attn_own, cot, hidden, dh_two_mine, dh_two_other, second_terms = region(given, middle)
     second_sum = lax.psum_scatter(second_terms, "dp", scatter_dimension=0, tiled=True)
 
     def backward():
-        dh_two_sums = mp_join(dh_two_chip, dh_two_far)
+        dh_two_chip = add_blocks(dh_two_mine, dh_two_other)
+        (ffn_part,) = call(
+            lambda a, outs, x: feed_forward_end(*a, *outs),
+            [[(hidden, whole), (second, last)]],
+            [(wide(BF16), whole)],
+            [],
+            1,
+        )
+        dh_two_sums = mp_join(dh_two_chip, swap(dh_two_chip, "mp", 2), ffn_part)
         dmid, dattn, draw, mine, theirs, dmods_part, qgain, kgain = call(
             lambda p, w, s, a, outs, x: attention_backward(heads, p[0], w[0], s, *a, outs, x),
             [
@@ -823,7 +853,9 @@
         )
         ffn_own = mp_quarter(ffn_part)
         first_beside = dp_cross(first_terms)
-        dh_one_sums = mp_total(mine, theirs, tuple(first_terms))
+        end_half = [add_blocks(first_terms[6], first_beside[3])] if on_line else []
+        last_line = [swap(half_sum, "dp", 6) for half_sum in end_half]
+        dh_one_sums = mp_total(mine, theirs, (*first_terms, *first_beside[3:]))
         block_out, latent_grad, dmods = call(
             lambda p, w, k, s, a, _, outs, x: last_steps(p[0], w[0], k[0], s, *a, outs, x),
             [
@@ -840,7 +872,7 @@
                     (ffn_own, each),
                     (dmods_part, each),
                 ],
-                [(a, token) for a in first_beside[3:]],
+                [(a, token) for a in end_half],
             ],
             [
                 (shaped((images, quarter, patches), BF16), each),
@@ -851,19 +883,21 @@
             images,
         )
 
+        halves = dp_pair_sums(first_terms, first_beside[:3], dmods) if on_line else []
+
         gain_terms = jnp.concatenate([jnp.sum(qgain[:, 0], axis=0), jnp.sum(kgain[:, 0], axis=0)])
         high = gain_terms.astype(BF16)
         low = (gain_terms - high.astype(F32)).astype(BF16)
         beside = jnp.concatenate([high, low])[None]
         beside = jnp.concatenate([beside, jnp.zeros((images - 1, beside.shape[1]), BF16)], axis=0)
         rounded = dmods[:, :6].astype(BF16).reshape(images, 6 * quarter)
-        rounded = after(jnp.concatenate([rounded, beside], axis=1), *first_beside[2:3])
+        rounded = after(jnp.concatenate([rounded, beside], axis=1), *halves, *last_line)
         told_back = gather_rows(rounded, "dp")
-        halves = dp_pair_sums(first_terms, first_beside) if count > 1 else []
-        return block_out, latent_grad, told_back, first_terms[0], first_beside[0], halves
-
-    block_out, latent_grad, told_back, first_own, first_beside, halves = region(given, backward)
-    first_far = dp_lines(halves)
+        own = first_terms[:2] if count > 1 else first_beside
+        return block_out, latent_grad, told_back, own, halves, last_line
+
+    block_out, latent_grad, told_back, own, halves, last_line = region(given, backward)
+    first_far = dp_lines(halves) + last_line
 
     def modulation_grads():
         dmods_all = told_back[:, : 6 * quarter].reshape(all_images, 6, quarter)
@@ -878,29 +912,26 @@
         return ada_grad, bias_grad, gain_sum, cond_sum
 
     ada_grad, bias_grad, gain_sum, cond_sum = region(given, modulation_grads)
-    first_sum = first_beside.astype(F32)
+    last_terms = [own[0], *first_far]
     if count > 1:
-        first_sum = first_sum + first_own.astype(F32)
-    for line in first_far:
-        first_sum = first_sum + line.astype(F32)
+        last_terms.insert(1, swap(own[1], "dp", 1))
+    qkv_grad, out_grad = unpacked(last_terms, quarter)
+    second_sum = second_sum.astype(F32)
+    gateup_grad = jnp.stack([second_sum[:, :units], second_sum[:, units : 2 * units]], axis=1)
+    down_grad = second_sum[:, 2 * units :].T
     cond_own = condition.astype(F32)
     sig = jax.nn.sigmoid(cond_own)
     condition_grad = (cond_sum * sig * (1.0 + cond_own * (1.0 - sig))).astype(BF16)
-    second_sum = second_sum.astype(F32)
-    gateup_grad = jnp.stack([second_sum[:, :units], second_sum[:, units : 2 * units]], axis=1)
-    down_grad = second_sum[:, 2 * units :].T
-    qkv_grad = first_sum[:, : 3 * quarter].reshape(rows, 3, quarter)
-    out_grad = first_sum[:, 3 * quarter :].T
     return (
         jnp.transpose(block_out, (0, 2, 1)),
         jnp.transpose(latent_grad, (0, 2, 1)),
         condition_grad,
         jnp.transpose(ada_grad, (1, 0, 2)),
         bias_grad,
-        qkv_grad,
+        jnp.transpose(qkv_grad, (1, 0, 2)),
         gain_sum[:head_size],
         gain_sum[head_size:],
-        out_grad,
+        out_grad.T,
         gateup_grad,
         down_grad,
     )

time: 334 us -> 325 us (0.973)
  starting transfers between devices: 68.7 us -> 58.8 us
  waiting for transfers between devices: 125 us -> 116 us
  Pallas kernels: 83.7 us -> 90.1 us
    ppermute x44, waiting for transfers between devices: 96.9 us -> 77.9 us  [swap(): return lax.ppermute(value, axis, [(i, i ^ bit) for i in range(size)])]
    ppermute x5, waiting for transfers between devices: 28.5 us -> 37.7 us  [along(): lax.ppermute(value, 'dp', [(2 * a + y, 2 * b + y) for a, b in pairs for y...]
    ppermute x44, starting transfers between devices: 58.6 us -> 49.5 us  [swap(): return lax.ppermute(value, axis, [(i, i ^ bit) for i in range(size)])]
    pallas_call x7 -> x8, Pallas kernels: 58.8 us -> 61.5 us  [call(): pl.pallas_call(kernel, grid=(images,), in_specs=specs, out_specs=[kind(o)...]
    unnamed x56 -> x75, local copies, waits for them, and re-layouts: 7.74 us -> 10.4 us
  transfers between devices with their start and end apart: 51 -> 51, of which waited for: 27 -> 27; matrix products, arithmetic and copies ran while one was open for 7% -> 7% of each run, Pallas kernels for 21% -> 24%
where the time goes in v4:
time: 325 us; the launch traced here: 323 us
  waiting for transfers between devices  116 us (36%)
  Pallas kernels  90.1 us (28%)
  starting transfers between devices  58.8 us (18%)
  local copies, waits for them, and re-layouts  26.5 us (8%)
  between operations  14.7 us (5%)
  other arithmetic  13.7 us (4%)
  matrix products  3.3 us (1%)
    ppermute x44, waiting for transfers between devices, swap(): return lax.ppermute(value, axis, [(i, i ^ bit) for i in range(size)])  77.9 us
    pallas_call x8, Pallas kernels, call(): pl.pallas_call(kernel, grid=(images,), in_specs=specs, out_specs=[kind(o)...  61.5 us
    ppermute x44, starting transfers between devices, swap(): return lax.ppermute(value, axis, [(i, i ^ bit) for i in range(size)])  49.5 us
    ppermute x5, waiting for transfers between devices, along(): lax.ppermute(value, 'dp', [(2 * a + y, 2 * b + y) for a, b in pairs for y...  37.7 us
    pallas_call x9, Pallas kernels, add_blocks(): pl.pallas_call(kernel, in_specs=[pl.BlockSpec(memory_space=pltpu.VMEM)] *...  18 us
    unnamed x75, local copies, waits for them, and re-layouts  10.4 us
    ppermute x5, starting transfers between devices, along(): lax.ppermute(value, 'dp', [(2 * a + y, 2 * b + y) for a, b in pairs for y...  9.14 us
  transfers between devices with their start and end apart: 51, of which 27 were waited for; matrix products, arithmetic and copies ran while one was open for 7% of the time, Pallas kernels for 24%

profile of v4, /device:TPU:0, one launch (start us, length us, event | category | flops | bytes accessed | tf_op | source)
XLA Modules:
  0.0 323.4 jit_solution(10842931584986648144)
XLA Ops:
  8.4 1.9 concatenate.49
  10.9 17.9 %conditional.4 = (bf16[16,144]{1,0:T(8,128)(2,1)}, f32[2]{0:T(128)S(1)}, bf16[144,2304]{1,0:T(8,128)(2,1)S(1)}) conditional(s32[]{:T(128)} %bitcast.28, () %tuple.44, (s32[2]{0:T(128)S(1)}, s32[2]{0:T(128)S(1)}, bf16[2,1152]{1,0:T(2,128)(2,1)S(1)}, s32[]{:T(128)}, f32[2]{0:T(128)}, /*index=5*/bf16[144,2,768]{2,1,0:T(2,128)(2,1)S(1)}, ...), branch_computations={%region_0.1_spmd, %region_1.5_spmd} | conditional | flops 101409 | bytes 1573591 | solution.py:39
  11.3 3.0 collective-permute-start.15
  14.3 1.6 collective-permute-done.15
  16.0 3.1 collective-permute-start.16
  19.1 1.7 collective-permute-done.16
  20.8 1.9 collective-permute-start.17
  29.9 3.0 collective-permute-start.26
  33.1 5.3 %collective-permute-done.26 = f32[8,1728]{1,0:T(8,128)S(1)} collective-permute-done((f32[8,1728]{1,0:T(8,128)S(1)}, f32[8,1728]{1,0:T(8,128)S(1)}, u32[]{:S(2)}, u32[]{:S(2)}) %collective-permute-start.26) | collective-permute-done | bytes 55328 | tf_op jit(solution)/shard_map/ppermute | solution.py:30
  39.8 4.6 %collective-permute-start.32 = (bf16[144,2304]{1,0:T(8,128)(2,1)S(1)}, bf16[144,2304]{1,0:T(8,128)(2,1)S(1)}, u32[]{:S(2)}, u32[]{:S(2)}) collective-permute-start(bf16[144,2304]{1,0:T(8,128)(2,1)S(1)} %get-tuple-element.195.refs_1_), channel_id=1, source_target_pairs={{0,8},{4,12},{8,16},{12,20},{16,24},{20,28},{1,9},{5,13},{9,17},{1... | collective-permute-start | bytes 1990664 | tf_op jit(solution)/shard_map/ppermute | solution.py:137
  44.4 1.6 collective-permute-start.29
  46.6 19.1 %collective-permute-done.33.right_ref = bf16[144,2304]{1,0:T(8,128)(2,1)S(1)} collective-permute-done((bf16[144,2304]{1,0:T(8,128)(2,1)S(1)}, bf16[144,2304]{1,0:T(8,128)(2,1)S(1)}, u32[]{:S(2)}, u32[]{:S(2)}) %collective-permute-start.33) | collective-permute-done | bytes 663584 | tf_op jit(solution)/shard_map/ppermute | solution.py:137
  65.7 2.6 collective-permute-done.32.left_ref._
  69.2 2.2 shard_map.224.refs_2_
  71.4 1.5 collective-permute-start.34
  78.5 1.5 collective-permute-start.30
  80.0 14.7 %collective-permute-done.36.right_ref = bf16[144,2304]{1,0:T(8,128)(2,1)S(1)} collective-permute-done((bf16[144,2304]{1,0:T(8,128)(2,1)}, bf16[144,2304]{1,0:T(8,128)(2,1)S(1)}, u32[]{:S(2)}, u32[]{:S(2)}) %collective-permute-start.36) | collective-permute-done | bytes 663584 | tf_op jit(solution)/shard_map/ppermute | solution.py:137
  94.7 1.4 collective-permute-start.23
  97.2 2.2 shard_map.225.refs_11_.refs_3_
  104.5 11.0 %shard_map.226 = (bf16[2,1152,256]{2,1,0:T(8,128)(2,1)}, bf16[2,1152,256]{2,1,0:T(8,128)(2,1)}, f32[2,864,256]{2,1,0:T(8,128)}, f32[2,4,256]{2,1,0:T(4,128)}, bf...) custom-call(s32[13]{0:T(128)S(1)} %stack.128.refs_0_, ...), custom_call_target="tpu_custom_call" | custom-call | flops 1 | bytes 1 | tf_op jit(solution)/shard_map/pallas_call | solution.py:611
  118.9 1.9 collective-permute-done.38.refs_2_.refs_7_
  121.9 2.2 shard_map.227.refs_0_
  126.1 8.6 %collective-permute-done.41.refs_2_.refs_8_ = bf16[144,2304]{1,0:T(8,128)(2,1)S(1)} collective-permute-done((bf16[144,2304]{1,0:T(8,128)(2,1)S(1)}, bf16[144,2304]{1,0:T(8,128)(2,1)S(1)}, u32[]{:S(2)}, u32[]{:S(2)}) %collective-permute-start.41) | collective-permute-done | bytes 663584 | tf_op jit(solution)/shard_map/ppermute | solution.py:30
  134.7 5.9 %collective-permute-done.39.refs_1_ = bf16[2,576,256]{2,1,0:T(8,128)(2,1)S(1)} collective-permute-done((bf16[2,576,256]{2,1,0:T(8,128)(2,1)}, bf16[2,576,256]{2,1,0:T(8,128)(2,1)S(1)}, u32[]{:S(2)}, u32[]{:S(2)}) %collective-permute-start.39) | collective-permute-done | bytes 589856 | tf_op jit(solution)/shard_map/ppermute | solution.py:30
  143.4 1.9 collective-permute-done.43
  146.0 2.6 shard_map.229
  148.6 2.3 copy-done
  151.0 21.9 %conditional.5 = (f32[2,1152,256]{2,1,0:T(8,128)S(1)}, f32[2,288,256]{2,1,0:T(8,128)}, bf16[2,1152,256]{2,1,0:T(8,128)(2,1)}, bf16[2,768,256]{2,1,0:T(8,128)(2,1...) conditional(s32[]{:T(128)} %bitcast.28, () %tuple.43, ...), branch_computations={%region_5.6_spmd, %region_6.7_spmd} | conditional | flops 2 | bytes 11403338 | solution.py:39
  152.0 12.6 %branch_1_fun.16 = (f32[2,1152,256]{2,1,0:T(8,128)S(1)}, f32[2,288,256]{2,1,0:T(8,128)}, bf16[2,1152,256]{2,1,0:T(8,128)(2,1)}, bf16[2,768,256]{2,1,0:T(8,128)(2...) custom-call(s32[13]{0:T(128)S(1)} %get-tuple-element.89.refs_0_, ...), custom_call_target="tpu_custom_call" | custom-call | flops 1 | bytes 1 | tf_op jit(solution)/shard_map/cond/branch_1_fun/pallas_call | solution.py:611
  165.2 7.6 %branch_1_fun.17 = bf16[1152,2304]{1,0:T(8,128)(2,1)} custom-call(bf16[2,1152,256]{2,1,0:T(8,128)(2,1)} %get-tuple-element.106.refs_0_, bf16[2,768,256]{2,1,0:T(8,128)(2,1)} %get-tuple-element.400.refs_1_, bf16[2,1152,256]{2,1,0:T(8,128)(2,1)} %get-tuple-element.107.refs_2_, bf16[2,1536,256]{2,1,0:T(8,128)(2,1)} %get-tuple-element.108.refs_3_), custom_call_target="tpu_custom_call" | custom-call | flops 1 | bytes 1 | tf_op jit(solution)/shard_map/cond/branch_1_fun/pallas_call | solution.py:611
  173.7 108.8 %conditional.6 = (bf16[2,288,256]{2,1,0:T(8,128)(2,1)S(1)}, bf16[2,288,256]{2,1,0:T(8,128)(2,1)S(1)}, bf16[16,2016]{1,0:T(8,128)(2,1)S(1)}, bf16[144,1152]{1,0:T...) conditional(s32[]{:T(128)} %bitcast.28, () %tuple.42, ...), branch_computations={%region_7.8_spmd, %region_8.11_spmd} | conditional | flops 2228348 | bytes 74185400 | solution.py:39
  173.7 2.0 branch_1_fun.18.refs_0_
  177.2 3.9 %branch_1_fun.19.refs_2_ = bf16[2,1152,256]{2,1,0:T(8,128)(2,1)} custom-call(bf16[2,768,256]{2,1,0:T(8,128)(2,1)} %get-tuple-element.114.refs_0_, bf16[1152,2304]{1,0:T(8,128)(2,1)} %get-tuple-element.115.refs_1_), custom_call_target="tpu_custom_call" | custom-call | flops 1 | bytes 1 | tf_op jit(solution)/shard_map/cond/branch_1_fun/pallas_call | solution.py:611
  181.0 10.2 %collective-permute-done.1.refs_1_ = bf16[2,576,256]{2,1,0:T(8,128)(2,1)S(1)} collective-permute-done((bf16[2,576,256]{2,1,0:T(8,128)(2,1)}, bf16[2,576,256]{2,1,0:T(8,128)(2,1)S(1)}, u32[]{:S(2)}, u32[]{:S(2)}) %collective-permute-start.1) | collective-permute-done | bytes 589856 | tf_op jit(solution)/shard_map/cond/branch_1_fun/ppermute | solution.py:30
  192.0 2.3 branch_1_fun.20.refs_2_
  195.1 1.5 fusion.32
  197.0 12.7 %branch_1_fun.21 = (f32[2,1152,256]{2,1,0:T(8,128)}, bf16[2,1152,256]{2,1,0:T(8,128)(2,1)}, bf16[2,896,256]{2,1,0:T(8,128)(2,1)}, bf16[2,576,256]{2,1,0:T(8,128)...) custom-call(s32[13]{0:T(128)S(1)} %get-tuple-element.109.refs_0_, ...), custom_call_target="tpu_custom_call" | custom-call | flops 1 | bytes 1 | tf_op jit(solution)/shard_map/cond/branch_1_fun/pallas_call | solution.py:611
  212.3 2.3 branch_1_fun.22.refs_0_
  214.5 1.4 collective-permute-start.4
  217.3 5.1 %branch_1_fun.23 = (bf16[144,1152]{1,0:T(8,128)(2,1)S(1)}, bf16[144,1152]{1,0:T(8,128)(2,1)}, bf16[144,1152]{1,0:T(8,128)(2,1)}, bf16[144,1152]{1,0:T(8,128)(2,1...) custom-call(s32[13]{0:T(128)S(1)} %get-tuple-element.109.refs_0_, ...), custom_call_target="tpu_custom_call" | custom-call | flops 1 | bytes 1 | tf_op jit(solution)/shard_map/cond/branch_1_fun/pallas_call | solution.py:611
  224.0 13.0 %collective-permute-done.5.refs_10_.refs_1_ = bf16[144,1152]{1,0:T(8,128)(2,1)S(1)} collective-permute-done((bf16[144,1152]{1,0:T(8,128)(2,1)}, bf16[144,1152]{1,0:T(8,128)(2,1)S(1)}, u32[]{:S(2)}, u32[]{:S(2)}) %collective-permute-start.5) | collective-permute-done | bytes 331808 | tf_op jit(solution)/shard_map/cond/branch_1_fun/ppermute | solution.py:30
  238.0 2.2 branch_1_fun.24.refs_3_
  241.8 1.5 collective-permute-start.10
  244.2 1.9 branch_1_fun.25.refs_12_
  246.1 1.8 collective-permute-start.11
  248.9 5.9 %branch_1_fun.26 = (bf16[2,288,256]{2,1,0:T(8,128)(2,1)}, bf16[2,288,256]{2,1,0:T(8,128)(2,1)}, f32[2,8,288]{2,1,0:T(8,128)}) custom-call(s32[13]{0:T(128)S(1)} %get-tuple-element.109.refs_0_, f32[2]{0:T(128)S(1)} %get-tuple-element.110.refs_1_, f32[2]{0:T(128)} %get-tuple-element.111.refs_2_, bf16[2,576,256]{2,1,0:T(8,128)(2,1)} %branch_1_fun.24.refs_3_, ...), custom_call_target="tpu_custom_call" | custom-call | flops 1 | bytes 1 | tf_op jit(solution)/shard_map/cond/branch_1_fun/pallas_call | solution.py:611
  254.8 3.9 %collective-permute-done.10.refs_1_ = bf16[144,1152]{1,0:T(8,128)(2,1)S(1)} collective-permute-done((bf16[144,1152]{1,0:T(8,128)(2,1)S(1)}, bf16[144,1152]{1,0:T(8,128)(2,1)S(1)}, u32[]{:S(2)}, u32[]{:S(2)}) %collective-permute-start.10) | collective-permute-done | bytes 331808 | tf_op jit(solution)/shard_map/cond/branch_1_fun/ppermute | solution.py:30
  259.4 1.9 branch_1_fun.28.refs_2_
  262.1 1.9 branch_1_fun.27.refs_1_
  267.2 2.9 collective-permute-done.12
  270.8 3.7 %collective-permute-start.13 = (bf16[2,2,2016]{2,1,0:T(2,128)(2,1)S(1)}, bf16[2,2,2016]{2,1,0:T(2,128)(2,1)S(1)}, u32[]{:S(2)}, u32[]{:S(2)}) collective-permute-start(bf16[2,2,2016]{2,1,0:T(2,128)(2,1)S(1)} %pad_maximum_fusion.1), channel_id=1, source_target_pairs={{0,16},{4,20},{8,24},{12,28},{16,0},{20,4},{24,8},{28,12},{1,17},{... | collective-permute-start | bytes 48392 | tf_op jit(solution)/shard_map/cond/branch_1_fun/ppermute | solution.py:30
  274.5 2.6 collective-permute-done.13
  277.2 3.0 collective-permute-start.14
  280.1 1.9 collective-permute-done.14
  282.6 2.1 collective-permute-start.46
  285.9 3.6 %collective-permute-start.48 = (bf16[144,1152]{1,0:T(8,128)(2,1)}, bf16[144,1152]{1,0:T(8,128)(2,1)S(1)}, u32[]{:S(2)}, u32[]{:S(2)}) collective-permute-start(bf16[144,1152]{1,0:T(8,128)(2,1)} %get-tuple-element.218), channel_id=1, source_target_pairs={{0,16},{4,20},{8,24},{12,28},{16,0},{20,4},{24,8},{28,12},{1,17},{... | collective-permute-start | bytes 995336 | tf_op jit(solution)/shard_map/ppermute | solution.py:30
  289.5 19.2 %conditional.7 = (f32[6,144,288]{2,1,0:T(8,128)S(1)}, f32[6,288]{1,0:T(8,128)S(1)}, bf16[144]{0:T(256)(128)(2,1)S(1)}, f32[2,1152]{1,0:T(2,128)S(1)}, f32[72]{0:T(128)S(1)}, /*index=5*/f32[72]{0:T(128)S(1)}) conditional(s32[]{:T(128)} %bitcast.28, () %tuple.48, (bf16[16,2016]{1,0:T(8,128)(2,1)S(1)}, bf16[16,144]{1,0:T(8,128)(2,1)}, ...), branch_computations={%region_11.12_spmd, %region_12.15_spmd} | conditional | flops 16018473 | bytes 2418740 | solution.py:39
  291.3 1.6 collective-permute-start.18
  292.8 2.2 collective-permute-done.18
  298.0 2.1 collective-permute-done.20
  300.4 3.5 %collective-permute-done.21 = f32[4,288]{1,0:T(4,128)S(1)} collective-permute-done((f32[4,288]{1,0:T(4,128)S(1)}, f32[4,288]{1,0:T(4,128)S(1)}, u32[]{:S(2)}, u32[]{:S(2)}) %collective-permute-start.21) | collective-permute-done | bytes 4640 | tf_op jit(solution)/shard_map/cond/branch_1_fun/ppermute | solution.py:30
  304.9 3.8 %collective-permute-done.22 = f32[2,576]{1,0:T(2,128)S(1)} collective-permute-done((f32[2,576]{1,0:T(2,128)S(1)}, f32[2,576]{1,0:T(2,128)S(1)}, u32[]{:S(2)}, u32[]{:S(2)}) %collective-permute-start.22) | collective-permute-done | bytes 4640 | tf_op jit(solution)/shard_map/cond/branch_1_fun/ppermute | solution.py:30
  310.4 2.4 shard_map.230
  314.9 1.6 copy.82
  (295 shorter events, 66.0 us)
Async XLA Ops:
  7.2 97.3 %all-gather.2.cloned.1.call-start = ((), (), s32[]{:S(2)}) async-start(), calls=%async_computation.1 | async-start | bytes 2985984 | tf_op jit(solution)/shard_map/all_gather | solution.py:658
  10.3 302.5 %reduce-scatter.2.cloned.1.call-start = ((), (), s32[]{:S(2)}) async-start(), calls=%async_computation.2 | async-start | bytes 5971968 | tf_op jit(solution)/shard_map/reduce_scatter | solution.py:801
  10.9 18.0 %copy-start.10 = (bf16[144,6,288]{2,0,1:T(8,128)(2,1)S(1)}, bf16[144,6,288]{2,0,1:T(8,128)(2,1)}, u32[]{:S(2)}) copy-start(bf16[144,6,288]{2,0,1:T(8,128)(2,1)} %param.26) | copy-start | bytes 1492996
  11.3 4.6 %collective-permute-start.15 = (bf16[2,1280]{1,0:T(2,128)(2,1)S(1)}, bf16[2,1280]{1,0:T(2,128)(2,1)S(1)}, u32[]{:S(2)}, u32[]{:S(2)}) collective-permute-start(bf16[2,1280]{1,0:T(2,128)(2,1)S(1)} %concatenate.33), channel_id=1, source_target_pairs={{0,8},{4,12},{8,0},{12,4},{16,24},{20,28},{24,16},{28,20},{1,9},{5... | collective-permute-start | bytes 15368 | tf_op jit(solution)/shard_map/cond/branch_1_fun/ppermute | solution.py:30
  16.0 4.8 %collective-permute-start.16 = (bf16[2,2,1280]{2,1,0:T(2,128)(2,1)S(1)}, bf16[2,2,1280]{2,1,0:T(2,128)(2,1)S(1)}, u32[]{:S(2)}, u32[]{:S(2)}) collective-permute-start(bf16[2,2,1280]{2,1,0:T(2,128)(2,1)S(1)} %pad_maximum_fusion.9), channel_id=1, source_target_pairs={{0,16},{4,20},{8,24},{12,28},{16,0},{20,4},{24,8},{28,12},{1,17},{... | collective-permute-start | bytes 30728 | tf_op jit(solution)/shard_map/cond/branch_1_fun/ppermute | solution.py:30
  20.8 3.9 %collective-permute-start.17 = (bf16[2,2,2,1280]{3,2,1,0:T(2,128)(2,1)S(1)}, bf16[2,2,2,1280]{3,2,1,0:T(2,128)(2,1)S(1)}, u32[]{:S(2)}, u32[]{:S(2)}) collective-permute-start(bf16[2,2,2,1280]{3,2,1,0:T(2,128)(2,1)S(1)} %pad_maximum_fusion.8), channel_id=1, source_target_pairs={{0,4},{4,0},{8,12},{12,8},{16,20},{20,16},{24,28},{28,24},{1,5},{5... | collective-permute-start | bytes 61448 | tf_op jit(solution)/shard_map/cond/branch_1_fun/ppermute | solution.py:30
  29.9 8.4 %collective-permute-start.26 = (f32[8,1728]{1,0:T(8,128)S(1)}, f32[8,1728]{1,0:T(8,128)S(1)}, u32[]{:S(2)}, u32[]{:S(2)}) collective-permute-start(f32[8,1728]{1,0:T(8,128)S(1)} %select_n.462), channel_id=1, source_target_pairs={{0,16},{4,20},{8,24},{12,28},{16,0},{20,4},{24,8},{28,12},{1,17},{... | collective-permute-start | bytes 165896 | tf_op jit(solution)/shard_map/ppermute | solution.py:30
  38.4 7.6 %collective-permute-start.27 = (f32[4,1728]{1,0:T(4,128)S(1)}, f32[4,1728]{1,0:T(4,128)S(1)}, u32[]{:S(2)}, u32[]{:S(2)}) collective-permute-start(f32[4,1728]{1,0:T(4,128)S(1)} %slice_select_fusion.2), channel_id=1, source_target_pairs={{0,8},{4,12},{8,0},{12,4},{16,24},{20,28},{24,16},{28,20},{1,9},{5... | collective-permute-start | bytes 82952 | tf_op jit(solution)/shard_map/ppermute | solution.py:30
  38.5 27.2 %collective-permute-start.33 = (bf16[144,2304]{1,0:T(8,128)(2,1)S(1)}, bf16[144,2304]{1,0:T(8,128)(2,1)S(1)}, u32[]{:S(2)}, u32[]{:S(2)}) collective-permute-start(bf16[144,2304]{1,0:T(8,128)(2,1)S(1)} %get-tuple-element.195.refs_1_), channel_id=1, source_target_pairs={{8,0},{12,4},{16,8},{20,12},{24,16},{28,20},{9,1},{13,5},{17,9},{2... | collective-permute-start | bytes 1990664 | tf_op jit(solution)/shard_map/ppermute | solution.py:137
  39.8 28.5 %collective-permute-start.32 = (bf16[144,2304]{1,0:T(8,128)(2,1)S(1)}, bf16[144,2304]{1,0:T(8,128)(2,1)S(1)}, u32[]{:S(2)}, u32[]{:S(2)}) collective-permute-start(bf16[144,2304]{1,0:T(8,128)(2,1)S(1)} %get-tuple-element.195.refs_1_), channel_id=1, source_target_pairs={{0,8},{4,12},{8,16},{12,20},{16,24},{20,28},{1,9},{5,13},{9,17},{1... | collective-permute-start | bytes 1990664 | tf_op jit(solution)/shard_map/ppermute | solution.py:137
  44.4 31.1 %collective-permute-start.29 = (bf16[144,2304]{1,0:T(8,128)(2,1)S(1)}, bf16[144,2304]{1,0:T(8,128)(2,1)S(1)}, u32[]{:S(2)}, u32[]{:S(2)}) collective-permute-start(bf16[144,2304]{1,0:T(8,128)(2,1)S(1)} %get-tuple-element.195.refs_1_), channel_id=1, source_target_pairs={{0,4},{4,0},{8,12},{12,8},{16,20},{20,16},{24,28},{28,24},{1,5},{5... | collective-permute-start | bytes 1990664 | tf_op jit(solution)/shard_map/ppermute | solution.py:30
  46.0 28.9 %collective-permute-start.28 = (f32[2,1728]{1,0:T(2,128)S(1)}, f32[2,1728]{1,0:T(2,128)S(1)}, u32[]{:S(2)}, u32[]{:S(2)}) collective-permute-start(f32[2,1728]{1,0:T(2,128)S(1)} %broadcast_select_fusion.21), channel_id=1, source_target_pairs={{0,4},{4,0},{8,12},{12,8},{16,20},{20,16},{24,28},{28,24},{1,5},{5... | collective-permute-start | bytes 41480 | tf_op jit(solution)/shard_map/ppermute | solution.py:30
  69.2 9.3 %copy-start.51 = (f32[6,288]{1,0:T(8,128)S(1)}, f32[6,288]{1,0:T(8,128)}, u32[]{:S(2)}) copy-start(f32[6,288]{1,0:T(8,128)} %param.27) | copy-start | bytes 20740
  71.4 24.8 %collective-permute-start.34 = (bf16[144,2304]{1,0:T(8,128)(2,1)}, bf16[144,2304]{1,0:T(8,128)(2,1)S(1)}, u32[]{:S(2)}, u32[]{:S(2)}) collective-permute-start(bf16[144,2304]{1,0:T(8,128)(2,1)} %shard_map.224.refs_2_), channel_id=1, source_target_pairs={{0,4},{4,0},{8,12},{12,8},{16,20},{20,16},{24,28},{28,24},{1,5},{5... | collective-permute-start | bytes 1990664 | tf_op jit(solution)/shard_map/ppermute | solution.py:30
  72.9 21.8 %collective-permute-start.36 = (bf16[144,2304]{1,0:T(8,128)(2,1)}, bf16[144,2304]{1,0:T(8,128)(2,1)S(1)}, u32[]{:S(2)}, u32[]{:S(2)}) collective-permute-start(bf16[144,2304]{1,0:T(8,128)(2,1)} %copy-done.11), channel_id=1, source_target_pairs={{8,0},{12,4},{16,8},{20,12},{9,1},{13,5},{17,9},{21,13},{10,2},{14... | collective-permute-start | bytes 1990664 | tf_op jit(solution)/shard_map/ppermute | solution.py:137
  74.2 22.0 %collective-permute-start.35 = (bf16[144,2304]{1,0:T(8,128)(2,1)}, bf16[144,2304]{1,0:T(8,128)(2,1)S(1)}, u32[]{:S(2)}, u32[]{:S(2)}) collective-permute-start(bf16[144,2304]{1,0:T(8,128)(2,1)} %copy-done.1), channel_id=1, source_target_pairs={{8,16},{12,20},{16,24},{20,28},{9,17},{13,21},{17,25},{21,29},{10,... | collective-permute-start | bytes 1990664 | tf_op jit(solution)/shard_map/ppermute | solution.py:137
  78.5 22.3 %collective-permute-start.30 = (f32[2,8,288]{2,1,0:T(8,128)S(1)}, f32[2,8,288]{2,1,0:T(8,128)S(1)}, u32[]{:S(2)}, u32[]{:S(2)}) collective-permute-start(f32[2,8,288]{2,1,0:T(8,128)S(1)} %pad.5), channel_id=1, source_target_pairs={{0,2},{1,3},{2,0},{3,1},{4,6},{5,7},{6,4},{7,5},{8,10},{9,11},{10,... | collective-permute-start | bytes 55304 | tf_op jit(solution)/shard_map/ppermute | solution.py:30
  80.0 24.0 %collective-permute-start.24 = (bf16[2,288,256]{2,1,0:T(8,128)(2,1)}, bf16[2,288,256]{2,1,0:T(8,128)(2,1)}, u32[]{:S(2)}, u32[]{:S(2)}) collective-permute-start(bf16[2,288,256]{2,1,0:T(8,128)(2,1)} %bitcast.129), channel_id=1, source_target_pairs={{0,1},{1,0},{2,3},{3,2},{4,5},{5,4},{6,7},{7,6},{8,9},{9,8},{10,11... | collective-permute-start | bytes 884744 | tf_op jit(solution)/shard_map/ppermute | solution.py:30
  94.7 7.9 %collective-permute-start.23 = (bf16[2,288,256]{2,1,0:T(8,128)(2,1)}, bf16[2,288,256]{2,1,0:T(8,128)(2,1)}, u32[]{:S(2)}, u32[]{:S(2)}) collective-permute-start(bf16[2,288,256]{2,1,0:T(8,128)(2,1)} %bitcast.130), channel_id=1, source_target_pairs={{0,2},{1,3},{2,0},{3,1},{4,6},{5,7},{6,4},{7,5},{8,10},{9,11},{10,... | collective-permute-start | bytes 884744 | tf_op jit(solution)/shard_map/ppermute | solution.py:30
  99.5 17.6 %collective-permute-start.40 = (bf16[144,2304]{1,0:T(8,128)(2,1)}, bf16[144,2304]{1,0:T(8,128)(2,1)}, u32[]{:S(2)}, u32[]{:S(2)}) collective-permute-start(bf16[144,2304]{1,0:T(8,128)(2,1)} %shard_map.225.refs_11_.refs_3_), channel_id=1, source_target_pairs={{8,0},{12,4},{16,24},{20,28},{9,1},{13,5},{17,25},{21,29},{10,2},{... | collective-permute-start | bytes 1990664 | tf_op jit(solution)/shard_map/ppermute | solution.py:137
  100.8 1.8 collective-permute-start.31
  102.6 1.9 collective-permute-start.25
  102.9 12.7 %copy-start.17 = (f32[2,8,1152]{2,1,0:T(8,128)}, f32[2,8,1152]{2,1,0:T(8,128)S(1)}, u32[]{:S(2)}) copy-start(f32[2,8,1152]{2,1,0:T(8,128)S(1)} %reshape.145.refs_5_) | copy-start | bytes 221188
  102.9 14.2 %copy-start.2 = (bf16[144,2304]{1,0:T(8,128)(2,1)S(1)}, bf16[144,2304]{1,0:T(8,128)(2,1)}, u32[]{:S(2)}) copy-start(bf16[144,2304]{1,0:T(8,128)(2,1)} %copy-done.1) | copy-start | bytes 1990660
  102.9 14.2 %copy-start.12 = (bf16[144,2304]{1,0:T(8,128)(2,1)S(1)}, bf16[144,2304]{1,0:T(8,128)(2,1)}, u32[]{:S(2)}) copy-start(bf16[144,2304]{1,0:T(8,128)(2,1)} %copy-done.11) | copy-start | bytes 1990660
  102.9 18.0 %collective-permute-start.38 = (bf16[144,2304]{1,0:T(8,128)(2,1)}, bf16[144,2304]{1,0:T(8,128)(2,1)S(1)}, u32[]{:S(2)}, u32[]{:S(2)}) collective-permute-start(bf16[144,2304]{1,0:T(8,128)(2,1)} %shard_map.225.refs_11_.refs_3_), channel_id=1, source_target_pairs={{0,4},{4,0},{8,12},{12,8},{16,20},{20,16},{24,28},{28,24},{1,5},{5... | collective-permute-start | bytes 1990664 | tf_op jit(solution)/shard_map/ppermute | solution.py:30
  115.6 5.3 %collective-permute-start.37 = (bf16[2,576,256]{2,1,0:T(8,128)(2,1)}, bf16[2,576,256]{2,1,0:T(8,128)(2,1)S(1)}, u32[]{:S(2)}, u32[]{:S(2)}) collective-permute-start(bf16[2,576,256]{2,1,0:T(8,128)(2,1)} %get-tuple-element.198), channel_id=1, source_target_pairs={{0,1},{1,0},{2,3},{3,2},{4,5},{5,4},{6,7},{7,6},{8,9},{9,8},{10,11... | collective-permute-start | bytes 1769480 | tf_op jit(solution)/shard_map/ppermute | solution.py:30
  118.3 27.7 %copy-start.14 = (bf16[144,2304]{1,0:T(8,128)(2,1)}, bf16[144,2304]{1,0:T(8,128)(2,1)S(1)}, u32[]{:S(2)}) copy-start(bf16[144,2304]{1,0:T(8,128)(2,1)S(1)} %select_select_fusion.refs_4_) | copy-start | bytes 1990660
  118.3 16.4 %collective-permute-start.41 = (bf16[144,2304]{1,0:T(8,128)(2,1)S(1)}, bf16[144,2304]{1,0:T(8,128)(2,1)S(1)}, u32[]{:S(2)}, u32[]{:S(2)}) collective-permute-start(bf16[144,2304]{1,0:T(8,128)(2,1)S(1)} %select_select_fusion.refs_4_), channel_id=1, source_target_pairs={{0,4},{4,0},{8,12},{12,8},{16,20},{20,16},{24,28},{28,24},{1,5},{5... | collective-permute-start | bytes 1990664 | tf_op jit(solution)/shard_map/ppermute | solution.py:30
  124.1 16.5 %collective-permute-start.39 = (bf16[2,576,256]{2,1,0:T(8,128)(2,1)}, bf16[2,576,256]{2,1,0:T(8,128)(2,1)S(1)}, u32[]{:S(2)}, u32[]{:S(2)}) collective-permute-start(bf16[2,576,256]{2,1,0:T(8,128)(2,1)} %shard_map.227.refs_0_), channel_id=1, source_target_pairs={{0,2},{1,3},{2,0},{3,1},{4,6},{5,7},{6,4},{7,5},{8,10},{9,11},{10,... | collective-permute-start | bytes 1769480 | tf_op jit(solution)/shard_map/ppermute | solution.py:30
  125.5 19.8 %collective-permute-start.43 = (bf16[2,288,256]{2,1,0:T(8,128)(2,1)}, bf16[2,288,256]{2,1,0:T(8,128)(2,1)}, u32[]{:S(2)}, u32[]{:S(2)}) collective-permute-start(bf16[2,288,256]{2,1,0:T(8,128)(2,1)} %bitcast.59), channel_id=1, source_target_pairs={{0,2},{1,3},{2,0},{3,1},{4,6},{5,7},{6,4},{7,5},{8,10},{9,11},{10,... | collective-permute-start | bytes 884744 | tf_op jit(solution)/shard_map/ppermute | solution.py:30
  142.8 5.8 %collective-permute-start.42 = (bf16[2,576,256]{2,1,0:T(8,128)(2,1)S(1)}, bf16[2,576,256]{2,1,0:T(8,128)(2,1)S(1)}, u32[]{:S(2)}, u32[]{:S(2)}) collective-permute-start(bf16[2,576,256]{2,1,0:T(8,128)(2,1)S(1)} %shard_map.228), channel_id=1, source_target_pairs={{0,1},{1,0},{2,3},{3,2},{4,5},{5,4},{6,7},{7,6},{8,9},{9,8},{10,11... | collective-permute-start | bytes 1769480 | tf_op jit(solution)/shard_map/ppermute | solution.py:30
  142.9 5.7 %collective-permute-start.44 = (bf16[2,288,256]{2,1,0:T(8,128)(2,1)}, bf16[2,288,256]{2,1,0:T(8,128)(2,1)}, u32[]{:S(2)}, u32[]{:S(2)}) collective-permute-start(bf16[2,288,256]{2,1,0:T(8,128)(2,1)} %bitcast.59), channel_id=1, source_target_pairs={{0,1},{1,0},{2,3},{3,2},{4,5},{5,4},{6,7},{7,6},{8,9},{9,8},{10,11... | collective-permute-start | bytes 884744 | tf_op jit(solution)/shard_map/ppermute | solution.py:30
  145.3 3.3 %collective-permute-start.45 = (bf16[2,288,256]{2,1,0:T(8,128)(2,1)}, bf16[2,288,256]{2,1,0:T(8,128)(2,1)}, u32[]{:S(2)}, u32[]{:S(2)}) collective-permute-start(bf16[2,288,256]{2,1,0:T(8,128)(2,1)} %collective-permute-done.43), channel_id=1, source_target_pairs={{0,1},{1,0},{2,3},{3,2},{4,5},{5,4},{6,7},{7,6},{8,9},{9,8},{10,11... | collective-permute-start | bytes 884744 | tf_op jit(solution)/shard_map/ppermute | solution.py:30
  164.6 8.2 %collective-permute-start = (bf16[2,576,256]{2,1,0:T(8,128)(2,1)}, bf16[2,576,256]{2,1,0:T(8,128)(2,1)}, u32[]{:S(2)}, u32[]{:S(2)}) collective-permute-start(bf16[2,576,256]{2,1,0:T(8,128)(2,1)} %get-tuple-element.105), channel_id=1, source_target_pairs={{0,1},{1,0},{2,3},{3,2},{4,5},{5,4},{6,7},{7,6},{8,9},{9,8},{10,11... | collective-permute-start | bytes 1769480 | tf_op jit(solution)/shard_map/cond/branch_1_fun/ppermute | solution.py:30
  175.8 15.5 %collective-permute-start.1 = (bf16[2,576,256]{2,1,0:T(8,128)(2,1)}, bf16[2,576,256]{2,1,0:T(8,128)(2,1)S(1)}, u32[]{:S(2)}, u32[]{:S(2)}) collective-permute-start(bf16[2,576,256]{2,1,0:T(8,128)(2,1)} %branch_1_fun.18.refs_0_), channel_id=1, source_target_pairs={{0,2},{1,3},{2,0},{3,1},{4,6},{5,7},{6,4},{7,5},{8,10},{9,11},{10,... | collective-permute-start | bytes 1769480 | tf_op jit(solution)/shard_map/cond/branch_1_fun/ppermute | solution.py:30
  181.0 13.3 %copy-start.53 = (f32[72,2]{0,1:T(2,128)S(1)}, f32[72,2]{0,1:T(2,128)}, u32[]{:S(2)}) copy-start(f32[72,2]{0,1:T(2,128)} %get-tuple-element.321) | copy-start | bytes 1732 | tf_op jit(solution)/shard_map/cond
  194.3 2.3 collective-permute-start.2
  196.5 13.8 %copy-start.5 = (bf16[2,2,1,288,256]{4,3,2,1,0:T(8,128)(2,1)}, bf16[2,2,1,288,256]{4,3,2,1,0:T(8,128)(2,1)S(1)}, u32[]{:S(2)}) copy-start(bf16[2,2,1,288,256]{4,3,2,1,0:T(8,128)(2,1)S(1)} %get-tuple-element.343) | copy-start | bytes 1769476 | tf_op jit(solution)/shard_map/cond
  209.7 2.6 collective-permute-start.3
  211.2 4.8 %collective-permute-start.7 = (bf16[2,2,288,256]{3,2,0,1:T(8,128)(2,1)}, bf16[2,2,288,256]{3,2,0,1:T(8,128)(2,1)}, u32[]{:S(2)}, u32[]{:S(2)}) collective-permute-start(bf16[2,2,288,256]{3,2,0,1:T(8,128)(2,1)} %select_bitcast_fusion), channel_id=1, source_target_pairs={{0,1},{1,0},{2,3},{3,2},{4,5},{5,4},{6,7},{7,6},{8,9},{9,8},{10,11... | collective-permute-start | bytes 1769480 | tf_op jit(solution)/shard_map/cond/branch_1_fun/ppermute | solution.py:30
  214.5 22.5 %collective-permute-start.4 = (bf16[2,576,256]{2,1,0:T(8,128)(2,1)}, bf16[2,576,256]{2,1,0:T(8,128)(2,1)S(1)}, u32[]{:S(2)}, u32[]{:S(2)}) collective-permute-start(bf16[2,576,256]{2,1,0:T(8,128)(2,1)} %branch_1_fun.22.refs_0_), channel_id=1, source_target_pairs={{0,2},{1,3},{2,0},{3,1},{4,6},{5,7},{6,4},{7,5},{8,10},{9,11},{10,... | collective-permute-start | bytes 1769480 | tf_op jit(solution)/shard_map/cond/branch_1_fun/ppermute | solution.py:30
  222.4 17.9 %copy-start.8 = (bf16[144,1152]{1,0:T(8,128)(2,1)}, bf16[144,1152]{1,0:T(8,128)(2,1)S(1)}, u32[]{:S(2)}) copy-start(bf16[144,1152]{1,0:T(8,128)(2,1)S(1)} %get-tuple-element.415.refs_2_) | copy-start | bytes 995332 | tf_op jit(solution)/shard_map/cond
  222.4 14.7 %collective-permute-start.5 = (bf16[144,1152]{1,0:T(8,128)(2,1)}, bf16[144,1152]{1,0:T(8,128)(2,1)S(1)}, u32[]{:S(2)}, u32[]{:S(2)}) collective-permute-start(bf16[144,1152]{1,0:T(8,128)(2,1)} %get-tuple-element.138.refs_9_), channel_id=1, source_target_pairs={{0,4},{4,0},{8,12},{12,8},{16,20},{20,16},{24,28},{28,24},{1,5},{5... | collective-permute-start | bytes 995336 | tf_op jit(solution)/shard_map/cond/branch_1_fun/ppermute | solution.py:30
  223.0 17.4 %collective-permute-start.8 = (bf16[2,288,256]{2,1,0:T(8,128)(2,1)S(1)}, bf16[2,288,256]{2,1,0:T(8,128)(2,1)S(1)}, u32[]{:S(2)}, u32[]{:S(2)}) collective-permute-start(bf16[2,288,256]{2,1,0:T(8,128)(2,1)S(1)} %fusion), channel_id=1, source_target_pairs={{0,2},{1,3},{2,0},{3,1},{4,6},{5,7},{6,4},{7,5},{8,10},{9,11},{10,... | collective-permute-start | bytes 884744 | tf_op jit(solution)/shard_map/cond/branch_1_fun/ppermute | solution.py:30
  240.3 7.8 %collective-permute-start.6 = (bf16[2,576,256]{2,1,0:T(8,128)(2,1)}, bf16[2,576,256]{2,1,0:T(8,128)(2,1)S(1)}, u32[]{:S(2)}, u32[]{:S(2)}) collective-permute-start(bf16[2,576,256]{2,1,0:T(8,128)(2,1)} %branch_1_fun.24.refs_3_), channel_id=1, source_target_pairs={{0,1},{1,0},{2,3},{3,2},{4,5},{5,4},{6,7},{7,6},{8,9},{9,8},{10,11... | collective-permute-start | bytes 1769480 | tf_op jit(solution)/shard_map/cond/branch_1_fun/ppermute | solution.py:30
  241.3 20.0 %collective-permute-start.9 = (bf16[144,1152]{1,0:T(8,128)(2,1)S(1)}, bf16[144,1152]{1,0:T(8,128)(2,1)S(1)}, u32[]{:S(2)}, u32[]{:S(2)}) collective-permute-start(bf16[144,1152]{1,0:T(8,128)(2,1)S(1)} %copy-done.40), channel_id=1, source_target_pairs={{0,4},{4,0},{8,12},{12,8},{16,20},{20,16},{24,28},{28,24},{1,5},{5... | collective-permute-start | bytes 995336 | tf_op jit(solution)/shard_map/cond/branch_1_fun/ppermute | solution.py:30
  241.8 16.9 %collective-permute-start.10 = (bf16[144,1152]{1,0:T(8,128)(2,1)S(1)}, bf16[144,1152]{1,0:T(8,128)(2,1)S(1)}, u32[]{:S(2)}, u32[]{:S(2)}) collective-permute-start(bf16[144,1152]{1,0:T(8,128)(2,1)S(1)} %copy-done.41), channel_id=1, source_target_pairs={{0,4},{4,0},{8,12},{12,8},{16,20},{20,16},{24,28},{28,24},{1,5},{5... | collective-permute-start | bytes 995336 | tf_op jit(solution)/shard_map/cond/branch_1_fun/ppermute | solution.py:30
  246.1 18.6 %collective-permute-start.11 = (bf16[144,1152]{1,0:T(8,128)(2,1)}, bf16[144,1152]{1,0:T(8,128)(2,1)}, u32[]{:S(2)}, u32[]{:S(2)}) collective-permute-start(bf16[144,1152]{1,0:T(8,128)(2,1)} %branch_1_fun.25.refs_12_), channel_id=1, source_target_pairs={{0,24},{4,28},{8,16},{12,20},{16,8},{20,12},{24,0},{28,4},{1,25},{... | collective-permute-start | bytes 995336 | tf_op jit(solution)/shard_map/cond/branch_1_fun/ppermute | solution.py:30
  261.3 21.0 %copy-start.9 = (bf16[144,1152]{1,0:T(8,128)(2,1)S(1)}, bf16[144,1152]{1,0:T(8,128)(2,1)}, u32[]{:S(2)}) copy-start(bf16[144,1152]{1,0:T(8,128)(2,1)} %copy-done.8) | copy-start | bytes 995332 | tf_op jit(solution)/shard_map/cond
  261.3 21.0 %copy-start.42 = (bf16[2,288,256]{2,1,0:T(8,128)(2,1)S(1)}, bf16[2,288,256]{2,1,0:T(8,128)(2,1)}, u32[]{:S(2)}) copy-start(bf16[2,288,256]{2,1,0:T(8,128)(2,1)} %get-tuple-element.413) | copy-start | bytes 884740 | tf_op jit(solution)/shard_map/cond
  261.3 21.0 %copy-start.44 = (bf16[2,288,256]{2,1,0:T(8,128)(2,1)S(1)}, bf16[2,288,256]{2,1,0:T(8,128)(2,1)}, u32[]{:S(2)}) copy-start(bf16[2,288,256]{2,1,0:T(8,128)(2,1)} %get-tuple-element.412) | copy-start | bytes 884740 | tf_op jit(solution)/shard_map/cond
  266.0 4.0 %collective-permute-start.12 = (bf16[2,2016]{1,0:T(2,128)(2,1)}, bf16[2,2016]{1,0:T(2,128)(2,1)S(1)}, u32[]{:S(2)}, u32[]{:S(2)}) collective-permute-start(bf16[2,2016]{1,0:T(2,128)(2,1)} %branch_1_fun.29), channel_id=1, source_target_pairs={{0,8},{4,12},{8,0},{12,4},{16,24},{20,28},{24,16},{28,20},{1,9},{5... | collective-permute-start | bytes 24200 | tf_op jit(solution)/shard_map/cond/branch_1_fun/ppermute | solution.py:30
  270.8 6.3 %collective-permute-start.13 = (bf16[2,2,2016]{2,1,0:T(2,128)(2,1)S(1)}, bf16[2,2,2016]{2,1,0:T(2,128)(2,1)S(1)}, u32[]{:S(2)}, u32[]{:S(2)}) collective-permute-start(bf16[2,2,2016]{2,1,0:T(2,128)(2,1)S(1)} %pad_maximum_fusion.1), channel_id=1, source_target_pairs={{0,16},{4,20},{8,24},{12,28},{16,0},{20,4},{24,8},{28,12},{1,17},{... | collective-permute-start | bytes 48392 | tf_op jit(solution)/shard_map/cond/branch_1_fun/ppermute | solution.py:30
  277.2 4.9 %collective-permute-start.14 = (bf16[2,2,2,2016]{3,2,1,0:T(2,128)(2,1)S(1)}, bf16[2,2,2,2016]{3,2,1,0:T(2,128)(2,1)S(1)}, u32[]{:S(2)}, u32[]{:S(2)}) collective-permute-start(bf16[2,2,2,2016]{3,2,1,0:T(2,128)(2,1)S(1)} %pad_maximum_fusion), channel_id=1, source_target_pairs={{0,4},{4,0},{8,12},{12,8},{16,20},{20,16},{24,28},{28,24},{1,5},{5... | collective-permute-start | bytes 96776 | tf_op jit(solution)/shard_map/cond/branch_1_fun/ppermute | solution.py:30
  282.6 26.8 %collective-permute-start.46 = (bf16[144,1152]{1,0:T(8,128)(2,1)}, bf16[144,1152]{1,0:T(8,128)(2,1)S(1)}, u32[]{:S(2)}, u32[]{:S(2)}) collective-permute-start(bf16[144,1152]{1,0:T(8,128)(2,1)} %get-tuple-element.216), channel_id=1, source_target_pairs={{0,4},{4,0},{8,12},{12,8},{16,20},{20,16},{24,28},{28,24},{1,5},{5... | collective-permute-start | bytes 995336 | tf_op jit(solution)/shard_map/ppermute | solution.py:30
  284.7 24.7 %collective-permute-start.47 = (bf16[144,1152]{1,0:T(8,128)(2,1)}, bf16[144,1152]{1,0:T(8,128)(2,1)S(1)}, u32[]{:S(2)}, u32[]{:S(2)}) collective-permute-start(bf16[144,1152]{1,0:T(8,128)(2,1)} %get-tuple-element.217), channel_id=1, source_target_pairs={{0,8},{4,12},{8,0},{12,4},{16,24},{20,28},{24,16},{28,20},{1,9},{5... | collective-permute-start | bytes 995336 | tf_op jit(solution)/shard_map/ppermute | solution.py:30
  285.9 23.6 %collective-permute-start.48 = (bf16[144,1152]{1,0:T(8,128)(2,1)}, bf16[144,1152]{1,0:T(8,128)(2,1)S(1)}, u32[]{:S(2)}, u32[]{:S(2)}) collective-permute-start(bf16[144,1152]{1,0:T(8,128)(2,1)} %get-tuple-element.218), channel_id=1, source_target_pairs={{0,16},{4,20},{8,24},{12,28},{16,0},{20,4},{24,8},{28,12},{1,17},{... | collective-permute-start | bytes 995336 | tf_op jit(solution)/shard_map/ppermute | solution.py:30
  289.5 19.3 %copy-start.49 = (bf16[2,1152]{1,0:T(2,128)(2,1)S(1)}, bf16[2,1152]{1,0:T(2,128)(2,1)}, u32[]{:S(2)}) copy-start(bf16[2,1152]{1,0:T(2,128)(2,1)} %param.23) | copy-start | bytes 13828
  291.3 3.8 %collective-permute-start.18 = (f32[2448]{0:T(1024)S(1)}, f32[2448]{0:T(1024)S(1)}, u32[]{:S(2)}, u32[]{:S(2)}) collective-permute-start(f32[2448]{0:T(1024)S(1)} %pad_maximum_fusion.4), channel_id=1, source_target_pairs={{0,2},{1,3},{2,0},{3,1},{4,6},{5,7},{6,4},{7,5},{8,10},{9,11},{10,... | collective-permute-start | bytes 29384 | tf_op jit(solution)/shard_map/cond/branch_1_fun/ppermute | solution.py:30
  295.1 1.2 collective-permute-start.19
  296.4 3.7 %collective-permute-start.20 = (f32[8,144]{1,0:T(8,128)S(1)}, f32[8,144]{1,0:T(8,128)S(1)}, u32[]{:S(2)}, u32[]{:S(2)}) collective-permute-start(f32[8,144]{1,0:T(8,128)S(1)} %select_n.401), channel_id=1, source_target_pairs={{0,4},{4,0},{8,12},{12,8},{16,20},{20,16},{24,28},{28,24},{1,5},{5... | collective-permute-start | bytes 13832 | tf_op jit(solution)/shard_map/cond/branch_1_fun/ppermute | solution.py:30
  300.2 3.7 %collective-permute-start.21 = (f32[4,288]{1,0:T(4,128)S(1)}, f32[4,288]{1,0:T(4,128)S(1)}, u32[]{:S(2)}, u32[]{:S(2)}) collective-permute-start(f32[4,288]{1,0:T(4,128)S(1)} %select_n.407), channel_id=1, source_target_pairs={{0,8},{4,12},{8,0},{12,4},{16,24},{20,28},{24,16},{28,20},{1,9},{5... | collective-permute-start | bytes 13832 | tf_op jit(solution)/shard_map/cond/branch_1_fun/ppermute | solution.py:30
  304.0 4.6 %collective-permute-start.22 = (f32[2,576]{1,0:T(2,128)S(1)}, f32[2,576]{1,0:T(2,128)S(1)}, u32[]{:S(2)}, u32[]{:S(2)}) collective-permute-start(f32[2,576]{1,0:T(2,128)S(1)} %select_bitcast_fusion.1), channel_id=1, source_target_pairs={{0,16},{4,20},{8,24},{12,28},{16,0},{20,4},{24,8},{28,12},{1,17},{... | collective-permute-start | bytes 13832 | tf_op jit(solution)/shard_map/cond/branch_1_fun/ppermute | solution.py:30
  (48 other events, 138.5 us)
Sparse Core Ops, SparseCore 0:
  10.4 74.6 all-gather.1
  173.0 116.9 reduce-scatter.1

commit v5 on v4

--- a/solution.py
+++ b/solution.py
@@ -755,7 +755,7 @@
             [],
             1,
         )
-        attn_sums = mp_join(attn_chip, swap(attn_chip, "mp", 2), blocks[7])
+        attn_sums = mp_join(attn_chip, swap(attn_chip, "mp", 2), second)
     else:
         second = lax.all_gather(second_pack, "dp", axis=0, tiled=True)
         attn_sums = mp_total(*attn_terms)

time: 325 us -> 321 us (0.988)
  waiting for transfers between devices: 116 us -> 112 us
    ppermute x44, waiting for transfers between devices: 77.9 us -> 74.5 us  [swap(): return lax.ppermute(value, axis, [(i, i ^ bit) for i in range(size)])]
where the time goes in v5:
time: 321 us; the launch traced here: 320 us
  waiting for transfers between devices  112 us (35%)
  Pallas kernels  90 us (28%)
  starting transfers between devices  60.3 us (19%)
  local copies, waits for them, and re-layouts  25.2 us (8%)
  between operations  14.7 us (5%)
  other arithmetic  13.8 us (4%)
  matrix products  3.3 us (1%)
    ppermute x44, waiting for transfers between devices, swap(): return lax.ppermute(value, axis, [(i, i ^ bit) for i in range(size)])  74.5 us
    pallas_call x8, Pallas kernels, call(): pl.pallas_call(kernel, grid=(images,), in_specs=specs, out_specs=[kind(o)...  61.5 us
    ppermute x44, starting transfers between devices, swap(): return lax.ppermute(value, axis, [(i, i ^ bit) for i in range(size)])  51.1 us
    ppermute x5, waiting for transfers between devices, along(): lax.ppermute(value, 'dp', [(2 * a + y, 2 * b + y) for a, b in pairs for y...  37.2 us
    pallas_call x9, Pallas kernels, add_blocks(): pl.pallas_call(kernel, in_specs=[pl.BlockSpec(memory_space=pltpu.VMEM)] *...  18 us
    ppermute x5, starting transfers between devices, along(): lax.ppermute(value, 'dp', [(2 * a + y, 2 * b + y) for a, b in pairs for y...  9.14 us
    unnamed x75, local copies, waits for them, and re-layouts  8.91 us
  transfers between devices with their start and end apart: 51, of which 27 were waited for; matrix products, arithmetic and copies ran while one was open for 7% of the time, Pallas kernels for 24%

profile of v5, /device:TPU:0, one launch (start us, length us, event | category | flops | bytes accessed | tf_op | source)
XLA Modules:
  0.0 319.8 jit_solution(1538229527273730074)
XLA Ops:
  8.4 1.9 concatenate.49
  11.0 17.9 %conditional.4 = (bf16[16,144]{1,0:T(8,128)(2,1)}, f32[2]{0:T(128)S(1)}, bf16[144,2304]{1,0:T(8,128)(2,1)S(1)}) conditional(s32[]{:T(128)} %bitcast.28, () %tuple.44, (s32[2]{0:T(128)S(1)}, s32[2]{0:T(128)S(1)}, bf16[2,1152]{1,0:T(2,128)(2,1)S(1)}, s32[]{:T(128)}, f32[2]{0:T(128)}, /*index=5*/bf16[144,2,768]{2,1,0:T(2,128)(2,1)S(1)}, ...), branch_computations={%region_0.1_spmd, %region_1.5_spmd} | conditional | flops 101409 | bytes 1573591 | solution.py:39
  11.4 3.0 collective-permute-start.15
  14.4 1.6 collective-permute-done.15
  16.0 3.1 collective-permute-start.16
  19.1 1.7 collective-permute-done.16
  20.9 1.9 collective-permute-start.17
  30.0 3.1 collective-permute-start.26
  33.2 5.2 %collective-permute-done.26 = f32[8,1728]{1,0:T(8,128)S(1)} collective-permute-done((f32[8,1728]{1,0:T(8,128)S(1)}, f32[8,1728]{1,0:T(8,128)S(1)}, u32[]{:S(2)}, u32[]{:S(2)}) %collective-permute-start.26) | collective-permute-done | bytes 55328 | tf_op jit(solution)/shard_map/ppermute | solution.py:30
  39.9 4.6 %collective-permute-start.32 = (bf16[144,2304]{1,0:T(8,128)(2,1)S(1)}, bf16[144,2304]{1,0:T(8,128)(2,1)S(1)}, u32[]{:S(2)}, u32[]{:S(2)}) collective-permute-start(bf16[144,2304]{1,0:T(8,128)(2,1)S(1)} %get-tuple-element.195.refs_1_), channel_id=1, source_target_pairs={{0,8},{4,12},{8,16},{12,20},{16,24},{20,28},{1,9},{5,13},{9,17},{1... | collective-permute-start | bytes 1990664 | tf_op jit(solution)/shard_map/ppermute | solution.py:137
  46.7 19.6 %collective-permute-done.33.right_ref = bf16[144,2304]{1,0:T(8,128)(2,1)S(1)} collective-permute-done((bf16[144,2304]{1,0:T(8,128)(2,1)S(1)}, bf16[144,2304]{1,0:T(8,128)(2,1)S(1)}, u32[]{:S(2)}, u32[]{:S(2)}) %collective-permute-start.33) | collective-permute-done | bytes 663584 | tf_op jit(solution)/shard_map/ppermute | solution.py:137
  66.3 2.6 collective-permute-done.32.left_ref._
  69.7 2.2 shard_map.224.refs_2_
  78.9 1.5 collective-permute-start.30
  80.4 14.0 %collective-permute-done.36.right_ref = bf16[144,2304]{1,0:T(8,128)(2,1)S(1)} collective-permute-done((bf16[144,2304]{1,0:T(8,128)(2,1)}, bf16[144,2304]{1,0:T(8,128)(2,1)S(1)}, u32[]{:S(2)}, u32[]{:S(2)}) %collective-permute-start.36) | collective-permute-done | bytes 663584 | tf_op jit(solution)/shard_map/ppermute | solution.py:137
  96.8 2.2 shard_map.225.refs_11_.refs_3_
  102.2 1.8 collective-permute-start.38
  103.9 11.1 %shard_map.226 = (bf16[2,1152,256]{2,1,0:T(8,128)(2,1)}, bf16[2,1152,256]{2,1,0:T(8,128)(2,1)}, f32[2,864,256]{2,1,0:T(8,128)}, f32[2,4,256]{2,1,0:T(4,128)}, bf...) custom-call(s32[13]{0:T(128)S(1)} %stack.128.refs_0_, ...), custom_call_target="tpu_custom_call" | custom-call | flops 1 | bytes 1 | tf_op jit(solution)/shard_map/pallas_call | solution.py:611
  117.5 1.6 collective-permute-start.41
  120.9 2.2 shard_map.227.refs_0_
  125.8 8.1 %collective-permute-done.41.refs_8_ = bf16[144,2304]{1,0:T(8,128)(2,1)S(1)} collective-permute-done((bf16[144,2304]{1,0:T(8,128)(2,1)S(1)}, bf16[144,2304]{1,0:T(8,128)(2,1)S(1)}, u32[]{:S(2)}, u32[]{:S(2)}) %collective-permute-start.41) | collective-permute-done | bytes 663584 | tf_op jit(solution)/shard_map/ppermute | solution.py:30
  134.8 2.6 shard_map.228.refs_2_
  137.4 2.1 collective-permute-done.39.refs_1_
  142.3 2.1 collective-permute-done.43
  144.5 1.8 collective-permute-done.45
  146.3 21.6 %conditional.5 = (f32[2,1152,256]{2,1,0:T(8,128)S(1)}, f32[2,288,256]{2,1,0:T(8,128)}, bf16[2,1152,256]{2,1,0:T(8,128)(2,1)}, bf16[2,768,256]{2,1,0:T(8,128)(2,1...) conditional(s32[]{:T(128)} %bitcast.28, () %tuple.43, ...), branch_computations={%region_5.6_spmd, %region_6.7_spmd} | conditional | flops 2 | bytes 11403338 | solution.py:39
  147.5 12.6 %branch_1_fun.16 = (f32[2,1152,256]{2,1,0:T(8,128)S(1)}, f32[2,288,256]{2,1,0:T(8,128)}, bf16[2,1152,256]{2,1,0:T(8,128)(2,1)}, bf16[2,768,256]{2,1,0:T(8,128)(2...) custom-call(s32[13]{0:T(128)S(1)} %get-tuple-element.89.refs_0_, ...), custom_call_target="tpu_custom_call" | custom-call | flops 1 | bytes 1 | tf_op jit(solution)/shard_map/cond/branch_1_fun/pallas_call | solution.py:611
  160.3 7.6 %branch_1_fun.17 = bf16[1152,2304]{1,0:T(8,128)(2,1)} custom-call(bf16[2,1152,256]{2,1,0:T(8,128)(2,1)} %get-tuple-element.106.refs_0_, bf16[2,768,256]{2,1,0:T(8,128)(2,1)} %get-tuple-element.400.refs_1_, bf16[2,1152,256]{2,1,0:T(8,128)(2,1)} %get-tuple-element.107.refs_2_, bf16[2,1536,256]{2,1,0:T(8,128)(2,1)} %get-tuple-element.108.refs_3_), custom_call_target="tpu_custom_call" | custom-call | flops 1 | bytes 1 | tf_op jit(solution)/shard_map/cond/branch_1_fun/pallas_call | solution.py:611
  168.8 109.3 %conditional.6 = (bf16[2,288,256]{2,1,0:T(8,128)(2,1)S(1)}, bf16[2,288,256]{2,1,0:T(8,128)(2,1)S(1)}, bf16[16,2016]{1,0:T(8,128)(2,1)S(1)}, bf16[144,1152]{1,0:T...) conditional(s32[]{:T(128)} %bitcast.28, () %tuple.42, ...), branch_computations={%region_7.8_spmd, %region_8.11_spmd} | conditional | flops 2228348 | bytes 74185400 | solution.py:39
  168.8 2.0 branch_1_fun.18.refs_0_
  170.8 1.7 collective-permute-start.1
  172.5 3.9 %branch_1_fun.19.refs_2_ = bf16[2,1152,256]{2,1,0:T(8,128)(2,1)} custom-call(bf16[2,768,256]{2,1,0:T(8,128)(2,1)} %get-tuple-element.114.refs_0_, bf16[1152,2304]{1,0:T(8,128)(2,1)} %get-tuple-element.115.refs_1_), custom_call_target="tpu_custom_call" | custom-call | flops 1 | bytes 1 | tf_op jit(solution)/shard_map/cond/branch_1_fun/pallas_call | solution.py:611
  176.4 10.2 %collective-permute-done.1.refs_1_ = bf16[2,576,256]{2,1,0:T(8,128)(2,1)S(1)} collective-permute-done((bf16[2,576,256]{2,1,0:T(8,128)(2,1)}, bf16[2,576,256]{2,1,0:T(8,128)(2,1)S(1)}, u32[]{:S(2)}, u32[]{:S(2)}) %collective-permute-start.1) | collective-permute-done | bytes 589856 | tf_op jit(solution)/shard_map/cond/branch_1_fun/ppermute | solution.py:30
  187.5 2.2 branch_1_fun.20.refs_2_
  192.4 12.7 %branch_1_fun.21 = (f32[2,1152,256]{2,1,0:T(8,128)}, bf16[2,1152,256]{2,1,0:T(8,128)(2,1)}, bf16[2,896,256]{2,1,0:T(8,128)(2,1)}, bf16[2,576,256]{2,1,0:T(8,128)...) custom-call(s32[13]{0:T(128)S(1)} %get-tuple-element.109.refs_0_, ...), custom_call_target="tpu_custom_call" | custom-call | flops 1 | bytes 1 | tf_op jit(solution)/shard_map/cond/branch_1_fun/pallas_call | solution.py:611
  207.6 2.2 branch_1_fun.22.refs_0_
  209.8 1.8 collective-permute-start.4
  212.9 5.1 %branch_1_fun.23 = (bf16[144,1152]{1,0:T(8,128)(2,1)S(1)}, bf16[144,1152]{1,0:T(8,128)(2,1)}, bf16[144,1152]{1,0:T(8,128)(2,1)}, bf16[144,1152]{1,0:T(8,128)(2,1...) custom-call(s32[13]{0:T(128)S(1)} %get-tuple-element.109.refs_0_, ...), custom_call_target="tpu_custom_call" | custom-call | flops 1 | bytes 1 | tf_op jit(solution)/shard_map/cond/branch_1_fun/pallas_call | solution.py:611
  218.0 1.5 collective-permute-start.5
  220.3 12.8 %collective-permute-done.5.refs_10_.refs_1_ = bf16[144,1152]{1,0:T(8,128)(2,1)S(1)} collective-permute-done((bf16[144,1152]{1,0:T(8,128)(2,1)}, bf16[144,1152]{1,0:T(8,128)(2,1)S(1)}, u32[]{:S(2)}, u32[]{:S(2)}) %collective-permute-start.5) | collective-permute-done | bytes 331808 | tf_op jit(solution)/shard_map/cond/branch_1_fun/ppermute | solution.py:30
  234.0 2.2 branch_1_fun.24.refs_3_
  237.8 1.5 collective-permute-start.10
  240.2 1.9 branch_1_fun.25.refs_12_
  242.1 1.8 collective-permute-start.11
  244.8 5.9 %branch_1_fun.26 = (bf16[2,288,256]{2,1,0:T(8,128)(2,1)}, bf16[2,288,256]{2,1,0:T(8,128)(2,1)}, f32[2,8,288]{2,1,0:T(8,128)}) custom-call(s32[13]{0:T(128)S(1)} %get-tuple-element.109.refs_0_, f32[2]{0:T(128)S(1)} %get-tuple-element.110.refs_1_, f32[2]{0:T(128)} %get-tuple-element.111.refs_2_, bf16[2,576,256]{2,1,0:T(8,128)(2,1)} %branch_1_fun.24.refs_3_, ...), custom_call_target="tpu_custom_call" | custom-call | flops 1 | bytes 1 | tf_op jit(solution)/shard_map/cond/branch_1_fun/pallas_call | solution.py:611
  250.8 3.8 %collective-permute-done.10.refs_1_ = bf16[144,1152]{1,0:T(8,128)(2,1)S(1)} collective-permute-done((bf16[144,1152]{1,0:T(8,128)(2,1)S(1)}, bf16[144,1152]{1,0:T(8,128)(2,1)S(1)}, u32[]{:S(2)}, u32[]{:S(2)}) %collective-permute-start.10) | collective-permute-done | bytes 331808 | tf_op jit(solution)/shard_map/cond/branch_1_fun/ppermute | solution.py:30
  255.3 1.9 branch_1_fun.28.refs_2_
  258.0 1.9 branch_1_fun.27.refs_1_
  263.1 3.1 collective-permute-done.12
  267.0 2.9 collective-permute-start.13
  269.9 3.2 %collective-permute-done.13 = bf16[2,2,2016]{2,1,0:T(2,128)(2,1)S(1)} collective-permute-done((bf16[2,2,2016]{2,1,0:T(2,128)(2,1)S(1)}, bf16[2,2,2016]{2,1,0:T(2,128)(2,1)S(1)}, u32[]{:S(2)}, u32[]{:S(2)}) %collective-permute-start.13) | collective-permute-done | bytes 16160 | tf_op jit(solution)/shard_map/cond/branch_1_fun/ppermute | solution.py:30
  273.2 2.5 collective-permute-start.14
  275.7 1.9 collective-permute-done.14
  278.1 2.1 collective-permute-start.46
  280.2 1.8 collective-permute-start.47
  282.0 3.8 %collective-permute-start.48 = (bf16[144,1152]{1,0:T(8,128)(2,1)}, bf16[144,1152]{1,0:T(8,128)(2,1)S(1)}, u32[]{:S(2)}, u32[]{:S(2)}) collective-permute-start(bf16[144,1152]{1,0:T(8,128)(2,1)} %get-tuple-element.218), channel_id=1, source_target_pairs={{0,16},{4,20},{8,24},{12,28},{16,0},{20,4},{24,8},{28,12},{1,17},{... | collective-permute-start | bytes 995336 | tf_op jit(solution)/shard_map/ppermute | solution.py:30
  285.9 19.2 %conditional.7 = (f32[6,144,288]{2,1,0:T(8,128)S(1)}, f32[6,288]{1,0:T(8,128)S(1)}, bf16[144]{0:T(256)(128)(2,1)S(1)}, f32[2,1152]{1,0:T(2,128)S(1)}, f32[72]{0:T(128)S(1)}, /*index=5*/f32[72]{0:T(128)S(1)}) conditional(s32[]{:T(128)} %bitcast.28, () %tuple.48, (bf16[16,2016]{1,0:T(8,128)(2,1)S(1)}, bf16[16,144]{1,0:T(8,128)(2,1)}, ...), branch_computations={%region_11.12_spmd, %region_12.15_spmd} | conditional | flops 16018473 | bytes 2418740 | solution.py:39
  287.7 1.5 collective-permute-start.18
  289.2 2.2 collective-permute-done.18
  294.0 2.5 collective-permute-done.20
  296.8 3.5 %collective-permute-done.21 = f32[4,288]{1,0:T(4,128)S(1)} collective-permute-done((f32[4,288]{1,0:T(4,128)S(1)}, f32[4,288]{1,0:T(4,128)S(1)}, u32[]{:S(2)}, u32[]{:S(2)}) %collective-permute-start.21) | collective-permute-done | bytes 4640 | tf_op jit(solution)/shard_map/cond/branch_1_fun/ppermute | solution.py:30
  301.2 3.8 %collective-permute-done.22 = f32[2,576]{1,0:T(2,128)S(1)} collective-permute-done((f32[2,576]{1,0:T(2,128)S(1)}, f32[2,576]{1,0:T(2,128)S(1)}, u32[]{:S(2)}, u32[]{:S(2)}) %collective-permute-start.22) | collective-permute-done | bytes 4640 | tf_op jit(solution)/shard_map/cond/branch_1_fun/ppermute | solution.py:30
  306.8 2.4 shard_map.230
  311.3 1.6 copy.82
  (299 shorter events, 66.4 us)
Async XLA Ops:
  7.2 96.7 %all-gather.2.cloned.1.call-start = ((), (), s32[]{:S(2)}) async-start(), calls=%async_computation.1 | async-start | bytes 2985984 | tf_op jit(solution)/shard_map/all_gather | solution.py:658
  10.3 298.9 %reduce-scatter.2.cloned.1.call-start = ((), (), s32[]{:S(2)}) async-start(), calls=%async_computation.2 | async-start | bytes 5971968 | tf_op jit(solution)/shard_map/reduce_scatter | solution.py:801
  11.0 18.0 %copy-start.10 = (bf16[144,6,288]{2,0,1:T(8,128)(2,1)S(1)}, bf16[144,6,288]{2,0,1:T(8,128)(2,1)}, u32[]{:S(2)}) copy-start(bf16[144,6,288]{2,0,1:T(8,128)(2,1)} %param.26) | copy-start | bytes 1492996
  11.4 4.6 %collective-permute-start.15 = (bf16[2,1280]{1,0:T(2,128)(2,1)S(1)}, bf16[2,1280]{1,0:T(2,128)(2,1)S(1)}, u32[]{:S(2)}, u32[]{:S(2)}) collective-permute-start(bf16[2,1280]{1,0:T(2,128)(2,1)S(1)} %concatenate.33), channel_id=1, source_target_pairs={{0,8},{4,12},{8,0},{12,4},{16,24},{20,28},{24,16},{28,20},{1,9},{5... | collective-permute-start | bytes 15368 | tf_op jit(solution)/shard_map/cond/branch_1_fun/ppermute | solution.py:30
  16.0 4.8 %collective-permute-start.16 = (bf16[2,2,1280]{2,1,0:T(2,128)(2,1)S(1)}, bf16[2,2,1280]{2,1,0:T(2,128)(2,1)S(1)}, u32[]{:S(2)}, u32[]{:S(2)}) collective-permute-start(bf16[2,2,1280]{2,1,0:T(2,128)(2,1)S(1)} %pad_maximum_fusion.9), channel_id=1, source_target_pairs={{0,16},{4,20},{8,24},{12,28},{16,0},{20,4},{24,8},{28,12},{1,17},{... | collective-permute-start | bytes 30728 | tf_op jit(solution)/shard_map/cond/branch_1_fun/ppermute | solution.py:30
  20.9 3.9 %collective-permute-start.17 = (bf16[2,2,2,1280]{3,2,1,0:T(2,128)(2,1)S(1)}, bf16[2,2,2,1280]{3,2,1,0:T(2,128)(2,1)S(1)}, u32[]{:S(2)}, u32[]{:S(2)}) collective-permute-start(bf16[2,2,2,1280]{3,2,1,0:T(2,128)(2,1)S(1)} %pad_maximum_fusion.8), channel_id=1, source_target_pairs={{0,4},{4,0},{8,12},{12,8},{16,20},{20,16},{24,28},{28,24},{1,5},{5... | collective-permute-start | bytes 61448 | tf_op jit(solution)/shard_map/cond/branch_1_fun/ppermute | solution.py:30
  30.0 8.5 %collective-permute-start.26 = (f32[8,1728]{1,0:T(8,128)S(1)}, f32[8,1728]{1,0:T(8,128)S(1)}, u32[]{:S(2)}, u32[]{:S(2)}) collective-permute-start(f32[8,1728]{1,0:T(8,128)S(1)} %select_n.462), channel_id=1, source_target_pairs={{0,16},{4,20},{8,24},{12,28},{16,0},{20,4},{24,8},{28,12},{1,17},{... | collective-permute-start | bytes 165896 | tf_op jit(solution)/shard_map/ppermute | solution.py:30
  38.5 7.5 %collective-permute-start.27 = (f32[4,1728]{1,0:T(4,128)S(1)}, f32[4,1728]{1,0:T(4,128)S(1)}, u32[]{:S(2)}, u32[]{:S(2)}) collective-permute-start(f32[4,1728]{1,0:T(4,128)S(1)} %slice_select_fusion.2), channel_id=1, source_target_pairs={{0,8},{4,12},{8,0},{12,4},{16,24},{20,28},{24,16},{28,20},{1,9},{5... | collective-permute-start | bytes 82952 | tf_op jit(solution)/shard_map/ppermute | solution.py:30
  38.6 27.7 %collective-permute-start.33 = (bf16[144,2304]{1,0:T(8,128)(2,1)S(1)}, bf16[144,2304]{1,0:T(8,128)(2,1)S(1)}, u32[]{:S(2)}, u32[]{:S(2)}) collective-permute-start(bf16[144,2304]{1,0:T(8,128)(2,1)S(1)} %get-tuple-element.195.refs_1_), channel_id=1, source_target_pairs={{8,0},{12,4},{16,8},{20,12},{24,16},{28,20},{9,1},{13,5},{17,9},{2... | collective-permute-start | bytes 1990664 | tf_op jit(solution)/shard_map/ppermute | solution.py:137
  39.9 29.0 %collective-permute-start.32 = (bf16[144,2304]{1,0:T(8,128)(2,1)S(1)}, bf16[144,2304]{1,0:T(8,128)(2,1)S(1)}, u32[]{:S(2)}, u32[]{:S(2)}) collective-permute-start(bf16[144,2304]{1,0:T(8,128)(2,1)S(1)} %get-tuple-element.195.refs_1_), channel_id=1, source_target_pairs={{0,8},{4,12},{8,16},{12,20},{16,24},{20,28},{1,9},{5,13},{9,17},{1... | collective-permute-start | bytes 1990664 | tf_op jit(solution)/shard_map/ppermute | solution.py:137
  44.5 31.4 %collective-permute-start.29 = (bf16[144,2304]{1,0:T(8,128)(2,1)S(1)}, bf16[144,2304]{1,0:T(8,128)(2,1)S(1)}, u32[]{:S(2)}, u32[]{:S(2)}) collective-permute-start(bf16[144,2304]{1,0:T(8,128)(2,1)S(1)} %get-tuple-element.195.refs_1_), channel_id=1, source_target_pairs={{0,4},{4,0},{8,12},{12,8},{16,20},{20,16},{24,28},{28,24},{1,5},{5... | collective-permute-start | bytes 1990664 | tf_op jit(solution)/shard_map/ppermute | solution.py:30
  46.0 29.3 %collective-permute-start.28 = (f32[2,1728]{1,0:T(2,128)S(1)}, f32[2,1728]{1,0:T(2,128)S(1)}, u32[]{:S(2)}, u32[]{:S(2)}) collective-permute-start(f32[2,1728]{1,0:T(2,128)S(1)} %broadcast_select_fusion.21), channel_id=1, source_target_pairs={{0,4},{4,0},{8,12},{12,8},{16,20},{20,16},{24,28},{28,24},{1,5},{5... | collective-permute-start | bytes 41480 | tf_op jit(solution)/shard_map/ppermute | solution.py:30
  72.0 23.8 %collective-permute-start.34 = (bf16[144,2304]{1,0:T(8,128)(2,1)}, bf16[144,2304]{1,0:T(8,128)(2,1)S(1)}, u32[]{:S(2)}, u32[]{:S(2)}) collective-permute-start(bf16[144,2304]{1,0:T(8,128)(2,1)} %shard_map.224.refs_2_), channel_id=1, source_target_pairs={{0,4},{4,0},{8,12},{12,8},{16,20},{20,16},{24,28},{28,24},{1,5},{5... | collective-permute-start | bytes 1990664 | tf_op jit(solution)/shard_map/ppermute | solution.py:30
  73.3 21.1 %collective-permute-start.36 = (bf16[144,2304]{1,0:T(8,128)(2,1)}, bf16[144,2304]{1,0:T(8,128)(2,1)S(1)}, u32[]{:S(2)}, u32[]{:S(2)}) collective-permute-start(bf16[144,2304]{1,0:T(8,128)(2,1)} %copy-done.11), channel_id=1, source_target_pairs={{8,0},{12,4},{16,8},{20,12},{9,1},{13,5},{17,9},{21,13},{10,2},{14... | collective-permute-start | bytes 1990664 | tf_op jit(solution)/shard_map/ppermute | solution.py:137
  74.5 21.2 %collective-permute-start.35 = (bf16[144,2304]{1,0:T(8,128)(2,1)}, bf16[144,2304]{1,0:T(8,128)(2,1)S(1)}, u32[]{:S(2)}, u32[]{:S(2)}) collective-permute-start(bf16[144,2304]{1,0:T(8,128)(2,1)} %copy-done.1), channel_id=1, source_target_pairs={{8,16},{12,20},{16,24},{20,28},{9,17},{13,21},{17,25},{21,29},{10,... | collective-permute-start | bytes 1990664 | tf_op jit(solution)/shard_map/ppermute | solution.py:137
  78.9 21.5 %collective-permute-start.30 = (f32[2,8,288]{2,1,0:T(8,128)S(1)}, f32[2,8,288]{2,1,0:T(8,128)S(1)}, u32[]{:S(2)}, u32[]{:S(2)}) collective-permute-start(f32[2,8,288]{2,1,0:T(8,128)S(1)} %pad.5), channel_id=1, source_target_pairs={{0,2},{1,3},{2,0},{3,1},{4,6},{5,7},{6,4},{7,5},{8,10},{9,11},{10,... | collective-permute-start | bytes 55304 | tf_op jit(solution)/shard_map/ppermute | solution.py:30
  80.4 23.5 %collective-permute-start.24 = (bf16[2,288,256]{2,1,0:T(8,128)(2,1)}, bf16[2,288,256]{2,1,0:T(8,128)(2,1)}, u32[]{:S(2)}, u32[]{:S(2)}) collective-permute-start(bf16[2,288,256]{2,1,0:T(8,128)(2,1)} %bitcast.129), channel_id=1, source_target_pairs={{0,1},{1,0},{2,3},{3,2},{4,5},{5,4},{6,7},{7,6},{8,9},{9,8},{10,11... | collective-permute-start | bytes 884744 | tf_op jit(solution)/shard_map/ppermute | solution.py:30
  94.4 7.3 %collective-permute-start.23 = (bf16[2,288,256]{2,1,0:T(8,128)(2,1)}, bf16[2,288,256]{2,1,0:T(8,128)(2,1)}, u32[]{:S(2)}, u32[]{:S(2)}) collective-permute-start(bf16[2,288,256]{2,1,0:T(8,128)(2,1)} %bitcast.130), channel_id=1, source_target_pairs={{0,2},{1,3},{2,0},{3,1},{4,6},{5,7},{6,4},{7,5},{8,10},{9,11},{10,... | collective-permute-start | bytes 884744 | tf_op jit(solution)/shard_map/ppermute | solution.py:30
  99.0 17.2 %collective-permute-start.40 = (bf16[144,2304]{1,0:T(8,128)(2,1)}, bf16[144,2304]{1,0:T(8,128)(2,1)}, u32[]{:S(2)}, u32[]{:S(2)}) collective-permute-start(bf16[144,2304]{1,0:T(8,128)(2,1)} %shard_map.225.refs_11_.refs_3_), channel_id=1, source_target_pairs={{8,0},{12,4},{16,24},{20,28},{9,1},{13,5},{17,25},{21,29},{10,2},{... | collective-permute-start | bytes 1990664 | tf_op jit(solution)/shard_map/ppermute | solution.py:137
  100.4 1.5 collective-permute-start.31
  101.7 2.2 collective-permute-start.25
  102.1 12.9 %copy-start.16 = (f32[2,8,1152]{2,1,0:T(8,128)}, f32[2,8,1152]{2,1,0:T(8,128)S(1)}, u32[]{:S(2)}) copy-start(f32[2,8,1152]{2,1,0:T(8,128)S(1)} %reshape.145.refs_5_) | copy-start | bytes 221188
  102.1 14.1 %copy-start.2 = (bf16[144,2304]{1,0:T(8,128)(2,1)S(1)}, bf16[144,2304]{1,0:T(8,128)(2,1)}, u32[]{:S(2)}) copy-start(bf16[144,2304]{1,0:T(8,128)(2,1)} %copy-done.1) | copy-start | bytes 1990660
  102.2 14.1 %copy-start.12 = (bf16[144,2304]{1,0:T(8,128)(2,1)S(1)}, bf16[144,2304]{1,0:T(8,128)(2,1)}, u32[]{:S(2)}) copy-start(bf16[144,2304]{1,0:T(8,128)(2,1)} %copy-done.11) | copy-start | bytes 1990660
  102.2 17.7 %collective-permute-start.38 = (bf16[144,2304]{1,0:T(8,128)(2,1)}, bf16[144,2304]{1,0:T(8,128)(2,1)S(1)}, u32[]{:S(2)}, u32[]{:S(2)}) collective-permute-start(bf16[144,2304]{1,0:T(8,128)(2,1)} %shard_map.225.refs_11_.refs_3_), channel_id=1, source_target_pairs={{0,4},{4,0},{8,12},{12,8},{16,20},{20,16},{24,28},{28,24},{1,5},{5... | collective-permute-start | bytes 1990664 | tf_op jit(solution)/shard_map/ppermute | solution.py:30
  115.0 4.8 %collective-permute-start.37 = (bf16[2,576,256]{2,1,0:T(8,128)(2,1)}, bf16[2,576,256]{2,1,0:T(8,128)(2,1)S(1)}, u32[]{:S(2)}, u32[]{:S(2)}) collective-permute-start(bf16[2,576,256]{2,1,0:T(8,128)(2,1)} %get-tuple-element.198), channel_id=1, source_target_pairs={{0,1},{1,0},{2,3},{3,2},{4,5},{5,4},{6,7},{7,6},{8,9},{9,8},{10,11... | collective-permute-start | bytes 1769480 | tf_op jit(solution)/shard_map/ppermute | solution.py:30
  117.5 16.4 %copy-start.14 = (bf16[144,2304]{1,0:T(8,128)(2,1)}, bf16[144,2304]{1,0:T(8,128)(2,1)S(1)}, u32[]{:S(2)}) copy-start(bf16[144,2304]{1,0:T(8,128)(2,1)S(1)} %select_select_fusion.refs_4_) | copy-start | bytes 1990660
  117.5 16.4 %collective-permute-start.41 = (bf16[144,2304]{1,0:T(8,128)(2,1)S(1)}, bf16[144,2304]{1,0:T(8,128)(2,1)S(1)}, u32[]{:S(2)}, u32[]{:S(2)}) collective-permute-start(bf16[144,2304]{1,0:T(8,128)(2,1)S(1)} %select_select_fusion.refs_4_), channel_id=1, source_target_pairs={{0,4},{4,0},{8,12},{12,8},{16,20},{20,16},{24,28},{28,24},{1,5},{5... | collective-permute-start | bytes 1990664 | tf_op jit(solution)/shard_map/ppermute | solution.py:30
  123.1 16.5 %collective-permute-start.39 = (bf16[2,576,256]{2,1,0:T(8,128)(2,1)}, bf16[2,576,256]{2,1,0:T(8,128)(2,1)S(1)}, u32[]{:S(2)}, u32[]{:S(2)}) collective-permute-start(bf16[2,576,256]{2,1,0:T(8,128)(2,1)} %shard_map.227.refs_0_), channel_id=1, source_target_pairs={{0,2},{1,3},{2,0},{3,1},{4,6},{5,7},{6,4},{7,5},{8,10},{9,11},{10,... | collective-permute-start | bytes 1769480 | tf_op jit(solution)/shard_map/ppermute | solution.py:30
  124.6 19.9 %collective-permute-start.43 = (bf16[2,288,256]{2,1,0:T(8,128)(2,1)}, bf16[2,288,256]{2,1,0:T(8,128)(2,1)}, u32[]{:S(2)}, u32[]{:S(2)}) collective-permute-start(bf16[2,288,256]{2,1,0:T(8,128)(2,1)} %bitcast.67), channel_id=1, source_target_pairs={{0,2},{1,3},{2,0},{3,1},{4,6},{5,7},{6,4},{7,5},{8,10},{9,11},{10,... | collective-permute-start | bytes 884744 | tf_op jit(solution)/shard_map/ppermute | solution.py:30
  141.7 4.5 %collective-permute-start.42 = (bf16[2,576,256]{2,1,0:T(8,128)(2,1)S(1)}, bf16[2,576,256]{2,1,0:T(8,128)(2,1)S(1)}, u32[]{:S(2)}, u32[]{:S(2)}) collective-permute-start(bf16[2,576,256]{2,1,0:T(8,128)(2,1)S(1)} %shard_map.229), channel_id=1, source_target_pairs={{0,1},{1,0},{2,3},{3,2},{4,5},{5,4},{6,7},{7,6},{8,9},{9,8},{10,11... | collective-permute-start | bytes 1769480 | tf_op jit(solution)/shard_map/ppermute | solution.py:30
  141.8 2.7 collective-permute-start.44
  144.5 1.8 collective-permute-start.45
  160.1 7.8 %collective-permute-start = (bf16[2,576,256]{2,1,0:T(8,128)(2,1)}, bf16[2,576,256]{2,1,0:T(8,128)(2,1)}, u32[]{:S(2)}, u32[]{:S(2)}) collective-permute-start(bf16[2,576,256]{2,1,0:T(8,128)(2,1)} %get-tuple-element.105), channel_id=1, source_target_pairs={{0,1},{1,0},{2,3},{3,2},{4,5},{5,4},{6,7},{7,6},{8,9},{9,8},{10,11... | collective-permute-start | bytes 1769480 | tf_op jit(solution)/shard_map/cond/branch_1_fun/ppermute | solution.py:30
  170.8 15.8 %collective-permute-start.1 = (bf16[2,576,256]{2,1,0:T(8,128)(2,1)}, bf16[2,576,256]{2,1,0:T(8,128)(2,1)S(1)}, u32[]{:S(2)}, u32[]{:S(2)}) collective-permute-start(bf16[2,576,256]{2,1,0:T(8,128)(2,1)} %branch_1_fun.18.refs_0_), channel_id=1, source_target_pairs={{0,2},{1,3},{2,0},{3,1},{4,6},{5,7},{6,4},{7,5},{8,10},{9,11},{10,... | collective-permute-start | bytes 1769480 | tf_op jit(solution)/shard_map/cond/branch_1_fun/ppermute | solution.py:30
  176.4 13.4 %copy-start.55 = (f32[72,2]{0,1:T(2,128)S(1)}, f32[72,2]{0,1:T(2,128)}, u32[]{:S(2)}) copy-start(f32[72,2]{0,1:T(2,128)} %get-tuple-element.321) | copy-start | bytes 1732 | tf_op jit(solution)/shard_map/cond
  189.7 2.3 collective-permute-start.2
  191.9 13.7 %copy-start.5 = (bf16[2,2,1,288,256]{4,3,2,1,0:T(8,128)(2,1)}, bf16[2,2,1,288,256]{4,3,2,1,0:T(8,128)(2,1)S(1)}, u32[]{:S(2)}) copy-start(bf16[2,2,1,288,256]{4,3,2,1,0:T(8,128)(2,1)S(1)} %get-tuple-element.343) | copy-start | bytes 1769476 | tf_op jit(solution)/shard_map/cond
  205.1 2.5 collective-permute-start.3
  206.5 5.2 %collective-permute-start.7 = (bf16[2,2,288,256]{3,2,0,1:T(8,128)(2,1)}, bf16[2,2,288,256]{3,2,0,1:T(8,128)(2,1)}, u32[]{:S(2)}, u32[]{:S(2)}) collective-permute-start(bf16[2,2,288,256]{3,2,0,1:T(8,128)(2,1)} %select_bitcast_fusion), channel_id=1, source_target_pairs={{0,1},{1,0},{2,3},{3,2},{4,5},{5,4},{6,7},{7,6},{8,9},{9,8},{10,11... | collective-permute-start | bytes 1769480 | tf_op jit(solution)/shard_map/cond/branch_1_fun/ppermute | solution.py:30
  209.8 23.2 %collective-permute-start.4 = (bf16[2,576,256]{2,1,0:T(8,128)(2,1)}, bf16[2,576,256]{2,1,0:T(8,128)(2,1)S(1)}, u32[]{:S(2)}, u32[]{:S(2)}) collective-permute-start(bf16[2,576,256]{2,1,0:T(8,128)(2,1)} %branch_1_fun.22.refs_0_), channel_id=1, source_target_pairs={{0,2},{1,3},{2,0},{3,1},{4,6},{5,7},{6,4},{7,5},{8,10},{9,11},{10,... | collective-permute-start | bytes 1769480 | tf_op jit(solution)/shard_map/cond/branch_1_fun/ppermute | solution.py:30
  218.0 18.2 %copy-start.8 = (bf16[144,1152]{1,0:T(8,128)(2,1)}, bf16[144,1152]{1,0:T(8,128)(2,1)S(1)}, u32[]{:S(2)}) copy-start(bf16[144,1152]{1,0:T(8,128)(2,1)S(1)} %get-tuple-element.415.refs_2_) | copy-start | bytes 995332 | tf_op jit(solution)/shard_map/cond
  218.0 15.0 %collective-permute-start.5 = (bf16[144,1152]{1,0:T(8,128)(2,1)}, bf16[144,1152]{1,0:T(8,128)(2,1)S(1)}, u32[]{:S(2)}, u32[]{:S(2)}) collective-permute-start(bf16[144,1152]{1,0:T(8,128)(2,1)} %get-tuple-element.138.refs_9_), channel_id=1, source_target_pairs={{0,4},{4,0},{8,12},{12,8},{16,20},{20,16},{24,28},{28,24},{1,5},{5... | collective-permute-start | bytes 995336 | tf_op jit(solution)/shard_map/cond/branch_1_fun/ppermute | solution.py:30
  219.7 16.7 %collective-permute-start.8 = (bf16[2,288,256]{2,1,0:T(8,128)(2,1)S(1)}, bf16[2,288,256]{2,1,0:T(8,128)(2,1)S(1)}, u32[]{:S(2)}, u32[]{:S(2)}) collective-permute-start(bf16[2,288,256]{2,1,0:T(8,128)(2,1)S(1)} %fusion), channel_id=1, source_target_pairs={{0,2},{1,3},{2,0},{3,1},{4,6},{5,7},{6,4},{7,5},{8,10},{9,11},{10,... | collective-permute-start | bytes 884744 | tf_op jit(solution)/shard_map/cond/branch_1_fun/ppermute | solution.py:30
  236.2 7.8 %collective-permute-start.6 = (bf16[2,576,256]{2,1,0:T(8,128)(2,1)}, bf16[2,576,256]{2,1,0:T(8,128)(2,1)S(1)}, u32[]{:S(2)}, u32[]{:S(2)}) collective-permute-start(bf16[2,576,256]{2,1,0:T(8,128)(2,1)} %branch_1_fun.24.refs_3_), channel_id=1, source_target_pairs={{0,1},{1,0},{2,3},{3,2},{4,5},{5,4},{6,7},{7,6},{8,9},{9,8},{10,11... | collective-permute-start | bytes 1769480 | tf_op jit(solution)/shard_map/cond/branch_1_fun/ppermute | solution.py:30
  237.3 19.9 %collective-permute-start.9 = (bf16[144,1152]{1,0:T(8,128)(2,1)S(1)}, bf16[144,1152]{1,0:T(8,128)(2,1)S(1)}, u32[]{:S(2)}, u32[]{:S(2)}) collective-permute-start(bf16[144,1152]{1,0:T(8,128)(2,1)S(1)} %copy-done.40), channel_id=1, source_target_pairs={{0,4},{4,0},{8,12},{12,8},{16,20},{20,16},{24,28},{28,24},{1,5},{5... | collective-permute-start | bytes 995336 | tf_op jit(solution)/shard_map/cond/branch_1_fun/ppermute | solution.py:30
  237.8 16.8 %collective-permute-start.10 = (bf16[144,1152]{1,0:T(8,128)(2,1)S(1)}, bf16[144,1152]{1,0:T(8,128)(2,1)S(1)}, u32[]{:S(2)}, u32[]{:S(2)}) collective-permute-start(bf16[144,1152]{1,0:T(8,128)(2,1)S(1)} %copy-done.41), channel_id=1, source_target_pairs={{0,4},{4,0},{8,12},{12,8},{16,20},{20,16},{24,28},{28,24},{1,5},{5... | collective-permute-start | bytes 995336 | tf_op jit(solution)/shard_map/cond/branch_1_fun/ppermute | solution.py:30
  242.1 18.6 %collective-permute-start.11 = (bf16[144,1152]{1,0:T(8,128)(2,1)}, bf16[144,1152]{1,0:T(8,128)(2,1)}, u32[]{:S(2)}, u32[]{:S(2)}) collective-permute-start(bf16[144,1152]{1,0:T(8,128)(2,1)} %branch_1_fun.25.refs_12_), channel_id=1, source_target_pairs={{0,24},{4,28},{8,16},{12,20},{16,8},{20,12},{24,0},{28,4},{1,25},{... | collective-permute-start | bytes 995336 | tf_op jit(solution)/shard_map/cond/branch_1_fun/ppermute | solution.py:30
  250.7 9.1 %copy-start.49 = (f32[2,8,288]{2,1,0:T(8,128)S(1)}, f32[2,8,288]{2,1,0:T(8,128)}, u32[]{:S(2)}) copy-start(f32[2,8,288]{2,1,0:T(8,128)} %get-tuple-element.144.refs_2_) | copy-start | bytes 55300 | tf_op jit(solution)/shard_map/cond
  257.2 20.7 %copy-start.9 = (bf16[144,1152]{1,0:T(8,128)(2,1)S(1)}, bf16[144,1152]{1,0:T(8,128)(2,1)}, u32[]{:S(2)}) copy-start(bf16[144,1152]{1,0:T(8,128)(2,1)} %copy-done.8) | copy-start | bytes 995332 | tf_op jit(solution)/shard_map/cond
  257.2 20.7 %copy-start.44 = (bf16[2,288,256]{2,1,0:T(8,128)(2,1)S(1)}, bf16[2,288,256]{2,1,0:T(8,128)(2,1)}, u32[]{:S(2)}) copy-start(bf16[2,288,256]{2,1,0:T(8,128)(2,1)} %get-tuple-element.413) | copy-start | bytes 884740 | tf_op jit(solution)/shard_map/cond
  257.2 20.7 %copy-start.46 = (bf16[2,288,256]{2,1,0:T(8,128)(2,1)S(1)}, bf16[2,288,256]{2,1,0:T(8,128)(2,1)}, u32[]{:S(2)}) copy-start(bf16[2,288,256]{2,1,0:T(8,128)(2,1)} %get-tuple-element.412) | copy-start | bytes 884740 | tf_op jit(solution)/shard_map/cond
  262.0 4.3 %collective-permute-start.12 = (bf16[2,2016]{1,0:T(2,128)(2,1)}, bf16[2,2016]{1,0:T(2,128)(2,1)S(1)}, u32[]{:S(2)}, u32[]{:S(2)}) collective-permute-start(bf16[2,2016]{1,0:T(2,128)(2,1)} %branch_1_fun.29), channel_id=1, source_target_pairs={{0,8},{4,12},{8,0},{12,4},{16,24},{20,28},{24,16},{28,20},{1,9},{5... | collective-permute-start | bytes 24200 | tf_op jit(solution)/shard_map/cond/branch_1_fun/ppermute | solution.py:30
  267.0 6.1 %collective-permute-start.13 = (bf16[2,2,2016]{2,1,0:T(2,128)(2,1)S(1)}, bf16[2,2,2016]{2,1,0:T(2,128)(2,1)S(1)}, u32[]{:S(2)}, u32[]{:S(2)}) collective-permute-start(bf16[2,2,2016]{2,1,0:T(2,128)(2,1)S(1)} %pad_maximum_fusion.1), channel_id=1, source_target_pairs={{0,16},{4,20},{8,24},{12,28},{16,0},{20,4},{24,8},{28,12},{1,17},{... | collective-permute-start | bytes 48392 | tf_op jit(solution)/shard_map/cond/branch_1_fun/ppermute | solution.py:30
  273.2 4.3 %collective-permute-start.14 = (bf16[2,2,2,2016]{3,2,1,0:T(2,128)(2,1)S(1)}, bf16[2,2,2,2016]{3,2,1,0:T(2,128)(2,1)S(1)}, u32[]{:S(2)}, u32[]{:S(2)}) collective-permute-start(bf16[2,2,2,2016]{3,2,1,0:T(2,128)(2,1)S(1)} %pad_maximum_fusion), channel_id=1, source_target_pairs={{0,4},{4,0},{8,12},{12,8},{16,20},{20,16},{24,28},{28,24},{1,5},{5... | collective-permute-start | bytes 96776 | tf_op jit(solution)/shard_map/cond/branch_1_fun/ppermute | solution.py:30
  278.1 27.7 %collective-permute-start.46 = (bf16[144,1152]{1,0:T(8,128)(2,1)}, bf16[144,1152]{1,0:T(8,128)(2,1)S(1)}, u32[]{:S(2)}, u32[]{:S(2)}) collective-permute-start(bf16[144,1152]{1,0:T(8,128)(2,1)} %get-tuple-element.216), channel_id=1, source_target_pairs={{0,4},{4,0},{8,12},{12,8},{16,20},{20,16},{24,28},{28,24},{1,5},{5... | collective-permute-start | bytes 995336 | tf_op jit(solution)/shard_map/ppermute | solution.py:30
  280.2 25.6 %collective-permute-start.47 = (bf16[144,1152]{1,0:T(8,128)(2,1)}, bf16[144,1152]{1,0:T(8,128)(2,1)S(1)}, u32[]{:S(2)}, u32[]{:S(2)}) collective-permute-start(bf16[144,1152]{1,0:T(8,128)(2,1)} %get-tuple-element.217), channel_id=1, source_target_pairs={{0,8},{4,12},{8,0},{12,4},{16,24},{20,28},{24,16},{28,20},{1,9},{5... | collective-permute-start | bytes 995336 | tf_op jit(solution)/shard_map/ppermute | solution.py:30
  282.0 23.8 %collective-permute-start.48 = (bf16[144,1152]{1,0:T(8,128)(2,1)}, bf16[144,1152]{1,0:T(8,128)(2,1)S(1)}, u32[]{:S(2)}, u32[]{:S(2)}) collective-permute-start(bf16[144,1152]{1,0:T(8,128)(2,1)} %get-tuple-element.218), channel_id=1, source_target_pairs={{0,16},{4,20},{8,24},{12,28},{16,0},{20,4},{24,8},{28,12},{1,17},{... | collective-permute-start | bytes 995336 | tf_op jit(solution)/shard_map/ppermute | solution.py:30
  285.8 19.3 %copy-start.51 = (bf16[2,1152]{1,0:T(2,128)(2,1)S(1)}, bf16[2,1152]{1,0:T(2,128)(2,1)}, u32[]{:S(2)}) copy-start(bf16[2,1152]{1,0:T(2,128)(2,1)} %param.23) | copy-start | bytes 13828
  287.7 3.8 %collective-permute-start.18 = (f32[2448]{0:T(1024)S(1)}, f32[2448]{0:T(1024)S(1)}, u32[]{:S(2)}, u32[]{:S(2)}) collective-permute-start(f32[2448]{0:T(1024)S(1)} %pad_maximum_fusion.4), channel_id=1, source_target_pairs={{0,2},{1,3},{2,0},{3,1},{4,6},{5,7},{6,4},{7,5},{8,10},{9,11},{10,... | collective-permute-start | bytes 29384 | tf_op jit(solution)/shard_map/cond/branch_1_fun/ppermute | solution.py:30
  291.4 1.2 collective-permute-start.19
  292.8 3.7 %collective-permute-start.20 = (f32[8,144]{1,0:T(8,128)S(1)}, f32[8,144]{1,0:T(8,128)S(1)}, u32[]{:S(2)}, u32[]{:S(2)}) collective-permute-start(f32[8,144]{1,0:T(8,128)S(1)} %select_n.401), channel_id=1, source_target_pairs={{0,4},{4,0},{8,12},{12,8},{16,20},{20,16},{24,28},{28,24},{1,5},{5... | collective-permute-start | bytes 13832 | tf_op jit(solution)/shard_map/cond/branch_1_fun/ppermute | solution.py:30
  296.6 3.7 %collective-permute-start.21 = (f32[4,288]{1,0:T(4,128)S(1)}, f32[4,288]{1,0:T(4,128)S(1)}, u32[]{:S(2)}, u32[]{:S(2)}) collective-permute-start(f32[4,288]{1,0:T(4,128)S(1)} %select_n.407), channel_id=1, source_target_pairs={{0,8},{4,12},{8,0},{12,4},{16,24},{20,28},{24,16},{28,20},{1,9},{5... | collective-permute-start | bytes 13832 | tf_op jit(solution)/shard_map/cond/branch_1_fun/ppermute | solution.py:30
  300.4 4.6 %collective-permute-start.22 = (f32[2,576]{1,0:T(2,128)S(1)}, f32[2,576]{1,0:T(2,128)S(1)}, u32[]{:S(2)}, u32[]{:S(2)}) collective-permute-start(f32[2,576]{1,0:T(2,128)S(1)} %select_bitcast_fusion.1), channel_id=1, source_target_pairs={{0,16},{4,20},{8,24},{12,28},{16,0},{20,4},{24,8},{28,12},{1,17},{... | collective-permute-start | bytes 13832 | tf_op jit(solution)/shard_map/cond/branch_1_fun/ppermute | solution.py:30
  (50 other events, 144.6 us)
Sparse Core Ops, SparseCore 0:
  10.4 74.7 all-gather.1
  168.0 118.1 reduce-scatter.1

commit v6 on v5

--- a/solution.py
+++ b/solution.py
@@ -855,7 +855,8 @@
         first_beside = dp_cross(first_terms)
         end_half = [add_blocks(first_terms[6], first_beside[3])] if on_line else []
         last_line = [swap(half_sum, "dp", 6) for half_sum in end_half]
-        dh_one_sums = mp_total(mine, theirs, (*first_terms, *first_beside[3:]))
+        dh_one_chip = mp_chip(mine, theirs, *first_terms)
+        dh_one_sums = mp_join(dh_one_chip, swap(dh_one_chip, "mp", 2), *first_beside[3:])
         block_out, latent_grad, dmods = call(
             lambda p, w, k, s, a, _, outs, x: last_steps(p[0], w[0], k[0], s, *a, outs, x),
             [
@@ -891,7 +892,7 @@
         beside = jnp.concatenate([high, low])[None]
         beside = jnp.concatenate([beside, jnp.zeros((images - 1, beside.shape[1]), BF16)], axis=0)
         rounded = dmods[:, :6].astype(BF16).reshape(images, 6 * quarter)
-        rounded = after(jnp.concatenate([rounded, beside], axis=1), *halves, *last_line)
+        rounded = after(jnp.concatenate([rounded, beside], axis=1), *halves[1:], *last_line)
         told_back = gather_rows(rounded, "dp")
         own = first_terms[:2] if count > 1 else first_beside
         return block_out, latent_grad, told_back, own, halves, last_line

time: 321 us -> 319 us (level)
    ppermute x44, waiting for transfers between devices: 74.5 us -> 71.1 us  [swap(): return lax.ppermute(value, axis, [(i, i ^ bit) for i in range(size)])]
  transfers between devices with their start and end apart: 51 -> 51, of which waited for: 27 -> 28; matrix products, arithmetic and copies ran while one was open for 7% -> 7% of each run, Pallas kernels for 24% -> 25%
where the time goes in v6:
time: 319 us; the launch traced here: 318 us
  waiting for transfers between devices  109 us (34%)
  Pallas kernels  90.6 us (28%)
  starting transfers between devices  59.2 us (19%)
  local copies, waits for them, and re-layouts  26.5 us (8%)
  between operations  14.7 us (5%)
  other arithmetic  14 us (4%)
  matrix products  3.3 us (1%)
    ppermute x44, waiting for transfers between devices, swap(): return lax.ppermute(value, axis, [(i, i ^ bit) for i in range(size)])  71.1 us
    pallas_call x8, Pallas kernels, call(): pl.pallas_call(kernel, grid=(images,), in_specs=specs, out_specs=[kind(o)...  62 us
    ppermute x44, starting transfers between devices, swap(): return lax.ppermute(value, axis, [(i, i ^ bit) for i in range(size)])  50 us
    ppermute x5, waiting for transfers between devices, along(): lax.ppermute(value, 'dp', [(2 * a + y, 2 * b + y) for a, b in pairs for y...  37.5 us
    pallas_call x9, Pallas kernels, add_blocks(): pl.pallas_call(kernel, in_specs=[pl.BlockSpec(memory_space=pltpu.VMEM)] *...  18.1 us
    ppermute x5, starting transfers between devices, along(): lax.ppermute(value, 'dp', [(2 * a + y, 2 * b + y) for a, b in pairs for y...  9.14 us
    unnamed x75, local copies, waits for them, and re-layouts  8.94 us
  transfers between devices with their start and end apart: 51, of which 28 were waited for; matrix products, arithmetic and copies ran while one was open for 7% of the time, Pallas kernels for 25%

profile of v6, /device:TPU:0, one launch (start us, length us, event | category | flops | bytes accessed | tf_op | source)
XLA Modules:
  0.0 317.6 jit_solution(14053563144771323080)
XLA Ops:
  8.4 1.9 concatenate.49
  11.1 18.0 %conditional.4 = (bf16[16,144]{1,0:T(8,128)(2,1)}, f32[2]{0:T(128)S(1)}, bf16[144,2304]{1,0:T(8,128)(2,1)S(1)}) conditional(s32[]{:T(128)} %bitcast.28, () %tuple.44, (s32[2]{0:T(128)S(1)}, s32[2]{0:T(128)S(1)}, bf16[2,1152]{1,0:T(2,128)(2,1)S(1)}, s32[]{:T(128)}, f32[2]{0:T(128)}, /*index=5*/bf16[144,2,768]{2,1,0:T(2,128)(2,1)S(1)}, ...), branch_computations={%region_0.1_spmd, %region_1.5_spmd} | conditional | flops 101409 | bytes 1573591 | solution.py:39
  11.4 3.0 collective-permute-start.15
  14.4 1.6 collective-permute-done.15
  16.1 3.1 collective-permute-start.16
  19.2 1.7 collective-permute-done.16
  20.9 1.9 collective-permute-start.17
  30.1 3.1 collective-permute-start.26
  33.3 5.1 %collective-permute-done.26 = f32[8,1728]{1,0:T(8,128)S(1)} collective-permute-done((f32[8,1728]{1,0:T(8,128)S(1)}, f32[8,1728]{1,0:T(8,128)S(1)}, u32[]{:S(2)}, u32[]{:S(2)}) %collective-permute-start.26) | collective-permute-done | bytes 55328 | tf_op jit(solution)/shard_map/ppermute | solution.py:30
  39.9 4.6 %collective-permute-start.32 = (bf16[144,2304]{1,0:T(8,128)(2,1)S(1)}, bf16[144,2304]{1,0:T(8,128)(2,1)S(1)}, u32[]{:S(2)}, u32[]{:S(2)}) collective-permute-start(bf16[144,2304]{1,0:T(8,128)(2,1)S(1)} %get-tuple-element.195.refs_1_), channel_id=1, source_target_pairs={{0,8},{4,12},{8,16},{12,20},{16,24},{20,28},{1,9},{5,13},{9,17},{1... | collective-permute-start | bytes 1990664 | tf_op jit(solution)/shard_map/ppermute | solution.py:137
  44.5 1.5 collective-permute-start.29
  46.7 19.6 %collective-permute-done.33.right_ref = bf16[144,2304]{1,0:T(8,128)(2,1)S(1)} collective-permute-done((bf16[144,2304]{1,0:T(8,128)(2,1)S(1)}, bf16[144,2304]{1,0:T(8,128)(2,1)S(1)}, u32[]{:S(2)}, u32[]{:S(2)}) %collective-permute-start.33) | collective-permute-done | bytes 663584 | tf_op jit(solution)/shard_map/ppermute | solution.py:137
  66.3 2.6 collective-permute-done.32.left_ref._
  69.8 2.2 shard_map.224.refs_2_
  78.9 1.8 collective-permute-start.30
  80.7 13.8 %collective-permute-done.36.right_ref = bf16[144,2304]{1,0:T(8,128)(2,1)S(1)} collective-permute-done((bf16[144,2304]{1,0:T(8,128)(2,1)}, bf16[144,2304]{1,0:T(8,128)(2,1)S(1)}, u32[]{:S(2)}, u32[]{:S(2)}) %collective-permute-start.36) | collective-permute-done | bytes 663584 | tf_op jit(solution)/shard_map/ppermute | solution.py:137
  94.4 1.9 collective-permute-start.23
  97.5 2.2 shard_map.225.refs_11_.refs_3_
  104.5 11.0 %shard_map.226 = (bf16[2,1152,256]{2,1,0:T(8,128)(2,1)}, bf16[2,1152,256]{2,1,0:T(8,128)(2,1)}, f32[2,864,256]{2,1,0:T(8,128)}, f32[2,4,256]{2,1,0:T(4,128)}, bf...) custom-call(s32[13]{0:T(128)S(1)} %stack.128.refs_0_, ...), custom_call_target="tpu_custom_call" | custom-call | flops 1 | bytes 1 | tf_op jit(solution)/shard_map/pallas_call | solution.py:611
  115.8 1.5 collective-permute-done.40
  119.5 1.4 collective-permute-done.38.refs_2_.refs_7_
  121.9 2.2 shard_map.227.refs_0_
  124.1 1.7 collective-permute-start.39
  126.7 8.0 %collective-permute-done.41.refs_8_ = bf16[144,2304]{1,0:T(8,128)(2,1)S(1)} collective-permute-done((bf16[144,2304]{1,0:T(8,128)(2,1)S(1)}, bf16[144,2304]{1,0:T(8,128)(2,1)S(1)}, u32[]{:S(2)}, u32[]{:S(2)}) %collective-permute-start.41) | collective-permute-done | bytes 663584 | tf_op jit(solution)/shard_map/ppermute | solution.py:30
  135.6 2.6 shard_map.228.refs_2_
  138.2 2.4 collective-permute-done.39.refs_1_
  141.4 1.4 shard_map.229
  143.3 2.0 collective-permute-done.43
  145.5 1.6 collective-permute-done.45
  147.1 21.6 %conditional.5 = (f32[2,1152,256]{2,1,0:T(8,128)S(1)}, f32[2,288,256]{2,1,0:T(8,128)}, bf16[2,1152,256]{2,1,0:T(8,128)(2,1)}, bf16[2,768,256]{2,1,0:T(8,128)(2,1...) conditional(s32[]{:T(128)} %bitcast.28, () %tuple.43, ...), branch_computations={%region_5.6_spmd, %region_6.7_spmd} | conditional | flops 2 | bytes 11403338 | solution.py:39
  148.3 12.6 %branch_1_fun.16 = (f32[2,1152,256]{2,1,0:T(8,128)S(1)}, f32[2,288,256]{2,1,0:T(8,128)}, bf16[2,1152,256]{2,1,0:T(8,128)(2,1)}, bf16[2,768,256]{2,1,0:T(8,128)(2...) custom-call(s32[13]{0:T(128)S(1)} %get-tuple-element.89.refs_0_, ...), custom_call_target="tpu_custom_call" | custom-call | flops 1 | bytes 1 | tf_op jit(solution)/shard_map/cond/branch_1_fun/pallas_call | solution.py:611
  161.1 7.6 %branch_1_fun.17 = bf16[1152,2304]{1,0:T(8,128)(2,1)} custom-call(bf16[2,1152,256]{2,1,0:T(8,128)(2,1)} %get-tuple-element.106.refs_0_, bf16[2,768,256]{2,1,0:T(8,128)(2,1)} %get-tuple-element.400.refs_1_, bf16[2,1152,256]{2,1,0:T(8,128)(2,1)} %get-tuple-element.107.refs_2_, bf16[2,1536,256]{2,1,0:T(8,128)(2,1)} %get-tuple-element.108.refs_3_), custom_call_target="tpu_custom_call" | custom-call | flops 1 | bytes 1 | tf_op jit(solution)/shard_map/cond/branch_1_fun/pallas_call | solution.py:611
  169.6 109.7 %conditional.6 = (bf16[2,288,256]{2,1,0:T(8,128)(2,1)}, bf16[2,288,256]{2,1,0:T(8,128)(2,1)}, bf16[16,2016]{1,0:T(8,128)(2,1)S(1)}, bf16[144,1152]{1,0:T(8,128)(...) conditional(s32[]{:T(128)} %bitcast.28, () %tuple.42, ...), branch_computations={%region_7.8_spmd, %region_8.11_spmd} | conditional | flops 2228348 | bytes 66752748 | solution.py:39
  169.6 2.0 branch_1_fun.18.refs_0_
  171.6 1.8 collective-permute-start.1
  173.4 3.8 %branch_1_fun.19.refs_2_ = bf16[2,1152,256]{2,1,0:T(8,128)(2,1)} custom-call(bf16[2,768,256]{2,1,0:T(8,128)(2,1)} %get-tuple-element.114.refs_0_, bf16[1152,2304]{1,0:T(8,128)(2,1)} %get-tuple-element.115.refs_1_), custom_call_target="tpu_custom_call" | custom-call | flops 1 | bytes 1 | tf_op jit(solution)/shard_map/cond/branch_1_fun/pallas_call | solution.py:611
  177.2 10.2 %collective-permute-done.1.refs_1_ = bf16[2,576,256]{2,1,0:T(8,128)(2,1)S(1)} collective-permute-done((bf16[2,576,256]{2,1,0:T(8,128)(2,1)}, bf16[2,576,256]{2,1,0:T(8,128)(2,1)S(1)}, u32[]{:S(2)}, u32[]{:S(2)}) %collective-permute-start.1) | collective-permute-done | bytes 589856 | tf_op jit(solution)/shard_map/cond/branch_1_fun/ppermute | solution.py:30
  188.3 2.2 branch_1_fun.20.refs_2_
  191.2 1.5 fusion.32
  193.1 12.7 %branch_1_fun.21 = (f32[2,1152,256]{2,1,0:T(8,128)}, bf16[2,1152,256]{2,1,0:T(8,128)(2,1)}, bf16[2,896,256]{2,1,0:T(8,128)(2,1)}, bf16[2,576,256]{2,1,0:T(8,128)...) custom-call(s32[13]{0:T(128)S(1)} %get-tuple-element.109.refs_0_, ...), custom_call_target="tpu_custom_call" | custom-call | flops 1 | bytes 1 | tf_op jit(solution)/shard_map/cond/branch_1_fun/pallas_call | solution.py:611
  207.4 5.6 %branch_1_fun.22 = (bf16[144,1152]{1,0:T(8,128)(2,1)S(1)}, bf16[144,1152]{1,0:T(8,128)(2,1)}, bf16[144,1152]{1,0:T(8,128)(2,1)}, bf16[144,1152]{1,0:T(8,128)(2,1...) custom-call(s32[13]{0:T(128)S(1)} %get-tuple-element.109.refs_0_, ...), custom_call_target="tpu_custom_call" | custom-call | flops 1 | bytes 1 | tf_op jit(solution)/shard_map/cond/branch_1_fun/pallas_call | solution.py:611
  213.0 2.4 branch_1_fun.23.refs_0_
  215.3 1.8 collective-permute-start.4
  219.7 13.8 %collective-permute-done.5.refs_2_.refs_1_ = bf16[144,1152]{1,0:T(8,128)(2,1)S(1)} collective-permute-done((bf16[144,1152]{1,0:T(8,128)(2,1)S(1)}, bf16[144,1152]{1,0:T(8,128)(2,1)S(1)}, u32[]{:S(2)}, u32[]{:S(2)}) %collective-permute-start.5) | collective-permute-done | bytes 331808 | tf_op jit(solution)/shard_map/cond/branch_1_fun/ppermute | solution.py:30
  235.1 2.2 branch_1_fun.24.refs_3_
  240.2 1.9 branch_1_fun.25.refs_12_
  244.0 5.9 %branch_1_fun.26 = (bf16[2,288,256]{2,1,0:T(8,128)(2,1)}, bf16[2,288,256]{2,1,0:T(8,128)(2,1)}, f32[2,8,288]{2,1,0:T(8,128)}) custom-call(s32[13]{0:T(128)S(1)} %get-tuple-element.109.refs_0_, f32[2]{0:T(128)S(1)} %get-tuple-element.110.refs_1_, f32[2]{0:T(128)} %get-tuple-element.111.refs_2_, bf16[2,576,256]{2,1,0:T(8,128)(2,1)} %branch_1_fun.24.refs_3_, ...), custom_call_target="tpu_custom_call" | custom-call | flops 1 | bytes 1 | tf_op jit(solution)/shard_map/cond/branch_1_fun/pallas_call | solution.py:611
  250.7 1.9 branch_1_fun.27.refs_1_
  255.4 7.2 %collective-permute-start.11 = (bf16[2,2016]{1,0:T(2,128)(2,1)}, bf16[2,2016]{1,0:T(2,128)(2,1)S(1)}, u32[]{:S(2)}, u32[]{:S(2)}) collective-permute-start(bf16[2,2016]{1,0:T(2,128)(2,1)} %branch_1_fun.28), channel_id=1, source_target_pairs={{0,8},{4,12},{8,0},{12,4},{16,24},{20,28},{24,16},{28,20},{1,9},{5... | collective-permute-start | bytes 24200 | tf_op jit(solution)/shard_map/cond/branch_1_fun/ppermute | solution.py:30
  262.6 2.8 collective-permute-done.11
  268.2 4.2 %collective-permute-done.12 = bf16[2,2,2016]{2,1,0:T(2,128)(2,1)S(1)} collective-permute-done((bf16[2,2,2016]{2,1,0:T(2,128)(2,1)S(1)}, bf16[2,2,2016]{2,1,0:T(2,128)(2,1)S(1)}, u32[]{:S(2)}, u32[]{:S(2)}) %collective-permute-start.12) | collective-permute-done | bytes 16160 | tf_op jit(solution)/shard_map/cond/branch_1_fun/ppermute | solution.py:30
  272.6 3.5 %collective-permute-done.14.refs_1_ = bf16[144,1152]{1,0:T(8,128)(2,1)S(1)} collective-permute-done((bf16[144,1152]{1,0:T(8,128)(2,1)S(1)}, bf16[144,1152]{1,0:T(8,128)(2,1)S(1)}, u32[]{:S(2)}, u32[]{:S(2)}) %collective-permute-start.14) | collective-permute-done | bytes 331808 | tf_op jit(solution)/shard_map/cond/branch_1_fun/ppermute | solution.py:30
  276.9 1.9 branch_1_fun.29
  281.2 2.4 collective-permute-start.48
  283.6 19.3 %conditional.7 = (f32[6,144,288]{2,1,0:T(8,128)S(1)}, f32[6,288]{1,0:T(8,128)S(1)}, bf16[144]{0:T(256)(128)(2,1)S(1)}, f32[2,1152]{1,0:T(2,128)S(1)}, f32[72]{0:T(128)S(1)}, /*index=5*/f32[72]{0:T(128)S(1)}) conditional(s32[]{:T(128)} %bitcast.28, () %tuple.48, (bf16[16,2016]{1,0:T(8,128)(2,1)S(1)}, bf16[16,144]{1,0:T(8,128)(2,1)}, ...), branch_computations={%region_11.12_spmd, %region_12.15_spmd} | conditional | flops 16018473 | bytes 2418740 | solution.py:39
  283.9 1.3 convolution_bitcast_fusion.1
  285.4 1.5 collective-permute-start.18
  287.0 2.2 collective-permute-done.18
  290.5 1.5 collective-permute-start.20
  295.1 2.9 collective-permute-done.21
  298.2 2.2 collective-permute-start.22
  300.4 2.4 collective-permute-done.22
  304.6 2.4 shard_map.230
  309.1 1.6 copy.82
  (287 shorter events, 64.6 us)
Async XLA Ops:
  7.2 97.3 %all-gather.2.cloned.1.call-start = ((), (), s32[]{:S(2)}) async-start(), calls=%async_computation.1 | async-start | bytes 2985984 | tf_op jit(solution)/shard_map/all_gather | solution.py:658
  10.3 296.7 %reduce-scatter.2.cloned.1.call-start = ((), (), s32[]{:S(2)}) async-start(), calls=%async_computation.2 | async-start | bytes 5971968 | tf_op jit(solution)/shard_map/reduce_scatter | solution.py:801
  11.0 18.0 %copy-start.10 = (bf16[144,6,288]{2,0,1:T(8,128)(2,1)S(1)}, bf16[144,6,288]{2,0,1:T(8,128)(2,1)}, u32[]{:S(2)}) copy-start(bf16[144,6,288]{2,0,1:T(8,128)(2,1)} %param.26) | copy-start | bytes 1492996
  11.4 4.6 %collective-permute-start.15 = (bf16[2,1280]{1,0:T(2,128)(2,1)S(1)}, bf16[2,1280]{1,0:T(2,128)(2,1)S(1)}, u32[]{:S(2)}, u32[]{:S(2)}) collective-permute-start(bf16[2,1280]{1,0:T(2,128)(2,1)S(1)} %concatenate.33), channel_id=1, source_target_pairs={{0,8},{4,12},{8,0},{12,4},{16,24},{20,28},{24,16},{28,20},{1,9},{5... | collective-permute-start | bytes 15368 | tf_op jit(solution)/shard_map/cond/branch_1_fun/ppermute | solution.py:30
  16.1 4.8 %collective-permute-start.16 = (bf16[2,2,1280]{2,1,0:T(2,128)(2,1)S(1)}, bf16[2,2,1280]{2,1,0:T(2,128)(2,1)S(1)}, u32[]{:S(2)}, u32[]{:S(2)}) collective-permute-start(bf16[2,2,1280]{2,1,0:T(2,128)(2,1)S(1)} %pad_maximum_fusion.9), channel_id=1, source_target_pairs={{0,16},{4,20},{8,24},{12,28},{16,0},{20,4},{24,8},{28,12},{1,17},{... | collective-permute-start | bytes 30728 | tf_op jit(solution)/shard_map/cond/branch_1_fun/ppermute | solution.py:30
  20.9 3.9 %collective-permute-start.17 = (bf16[2,2,2,1280]{3,2,1,0:T(2,128)(2,1)S(1)}, bf16[2,2,2,1280]{3,2,1,0:T(2,128)(2,1)S(1)}, u32[]{:S(2)}, u32[]{:S(2)}) collective-permute-start(bf16[2,2,2,1280]{3,2,1,0:T(2,128)(2,1)S(1)} %pad_maximum_fusion.8), channel_id=1, source_target_pairs={{0,4},{4,0},{8,12},{12,8},{16,20},{20,16},{24,28},{28,24},{1,5},{5... | collective-permute-start | bytes 61448 | tf_op jit(solution)/shard_map/cond/branch_1_fun/ppermute | solution.py:30
  30.1 8.4 %collective-permute-start.26 = (f32[8,1728]{1,0:T(8,128)S(1)}, f32[8,1728]{1,0:T(8,128)S(1)}, u32[]{:S(2)}, u32[]{:S(2)}) collective-permute-start(f32[8,1728]{1,0:T(8,128)S(1)} %select_n.462), channel_id=1, source_target_pairs={{0,16},{4,20},{8,24},{12,28},{16,0},{20,4},{24,8},{28,12},{1,17},{... | collective-permute-start | bytes 165896 | tf_op jit(solution)/shard_map/ppermute | solution.py:30
  38.5 7.5 %collective-permute-start.27 = (f32[4,1728]{1,0:T(4,128)S(1)}, f32[4,1728]{1,0:T(4,128)S(1)}, u32[]{:S(2)}, u32[]{:S(2)}) collective-permute-start(f32[4,1728]{1,0:T(4,128)S(1)} %slice_select_fusion.2), channel_id=1, source_target_pairs={{0,8},{4,12},{8,0},{12,4},{16,24},{20,28},{24,16},{28,20},{1,9},{5... | collective-permute-start | bytes 82952 | tf_op jit(solution)/shard_map/ppermute | solution.py:30
  38.6 27.7 %collective-permute-start.33 = (bf16[144,2304]{1,0:T(8,128)(2,1)S(1)}, bf16[144,2304]{1,0:T(8,128)(2,1)S(1)}, u32[]{:S(2)}, u32[]{:S(2)}) collective-permute-start(bf16[144,2304]{1,0:T(8,128)(2,1)S(1)} %get-tuple-element.195.refs_1_), channel_id=1, source_target_pairs={{8,0},{12,4},{16,8},{20,12},{24,16},{28,20},{9,1},{13,5},{17,9},{2... | collective-permute-start | bytes 1990664 | tf_op jit(solution)/shard_map/ppermute | solution.py:137
  39.9 29.0 %collective-permute-start.32 = (bf16[144,2304]{1,0:T(8,128)(2,1)S(1)}, bf16[144,2304]{1,0:T(8,128)(2,1)S(1)}, u32[]{:S(2)}, u32[]{:S(2)}) collective-permute-start(bf16[144,2304]{1,0:T(8,128)(2,1)S(1)} %get-tuple-element.195.refs_1_), channel_id=1, source_target_pairs={{0,8},{4,12},{8,16},{12,20},{16,24},{20,28},{1,9},{5,13},{9,17},{1... | collective-permute-start | bytes 1990664 | tf_op jit(solution)/shard_map/ppermute | solution.py:137
  44.5 31.4 %collective-permute-start.29 = (bf16[144,2304]{1,0:T(8,128)(2,1)S(1)}, bf16[144,2304]{1,0:T(8,128)(2,1)S(1)}, u32[]{:S(2)}, u32[]{:S(2)}) collective-permute-start(bf16[144,2304]{1,0:T(8,128)(2,1)S(1)} %get-tuple-element.195.refs_1_), channel_id=1, source_target_pairs={{0,4},{4,0},{8,12},{12,8},{16,20},{20,16},{24,28},{28,24},{1,5},{5... | collective-permute-start | bytes 1990664 | tf_op jit(solution)/shard_map/ppermute | solution.py:30
  46.0 29.2 %collective-permute-start.28 = (f32[2,1728]{1,0:T(2,128)S(1)}, f32[2,1728]{1,0:T(2,128)S(1)}, u32[]{:S(2)}, u32[]{:S(2)}) collective-permute-start(f32[2,1728]{1,0:T(2,128)S(1)} %broadcast_select_fusion.21), channel_id=1, source_target_pairs={{0,4},{4,0},{8,12},{12,8},{16,20},{20,16},{24,28},{28,24},{1,5},{5... | collective-permute-start | bytes 41480 | tf_op jit(solution)/shard_map/ppermute | solution.py:30
  69.8 9.1 %copy-start.47 = (f32[6,288]{1,0:T(8,128)S(1)}, f32[6,288]{1,0:T(8,128)}, u32[]{:S(2)}) copy-start(f32[6,288]{1,0:T(8,128)} %param.27) | copy-start | bytes 20740
  72.0 24.4 %collective-permute-start.34 = (bf16[144,2304]{1,0:T(8,128)(2,1)}, bf16[144,2304]{1,0:T(8,128)(2,1)S(1)}, u32[]{:S(2)}, u32[]{:S(2)}) collective-permute-start(bf16[144,2304]{1,0:T(8,128)(2,1)} %shard_map.224.refs_2_), channel_id=1, source_target_pairs={{0,4},{4,0},{8,12},{12,8},{16,20},{20,16},{24,28},{28,24},{1,5},{5... | collective-permute-start | bytes 1990664 | tf_op jit(solution)/shard_map/ppermute | solution.py:30
  73.3 21.2 %collective-permute-start.36 = (bf16[144,2304]{1,0:T(8,128)(2,1)}, bf16[144,2304]{1,0:T(8,128)(2,1)S(1)}, u32[]{:S(2)}, u32[]{:S(2)}) collective-permute-start(bf16[144,2304]{1,0:T(8,128)(2,1)} %copy-done.11), channel_id=1, source_target_pairs={{8,0},{12,4},{16,8},{20,12},{9,1},{13,5},{17,9},{21,13},{10,2},{14... | collective-permute-start | bytes 1990664 | tf_op jit(solution)/shard_map/ppermute | solution.py:137
  74.5 21.8 %collective-permute-start.35 = (bf16[144,2304]{1,0:T(8,128)(2,1)}, bf16[144,2304]{1,0:T(8,128)(2,1)S(1)}, u32[]{:S(2)}, u32[]{:S(2)}) collective-permute-start(bf16[144,2304]{1,0:T(8,128)(2,1)} %copy-done.1), channel_id=1, source_target_pairs={{8,16},{12,20},{16,24},{20,28},{9,17},{13,21},{17,25},{21,29},{10,... | collective-permute-start | bytes 1990664 | tf_op jit(solution)/shard_map/ppermute | solution.py:137
  78.9 22.1 %collective-permute-start.30 = (f32[2,8,288]{2,1,0:T(8,128)S(1)}, f32[2,8,288]{2,1,0:T(8,128)S(1)}, u32[]{:S(2)}, u32[]{:S(2)}) collective-permute-start(f32[2,8,288]{2,1,0:T(8,128)S(1)} %pad.5), channel_id=1, source_target_pairs={{0,2},{1,3},{2,0},{3,1},{4,6},{5,7},{6,4},{7,5},{8,10},{9,11},{10,... | collective-permute-start | bytes 55304 | tf_op jit(solution)/shard_map/ppermute | solution.py:30
  80.7 23.2 %collective-permute-start.24 = (bf16[2,288,256]{2,1,0:T(8,128)(2,1)}, bf16[2,288,256]{2,1,0:T(8,128)(2,1)}, u32[]{:S(2)}, u32[]{:S(2)}) collective-permute-start(bf16[2,288,256]{2,1,0:T(8,128)(2,1)} %bitcast.129), channel_id=1, source_target_pairs={{0,1},{1,0},{2,3},{3,2},{4,5},{5,4},{6,7},{7,6},{8,9},{9,8},{10,11... | collective-permute-start | bytes 884744 | tf_op jit(solution)/shard_map/ppermute | solution.py:30
  94.4 8.2 %collective-permute-start.23 = (bf16[2,288,256]{2,1,0:T(8,128)(2,1)}, bf16[2,288,256]{2,1,0:T(8,128)(2,1)}, u32[]{:S(2)}, u32[]{:S(2)}) collective-permute-start(bf16[2,288,256]{2,1,0:T(8,128)(2,1)} %bitcast.130), channel_id=1, source_target_pairs={{0,2},{1,3},{2,0},{3,1},{4,6},{5,7},{6,4},{7,5},{8,10},{9,11},{10,... | collective-permute-start | bytes 884744 | tf_op jit(solution)/shard_map/ppermute | solution.py:30
  97.5 7.1 %copy-start.21 = (f32[3,72,256]{2,1,0:T(8,128)S(1)}, f32[3,72,256]{2,1,0:T(8,128)}, u32[]{:S(2)}) copy-start(f32[3,72,256]{2,1,0:T(8,128)} %constant.336.clone.refs_8_) | copy-start | bytes 663556
  99.7 17.6 %collective-permute-start.40 = (bf16[144,2304]{1,0:T(8,128)(2,1)}, bf16[144,2304]{1,0:T(8,128)(2,1)}, u32[]{:S(2)}, u32[]{:S(2)}) collective-permute-start(bf16[144,2304]{1,0:T(8,128)(2,1)} %shard_map.225.refs_11_.refs_3_), channel_id=1, source_target_pairs={{8,0},{12,4},{16,24},{20,28},{9,1},{13,5},{17,25},{21,29},{10,2},{... | collective-permute-start | bytes 1990664 | tf_op jit(solution)/shard_map/ppermute | solution.py:137
  101.0 1.6 collective-permute-start.31
  102.6 1.9 collective-permute-start.25
  102.9 12.7 %copy-start.16 = (f32[2,8,1152]{2,1,0:T(8,128)}, f32[2,8,1152]{2,1,0:T(8,128)S(1)}, u32[]{:S(2)}) copy-start(f32[2,8,1152]{2,1,0:T(8,128)S(1)} %reshape.145.refs_5_) | copy-start | bytes 221188
  102.9 14.4 %copy-start.2 = (bf16[144,2304]{1,0:T(8,128)(2,1)S(1)}, bf16[144,2304]{1,0:T(8,128)(2,1)}, u32[]{:S(2)}) copy-start(bf16[144,2304]{1,0:T(8,128)(2,1)} %copy-done.1) | copy-start | bytes 1990660
  102.9 14.4 %copy-start.12 = (bf16[144,2304]{1,0:T(8,128)(2,1)S(1)}, bf16[144,2304]{1,0:T(8,128)(2,1)}, u32[]{:S(2)}) copy-start(bf16[144,2304]{1,0:T(8,128)(2,1)} %copy-done.11) | copy-start | bytes 1990660
  102.9 18.0 %collective-permute-start.38 = (bf16[144,2304]{1,0:T(8,128)(2,1)}, bf16[144,2304]{1,0:T(8,128)(2,1)S(1)}, u32[]{:S(2)}, u32[]{:S(2)}) collective-permute-start(bf16[144,2304]{1,0:T(8,128)(2,1)} %shard_map.225.refs_11_.refs_3_), channel_id=1, source_target_pairs={{0,4},{4,0},{8,12},{12,8},{16,20},{20,16},{24,28},{28,24},{1,5},{5... | collective-permute-start | bytes 1990664 | tf_op jit(solution)/shard_map/ppermute | solution.py:30
  115.6 5.3 %collective-permute-start.37 = (bf16[2,576,256]{2,1,0:T(8,128)(2,1)}, bf16[2,576,256]{2,1,0:T(8,128)(2,1)S(1)}, u32[]{:S(2)}, u32[]{:S(2)}) collective-permute-start(bf16[2,576,256]{2,1,0:T(8,128)(2,1)} %get-tuple-element.198), channel_id=1, source_target_pairs={{0,1},{1,0},{2,3},{3,2},{4,5},{5,4},{6,7},{7,6},{8,9},{9,8},{10,11... | collective-permute-start | bytes 1769480 | tf_op jit(solution)/shard_map/ppermute | solution.py:30
  118.5 16.2 %copy-start.14 = (bf16[144,2304]{1,0:T(8,128)(2,1)}, bf16[144,2304]{1,0:T(8,128)(2,1)S(1)}, u32[]{:S(2)}) copy-start(bf16[144,2304]{1,0:T(8,128)(2,1)S(1)} %select_select_fusion.refs_4_) | copy-start | bytes 1990660
  118.5 16.2 %collective-permute-start.41 = (bf16[144,2304]{1,0:T(8,128)(2,1)S(1)}, bf16[144,2304]{1,0:T(8,128)(2,1)S(1)}, u32[]{:S(2)}, u32[]{:S(2)}) collective-permute-start(bf16[144,2304]{1,0:T(8,128)(2,1)S(1)} %select_select_fusion.refs_4_), channel_id=1, source_target_pairs={{0,4},{4,0},{8,12},{12,8},{16,20},{20,16},{24,28},{28,24},{1,5},{5... | collective-permute-start | bytes 1990664 | tf_op jit(solution)/shard_map/ppermute | solution.py:30
  124.1 16.5 %collective-permute-start.39 = (bf16[2,576,256]{2,1,0:T(8,128)(2,1)}, bf16[2,576,256]{2,1,0:T(8,128)(2,1)S(1)}, u32[]{:S(2)}, u32[]{:S(2)}) collective-permute-start(bf16[2,576,256]{2,1,0:T(8,128)(2,1)} %shard_map.227.refs_0_), channel_id=1, source_target_pairs={{0,2},{1,3},{2,0},{3,1},{4,6},{5,7},{6,4},{7,5},{8,10},{9,11},{10,... | collective-permute-start | bytes 1769480 | tf_op jit(solution)/shard_map/ppermute | solution.py:30
  125.8 19.5 %collective-permute-start.43 = (bf16[2,288,256]{2,1,0:T(8,128)(2,1)}, bf16[2,288,256]{2,1,0:T(8,128)(2,1)}, u32[]{:S(2)}, u32[]{:S(2)}) collective-permute-start(bf16[2,288,256]{2,1,0:T(8,128)(2,1)} %bitcast.67), channel_id=1, source_target_pairs={{0,2},{1,3},{2,0},{3,1},{4,6},{5,7},{6,4},{7,5},{8,10},{9,11},{10,... | collective-permute-start | bytes 884744 | tf_op jit(solution)/shard_map/ppermute | solution.py:30
  138.2 8.9 %copy-start = (bf16[1152,2304]{1,0:T(8,128)(2,1)}, bf16[1152,2304]{1,0:T(8,128)(2,1)S(1)}, u32[]{:S(2)}) copy-start(bf16[1152,2304]{1,0:T(8,128)(2,1)S(1)} %shard_map.228.refs_2_) | copy-start | bytes 15925252
  142.8 4.3 %collective-permute-start.42 = (bf16[2,576,256]{2,1,0:T(8,128)(2,1)S(1)}, bf16[2,576,256]{2,1,0:T(8,128)(2,1)S(1)}, u32[]{:S(2)}, u32[]{:S(2)}) collective-permute-start(bf16[2,576,256]{2,1,0:T(8,128)(2,1)S(1)} %shard_map.229), channel_id=1, source_target_pairs={{0,1},{1,0},{2,3},{3,2},{4,5},{5,4},{6,7},{7,6},{8,9},{9,8},{10,11... | collective-permute-start | bytes 1769480 | tf_op jit(solution)/shard_map/ppermute | solution.py:30
  142.8 2.6 collective-permute-start.44
  145.3 1.8 collective-permute-start.45
  160.9 7.8 %collective-permute-start = (bf16[2,576,256]{2,1,0:T(8,128)(2,1)}, bf16[2,576,256]{2,1,0:T(8,128)(2,1)}, u32[]{:S(2)}, u32[]{:S(2)}) collective-permute-start(bf16[2,576,256]{2,1,0:T(8,128)(2,1)} %get-tuple-element.105), channel_id=1, source_target_pairs={{0,1},{1,0},{2,3},{3,2},{4,5},{5,4},{6,7},{7,6},{8,9},{9,8},{10,11... | collective-permute-start | bytes 1769480 | tf_op jit(solution)/shard_map/cond/branch_1_fun/ppermute | solution.py:30
  171.6 15.8 %collective-permute-start.1 = (bf16[2,576,256]{2,1,0:T(8,128)(2,1)}, bf16[2,576,256]{2,1,0:T(8,128)(2,1)S(1)}, u32[]{:S(2)}, u32[]{:S(2)}) collective-permute-start(bf16[2,576,256]{2,1,0:T(8,128)(2,1)} %branch_1_fun.18.refs_0_), channel_id=1, source_target_pairs={{0,2},{1,3},{2,0},{3,1},{4,6},{5,7},{6,4},{7,5},{8,10},{9,11},{10,... | collective-permute-start | bytes 1769480 | tf_op jit(solution)/shard_map/cond/branch_1_fun/ppermute | solution.py:30
  190.5 2.3 collective-permute-start.2
  192.7 13.8 %copy-start.5 = (bf16[2,2,1,288,256]{4,3,2,1,0:T(8,128)(2,1)}, bf16[2,2,1,288,256]{4,3,2,1,0:T(8,128)(2,1)S(1)}, u32[]{:S(2)}) copy-start(bf16[2,2,1,288,256]{4,3,2,1,0:T(8,128)(2,1)S(1)} %get-tuple-element.343) | copy-start | bytes 1769476 | tf_op jit(solution)/shard_map/cond
  205.8 7.1 %collective-permute-start.3 = (bf16[2,576,256]{2,1,0:T(8,128)(2,1)}, bf16[2,576,256]{2,1,0:T(8,128)(2,1)}, u32[]{:S(2)}, u32[]{:S(2)}) collective-permute-start(bf16[2,576,256]{2,1,0:T(8,128)(2,1)} %get-tuple-element.126), channel_id=1, source_target_pairs={{0,1},{1,0},{2,3},{3,2},{4,5},{5,4},{6,7},{7,6},{8,9},{9,8},{10,11... | collective-permute-start | bytes 1769480 | tf_op jit(solution)/shard_map/cond/branch_1_fun/ppermute | solution.py:30
  207.4 9.8 %collective-permute-start.7 = (bf16[2,2,288,256]{3,2,0,1:T(8,128)(2,1)}, bf16[2,2,288,256]{3,2,0,1:T(8,128)(2,1)}, u32[]{:S(2)}, u32[]{:S(2)}) collective-permute-start(bf16[2,2,288,256]{3,2,0,1:T(8,128)(2,1)} %select_bitcast_fusion), channel_id=1, source_target_pairs={{0,1},{1,0},{2,3},{3,2},{4,5},{5,4},{6,7},{7,6},{8,9},{9,8},{10,11... | collective-permute-start | bytes 1769480 | tf_op jit(solution)/shard_map/cond/branch_1_fun/ppermute | solution.py:30
  215.3 18.2 %collective-permute-start.4 = (bf16[2,576,256]{2,1,0:T(8,128)(2,1)}, bf16[2,576,256]{2,1,0:T(8,128)(2,1)S(1)}, u32[]{:S(2)}, u32[]{:S(2)}) collective-permute-start(bf16[2,576,256]{2,1,0:T(8,128)(2,1)} %branch_1_fun.23.refs_0_), channel_id=1, source_target_pairs={{0,2},{1,3},{2,0},{3,1},{4,6},{5,7},{6,4},{7,5},{8,10},{9,11},{10,... | collective-permute-start | bytes 1769480 | tf_op jit(solution)/shard_map/cond/branch_1_fun/ppermute | solution.py:30
  218.4 15.1 %collective-permute-start.5 = (bf16[144,1152]{1,0:T(8,128)(2,1)S(1)}, bf16[144,1152]{1,0:T(8,128)(2,1)S(1)}, u32[]{:S(2)}, u32[]{:S(2)}) collective-permute-start(bf16[144,1152]{1,0:T(8,128)(2,1)S(1)} %copy-done.40), channel_id=1, source_target_pairs={{0,4},{4,0},{8,12},{12,8},{16,20},{20,16},{24,28},{28,24},{1,5},{5... | collective-permute-start | bytes 995336 | tf_op jit(solution)/shard_map/cond/branch_1_fun/ppermute | solution.py:30
  219.2 18.4 %collective-permute-start.8 = (bf16[2,288,256]{2,1,0:T(8,128)(2,1)S(1)}, bf16[2,288,256]{2,1,0:T(8,128)(2,1)S(1)}, u32[]{:S(2)}, u32[]{:S(2)}) collective-permute-start(bf16[2,288,256]{2,1,0:T(8,128)(2,1)S(1)} %fusion), channel_id=1, source_target_pairs={{0,2},{1,3},{2,0},{3,1},{4,6},{5,7},{6,4},{7,5},{8,10},{9,11},{10,... | collective-permute-start | bytes 884744 | tf_op jit(solution)/shard_map/cond/branch_1_fun/ppermute | solution.py:30
  237.3 6.7 %copy-start.7 = (bf16[2,1152,256]{2,1,0:T(8,128)(2,1)S(1)}, bf16[2,1152,256]{2,1,0:T(8,128)(2,1)}, u32[]{:S(2)}) copy-start(bf16[2,1152,256]{2,1,0:T(8,128)(2,1)} %get-tuple-element.139.refs_5_) | copy-start | bytes 3538948 | tf_op jit(solution)/shard_map/cond
  237.3 5.8 %collective-permute-start.6 = (bf16[2,576,256]{2,1,0:T(8,128)(2,1)}, bf16[2,576,256]{2,1,0:T(8,128)(2,1)S(1)}, u32[]{:S(2)}, u32[]{:S(2)}) collective-permute-start(bf16[2,576,256]{2,1,0:T(8,128)(2,1)} %branch_1_fun.24.refs_3_), channel_id=1, source_target_pairs={{0,1},{1,0},{2,3},{3,2},{4,5},{5,4},{6,7},{7,6},{8,9},{9,8},{10,11... | collective-permute-start | bytes 1769480 | tf_op jit(solution)/shard_map/cond/branch_1_fun/ppermute | solution.py:30
  238.6 11.4 %collective-permute-start.9 = (bf16[144,1152]{1,0:T(8,128)(2,1)S(1)}, bf16[144,1152]{1,0:T(8,128)(2,1)S(1)}, u32[]{:S(2)}, u32[]{:S(2)}) collective-permute-start(bf16[144,1152]{1,0:T(8,128)(2,1)S(1)} %copy-done.39), channel_id=1, source_target_pairs={{0,4},{4,0},{8,12},{12,8},{16,20},{20,16},{24,28},{28,24},{1,5},{5... | collective-permute-start | bytes 995336 | tf_op jit(solution)/shard_map/cond/branch_1_fun/ppermute | solution.py:30
  242.1 12.0 %collective-permute-start.10 = (bf16[144,1152]{1,0:T(8,128)(2,1)}, bf16[144,1152]{1,0:T(8,128)(2,1)}, u32[]{:S(2)}, u32[]{:S(2)}) collective-permute-start(bf16[144,1152]{1,0:T(8,128)(2,1)} %branch_1_fun.25.refs_12_), channel_id=1, source_target_pairs={{0,24},{4,28},{8,16},{12,20},{16,8},{20,12},{24,0},{28,4},{1,25},{... | collective-permute-start | bytes 995336 | tf_op jit(solution)/shard_map/cond/branch_1_fun/ppermute | solution.py:30
  249.9 17.4 %copy-start.38 = (bf16[144,1152]{1,0:T(8,128)(2,1)S(1)}, bf16[144,1152]{1,0:T(8,128)(2,1)}, u32[]{:S(2)}) copy-start(bf16[144,1152]{1,0:T(8,128)(2,1)} %get-tuple-element.134.refs_5_) | copy-start | bytes 995332 | tf_op jit(solution)/shard_map/cond
  252.6 26.5 %copy-start.9 = (bf16[144,1152]{1,0:T(8,128)(2,1)S(1)}, bf16[144,1152]{1,0:T(8,128)(2,1)}, u32[]{:S(2)}) copy-start(bf16[144,1152]{1,0:T(8,128)(2,1)} %copy-done.8) | copy-start | bytes 995332 | tf_op jit(solution)/shard_map/cond
  255.4 10.0 %collective-permute-start.11 = (bf16[2,2016]{1,0:T(2,128)(2,1)}, bf16[2,2016]{1,0:T(2,128)(2,1)S(1)}, u32[]{:S(2)}, u32[]{:S(2)}) collective-permute-start(bf16[2,2016]{1,0:T(2,128)(2,1)} %branch_1_fun.28), channel_id=1, source_target_pairs={{0,8},{4,12},{8,0},{12,4},{16,24},{20,28},{24,16},{28,20},{1,9},{5... | collective-permute-start | bytes 24200 | tf_op jit(solution)/shard_map/cond/branch_1_fun/ppermute | solution.py:30
  266.2 6.2 %collective-permute-start.12 = (bf16[2,2,2016]{2,1,0:T(2,128)(2,1)S(1)}, bf16[2,2,2016]{2,1,0:T(2,128)(2,1)S(1)}, u32[]{:S(2)}, u32[]{:S(2)}) collective-permute-start(bf16[2,2,2016]{2,1,0:T(2,128)(2,1)S(1)} %pad_maximum_fusion.1), channel_id=1, source_target_pairs={{0,16},{4,20},{8,24},{12,28},{16,0},{20,4},{24,8},{28,12},{1,17},{... | collective-permute-start | bytes 48392 | tf_op jit(solution)/shard_map/cond/branch_1_fun/ppermute | solution.py:30
  267.3 8.8 %collective-permute-start.14 = (bf16[144,1152]{1,0:T(8,128)(2,1)S(1)}, bf16[144,1152]{1,0:T(8,128)(2,1)S(1)}, u32[]{:S(2)}, u32[]{:S(2)}) collective-permute-start(bf16[144,1152]{1,0:T(8,128)(2,1)S(1)} %copy-done.38), channel_id=1, source_target_pairs={{0,4},{4,0},{8,12},{12,8},{16,20},{20,16},{24,28},{28,24},{1,5},{5... | collective-permute-start | bytes 995336 | tf_op jit(solution)/shard_map/cond/branch_1_fun/ppermute | solution.py:30
  272.5 6.2 %collective-permute-start.13 = (bf16[2,2,2,2016]{3,2,1,0:T(2,128)(2,1)S(1)}, bf16[2,2,2,2016]{3,2,1,0:T(2,128)(2,1)S(1)}, u32[]{:S(2)}, u32[]{:S(2)}) collective-permute-start(bf16[2,2,2,2016]{3,2,1,0:T(2,128)(2,1)S(1)} %pad_maximum_fusion), channel_id=1, source_target_pairs={{0,4},{4,0},{8,12},{12,8},{16,20},{20,16},{24,28},{28,24},{1,5},{5... | collective-permute-start | bytes 96776 | tf_op jit(solution)/shard_map/cond/branch_1_fun/ppermute | solution.py:30
  279.3 24.4 %collective-permute-start.46 = (bf16[144,1152]{1,0:T(8,128)(2,1)}, bf16[144,1152]{1,0:T(8,128)(2,1)S(1)}, u32[]{:S(2)}, u32[]{:S(2)}) collective-permute-start(bf16[144,1152]{1,0:T(8,128)(2,1)} %get-tuple-element.216), channel_id=1, source_target_pairs={{0,4},{4,0},{8,12},{12,8},{16,20},{20,16},{24,28},{28,24},{1,5},{5... | collective-permute-start | bytes 995336 | tf_op jit(solution)/shard_map/ppermute | solution.py:30
  279.9 23.7 %collective-permute-start.47 = (bf16[144,1152]{1,0:T(8,128)(2,1)}, bf16[144,1152]{1,0:T(8,128)(2,1)S(1)}, u32[]{:S(2)}, u32[]{:S(2)}) collective-permute-start(bf16[144,1152]{1,0:T(8,128)(2,1)} %get-tuple-element.217), channel_id=1, source_target_pairs={{0,8},{4,12},{8,0},{12,4},{16,24},{20,28},{24,16},{28,20},{1,9},{5... | collective-permute-start | bytes 995336 | tf_op jit(solution)/shard_map/ppermute | solution.py:30
  281.2 22.4 %collective-permute-start.48 = (bf16[144,1152]{1,0:T(8,128)(2,1)}, bf16[144,1152]{1,0:T(8,128)(2,1)S(1)}, u32[]{:S(2)}, u32[]{:S(2)}) collective-permute-start(bf16[144,1152]{1,0:T(8,128)(2,1)} %get-tuple-element.218), channel_id=1, source_target_pairs={{0,16},{4,20},{8,24},{12,28},{16,0},{20,4},{24,8},{28,12},{1,17},{... | collective-permute-start | bytes 995336 | tf_op jit(solution)/shard_map/ppermute | solution.py:30
  283.6 19.3 %copy-start.45 = (bf16[2,1152]{1,0:T(2,128)(2,1)S(1)}, bf16[2,1152]{1,0:T(2,128)(2,1)}, u32[]{:S(2)}) copy-start(bf16[2,1152]{1,0:T(2,128)(2,1)} %param.23) | copy-start | bytes 13828
  285.4 3.8 %collective-permute-start.18 = (f32[2448]{0:T(1024)S(1)}, f32[2448]{0:T(1024)S(1)}, u32[]{:S(2)}, u32[]{:S(2)}) collective-permute-start(f32[2448]{0:T(1024)S(1)} %pad_maximum_fusion.4), channel_id=1, source_target_pairs={{0,2},{1,3},{2,0},{3,1},{4,6},{5,7},{6,4},{7,5},{8,10},{9,11},{10,... | collective-permute-start | bytes 29384 | tf_op jit(solution)/shard_map/cond/branch_1_fun/ppermute | solution.py:30
  289.2 1.2 collective-permute-start.19
  290.5 3.7 %collective-permute-start.20 = (f32[8,144]{1,0:T(8,128)S(1)}, f32[8,144]{1,0:T(8,128)S(1)}, u32[]{:S(2)}, u32[]{:S(2)}) collective-permute-start(f32[8,144]{1,0:T(8,128)S(1)} %select_n.401), channel_id=1, source_target_pairs={{0,4},{4,0},{8,12},{12,8},{16,20},{20,16},{24,28},{28,24},{1,5},{5... | collective-permute-start | bytes 13832 | tf_op jit(solution)/shard_map/cond/branch_1_fun/ppermute | solution.py:30
  294.4 3.7 %collective-permute-start.21 = (f32[4,288]{1,0:T(4,128)S(1)}, f32[4,288]{1,0:T(4,128)S(1)}, u32[]{:S(2)}, u32[]{:S(2)}) collective-permute-start(f32[4,288]{1,0:T(4,128)S(1)} %select_n.407), channel_id=1, source_target_pairs={{0,8},{4,12},{8,0},{12,4},{16,24},{20,28},{24,16},{28,20},{1,9},{5... | collective-permute-start | bytes 13832 | tf_op jit(solution)/shard_map/cond/branch_1_fun/ppermute | solution.py:30
  298.2 4.6 %collective-permute-start.22 = (f32[2,576]{1,0:T(2,128)S(1)}, f32[2,576]{1,0:T(2,128)S(1)}, u32[]{:S(2)}, u32[]{:S(2)}) collective-permute-start(f32[2,576]{1,0:T(2,128)S(1)} %select_bitcast_fusion.1), channel_id=1, source_target_pairs={{0,16},{4,20},{8,24},{12,28},{16,0},{20,4},{24,8},{28,12},{1,17},{... | collective-permute-start | bytes 13832 | tf_op jit(solution)/shard_map/cond/branch_1_fun/ppermute | solution.py:30
  (44 other events, 92.4 us)
Sparse Core Ops, SparseCore 0:
  10.4 74.6 all-gather.1
  168.9 116.9 reduce-scatter.1

commit v7 on v6

--- a/solution.py
+++ b/solution.py
@@ -115,15 +115,11 @@
     return mp_join(chip, swap(chip, "mp", 2), *tokens)
 
 
-def mp_quarter(partial):
-    images, width, patches = partial.shape
-    quarter = width // 4
-    me = lax.axis_index("mp")
-    core, side = me % 2, me // 2
-    split = partial.reshape(images, 2, 2, quarter, patches)
-    send = jnp.where(core == 0, split[:, :, 1], split[:, :, 0])
-    keep = jnp.where(core == 0, split[:, :, 0], split[:, :, 1])
-    chip = keep.astype(F32) + swap(send, "mp", 1).astype(F32)
+def mp_quarter(mine, theirs):
+    images, rows, patches = mine.shape
+    side = lax.axis_index("mp") // 2
+    chip = mine.astype(F32) + swap(theirs, "mp", 1).astype(F32)
+    chip = chip.reshape(images, 2, rows // 2, patches)
     send = jnp.where(side == 0, chip[:, 1], chip[:, 0]).astype(BF16)
     keep = jnp.where(side == 0, chip[:, 0], chip[:, 1])
     return keep + swap(send, "mp", 2).astype(F32)
@@ -449,9 +445,16 @@
     grad_ref[:, 2 * units :] = over_images(dffn_ref, hidden_ref).astype(BF16)
 
 
-def feed_forward_end(hidden_ref, weight_ref, ffn_ref):
+def feed_forward_end(place, hidden_ref, weight_ref, outs, scratch):
+    mine_ref, theirs_ref = outs
+    (x_ref,) = scratch
+    core, quarter = place[4], mine_ref.shape[1] // 2
     for n in range(hidden_ref.shape[0]):
-        ffn_ref[n] = dot(weight_ref[...], hidden_ref[n], NN).astype(BF16)
+        x_ref[...] = dot(weight_ref[...], hidden_ref[n], NN)
+        for side in range(2):
+            rows = slice(side * quarter, (side + 1) * quarter)
+            mine_ref[n, rows] = x_ref[rows_at(2 * side + core, quarter), :].astype(BF16)
+            theirs_ref[n, rows] = x_ref[rows_at(2 * side + 1 - core, quarter), :].astype(BF16)
 
 
 def attention_backward(
@@ -802,14 +805,14 @@
 
     def backward():
         dh_two_chip = add_blocks(dh_two_mine, dh_two_other)
-        (ffn_part,) = call(
-            lambda a, outs, x: feed_forward_end(*a, *outs),
-            [[(hidden, whole), (second, last)]],
-            [(wide(BF16), whole)],
-            [],
+        ffn_terms = call(
+            lambda p, a, outs, x: feed_forward_end(p[0], *a, outs, x),
+            [[(place, scalars)], [(hidden, whole), (second, last)]],
+            [(half, whole), (half, whole)],
+            [tall],
             1,
         )
-        dh_two_sums = mp_join(dh_two_chip, swap(dh_two_chip, "mp", 2), ffn_part)
+        dh_two_sums = mp_join(dh_two_chip, swap(dh_two_chip, "mp", 2), ffn_terms[0])
         dmid, dattn, draw, mine, theirs, dmods_part, qgain, kgain = call(
             lambda p, w, s, a, outs, x: attention_backward(heads, p[0], w[0], s, *a, outs, x),
             [
@@ -851,7 +854,7 @@
             [pltpu.VMEM((width, full), F32)],
             1,
         )
-        ffn_own = mp_quarter(ffn_part)
+        ffn_own = mp_quarter(*ffn_terms)
         first_beside = dp_cross(first_terms)
         end_half = [add_blocks(first_terms[6], first_beside[3])] if on_line else []
         last_line = [swap(half_sum, "dp", 6) for half_sum in end_half]

time: 319 us -> 317 us (level)
    cond x40 -> x38, local copies, waits for them, and re-layouts: 6.17 us -> 6.79 us
where the time goes in v7:
time: 317 us; the launch traced here: 315 us
  waiting for transfers between devices  107 us (34%)
  Pallas kernels  90.5 us (29%)
  starting transfers between devices  60.8 us (19%)
  local copies, waits for them, and re-layouts  25.7 us (8%)
  between operations  14.7 us (5%)
  other arithmetic  12.8 us (4%)
  matrix products  3.3 us (1%)
    ppermute x44, waiting for transfers between devices, swap(): return lax.ppermute(value, axis, [(i, i ^ bit) for i in range(size)])  69.2 us
    pallas_call x8, Pallas kernels, call(): pl.pallas_call(kernel, grid=(images,), in_specs=specs, out_specs=[kind(o)...  61.8 us
    ppermute x44, starting transfers between devices, swap(): return lax.ppermute(value, axis, [(i, i ^ bit) for i in range(size)])  51.6 us
    ppermute x5, waiting for transfers between devices, along(): lax.ppermute(value, 'dp', [(2 * a + y, 2 * b + y) for a, b in pairs for y...  37.7 us
    pallas_call x9, Pallas kernels, add_blocks(): pl.pallas_call(kernel, in_specs=[pl.BlockSpec(memory_space=pltpu.VMEM)] *...  18.2 us
    ppermute x5, starting transfers between devices, along(): lax.ppermute(value, 'dp', [(2 * a + y, 2 * b + y) for a, b in pairs for y...  9.14 us
    unnamed x75, local copies, waits for them, and re-layouts  8.95 us
    cond x38, local copies, waits for them, and re-layouts  6.79 us
  transfers between devices with their start and end apart: 51, of which 28 were waited for; matrix products, arithmetic and copies ran while one was open for 7% of the time, Pallas kernels for 25%

profile of v7, /device:TPU:0, one launch (start us, length us, event | category | flops | bytes accessed | tf_op | source)
XLA Modules:
  0.0 315.4 jit_solution(18215064921339635252)
XLA Ops:
  8.4 1.9 concatenate.49
  10.9 17.9 %conditional.4 = (bf16[16,144]{1,0:T(8,128)(2,1)}, f32[2]{0:T(128)S(1)}, bf16[144,2304]{1,0:T(8,128)(2,1)S(1)}) conditional(s32[]{:T(128)} %bitcast.26, () %tuple.44, (s32[2]{0:T(128)S(1)}, s32[2]{0:T(128)S(1)}, bf16[2,1152]{1,0:T(2,128)(2,1)S(1)}, s32[]{:T(128)}, f32[2]{0:T(128)}, /*index=5*/bf16[144,2,768]{2,1,0:T(2,128)(2,1)S(1)}, ...), branch_computations={%region_0.1_spmd, %region_1.5_spmd} | conditional | flops 101409 | bytes 1573591 | solution.py:39
  11.3 3.0 collective-permute-start.15
  14.3 1.6 collective-permute-done.15
  16.0 3.1 collective-permute-start.16
  19.1 1.7 collective-permute-done.16
  20.8 1.9 collective-permute-start.17
  29.9 3.0 collective-permute-start.26
  33.1 5.3 %collective-permute-done.26 = f32[8,1728]{1,0:T(8,128)S(1)} collective-permute-done((f32[8,1728]{1,0:T(8,128)S(1)}, f32[8,1728]{1,0:T(8,128)S(1)}, u32[]{:S(2)}, u32[]{:S(2)}) %collective-permute-start.26) | collective-permute-done | bytes 55328 | tf_op jit(solution)/shard_map/ppermute | solution.py:30
  39.8 4.6 %collective-permute-start.32 = (bf16[144,2304]{1,0:T(8,128)(2,1)S(1)}, bf16[144,2304]{1,0:T(8,128)(2,1)S(1)}, u32[]{:S(2)}, u32[]{:S(2)}) collective-permute-start(bf16[144,2304]{1,0:T(8,128)(2,1)S(1)} %get-tuple-element.197.refs_1_), channel_id=1, source_target_pairs={{0,8},{4,12},{8,16},{12,20},{16,24},{20,28},{1,9},{5,13},{9,17},{1... | collective-permute-start | bytes 1990664 | tf_op jit(solution)/shard_map/ppermute | solution.py:133
  44.4 1.6 collective-permute-start.29
  46.6 19.1 %collective-permute-done.33.right_ref = bf16[144,2304]{1,0:T(8,128)(2,1)S(1)} collective-permute-done((bf16[144,2304]{1,0:T(8,128)(2,1)S(1)}, bf16[144,2304]{1,0:T(8,128)(2,1)S(1)}, u32[]{:S(2)}, u32[]{:S(2)}) %collective-permute-start.33) | collective-permute-done | bytes 663584 | tf_op jit(solution)/shard_map/ppermute | solution.py:133
  65.7 2.6 collective-permute-done.32.left_ref._
  69.1 2.2 shard_map.224.refs_2_
  71.4 1.5 collective-permute-start.34
  78.5 1.5 collective-permute-start.30
  80.0 14.7 %collective-permute-done.36.right_ref = bf16[144,2304]{1,0:T(8,128)(2,1)S(1)} collective-permute-done((bf16[144,2304]{1,0:T(8,128)(2,1)}, bf16[144,2304]{1,0:T(8,128)(2,1)S(1)}, u32[]{:S(2)}, u32[]{:S(2)}) %collective-permute-start.36) | collective-permute-done | bytes 663584 | tf_op jit(solution)/shard_map/ppermute | solution.py:133
  94.7 1.4 collective-permute-start.23
  97.3 2.2 shard_map.225.refs_11_.refs_3_
  104.5 11.0 %shard_map.226 = (bf16[2,1152,256]{2,1,0:T(8,128)(2,1)}, bf16[2,1152,256]{2,1,0:T(8,128)(2,1)}, f32[2,864,256]{2,1,0:T(8,128)}, f32[2,4,256]{2,1,0:T(4,128)}, bf...) custom-call(s32[13]{0:T(128)S(1)} %stack.128.refs_0_, ...), custom_call_target="tpu_custom_call" | custom-call | flops 1 | bytes 1 | tf_op jit(solution)/shard_map/pallas_call | solution.py:614
  119.0 1.9 collective-permute-done.38.refs_2_.refs_7_
  121.9 2.2 shard_map.227.refs_0_
  126.8 7.9 %collective-permute-done.41.refs_8_ = bf16[144,2304]{1,0:T(8,128)(2,1)S(1)} collective-permute-done((bf16[144,2304]{1,0:T(8,128)(2,1)S(1)}, bf16[144,2304]{1,0:T(8,128)(2,1)S(1)}, u32[]{:S(2)}, u32[]{:S(2)}) %collective-permute-start.41) | collective-permute-done | bytes 663584 | tf_op jit(solution)/shard_map/ppermute | solution.py:30
  135.5 2.6 shard_map.228.refs_2_
  138.2 2.4 collective-permute-done.39.refs_1_
  143.4 2.0 collective-permute-done.43
  145.5 1.6 collective-permute-done.45
  147.1 21.0 %conditional.5 = (f32[2,1152,256]{2,1,0:T(8,128)S(1)}, f32[2,288,256]{2,1,0:T(8,128)S(1)}, bf16[2,1152,256]{2,1,0:T(8,128)(2,1)}, bf16[2,768,256]{2,1,0:T(8,128)...) conditional(s32[]{:T(128)} %bitcast.26, () %tuple.43, ...), branch_computations={%region_5.6_spmd, %region_6.7_spmd} | conditional | flops 2 | bytes 11403338 | solution.py:39
  148.3 11.9 %branch_1_fun.16 = (f32[2,1152,256]{2,1,0:T(8,128)S(1)}, f32[2,288,256]{2,1,0:T(8,128)S(1)}, bf16[2,1152,256]{2,1,0:T(8,128)(2,1)}, bf16[2,768,256]{2,1,0:T(8,12...) custom-call(s32[13]{0:T(128)S(1)} %get-tuple-element.89.refs_0_, ...), custom_call_target="tpu_custom_call" | custom-call | flops 1 | bytes 1 | tf_op jit(solution)/shard_map/cond/branch_1_fun/pallas_call | solution.py:614
  160.4 7.6 %branch_1_fun.17 = bf16[1152,2304]{1,0:T(8,128)(2,1)} custom-call(bf16[2,1152,256]{2,1,0:T(8,128)(2,1)} %get-tuple-element.106.refs_0_, bf16[2,768,256]{2,1,0:T(8,128)(2,1)} %get-tuple-element.400.refs_1_, bf16[2,1152,256]{2,1,0:T(8,128)(2,1)} %get-tuple-element.107.refs_2_, bf16[2,1536,256]{2,1,0:T(8,128)(2,1)} %get-tuple-element.108.refs_3_), custom_call_target="tpu_custom_call" | custom-call | flops 1 | bytes 1 | tf_op jit(solution)/shard_map/cond/branch_1_fun/pallas_call | solution.py:614
  169.0 107.9 %conditional.6 = (bf16[2,288,256]{2,1,0:T(8,128)(2,1)}, bf16[2,288,256]{2,1,0:T(8,128)(2,1)}, bf16[16,2016]{1,0:T(8,128)(2,1)S(1)}, bf16[144,1152]{1,0:T(8,128)(...) conditional(s32[]{:T(128)} %bitcast.26, () %tuple.42, ...), branch_computations={%region_7.8_spmd, %region_8.11_spmd} | conditional | flops 1638519 | bytes 54956200 | solution.py:39
  169.0 2.2 branch_1_fun.18.refs_0_
  171.2 1.5 collective-permute-start.1
  172.7 4.1 %branch_1_fun.19 = (bf16[2,576,256]{2,1,0:T(8,128)(2,1)}, bf16[2,576,256]{2,1,0:T(8,128)(2,1)}) custom-call(s32[13]{0:T(128)S(1)} %get-tuple-element.109.refs_0_, bf16[2,768,256]{2,1,0:T(8,128)(2,1)} %get-tuple-element.114.refs_1_, bf16[1152,2304]{1,0:T(8,128)(2,1)} %get-tuple-element.115.refs_2_), custom_call_target="tpu_custom_call" | custom-call | flops 1 | bytes 1 | tf_op jit(solution)/shard_map/cond/branch_1_fun/pallas_call | solution.py:614
  176.8 10.3 %collective-permute-done.1.refs_1_ = bf16[2,576,256]{2,1,0:T(8,128)(2,1)S(1)} collective-permute-done((bf16[2,576,256]{2,1,0:T(8,128)(2,1)}, bf16[2,576,256]{2,1,0:T(8,128)(2,1)S(1)}, u32[]{:S(2)}, u32[]{:S(2)}) %collective-permute-start.1) | collective-permute-done | bytes 589856 | tf_op jit(solution)/shard_map/cond/branch_1_fun/ppermute | solution.py:30
  187.9 2.2 branch_1_fun.20.refs_2_
  190.8 1.6 collective-permute-done.2.refs_3_
  192.4 12.9 %branch_1_fun.21 = (f32[2,1152,256]{2,1,0:T(8,128)}, bf16[2,1152,256]{2,1,0:T(8,128)(2,1)}, bf16[2,896,256]{2,1,0:T(8,128)(2,1)}, bf16[2,576,256]{2,1,0:T(8,128)...) custom-call(s32[13]{0:T(128)S(1)} %get-tuple-element.109.refs_0_, ...), custom_call_target="tpu_custom_call" | custom-call | flops 1 | bytes 1 | tf_op jit(solution)/shard_map/cond/branch_1_fun/pallas_call | solution.py:614
  205.9 5.6 %branch_1_fun.22 = (bf16[144,1152]{1,0:T(8,128)(2,1)S(1)}, bf16[144,1152]{1,0:T(8,128)(2,1)}, bf16[144,1152]{1,0:T(8,128)(2,1)}, bf16[144,1152]{1,0:T(8,128)(2,1...) custom-call(s32[13]{0:T(128)S(1)} %get-tuple-element.109.refs_0_, ...), custom_call_target="tpu_custom_call" | custom-call | flops 1 | bytes 1 | tf_op jit(solution)/shard_map/cond/branch_1_fun/pallas_call | solution.py:614
  212.3 2.3 branch_1_fun.23.refs_0_
  214.6 1.5 collective-permute-start.4
  219.2 13.2 %collective-permute-done.5.refs_2_.refs_1_ = bf16[144,1152]{1,0:T(8,128)(2,1)S(1)} collective-permute-done((bf16[144,1152]{1,0:T(8,128)(2,1)S(1)}, bf16[144,1152]{1,0:T(8,128)(2,1)S(1)}, u32[]{:S(2)}, u32[]{:S(2)}) %collective-permute-start.5) | collective-permute-done | bytes 331808 | tf_op jit(solution)/shard_map/cond/branch_1_fun/ppermute | solution.py:30
  234.0 2.2 branch_1_fun.24.refs_3_
  239.5 1.9 branch_1_fun.25.refs_12_
  242.9 6.0 %branch_1_fun.26 = (bf16[2,288,256]{2,1,0:T(8,128)(2,1)}, bf16[2,288,256]{2,1,0:T(8,128)(2,1)}, f32[2,8,288]{2,1,0:T(8,128)}) custom-call(s32[13]{0:T(128)S(1)} %get-tuple-element.109.refs_0_, f32[2]{0:T(128)S(1)} %get-tuple-element.110.refs_1_, f32[2]{0:T(128)} %get-tuple-element.111.refs_2_, bf16[2,576,256]{2,1,0:T(8,128)(2,1)} %branch_1_fun.24.refs_3_, ...), custom_call_target="tpu_custom_call" | custom-call | flops 1 | bytes 1 | tf_op jit(solution)/shard_map/cond/branch_1_fun/pallas_call | solution.py:614
  249.6 1.9 branch_1_fun.27.refs_1_
  254.4 6.7 %collective-permute-start.11 = (bf16[2,2016]{1,0:T(2,128)(2,1)}, bf16[2,2016]{1,0:T(2,128)(2,1)S(1)}, u32[]{:S(2)}, u32[]{:S(2)}) collective-permute-start(bf16[2,2016]{1,0:T(2,128)(2,1)} %branch_1_fun.28), channel_id=1, source_target_pairs={{0,8},{4,12},{8,0},{12,4},{16,24},{20,28},{24,16},{28,20},{1,9},{5... | collective-permute-start | bytes 24200 | tf_op jit(solution)/shard_map/cond/branch_1_fun/ppermute | solution.py:30
  261.1 2.3 collective-permute-done.11
  264.1 1.5 collective-permute-start.12
  267.0 3.2 %collective-permute-done.12 = bf16[2,2,2016]{2,1,0:T(2,128)(2,1)S(1)} collective-permute-done((bf16[2,2,2016]{2,1,0:T(2,128)(2,1)S(1)}, bf16[2,2,2016]{2,1,0:T(2,128)(2,1)S(1)}, u32[]{:S(2)}, u32[]{:S(2)}) %collective-permute-start.12) | collective-permute-done | bytes 16160 | tf_op jit(solution)/shard_map/cond/branch_1_fun/ppermute | solution.py:30
  270.3 1.6 collective-permute-start.13
  271.9 1.9 collective-permute-done.14.refs_1_
  274.5 1.9 branch_1_fun.29
  276.9 1.6 collective-permute-start.46
  279.0 2.4 collective-permute-start.48
  281.4 19.3 %conditional.7 = (f32[6,144,288]{2,1,0:T(8,128)S(1)}, f32[6,288]{1,0:T(8,128)S(1)}, bf16[144]{0:T(256)(128)(2,1)S(1)}, f32[2,1152]{1,0:T(2,128)S(1)}, f32[72]{0:T(128)S(1)}, /*index=5*/f32[72]{0:T(128)S(1)}) conditional(s32[]{:T(128)} %bitcast.26, () %tuple.48, (bf16[16,2016]{1,0:T(8,128)(2,1)S(1)}, bf16[16,144]{1,0:T(8,128)(2,1)}, ...), branch_computations={%region_11.12_spmd, %region_12.15_spmd} | conditional | flops 16018473 | bytes 2418740 | solution.py:39
  283.3 1.9 collective-permute-start.18
  285.2 1.8 collective-permute-done.18
  288.3 1.6 collective-permute-start.20
  292.9 2.9 collective-permute-done.21
  296.0 2.2 collective-permute-start.22
  298.3 2.3 collective-permute-done.22
  302.4 2.4 shard_map.230
  307.0 1.6 copy.82
  (283 shorter events, 66.8 us)
Async XLA Ops:
  7.2 97.3 %all-gather.2.cloned.1.call-start = ((), (), s32[]{:S(2)}) async-start(), calls=%async_computation.1 | async-start | bytes 2985984 | tf_op jit(solution)/shard_map/all_gather | solution.py:661
  10.3 294.5 %reduce-scatter.2.cloned.1.call-start = ((), (), s32[]{:S(2)}) async-start(), calls=%async_computation.2 | async-start | bytes 5971968 | tf_op jit(solution)/shard_map/reduce_scatter | solution.py:804
  10.9 18.0 %copy-start.8 = (bf16[144,6,288]{2,0,1:T(8,128)(2,1)S(1)}, bf16[144,6,288]{2,0,1:T(8,128)(2,1)}, u32[]{:S(2)}) copy-start(bf16[144,6,288]{2,0,1:T(8,128)(2,1)} %param.26) | copy-start | bytes 1492996
  11.3 4.6 %collective-permute-start.15 = (bf16[2,1280]{1,0:T(2,128)(2,1)S(1)}, bf16[2,1280]{1,0:T(2,128)(2,1)S(1)}, u32[]{:S(2)}, u32[]{:S(2)}) collective-permute-start(bf16[2,1280]{1,0:T(2,128)(2,1)S(1)} %concatenate.33), channel_id=1, source_target_pairs={{0,8},{4,12},{8,0},{12,4},{16,24},{20,28},{24,16},{28,20},{1,9},{5... | collective-permute-start | bytes 15368 | tf_op jit(solution)/shard_map/cond/branch_1_fun/ppermute | solution.py:30
  16.0 4.8 %collective-permute-start.16 = (bf16[2,2,1280]{2,1,0:T(2,128)(2,1)S(1)}, bf16[2,2,1280]{2,1,0:T(2,128)(2,1)S(1)}, u32[]{:S(2)}, u32[]{:S(2)}) collective-permute-start(bf16[2,2,1280]{2,1,0:T(2,128)(2,1)S(1)} %pad_maximum_fusion.9), channel_id=1, source_target_pairs={{0,16},{4,20},{8,24},{12,28},{16,0},{20,4},{24,8},{28,12},{1,17},{... | collective-permute-start | bytes 30728 | tf_op jit(solution)/shard_map/cond/branch_1_fun/ppermute | solution.py:30
  20.8 3.9 %collective-permute-start.17 = (bf16[2,2,2,1280]{3,2,1,0:T(2,128)(2,1)S(1)}, bf16[2,2,2,1280]{3,2,1,0:T(2,128)(2,1)S(1)}, u32[]{:S(2)}, u32[]{:S(2)}) collective-permute-start(bf16[2,2,2,1280]{3,2,1,0:T(2,128)(2,1)S(1)} %pad_maximum_fusion.8), channel_id=1, source_target_pairs={{0,4},{4,0},{8,12},{12,8},{16,20},{20,16},{24,28},{28,24},{1,5},{5... | collective-permute-start | bytes 61448 | tf_op jit(solution)/shard_map/cond/branch_1_fun/ppermute | solution.py:30
  29.9 8.4 %collective-permute-start.26 = (f32[8,1728]{1,0:T(8,128)S(1)}, f32[8,1728]{1,0:T(8,128)S(1)}, u32[]{:S(2)}, u32[]{:S(2)}) collective-permute-start(f32[8,1728]{1,0:T(8,128)S(1)} %select_n.442), channel_id=1, source_target_pairs={{0,16},{4,20},{8,24},{12,28},{16,0},{20,4},{24,8},{28,12},{1,17},{... | collective-permute-start | bytes 165896 | tf_op jit(solution)/shard_map/ppermute | solution.py:30
  38.4 7.6 %collective-permute-start.27 = (f32[4,1728]{1,0:T(4,128)S(1)}, f32[4,1728]{1,0:T(4,128)S(1)}, u32[]{:S(2)}, u32[]{:S(2)}) collective-permute-start(f32[4,1728]{1,0:T(4,128)S(1)} %slice_select_fusion.2), channel_id=1, source_target_pairs={{0,8},{4,12},{8,0},{12,4},{16,24},{20,28},{24,16},{28,20},{1,9},{5... | collective-permute-start | bytes 82952 | tf_op jit(solution)/shard_map/ppermute | solution.py:30
  38.5 27.2 %collective-permute-start.33 = (bf16[144,2304]{1,0:T(8,128)(2,1)S(1)}, bf16[144,2304]{1,0:T(8,128)(2,1)S(1)}, u32[]{:S(2)}, u32[]{:S(2)}) collective-permute-start(bf16[144,2304]{1,0:T(8,128)(2,1)S(1)} %get-tuple-element.197.refs_1_), channel_id=1, source_target_pairs={{8,0},{12,4},{16,8},{20,12},{24,16},{28,20},{9,1},{13,5},{17,9},{2... | collective-permute-start | bytes 1990664 | tf_op jit(solution)/shard_map/ppermute | solution.py:133
  39.8 28.5 %collective-permute-start.32 = (bf16[144,2304]{1,0:T(8,128)(2,1)S(1)}, bf16[144,2304]{1,0:T(8,128)(2,1)S(1)}, u32[]{:S(2)}, u32[]{:S(2)}) collective-permute-start(bf16[144,2304]{1,0:T(8,128)(2,1)S(1)} %get-tuple-element.197.refs_1_), channel_id=1, source_target_pairs={{0,8},{4,12},{8,16},{12,20},{16,24},{20,28},{1,9},{5,13},{9,17},{1... | collective-permute-start | bytes 1990664 | tf_op jit(solution)/shard_map/ppermute | solution.py:133
  44.4 31.1 %collective-permute-start.29 = (bf16[144,2304]{1,0:T(8,128)(2,1)S(1)}, bf16[144,2304]{1,0:T(8,128)(2,1)S(1)}, u32[]{:S(2)}, u32[]{:S(2)}) collective-permute-start(bf16[144,2304]{1,0:T(8,128)(2,1)S(1)} %get-tuple-element.197.refs_1_), channel_id=1, source_target_pairs={{0,4},{4,0},{8,12},{12,8},{16,20},{20,16},{24,28},{28,24},{1,5},{5... | collective-permute-start | bytes 1990664 | tf_op jit(solution)/shard_map/ppermute | solution.py:30
  46.0 28.9 %collective-permute-start.28 = (f32[2,1728]{1,0:T(2,128)S(1)}, f32[2,1728]{1,0:T(2,128)S(1)}, u32[]{:S(2)}, u32[]{:S(2)}) collective-permute-start(f32[2,1728]{1,0:T(2,128)S(1)} %broadcast_select_fusion.21), channel_id=1, source_target_pairs={{0,4},{4,0},{8,12},{12,8},{16,20},{20,16},{24,28},{28,24},{1,5},{5... | collective-permute-start | bytes 41480 | tf_op jit(solution)/shard_map/ppermute | solution.py:30
  69.1 9.3 %copy-start.46 = (f32[6,288]{1,0:T(8,128)S(1)}, f32[6,288]{1,0:T(8,128)}, u32[]{:S(2)}) copy-start(f32[6,288]{1,0:T(8,128)} %param.27) | copy-start | bytes 20740
  71.4 24.8 %collective-permute-start.34 = (bf16[144,2304]{1,0:T(8,128)(2,1)}, bf16[144,2304]{1,0:T(8,128)(2,1)S(1)}, u32[]{:S(2)}, u32[]{:S(2)}) collective-permute-start(bf16[144,2304]{1,0:T(8,128)(2,1)} %shard_map.224.refs_2_), channel_id=1, source_target_pairs={{0,4},{4,0},{8,12},{12,8},{16,20},{20,16},{24,28},{28,24},{1,5},{5... | collective-permute-start | bytes 1990664 | tf_op jit(solution)/shard_map/ppermute | solution.py:30
  72.9 21.8 %collective-permute-start.36 = (bf16[144,2304]{1,0:T(8,128)(2,1)}, bf16[144,2304]{1,0:T(8,128)(2,1)S(1)}, u32[]{:S(2)}, u32[]{:S(2)}) collective-permute-start(bf16[144,2304]{1,0:T(8,128)(2,1)} %copy-done.9), channel_id=1, source_target_pairs={{8,0},{12,4},{16,8},{20,12},{9,1},{13,5},{17,9},{21,13},{10,2},{14... | collective-permute-start | bytes 1990664 | tf_op jit(solution)/shard_map/ppermute | solution.py:133
  74.2 22.0 %collective-permute-start.35 = (bf16[144,2304]{1,0:T(8,128)(2,1)}, bf16[144,2304]{1,0:T(8,128)(2,1)S(1)}, u32[]{:S(2)}, u32[]{:S(2)}) collective-permute-start(bf16[144,2304]{1,0:T(8,128)(2,1)} %copy-done.1), channel_id=1, source_target_pairs={{8,16},{12,20},{16,24},{20,28},{9,17},{13,21},{17,25},{21,29},{10,... | collective-permute-start | bytes 1990664 | tf_op jit(solution)/shard_map/ppermute | solution.py:133
  78.5 22.3 %collective-permute-start.30 = (f32[2,8,288]{2,1,0:T(8,128)S(1)}, f32[2,8,288]{2,1,0:T(8,128)S(1)}, u32[]{:S(2)}, u32[]{:S(2)}) collective-permute-start(f32[2,8,288]{2,1,0:T(8,128)S(1)} %pad.5), channel_id=1, source_target_pairs={{0,2},{1,3},{2,0},{3,1},{4,6},{5,7},{6,4},{7,5},{8,10},{9,11},{10,... | collective-permute-start | bytes 55304 | tf_op jit(solution)/shard_map/ppermute | solution.py:30
  80.0 24.0 %collective-permute-start.24 = (bf16[2,288,256]{2,1,0:T(8,128)(2,1)}, bf16[2,288,256]{2,1,0:T(8,128)(2,1)}, u32[]{:S(2)}, u32[]{:S(2)}) collective-permute-start(bf16[2,288,256]{2,1,0:T(8,128)(2,1)} %bitcast.141), channel_id=1, source_target_pairs={{0,1},{1,0},{2,3},{3,2},{4,5},{5,4},{6,7},{7,6},{8,9},{9,8},{10,11... | collective-permute-start | bytes 884744 | tf_op jit(solution)/shard_map/ppermute | solution.py:30
  94.7 7.9 %collective-permute-start.23 = (bf16[2,288,256]{2,1,0:T(8,128)(2,1)}, bf16[2,288,256]{2,1,0:T(8,128)(2,1)}, u32[]{:S(2)}, u32[]{:S(2)}) collective-permute-start(bf16[2,288,256]{2,1,0:T(8,128)(2,1)} %bitcast.142), channel_id=1, source_target_pairs={{0,2},{1,3},{2,0},{3,1},{4,6},{5,7},{6,4},{7,5},{8,10},{9,11},{10,... | collective-permute-start | bytes 884744 | tf_op jit(solution)/shard_map/ppermute | solution.py:30
  97.3 7.2 %copy-start.19 = (f32[3,72,256]{2,1,0:T(8,128)S(1)}, f32[3,72,256]{2,1,0:T(8,128)}, u32[]{:S(2)}) copy-start(f32[3,72,256]{2,1,0:T(8,128)} %constant.332.clone.refs_8_) | copy-start | bytes 663556
  99.5 17.6 %collective-permute-start.40 = (bf16[144,2304]{1,0:T(8,128)(2,1)}, bf16[144,2304]{1,0:T(8,128)(2,1)}, u32[]{:S(2)}, u32[]{:S(2)}) collective-permute-start(bf16[144,2304]{1,0:T(8,128)(2,1)} %shard_map.225.refs_11_.refs_3_), channel_id=1, source_target_pairs={{8,0},{12,4},{16,24},{20,28},{9,1},{13,5},{17,25},{21,29},{10,2},{... | collective-permute-start | bytes 1990664 | tf_op jit(solution)/shard_map/ppermute | solution.py:133
  100.8 1.8 collective-permute-start.31
  102.6 1.9 collective-permute-start.25
  102.9 12.7 %copy-start.15 = (f32[2,8,1152]{2,1,0:T(8,128)}, f32[2,8,1152]{2,1,0:T(8,128)S(1)}, u32[]{:S(2)}) copy-start(f32[2,8,1152]{2,1,0:T(8,128)S(1)} %reshape.139.refs_5_) | copy-start | bytes 221188
  102.9 14.2 %copy-start.2 = (bf16[144,2304]{1,0:T(8,128)(2,1)S(1)}, bf16[144,2304]{1,0:T(8,128)(2,1)}, u32[]{:S(2)}) copy-start(bf16[144,2304]{1,0:T(8,128)(2,1)} %copy-done.1) | copy-start | bytes 1990660
  102.9 14.2 %copy-start.10 = (bf16[144,2304]{1,0:T(8,128)(2,1)S(1)}, bf16[144,2304]{1,0:T(8,128)(2,1)}, u32[]{:S(2)}) copy-start(bf16[144,2304]{1,0:T(8,128)(2,1)} %copy-done.9) | copy-start | bytes 1990660
  102.9 18.0 %collective-permute-start.38 = (bf16[144,2304]{1,0:T(8,128)(2,1)}, bf16[144,2304]{1,0:T(8,128)(2,1)S(1)}, u32[]{:S(2)}, u32[]{:S(2)}) collective-permute-start(bf16[144,2304]{1,0:T(8,128)(2,1)} %shard_map.225.refs_11_.refs_3_), channel_id=1, source_target_pairs={{0,4},{4,0},{8,12},{12,8},{16,20},{20,16},{24,28},{28,24},{1,5},{5... | collective-permute-start | bytes 1990664 | tf_op jit(solution)/shard_map/ppermute | solution.py:30
  115.6 5.3 %collective-permute-start.37 = (bf16[2,576,256]{2,1,0:T(8,128)(2,1)}, bf16[2,576,256]{2,1,0:T(8,128)(2,1)S(1)}, u32[]{:S(2)}, u32[]{:S(2)}) collective-permute-start(bf16[2,576,256]{2,1,0:T(8,128)(2,1)} %get-tuple-element.200), channel_id=1, source_target_pairs={{0,1},{1,0},{2,3},{3,2},{4,5},{5,4},{6,7},{7,6},{8,9},{9,8},{10,11... | collective-permute-start | bytes 1769480 | tf_op jit(solution)/shard_map/ppermute | solution.py:30
  118.3 16.4 %copy-start.12 = (bf16[144,2304]{1,0:T(8,128)(2,1)}, bf16[144,2304]{1,0:T(8,128)(2,1)S(1)}, u32[]{:S(2)}) copy-start(bf16[144,2304]{1,0:T(8,128)(2,1)S(1)} %select_select_fusion.refs_4_) | copy-start | bytes 1990660
  118.3 16.4 %collective-permute-start.41 = (bf16[144,2304]{1,0:T(8,128)(2,1)S(1)}, bf16[144,2304]{1,0:T(8,128)(2,1)S(1)}, u32[]{:S(2)}, u32[]{:S(2)}) collective-permute-start(bf16[144,2304]{1,0:T(8,128)(2,1)S(1)} %select_select_fusion.refs_4_), channel_id=1, source_target_pairs={{0,4},{4,0},{8,12},{12,8},{16,20},{20,16},{24,28},{28,24},{1,5},{5... | collective-permute-start | bytes 1990664 | tf_op jit(solution)/shard_map/ppermute | solution.py:30
  124.1 16.5 %collective-permute-start.39 = (bf16[2,576,256]{2,1,0:T(8,128)(2,1)}, bf16[2,576,256]{2,1,0:T(8,128)(2,1)S(1)}, u32[]{:S(2)}, u32[]{:S(2)}) collective-permute-start(bf16[2,576,256]{2,1,0:T(8,128)(2,1)} %shard_map.227.refs_0_), channel_id=1, source_target_pairs={{0,2},{1,3},{2,0},{3,1},{4,6},{5,7},{6,4},{7,5},{8,10},{9,11},{10,... | collective-permute-start | bytes 1769480 | tf_op jit(solution)/shard_map/ppermute | solution.py:30
  125.5 19.8 %collective-permute-start.43 = (bf16[2,288,256]{2,1,0:T(8,128)(2,1)}, bf16[2,288,256]{2,1,0:T(8,128)(2,1)}, u32[]{:S(2)}, u32[]{:S(2)}) collective-permute-start(bf16[2,288,256]{2,1,0:T(8,128)(2,1)} %bitcast.65), channel_id=1, source_target_pairs={{0,2},{1,3},{2,0},{3,1},{4,6},{5,7},{6,4},{7,5},{8,10},{9,11},{10,... | collective-permute-start | bytes 884744 | tf_op jit(solution)/shard_map/ppermute | solution.py:30
  138.2 8.9 %copy-start = (bf16[1152,2304]{1,0:T(8,128)(2,1)}, bf16[1152,2304]{1,0:T(8,128)(2,1)S(1)}, u32[]{:S(2)}) copy-start(bf16[1152,2304]{1,0:T(8,128)(2,1)S(1)} %shard_map.228.refs_2_) | copy-start | bytes 15925252
  142.8 4.3 %collective-permute-start.42 = (bf16[2,576,256]{2,1,0:T(8,128)(2,1)S(1)}, bf16[2,576,256]{2,1,0:T(8,128)(2,1)S(1)}, u32[]{:S(2)}, u32[]{:S(2)}) collective-permute-start(bf16[2,576,256]{2,1,0:T(8,128)(2,1)S(1)} %shard_map.229), channel_id=1, source_target_pairs={{0,1},{1,0},{2,3},{3,2},{4,5},{5,4},{6,7},{7,6},{8,9},{9,8},{10,11... | collective-permute-start | bytes 1769480 | tf_op jit(solution)/shard_map/ppermute | solution.py:30
  142.9 2.6 collective-permute-start.44
  145.3 1.8 collective-permute-start.45
  160.2 7.9 %collective-permute-start = (bf16[2,576,256]{2,1,0:T(8,128)(2,1)}, bf16[2,576,256]{2,1,0:T(8,128)(2,1)}, u32[]{:S(2)}, u32[]{:S(2)}) collective-permute-start(bf16[2,576,256]{2,1,0:T(8,128)(2,1)} %get-tuple-element.105), channel_id=1, source_target_pairs={{0,1},{1,0},{2,3},{3,2},{4,5},{5,4},{6,7},{7,6},{8,9},{9,8},{10,11... | collective-permute-start | bytes 1769480 | tf_op jit(solution)/shard_map/cond/branch_1_fun/ppermute | solution.py:30
  171.2 15.8 %collective-permute-start.1 = (bf16[2,576,256]{2,1,0:T(8,128)(2,1)}, bf16[2,576,256]{2,1,0:T(8,128)(2,1)S(1)}, u32[]{:S(2)}, u32[]{:S(2)}) collective-permute-start(bf16[2,576,256]{2,1,0:T(8,128)(2,1)} %branch_1_fun.18.refs_0_), channel_id=1, source_target_pairs={{0,2},{1,3},{2,0},{3,1},{4,6},{5,7},{6,4},{7,5},{8,10},{9,11},{10,... | collective-permute-start | bytes 1769480 | tf_op jit(solution)/shard_map/cond/branch_1_fun/ppermute | solution.py:30
  176.8 15.7 %copy-start.20 = (f32[3,72,256]{2,1,0:T(8,128)S(1)}, f32[3,72,256]{2,1,0:T(8,128)}, u32[]{:S(2)}) copy-start(f32[3,72,256]{2,1,0:T(8,128)} %get-tuple-element.124.refs_11_) | copy-start | bytes 663556 | tf_op jit(solution)/shard_map/cond
  190.1 2.3 collective-permute-start.2
  205.3 6.2 %collective-permute-start.3 = (bf16[2,576,256]{2,1,0:T(8,128)(2,1)}, bf16[2,576,256]{2,1,0:T(8,128)(2,1)S(1)}, u32[]{:S(2)}, u32[]{:S(2)}) collective-permute-start(bf16[2,576,256]{2,1,0:T(8,128)(2,1)} %get-tuple-element.127), channel_id=1, source_target_pairs={{0,1},{1,0},{2,3},{3,2},{4,5},{5,4},{6,7},{7,6},{8,9},{9,8},{10,11... | collective-permute-start | bytes 1769480 | tf_op jit(solution)/shard_map/cond/branch_1_fun/ppermute | solution.py:30
  205.6 10.4 %collective-permute-start.7 = (bf16[2,576,256]{2,1,0:T(8,128)(2,1)}, bf16[2,576,256]{2,1,0:T(8,128)(2,1)}, u32[]{:S(2)}, u32[]{:S(2)}) collective-permute-start(bf16[2,576,256]{2,1,0:T(8,128)(2,1)} %get-tuple-element.142), channel_id=1, source_target_pairs={{0,1},{1,0},{2,3},{3,2},{4,5},{5,4},{6,7},{7,6},{8,9},{9,8},{10,11... | collective-permute-start | bytes 1769480 | tf_op jit(solution)/shard_map/cond/branch_1_fun/ppermute | solution.py:30
  214.6 17.8 %collective-permute-start.4 = (bf16[2,576,256]{2,1,0:T(8,128)(2,1)}, bf16[2,576,256]{2,1,0:T(8,128)(2,1)S(1)}, u32[]{:S(2)}, u32[]{:S(2)}) collective-permute-start(bf16[2,576,256]{2,1,0:T(8,128)(2,1)} %branch_1_fun.23.refs_0_), channel_id=1, source_target_pairs={{0,2},{1,3},{2,0},{3,1},{4,6},{5,7},{6,4},{7,5},{8,10},{9,11},{10,... | collective-permute-start | bytes 1769480 | tf_op jit(solution)/shard_map/cond/branch_1_fun/ppermute | solution.py:30
  217.3 15.1 %collective-permute-start.5 = (bf16[144,1152]{1,0:T(8,128)(2,1)S(1)}, bf16[144,1152]{1,0:T(8,128)(2,1)S(1)}, u32[]{:S(2)}, u32[]{:S(2)}) collective-permute-start(bf16[144,1152]{1,0:T(8,128)(2,1)S(1)} %copy-done.39), channel_id=1, source_target_pairs={{0,4},{4,0},{8,12},{12,8},{16,20},{20,16},{24,28},{28,24},{1,5},{5... | collective-permute-start | bytes 995336 | tf_op jit(solution)/shard_map/cond/branch_1_fun/ppermute | solution.py:30
  218.2 18.5 %collective-permute-start.8 = (bf16[2,288,256]{2,1,0:T(8,128)(2,1)S(1)}, bf16[2,288,256]{2,1,0:T(8,128)(2,1)S(1)}, u32[]{:S(2)}, u32[]{:S(2)}) collective-permute-start(bf16[2,288,256]{2,1,0:T(8,128)(2,1)S(1)} %fusion), channel_id=1, source_target_pairs={{0,2},{1,3},{2,0},{3,1},{4,6},{5,7},{6,4},{7,5},{8,10},{9,11},{10,... | collective-permute-start | bytes 884744 | tf_op jit(solution)/shard_map/cond/branch_1_fun/ppermute | solution.py:30
  236.2 6.7 %copy-start.5 = (bf16[2,1152,256]{2,1,0:T(8,128)(2,1)S(1)}, bf16[2,1152,256]{2,1,0:T(8,128)(2,1)}, u32[]{:S(2)}) copy-start(bf16[2,1152,256]{2,1,0:T(8,128)(2,1)} %get-tuple-element.140.refs_5_) | copy-start | bytes 3538948 | tf_op jit(solution)/shard_map/cond
  236.2 5.8 %collective-permute-start.6 = (bf16[2,576,256]{2,1,0:T(8,128)(2,1)}, bf16[2,576,256]{2,1,0:T(8,128)(2,1)S(1)}, u32[]{:S(2)}, u32[]{:S(2)}) collective-permute-start(bf16[2,576,256]{2,1,0:T(8,128)(2,1)} %branch_1_fun.24.refs_3_), channel_id=1, source_target_pairs={{0,1},{1,0},{2,3},{3,2},{4,5},{5,4},{6,7},{7,6},{8,9},{9,8},{10,11... | collective-permute-start | bytes 1769480 | tf_op jit(solution)/shard_map/cond/branch_1_fun/ppermute | solution.py:30
  237.6 11.3 %collective-permute-start.9 = (bf16[144,1152]{1,0:T(8,128)(2,1)S(1)}, bf16[144,1152]{1,0:T(8,128)(2,1)S(1)}, u32[]{:S(2)}, u32[]{:S(2)}) collective-permute-start(bf16[144,1152]{1,0:T(8,128)(2,1)S(1)} %copy-done.38), channel_id=1, source_target_pairs={{0,4},{4,0},{8,12},{12,8},{16,20},{20,16},{24,28},{28,24},{1,5},{5... | collective-permute-start | bytes 995336 | tf_op jit(solution)/shard_map/cond/branch_1_fun/ppermute | solution.py:30
  241.4 11.7 %collective-permute-start.10 = (bf16[144,1152]{1,0:T(8,128)(2,1)}, bf16[144,1152]{1,0:T(8,128)(2,1)}, u32[]{:S(2)}, u32[]{:S(2)}) collective-permute-start(bf16[144,1152]{1,0:T(8,128)(2,1)} %branch_1_fun.25.refs_12_), channel_id=1, source_target_pairs={{0,24},{4,28},{8,16},{12,20},{16,8},{20,12},{24,0},{28,4},{1,25},{... | collective-permute-start | bytes 995336 | tf_op jit(solution)/shard_map/cond/branch_1_fun/ppermute | solution.py:30
  248.8 16.8 %copy-start.37 = (bf16[144,1152]{1,0:T(8,128)(2,1)S(1)}, bf16[144,1152]{1,0:T(8,128)(2,1)}, u32[]{:S(2)}) copy-start(bf16[144,1152]{1,0:T(8,128)(2,1)} %get-tuple-element.135.refs_5_) | copy-start | bytes 995332 | tf_op jit(solution)/shard_map/cond
  251.5 25.2 %copy-start.7 = (bf16[144,1152]{1,0:T(8,128)(2,1)S(1)}, bf16[144,1152]{1,0:T(8,128)(2,1)}, u32[]{:S(2)}) copy-start(bf16[144,1152]{1,0:T(8,128)(2,1)} %copy-done.6) | copy-start | bytes 995332 | tf_op jit(solution)/shard_map/cond
  254.4 9.0 %collective-permute-start.11 = (bf16[2,2016]{1,0:T(2,128)(2,1)}, bf16[2,2016]{1,0:T(2,128)(2,1)S(1)}, u32[]{:S(2)}, u32[]{:S(2)}) collective-permute-start(bf16[2,2016]{1,0:T(2,128)(2,1)} %branch_1_fun.28), channel_id=1, source_target_pairs={{0,8},{4,12},{8,0},{12,4},{16,24},{20,28},{24,16},{28,20},{1,9},{5... | collective-permute-start | bytes 24200 | tf_op jit(solution)/shard_map/cond/branch_1_fun/ppermute | solution.py:30
  264.1 6.1 %collective-permute-start.12 = (bf16[2,2,2016]{2,1,0:T(2,128)(2,1)S(1)}, bf16[2,2,2016]{2,1,0:T(2,128)(2,1)S(1)}, u32[]{:S(2)}, u32[]{:S(2)}) collective-permute-start(bf16[2,2,2016]{2,1,0:T(2,128)(2,1)S(1)} %pad_maximum_fusion.1), channel_id=1, source_target_pairs={{0,16},{4,20},{8,24},{12,28},{16,0},{20,4},{24,8},{28,12},{1,17},{... | collective-permute-start | bytes 48392 | tf_op jit(solution)/shard_map/cond/branch_1_fun/ppermute | solution.py:30
  265.6 8.2 %collective-permute-start.14 = (bf16[144,1152]{1,0:T(8,128)(2,1)S(1)}, bf16[144,1152]{1,0:T(8,128)(2,1)S(1)}, u32[]{:S(2)}, u32[]{:S(2)}) collective-permute-start(bf16[144,1152]{1,0:T(8,128)(2,1)S(1)} %copy-done.37), channel_id=1, source_target_pairs={{0,4},{4,0},{8,12},{12,8},{16,20},{20,16},{24,28},{28,24},{1,5},{5... | collective-permute-start | bytes 995336 | tf_op jit(solution)/shard_map/cond/branch_1_fun/ppermute | solution.py:30
  270.3 6.1 %collective-permute-start.13 = (bf16[2,2,2,2016]{3,2,1,0:T(2,128)(2,1)S(1)}, bf16[2,2,2,2016]{3,2,1,0:T(2,128)(2,1)S(1)}, u32[]{:S(2)}, u32[]{:S(2)}) collective-permute-start(bf16[2,2,2,2016]{3,2,1,0:T(2,128)(2,1)S(1)} %pad_maximum_fusion), channel_id=1, source_target_pairs={{0,4},{4,0},{8,12},{12,8},{16,20},{20,16},{24,28},{28,24},{1,5},{5... | collective-permute-start | bytes 96776 | tf_op jit(solution)/shard_map/cond/branch_1_fun/ppermute | solution.py:30
  276.9 24.5 %collective-permute-start.46 = (bf16[144,1152]{1,0:T(8,128)(2,1)}, bf16[144,1152]{1,0:T(8,128)(2,1)S(1)}, u32[]{:S(2)}, u32[]{:S(2)}) collective-permute-start(bf16[144,1152]{1,0:T(8,128)(2,1)} %get-tuple-element.218), channel_id=1, source_target_pairs={{0,4},{4,0},{8,12},{12,8},{16,20},{20,16},{24,28},{28,24},{1,5},{5... | collective-permute-start | bytes 995336 | tf_op jit(solution)/shard_map/ppermute | solution.py:30
  278.5 23.0 %collective-permute-start.47 = (bf16[144,1152]{1,0:T(8,128)(2,1)}, bf16[144,1152]{1,0:T(8,128)(2,1)S(1)}, u32[]{:S(2)}, u32[]{:S(2)}) collective-permute-start(bf16[144,1152]{1,0:T(8,128)(2,1)} %get-tuple-element.219), channel_id=1, source_target_pairs={{0,8},{4,12},{8,0},{12,4},{16,24},{20,28},{24,16},{28,20},{1,9},{5... | collective-permute-start | bytes 995336 | tf_op jit(solution)/shard_map/ppermute | solution.py:30
  279.0 22.4 %collective-permute-start.48 = (bf16[144,1152]{1,0:T(8,128)(2,1)}, bf16[144,1152]{1,0:T(8,128)(2,1)S(1)}, u32[]{:S(2)}, u32[]{:S(2)}) collective-permute-start(bf16[144,1152]{1,0:T(8,128)(2,1)} %get-tuple-element.220), channel_id=1, source_target_pairs={{0,16},{4,20},{8,24},{12,28},{16,0},{20,4},{24,8},{28,12},{1,17},{... | collective-permute-start | bytes 995336 | tf_op jit(solution)/shard_map/ppermute | solution.py:30
  281.4 19.3 %copy-start.44 = (bf16[2,1152]{1,0:T(2,128)(2,1)S(1)}, bf16[2,1152]{1,0:T(2,128)(2,1)}, u32[]{:S(2)}) copy-start(bf16[2,1152]{1,0:T(2,128)(2,1)} %param.23) | copy-start | bytes 13828
  283.3 3.8 %collective-permute-start.18 = (f32[2448]{0:T(1024)S(1)}, f32[2448]{0:T(1024)S(1)}, u32[]{:S(2)}, u32[]{:S(2)}) collective-permute-start(f32[2448]{0:T(1024)S(1)} %pad_maximum_fusion.4), channel_id=1, source_target_pairs={{0,2},{1,3},{2,0},{3,1},{4,6},{5,7},{6,4},{7,5},{8,10},{9,11},{10,... | collective-permute-start | bytes 29384 | tf_op jit(solution)/shard_map/cond/branch_1_fun/ppermute | solution.py:30
  287.0 1.2 collective-permute-start.19
  288.3 3.7 %collective-permute-start.20 = (f32[8,144]{1,0:T(8,128)S(1)}, f32[8,144]{1,0:T(8,128)S(1)}, u32[]{:S(2)}, u32[]{:S(2)}) collective-permute-start(f32[8,144]{1,0:T(8,128)S(1)} %select_n.381), channel_id=1, source_target_pairs={{0,4},{4,0},{8,12},{12,8},{16,20},{20,16},{24,28},{28,24},{1,5},{5... | collective-permute-start | bytes 13832 | tf_op jit(solution)/shard_map/cond/branch_1_fun/ppermute | solution.py:30
  292.2 3.7 %collective-permute-start.21 = (f32[4,288]{1,0:T(4,128)S(1)}, f32[4,288]{1,0:T(4,128)S(1)}, u32[]{:S(2)}, u32[]{:S(2)}) collective-permute-start(f32[4,288]{1,0:T(4,128)S(1)} %select_n.387), channel_id=1, source_target_pairs={{0,8},{4,12},{8,0},{12,4},{16,24},{20,28},{24,16},{28,20},{1,9},{5... | collective-permute-start | bytes 13832 | tf_op jit(solution)/shard_map/cond/branch_1_fun/ppermute | solution.py:30
  296.0 4.6 %collective-permute-start.22 = (f32[2,576]{1,0:T(2,128)S(1)}, f32[2,576]{1,0:T(2,128)S(1)}, u32[]{:S(2)}, u32[]{:S(2)}) collective-permute-start(f32[2,576]{1,0:T(2,128)S(1)} %select_bitcast_fusion), channel_id=1, source_target_pairs={{0,16},{4,20},{8,24},{12,28},{16,0},{20,4},{24,8},{28,12},{1,17},{... | collective-permute-start | bytes 13832 | tf_op jit(solution)/shard_map/cond/branch_1_fun/ppermute | solution.py:30
  (43 other events, 88.5 us)
Sparse Core Ops, SparseCore 0:
  10.4 74.6 all-gather.1
  168.3 115.6 reduce-scatter.1
